TPU v7x, 128 devices: a whole 4x4x4 slice. The times are simulated.
128 devices in a mesh: dp: 2 (over y_lo), ctx: 16 (over x, y_hi, core), tensor: 4 (over z).
Axes of the slice: x: 4, y: 4 (y_hi: 2, y_lo: 2; y = y_hi * 2 + y_lo), z: 4, core: 2. Of those that a mesh axis runs over, the one named last changes fastest.
Arguments:
- tokens: bfloat16 [2, 8192, 2048], P('dp', 'ctx', 'tensor'), may hold values from -6 to 6
- lengths: int32 [2], P('dp'), may hold values from 2048 to 8192, as said below
- conv_first: float32 [4, 2048], P(None, 'tensor'), may hold values from -3 to 3
- conv_second: float32 [4, 2048], P(None, 'tensor'), may hold values from -3 to 3
- norm_gain: float32 [2048], replicated, may hold values from 0.1 to 1.9
- w_query: bfloat16 [2048, 2048], P(None, 'tensor'), may hold values from -0.125 to 0.125
- w_key: bfloat16 [2048, 2048], P(None, 'tensor'), may hold values from -0.125 to 0.125
- w_value: bfloat16 [2048, 2048], P(None, 'tensor'), may hold values from -0.125 to 0.125
- w_out: bfloat16 [2048, 2048], P(None, 'tensor'), may hold values from -0.5 to 0.5
- bias_table: float32 [32, 16], P(None, 'tensor'), may hold values from -8 to 260
- buckets: int32 [512], replicated, may hold values from 0 to 31, as said below
- up_gain: float32 [16, 2048], P(None, 'tensor'), may hold values from 0.1 to 1.9
- grad_out: bfloat16 [2, 8192, 2048], P('dp', 'ctx', 'tensor'), may hold values from -6 to 6
Outputs:
- update: bfloat16 [2, 8192, 2048], P('dp', 'ctx', 'tensor')
- grad_tokens: bfloat16 [2, 8192, 2048], P('dp', 'ctx', 'tensor')
- grad_w_query: float32 [2048, 2048], P(('dp', 'ctx'), 'tensor')
- grad_w_key: float32 [2048, 2048], P(('dp', 'ctx'), 'tensor')
- grad_w_value: float32 [2048, 2048], P(('dp', 'ctx'), 'tensor')
- grad_w_out: float32 [2048, 2048], P(('dp', 'ctx'), 'tensor')
Inputs may be any that keep to these rules, and one draw needn't show every extreme that they name: `lengths`: at least one document is exactly 8192 bytes long. `buckets`: non-decreasing in the distance, 0 at distance 0 and 31 at the largest distance.
All inputs are finite; a program needn't handle non-finite values.
Results may differ from a plain program's by a relative error of at most 0.03.
Values may be sent and summed in bfloat16 or wider, within the bound.
No kernel may reach another device: no remote copies, remote signals or barrier semaphores. Data moves between devices by JAX's collectives and lax.ppermute only.
A program may use at most 128 MiB of HBM per device.

v0:
```python
import math

import jax
import jax.numpy as jnp
from jax import lax
from jax.sharding import PartitionSpec as P


def passed_along(value, axis, steps):
    count = lax.axis_size(axis)
    initial, last = (max(0, -steps), min(count, count - steps))
    return lax.ppermute(value, axis, [(source, source + steps) for source in range(initial, last)])


def local(
    tokens,
    lengths,
    conv_first,
    conv_second,
    norm_gain,
    w_query,
    w_key,
    w_value,
    w_out,
    bias_table,
    buckets,
    up_gain,
    grad_out,
):
    seg_len = tokens.shape[1]
    width_loc = tokens.shape[2]
    coarse_len = seg_len // 16
    model_width = w_query.shape[0]
    heads_loc = bias_table.shape[1]
    head_size = width_loc // heads_loc
    total_keys = buckets.shape[0]
    score_scale = 1.0 / math.sqrt(head_size)
    rank_ctx = lax.axis_index("ctx")
    doc_len = lengths[0]
    positions = rank_ctx * seg_len + jnp.arange(seg_len, dtype=jnp.int32)
    byte_mask = (positions < doc_len).astype(jnp.float32)
    masked = tokens[0] * byte_mask[:, None].astype(jnp.bfloat16)
    rim_rows = passed_along(masked[seg_len - 15 :], "ctx", 1)
    shifted = jnp.concatenate([rim_rows, masked[: seg_len - 15]], axis=0).astype(jnp.float32)
    level_one = jnp.sum(shifted.reshape(seg_len // 4, 4, width_loc) * conv_first[None], axis=1)
    level_two = jnp.sum(level_one.reshape(coarse_len, 4, width_loc) * conv_second[None], axis=1)
    coarse_loc = level_two.astype(jnp.bfloat16)
    coarse = lax.all_gather(coarse_loc, "tensor", axis=1, tiled=True)
    coarse_f = coarse.astype(jnp.float32)
    inv_rms = lax.rsqrt(jnp.mean(coarse_f * coarse_f, axis=1, keepdims=True) + 1e-06)
    normed = (coarse_f * inv_rms * norm_gain[None]).astype(jnp.bfloat16)
    queries = jnp.dot(normed, w_query, preferred_element_type=jnp.float32).astype(jnp.bfloat16)
    keys_loc = jnp.dot(normed, w_key, preferred_element_type=jnp.float32).astype(jnp.bfloat16)
    values_loc = jnp.dot(normed, w_value, preferred_element_type=jnp.float32).astype(jnp.bfloat16)
    keys_all, values_all = (
        lax.all_gather(keys_loc, "ctx", axis=0, tiled=True),
        lax.all_gather(values_loc, "ctx", axis=0, tiled=True),
    )
    q_three = queries.reshape(coarse_len, heads_loc, head_size)
    k_three = keys_all.reshape(total_keys, heads_loc, head_size)
    v_three = values_all.reshape(total_keys, heads_loc, head_size)
    one_hot = (
        buckets[:, None] == jnp.arange(bias_table.shape[0], dtype=jnp.int32)[None, :]
    ).astype(jnp.float32)
    dist_bias = jnp.dot(one_hot, bias_table, precision=lax.Precision.HIGHEST)
    query_pos = rank_ctx * coarse_len + jnp.arange(coarse_len, dtype=jnp.int32)
    key_pos = jnp.arange(total_keys, dtype=jnp.int32)
    distance = query_pos[:, None] - key_pos[None, :]
    allowed = (distance >= 0) & (16 * key_pos < doc_len)[None, :]
    lookup = jnp.take(dist_bias, jnp.clip(distance, 0, total_keys - 1), axis=0)
    scores = jnp.einsum("qhd,khd->hqk", q_three, k_three, preferred_element_type=jnp.float32)
    scores = scores * score_scale + jnp.transpose(lookup, (2, 0, 1))
    scores = jnp.where(allowed[None], scores, -jnp.inf)
    row_max = jnp.max(scores, axis=2, keepdims=True)
    raised = jnp.exp(scores - row_max)
    probs = raised / jnp.sum(raised, axis=2, keepdims=True)
    probs_b = probs.astype(jnp.bfloat16)
    attended = jnp.einsum("hqk,khd->qhd", probs_b, v_three, preferred_element_type=jnp.float32)
    attended = attended.astype(jnp.bfloat16).reshape(coarse_len, width_loc)
    partial_out = jnp.einsum("id,ed->ie", attended, w_out, preferred_element_type=jnp.float32)
    outputs = lax.psum_scatter(
        partial_out.astype(jnp.bfloat16), "tensor", scatter_dimension=1, tiled=True
    ).astype(jnp.float32)
    spread = (outputs[:, None, :] * up_gain[None]).reshape(seg_len, width_loc)
    update = (spread * byte_mask[:, None]).astype(jnp.bfloat16)[None]
    weighted = grad_out[0].astype(jnp.float32) * byte_mask[:, None]
    grad_coarse_out = jnp.sum(
        weighted.reshape(coarse_len, 16, width_loc) * up_gain[None], axis=1
    ).astype(jnp.bfloat16)
    grad_out_full = lax.all_gather(grad_coarse_out, "tensor", axis=1, tiled=True)
    grad_wo = jnp.einsum("ie,id->ed", grad_out_full, attended, preferred_element_type=jnp.float32)
    grad_attended = jnp.dot(grad_out_full, w_out, preferred_element_type=jnp.float32).astype(
        jnp.bfloat16
    )
    ga_three = grad_attended.reshape(coarse_len, heads_loc, head_size)
    at_three = attended.reshape(coarse_len, heads_loc, head_size)
    dprob = jnp.einsum("qhd,khd->hqk", ga_three, v_three, preferred_element_type=jnp.float32)
    row_dot = jnp.sum(ga_three.astype(jnp.float32) * at_three.astype(jnp.float32), axis=2).T
    soft_grad = (probs * (dprob - row_dot[:, :, None])).astype(jnp.bfloat16)
    grad_queries = (
        jnp.einsum("hqk,khd->qhd", soft_grad, k_three, preferred_element_type=jnp.float32)
        * score_scale
    )
    grad_queries = grad_queries.astype(jnp.bfloat16).reshape(coarse_len, width_loc)
    term_key = (
        jnp.einsum("hqk,qhd->khd", soft_grad, q_three, preferred_element_type=jnp.float32)
        * score_scale
    )
    term_value = jnp.einsum("hqk,qhd->khd", probs_b, ga_three, preferred_element_type=jnp.float32)
    key_value_grads = lax.psum_scatter(
        jnp.concatenate(
            [
                term_key.reshape(lax.axis_size("ctx") * coarse_len, width_loc),
                term_value.reshape(lax.axis_size("ctx") * coarse_len, width_loc),
            ],
            axis=1,
        ).astype(jnp.bfloat16),
        "ctx",
        scatter_dimension=0,
        tiled=True,
    ).astype(jnp.float32)
    grad_keys = key_value_grads[:, :width_loc].astype(jnp.bfloat16)
    grad_values = key_value_grads[:, width_loc:].astype(jnp.bfloat16)
    grad_normed_part = jnp.einsum(
        "ic,dc->id", grad_queries, w_query, preferred_element_type=jnp.float32
    )
    grad_normed_part = grad_normed_part + jnp.einsum(
        "ic,dc->id", grad_keys, w_key, preferred_element_type=jnp.float32
    )
    grad_normed_part = grad_normed_part + jnp.einsum(
        "ic,dc->id", grad_values, w_value, preferred_element_type=jnp.float32
    )
    cube_rms = inv_rms * inv_rms * inv_rms
    grad_normed = lax.psum(grad_normed_part.astype(jnp.bfloat16), "tensor").astype(jnp.float32)
    gained = grad_normed * norm_gain[None]
    row_dots = jnp.sum(gained * coarse_f, axis=1, keepdims=True)
    grad_full = inv_rms * gained - coarse_f * cube_rms * row_dots / model_width
    grad_coarse = lax.dynamic_slice_in_dim(
        grad_full, lax.axis_index("tensor") * width_loc, width_loc, 1
    )
    grad_level_one = (grad_coarse[:, None, :] * conv_second[None]).reshape(seg_len // 4, width_loc)
    grad_shifted = (grad_level_one[:, None, :] * conv_first[None]).reshape(seg_len, width_loc)
    lead_rows = passed_along(grad_shifted[:15], "ctx", -1)
    grad_masked = jnp.concatenate([grad_shifted[15:], lead_rows], axis=0)
    grad_tokens = (grad_masked * byte_mask[:, None]).astype(jnp.bfloat16)[None]
    grad_wq = jnp.einsum("id,ic->dc", normed, grad_queries, preferred_element_type=jnp.float32)
    grad_wk = jnp.einsum("id,ic->dc", normed, grad_keys, preferred_element_type=jnp.float32)
    grad_wv = jnp.einsum("id,ic->dc", normed, grad_values, preferred_element_type=jnp.float32)
    summed = (
        lax.psum_scatter(
            grad_wq.astype(jnp.bfloat16), ("dp", "ctx"), scatter_dimension=0, tiled=True
        ).astype(jnp.float32),
        lax.psum_scatter(
            grad_wk.astype(jnp.bfloat16), ("dp", "ctx"), scatter_dimension=0, tiled=True
        ).astype(jnp.float32),
        lax.psum_scatter(
            grad_wv.astype(jnp.bfloat16), ("dp", "ctx"), scatter_dimension=0, tiled=True
        ).astype(jnp.float32),
        lax.psum_scatter(
            grad_wo.astype(jnp.bfloat16), ("dp", "ctx"), scatter_dimension=0, tiled=True
        ).astype(jnp.float32),
    )
    return (update, grad_tokens, summed[0], summed[1], summed[2], summed[3])


def solution(mesh):
    in_specs = (
        P("dp", "ctx", "tensor"),
        P("dp"),
        P(None, "tensor"),
        P(None, "tensor"),
        P(),
        P(None, "tensor"),
        P(None, "tensor"),
        P(None, "tensor"),
        P(None, "tensor"),
        P(None, "tensor"),
        P(),
        P(None, "tensor"),
        P("dp", "ctx", "tensor"),
    )
    out_specs = (
        P("dp", "ctx", "tensor"),
        P("dp", "ctx", "tensor"),
        P(("dp", "ctx"), "tensor"),
        P(("dp", "ctx"), "tensor"),
        P(("dp", "ctx"), "tensor"),
        P(("dp", "ctx"), "tensor"),
    )
    return jax.shard_map(local, mesh=mesh, in_specs=in_specs, out_specs=out_specs, check_vma=False)
```

profile of v0, /device:TPU:1, one launch (start us, length us, event | category | flops | bytes accessed | tf_op | source)
XLA Modules:
  0.0 840.1 jit_solution(8918217934594176441)
XLA Ops:
  9.2 6.2 collective-permute-start
  17.4 54.5 %gather_fusion = f32[16384,4]{1,0:T(8,128)} fusion(f32[512,4]{1,0:T(8,128)S(1)} %fusion.25, s32[16384]{0:T(1024)S(1)} %broadcast_clamp_fusion), kind=kCustom, calls=%fused_computation | custom fusion | bytes 589824 | tf_op jit(solution)/shard_map/jit(_take)/gather | solution.py:70
  71.9 5.3 copy.54
  78.3 1.6 reshape.324
  82.5 10.4 %all_gather.12 = bf16[32,2048]{1,0:T(8,128)(2,1)S(1)} all-gather(bf16[32,512]{1,0:T(8,128)(2,1)S(1)} %multiply_reduce_fusion.3), channel_id=1, replica_groups=mesh['dp'=2,'ctx'=16,'tensor'=4] {'tensor'}, dimensions={1}, use_global_device_ids=true | all-gather | bytes 163840 | tf_op jit(solution)/shard_map/all_gather | solution.py:48
  93.6 2.1 fusion.10
  96.3 25.8 %all_gather.14 = bf16[512,512]{1,0:T(8,128)(2,1)S(1)} all-gather(bf16[32,512]{1,0:T(8,128)(2,1)S(1)} %convolution_convert_fusion.8), channel_id=1, replica_groups=mesh['dp'=2,'ctx'=16,'tensor'=4] {'ctx'}, dimensions={0}, use_global_device_ids=true | all-gather | bytes 557056 | tf_op jit(solution)/shard_map/all_gather | solution.py:56
  124.3 20.7 %all_gather.13 = bf16[512,512]{1,0:T(8,128)(2,1)S(1)} all-gather(bf16[32,512]{1,0:T(8,128)(2,1)S(1)} %convolution_convert_fusion.10), channel_id=1, replica_groups=mesh['dp'=2,'ctx'=16,'tensor'=4] {'ctx'}, dimensions={0}, use_global_device_ids=true | all-gather | bytes 557056 | tf_op jit(solution)/shard_map/all_gather | solution.py:57
  145.0 1.7 convolution_convert_fusion.6
  146.7 2.1 convolution_convert_fusion.4
  149.5 16.2 %reduce-scatter.9.cloned.1.call-done = bf16[32,512]{1,0:T(8,128)(2,1)} async-done(((bf16[32,2048]{1,0:T(8,128)(2,1)}), bf16[32,512]{1,0:T(8,128)(2,1)}) %reduce-scatter.9.cloned.1.call-update) | async-done | bytes 32784 | tf_op jit(solution)/shard_map/reduce_scatter | solution.py:81
  166.5 2.3 fusion.15
  168.8 9.2 %all_gather.15 = bf16[32,2048]{1,0:T(8,128)(2,1)S(1)} all-gather(bf16[32,512]{1,0:T(8,128)(2,1)S(1)} %get-tuple-element.8), channel_id=1, replica_groups=mesh['dp'=2,'ctx'=16,'tensor'=4] {'tensor'}, dimensions={1}, use_global_device_ids=true | all-gather | bytes 163840 | tf_op jit(solution)/shard_map/all_gather | solution.py:90
  183.7 2.3 fusion.38
  186.0 66.0 %reduce-scatter.19.cloned.1.call-done = bf16[32,1024]{1,0:T(8,128)(2,1)} async-done(((bf16[512,1024]{1,0:T(8,128)(2,1)}), bf16[32,1024]{1,0:T(8,128)(2,1)}) %reduce-scatter.19.cloned.1.call-update) | async-done | bytes 65552
  252.0 2.5 convolution_add_fusion.1
  255.9 2.2 convolution_convert_fusion.3
  258.2 2.1 convolution_convert_fusion
  260.3 2.1 convolution_convert_fusion.2
  262.6 2.1 convolution_convert_fusion.1
  264.8 31.6 %all-reduce.2.cloned.1.call-done = bf16[32,2048]{1,0:T(8,128)(2,1)} async-done(((bf16[32,2048]{1,0:T(8,128)(2,1)}), bf16[32,2048]{1,0:T(8,128)(2,1)}) %all-reduce.2.cloned.1.call-update) | async-done | bytes 131088 | tf_op jit(solution)/shard_map/psum | solution.py:134
  298.9 1.6 mul.291
  300.5 4.8 collective-permute-start.1
  305.4 4.1 collective-permute-done.1
  310.6 120.4 %reduce-scatter.11.cloned.1.call-done = bf16[64,512]{1,0:T(8,128)(2,1)} async-done(((bf16[2048,512]{1,0:T(8,128)(2,1)}), bf16[64,512]{1,0:T(8,128)(2,1)}) %reduce-scatter.11.cloned.1.call-update) | async-done | bytes 65552 | tf_op jit(solution)/shard_map/reduce_scatter | solution.py:150
  431.0 1.5 convert_element_type.177
  432.5 132.0 %reduce-scatter.17.cloned.1.call-done = bf16[64,512]{1,0:T(8,128)(2,1)} async-done(((bf16[2048,512]{1,0:T(8,128)(2,1)}), bf16[64,512]{1,0:T(8,128)(2,1)}) %reduce-scatter.17.cloned.1.call-update) | async-done | bytes 65552 | tf_op jit(solution)/shard_map/reduce_scatter | solution.py:159
  564.4 1.5 convert_element_type.183
  566.0 132.1 %reduce-scatter.13.cloned.1.call-done = bf16[64,512]{1,0:T(8,128)(2,1)} async-done(((bf16[2048,512]{1,0:T(8,128)(2,1)}), bf16[64,512]{1,0:T(8,128)(2,1)}) %reduce-scatter.13.cloned.1.call-update) | async-done | bytes 65552 | tf_op jit(solution)/shard_map/reduce_scatter | solution.py:153
  698.1 1.5 convert_element_type.179
  699.6 132.2 %reduce-scatter.15.cloned.1.call-done = bf16[64,512]{1,0:T(8,128)(2,1)} async-done(((bf16[2048,512]{1,0:T(8,128)(2,1)}), bf16[64,512]{1,0:T(8,128)(2,1)}) %reduce-scatter.15.cloned.1.call-update) | async-done | bytes 65552 | tf_op jit(solution)/shard_map/reduce_scatter | solution.py:156
  831.8 1.5 convert_element_type.181
  (113 shorter events, 22.6 us)
Async XLA Ops:
  7.2 139.5 %copy-start = (bf16[2048,512]{1,0:T(8,128)(2,1)S(1)}, bf16[2048,512]{1,0:T(8,128)(2,1)}, u32[]{:S(2)}) copy-start(bf16[2048,512]{1,0:T(8,128)(2,1)} %param.21) | copy-start | bytes 6291460
  7.2 158.5 %reduce-scatter.9.cloned.1.call-start = ((), (), s32[]{:S(2)}) async-start(), calls=%async_computation.6 | async-start | bytes 163840 | tf_op jit(solution)/shard_map/reduce_scatter | solution.py:81
  9.2 62.6 %copy-start.5 = (bf16[512,512]{1,0:T(8,128)(2,1)}, bf16[512,512]{1,0:T(8,128)(2,1)S(1)}, u32[]{:S(2)}) copy-start(bf16[512,512]{1,0:T(8,128)(2,1)S(1)} %bitcast_multiply_fusion.1) | copy-start | bytes 1572868
  9.2 67.9 %collective-permute-start = (bf16[15,512]{1,0:T(8,128)(2,1)S(1)}, bf16[15,512]{1,0:T(8,128)(2,1)S(1)}, u32[]{:S(2)}, u32[]{:S(2)}) collective-permute-start(bf16[15,512]{1,0:T(8,128)(2,1)S(1)} %slice.28), channel_id=1, source_target_pairs={{0,4},{4,8},{8,12},{12,16},{16,20},{20,24},{24,28},{28,32},{32,36}... | collective-permute-start | bytes 46088 | tf_op jit(solution)/shard_map/ppermute | solution.py:12
  71.9 5.3 slice-start
  77.2 2.7 copy-start.21
  78.3 4.0 copy-start.22
  78.3 15.3 %copy-start.11 = (f32[2048]{0:T(1024)S(1)}, f32[2048]{0:T(1024)}, u32[]{:S(2)}) copy-start(f32[2048]{0:T(1024)} %param.17) | copy-start | bytes 24580
  82.3 13.4 %copy-start.3 = (bf16[2048,512]{1,0:T(8,128)(2,1)S(1)}, bf16[2048,512]{1,0:T(8,128)(2,1)}, u32[]{:S(2)}) copy-start(bf16[2048,512]{1,0:T(8,128)(2,1)} %param.19) | copy-start | bytes 6291460
  93.6 30.2 %copy-start.24 = (f32[32]{0:T(128)}, f32[32]{0:T(128)S(1)}, u32[]{:S(2)}) copy-start(f32[32]{0:T(128)S(1)} %get-tuple-element.13) | copy-start | bytes 388
  93.6 28.5 %copy-start.19 = (pred[32,512]{1,0:T(8,128)(4,1)S(1)}, pred[32,512]{1,0:T(8,128)(4,1)}, u32[]{:S(2)}) copy-start(pred[32,512]{1,0:T(8,128)(4,1)} %get-tuple-element.14) | copy-start | bytes 49156
  93.6 28.5 %copy-start.20 = (pred[32,512]{1,0:T(8,128)(4,1)S(1)}, pred[32,512]{1,0:T(8,128)(4,1)}, u32[]{:S(2)}) copy-start(pred[32,512]{1,0:T(8,128)(4,1)} %get-tuple-element.15) | copy-start | bytes 49156
  95.8 28.0 %copy-start.14 = (bf16[4,4,8,128]{3,2,1,0:T(8,128)(2,1)}, bf16[4,4,8,128]{3,2,1,0:T(8,128)(2,1)S(1)}, u32[]{:S(2)}) copy-start(bf16[4,4,8,128]{3,2,1,0:T(8,128)(2,1)S(1)} %fusion.10) | copy-start | bytes 98308
  95.8 28.0 %copy-start.1 = (bf16[2048,512]{1,0:T(8,128)(2,1)S(1)}, bf16[2048,512]{1,0:T(8,128)(2,1)}, u32[]{:S(2)}) copy-start(bf16[2048,512]{1,0:T(8,128)(2,1)} %param.20) | copy-start | bytes 6291460
  122.1 22.9 %copy-start.6 = (bf16[512,512]{1,0:T(8,128)(2,1)}, bf16[512,512]{1,0:T(8,128)(2,1)S(1)}, u32[]{:S(2)}) copy-start(bf16[512,512]{1,0:T(8,128)(2,1)S(1)} %all_gather.14) | copy-start | bytes 1572868
  145.0 21.5 %copy-start.8 = (bf16[512,512]{1,0:T(8,128)(2,1)}, bf16[512,512]{1,0:T(8,128)(2,1)S(1)}, u32[]{:S(2)}) copy-start(bf16[512,512]{1,0:T(8,128)(2,1)S(1)} %all_gather.13) | copy-start | bytes 1572868
  145.0 21.5 %copy-start.7 = (bf16[1,512,512]{2,1,0:T(8,128)(2,1)S(1)}, bf16[1,512,512]{2,1,0:T(8,128)(2,1)}, u32[]{:S(2)}) copy-start(bf16[1,512,512]{2,1,0:T(8,128)(2,1)} %param.25) | copy-start | bytes 1572868
  148.8 103.1 %reduce-scatter.19.cloned.1.call-start = ((), (), s32[]{:S(2)}) async-start(), calls=%async_computation.12 | async-start | bytes 1114112
  166.5 12.0 %copy-start.12 = (bf16[4,128,32]{1,2,0:T(8,128)(2,1)S(1)}, bf16[4,128,32]{1,2,0:T(8,128)(2,1)}, u32[]{:S(2)}) copy-start(bf16[4,128,32]{1,2,0:T(8,128)(2,1)} %convolution_convert_fusion.6) | copy-start | bytes 98308
  166.5 12.1 %copy-start.26 = (f32[4,32]{1,0:T(4,128)S(1)}, f32[4,32]{1,0:T(4,128)}, u32[]{:S(2)}) copy-start(f32[4,32]{1,0:T(4,128)} %get-tuple-element.16) | copy-start | bytes 1540
  168.8 11.1 %copy-start.9 = (bf16[512,512]{1,0:T(8,128)(2,1)S(1)}, bf16[512,512]{1,0:T(8,128)(2,1)}, u32[]{:S(2)}) copy-start(bf16[512,512]{1,0:T(8,128)(2,1)} %copy-done.8) | copy-start | bytes 1572868
  168.8 11.1 %copy-start.17 = (f32[4,32,512]{2,1,0:T(8,128)S(1)}, f32[4,32,512]{2,1,0:T(8,128)}, u32[]{:S(2)}) copy-start(f32[4,32,512]{2,1,0:T(8,128)} %get-tuple-element.17) | copy-start | bytes 786436
  182.3 114.1 %all-reduce.2.cloned.1.call-start = ((), (), s32[]{:S(2)}) async-start(), calls=%async_computation.7 | async-start | bytes 262144 | tf_op jit(solution)/shard_map/psum | solution.py:134
  186.0 70.0 %copy-start.25 = (f32[32]{0:T(128)S(1)}, f32[32]{0:T(128)}, u32[]{:S(2)}) copy-start(f32[32]{0:T(128)} %copy-done.24) | copy-start | bytes 388
  255.9 175.1 %reduce-scatter.11.cloned.1.call-start = ((), (), s32[]{:S(2)}) async-start(), calls=%async_computation.8 | async-start | bytes 2162688 | tf_op jit(solution)/shard_map/reduce_scatter | solution.py:150
  258.1 306.3 %reduce-scatter.17.cloned.1.call-start = ((), (), s32[]{:S(2)}) async-start(), calls=%async_computation.11 | async-start | bytes 2162688 | tf_op jit(solution)/shard_map/reduce_scatter | solution.py:159
  260.3 437.8 %reduce-scatter.13.cloned.1.call-start = ((), (), s32[]{:S(2)}) async-start(), calls=%async_computation.9 | async-start | bytes 2162688 | tf_op jit(solution)/shard_map/reduce_scatter | solution.py:153
  262.5 35.0 %copy-start.27 = (f32[32]{0:T(128)S(1)}, f32[32]{0:T(128)}, u32[]{:S(2)}) copy-start(f32[32]{0:T(128)} %get-tuple-element.12) | copy-start | bytes 388
  262.5 569.2 %reduce-scatter.15.cloned.1.call-start = ((), (), s32[]{:S(2)}) async-start(), calls=%async_computation.10 | async-start | bytes 2162688 | tf_op jit(solution)/shard_map/reduce_scatter | solution.py:156
  264.7 32.9 %copy-start.23 = (f32[4,512]{1,0:T(4,128)S(1)}, f32[4,512]{1,0:T(4,128)}, u32[]{:S(2)}) copy-start(f32[4,512]{1,0:T(4,128)} %param.16) | copy-start | bytes 24580
  300.5 9.0 %copy-start.4 = (f32[32,16,512]{2,1,0:T(8,128)S(1)}, f32[32,16,512]{2,1,0:T(8,128)}, u32[]{:S(2)}) copy-start(f32[32,16,512]{2,1,0:T(8,128)} %get-tuple-element.9) | copy-start | bytes 3145732
  300.5 9.0 %collective-permute-start.1 = (f32[15,512]{1,0:T(8,128)S(1)}, f32[15,512]{1,0:T(8,128)S(1)}, u32[]{:S(2)}, u32[]{:S(2)}) collective-permute-start(f32[15,512]{1,0:T(8,128)S(1)} %slice.33), channel_id=1, source_target_pairs={{4,0},{8,4},{12,8},{16,12},{20,16},{24,20},{28,24},{32,28},{36,32}... | collective-permute-start | bytes 92168 | tf_op jit(solution)/shard_map/ppermute | solution.py:12
  (6 other events, 11.1 us)
Sparse Core Ops, SparseCore 0:
  149.0 16.6 reduce-scatter.8
  182.4 69.4 reduce-scatter.18
  256.0 40.3 all-reduce.1
  298.8 132.1 reduce-scatter.10
  433.2 131.2 reduce-scatter.16
  566.8 131.2 reduce-scatter.12
  700.5 131.2 reduce-scatter.14
where the time goes:
time: 845 us; the launch traced here: 840 us
  waiting for transfers between devices  635 us (75%)
  blocking collectives  66.2 us (8%)
  local copies, waits for them, and re-layouts  66 us (8%)
  matrix products  26.5 us (3%)
  other arithmetic  20.1 us (2%)
  between operations  15.4 us (2%)
  starting transfers between devices  11.3 us (1%)
    reduce_scatter x1, waiting for transfers between devices, local(): lax.psum_scatter(grad_wv.astype(jnp.bfloat16), ('dp', 'ctx'), scatter_dim...  132 us
    reduce_scatter x1, waiting for transfers between devices, local(): lax.psum_scatter(grad_wk.astype(jnp.bfloat16), ('dp', 'ctx'), scatter_dim...  132 us
    reduce_scatter x1, waiting for transfers between devices, local(): lax.psum_scatter(grad_wo.astype(jnp.bfloat16), ('dp', 'ctx'), scatter_dim...  132 us
    reduce_scatter x1, waiting for transfers between devices, local(): lax.psum_scatter(grad_wq.astype(jnp.bfloat16), ('dp', 'ctx'), scatter_dim...  120 us
    unnamed x8, waiting for transfers between devices  66.1 us
    gather x2, local copies, waits for them, and re-layouts, local(): lookup = jnp.take(dist_bias, jnp.clip(distance, 0, total_keys - 1), axis=0)  59.8 us
    psum x1, waiting for transfers between devices, local(): lax.psum(grad_normed_part.astype(jnp.bfloat16), 'tensor')  31.6 us
    all_gather x1, blocking collectives, local(): lax.all_gather(keys_loc, 'ctx', axis=0, tiled=True)  25.8 us
  transfers between devices with their start and end apart: 9, of which 8 were waited for; matrix products, arithmetic and copies ran while one was open for 10% of the time, Pallas kernels for 0%

commit v1 on v0

v1 whole, which is shorter than its diff:
```python
import math

import jax
import jax.numpy as jnp
import numpy as np
from jax import lax
from jax.experimental import pallas as pl
from jax.experimental.pallas import tpu as pltpu
from jax.sharding import Mesh, PartitionSpec as P

F32 = jnp.float32
BF16 = jnp.bfloat16
NEG = float("-inf")
D = 2048
WL = 512
LC = 512
CL = 32
SEG = 512
HD = 128
NH = 4
SCALE = 1.0 / math.sqrt(HD)
ROWS = CL + 16
VM = pltpu.VMEM
SM = pltpu.SMEM


def dg(a, b, ca, cb):
    return lax.dot_general(a, b, (((ca,), (cb,)), ((), ())), preferred_element_type=F32)


def tap_weights(first, second):
    taps = jnp.concatenate([second[a : a + 1] * first for a in range(4)], axis=0)
    return jnp.concatenate([taps[15:16], taps[:15]], axis=0)


def byte_mask(ctx, doc_len):
    pos = ctx * SEG + 16 * lax.broadcasted_iota(jnp.int32, (CL, 16, WL), 0)
    pos = pos + lax.broadcasted_iota(jnp.int32, (CL, 16, WL), 1)
    return (pos < doc_len).astype(F32)


def before_kernel(sc, tokens, grad_out, first, second, up_gain, part, last, gco, shift):
    mask = byte_mask(sc[0], sc[1])
    taps = tap_weights(first[...], second[...])
    u = lax.broadcasted_iota(jnp.int32, (CL, 16, WL), 1)
    prod = tokens[...].astype(F32).reshape(CL, 16, WL) * mask * taps[None]
    own = jnp.sum(jnp.where(u == 0, prod, 0.0), axis=1)
    onward = jnp.sum(jnp.where(u == 0, 0.0, prod), axis=1)
    shift[0:8] = jnp.zeros((8, WL), F32)
    shift[8 : 8 + CL] = onward
    part[...] = own + shift[7 : 7 + CL]
    last[...] = jnp.broadcast_to(shift[7 + CL : 8 + CL], (8, WL))
    weighted = grad_out[...].astype(F32).reshape(CL, 16, WL) * mask * up_gain[...][None]
    gco[...] = jnp.sum(weighted, axis=1).astype(BF16)


def bias_kernel(near, table, strip):
    n = near.shape[1]
    which = near[0:1]
    for h in range(NH):
        row = jnp.full((1, n), NEG, F32)
        for b in range(table.shape[0]):
            row = jnp.where(which == b, table[b, h], row)
        rolled = pltpu.roll(jnp.broadcast_to(row, (128, n)), 0, 1, stride=1, stride_axis=0)
        strip[h] = rolled[:, :LC]


def middle_kernel(
    sc, own, rec, gain, wq, wk, wv, wo, strip,
    msg1, msg2, msg3, keep, cz, inv_out, dw_own, dw_send,
    nrm, gco, q, k, v, ga, att, gq, gk, gv, inv, acck, accv, tile,
):
    core, ctx, dp, z, doc_len = sc[0], sc[1], sc[2], sc[3], sc[4]

    def spread(i, carry):
        for src, c in ((own, core), (rec, 1 - core)):
            rows = pl.ds(pl.multiple_of((i * 2 + c) * CL, CL), CL)
            blocks = [src[i * 4 + t, 0:CL].astype(F32) for t in range(4)]
            total = sum(jnp.sum(b * b, axis=1, keepdims=True) for b in blocks)
            r = lax.rsqrt(total * (1.0 / D) + 1e-6)
            inv[rows] = jnp.broadcast_to(r, (CL, 128))
            for t in range(4):
                cols = slice(t * WL, t * WL + WL)
                nrm[rows, cols] = (blocks[t] * r * gain[0:1, cols]).astype(BF16)
                gco[rows, cols] = src[i * 4 + t, CL : 2 * CL]
        return carry

    lax.fori_loop(0, 8, spread, 0)

    def project(i, carry):
        rows = pl.ds(pl.multiple_of(i * 256, 256), 256)
        for dst, src, w in ((q, nrm, wq), (k, nrm, wk), (v, nrm, wv), (ga, gco, wo)):
            dst[rows] = jnp.dot(src[rows], w[...], preferred_element_type=F32).astype(BF16)
        return carry

    lax.fori_loop(0, 2, project, 0)

    key_pos = lax.broadcasted_iota(jnp.int32, (1, LC), 1)
    key_mask = jnp.where(16 * key_pos < doc_len, 0.0, NEG)

    def head(h, carry):
        cols = pl.ds(pl.multiple_of(h * HD, HD), HD)
        for b in (3, 2, 1, 0):
            rows = slice(b * 128, b * 128 + 128)
            n = b * 128 + 128
            qb, gb, kb, vb = q[rows, cols], ga[rows, cols], k[0:n, cols], v[0:n, cols]
            s = dg(qb, kb, 1, 1) * SCALE + strip[h, :, LC - n :] + key_mask[:, :n]
            e = jnp.exp(s - jnp.max(s, axis=1, keepdims=True))
            p = e * (1.0 / jnp.sum(e, axis=1, keepdims=True))
            pb = p.astype(BF16)
            ab = jnp.dot(pb, vb, preferred_element_type=F32).astype(BF16)
            att[rows, cols] = ab
            dot = jnp.sum(gb.astype(F32) * ab.astype(F32), axis=1, keepdims=True)
            sg = (p * (dg(gb, vb, 1, 1) - dot)).astype(BF16)
            gq[rows, cols] = (jnp.dot(sg, kb, preferred_element_type=F32) * SCALE).astype(BF16)
            tk = dg(sg, qb, 0, 0)
            tv = dg(pb, gb, 0, 0)
            if b == 3:
                acck[...] = tk
                accv[...] = tv
            else:
                acck[0:n] += tk
                accv[0:n] += tv
        gk[0:LC, cols] = (acck[...] * SCALE).astype(BF16)
        gv[0:LC, cols] = accv[...].astype(BF16)
        return carry

    lax.fori_loop(0, NH, head, 0)
    for g in (gq, gk, gv):
        g[LC : LC + 16] = jnp.zeros((16, WL), BF16)
    inv[LC : LC + 16] = jnp.zeros((16, 128), F32)

    half = pl.ds(pl.multiple_of(core * 64, 64), 64)
    for which, d in ((0, dp), (1, 1 - dp)):
        cols = pl.ds(pl.multiple_of((d * 8 + ctx // 2) * 128, 128), 128)
        for w, (src, g) in enumerate(((nrm, gq), (nrm, gk), (nrm, gv), (gco, att))):
            tile[...] = dg(src[:, cols], g[0:LC], 0, 0)
            if which == 0:
                dw_own[w] = tile[half]
            else:
                dw_send[w] = tile[half].astype(BF16)

    mine = pl.ds(pl.multiple_of(ctx * CL, CL), CL)
    more = pl.ds(pl.multiple_of(ctx * CL, CL), ROWS)
    here = ctx // 2
    there = jnp.minimum((ctx + 1) // 2, 7)
    gq_m, gk_m, gv_m, att_m = gq[more], gk[more], gv[more], att[mine]
    lane = lax.broadcasted_iota(jnp.int32, (ROWS, 128), 1)
    dots = jnp.zeros((ROWS, 1), F32)
    for shift, msg in ((1, msg1), (2, msg2), (3, msg3), (0, keep)):
        t = lax.rem(z + shift, 4)
        part = pl.ds(pl.multiple_of(t * WL, WL), WL)
        gn = dg(gq_m, wq[part], 1, 1) + dg(gk_m, wk[part], 1, 1) + dg(gv_m, wv[part], 1, 1)
        c0 = own[here * 4 + t, 0:CL]
        c1 = rec[there * 4 + t, 0:16]
        gained = gn * gain[0:1, part]
        d0 = jnp.sum(gained[0:CL] * c0.astype(F32), axis=1, keepdims=True)
        d1 = jnp.sum(gained[CL:ROWS] * c1.astype(F32), axis=1, keepdims=True)
        dots = dots + jnp.concatenate([d0, d1], axis=0)
        msg[0:CL, 0:WL] = dg(att_m, wo[part], 1, 1).astype(msg.dtype)
        msg[CL : CL + ROWS, 0:WL] = gn.astype(msg.dtype)
        msg[0:CL, WL : WL + 128] = jnp.zeros((CL, 128), msg.dtype)
        if shift == 0:
            cz[0:CL] = c0
            cz[CL:ROWS] = c1
    keep[CL : CL + ROWS, WL : WL + 128] = jnp.broadcast_to(dots, (ROWS, 128))
    hi = dots.astype(BF16)
    lo = (dots - hi.astype(F32)).astype(BF16)
    lo2 = (dots - hi.astype(F32) - lo.astype(F32)).astype(BF16)
    packed = jnp.where(lane == 0, hi.astype(F32), jnp.where(lane == 1, lo.astype(F32), lo2.astype(F32)))
    packed = jnp.where(lane < 3, packed, 0.0).astype(BF16)
    for msg in (msg1, msg2, msg3):
        msg[CL : CL + ROWS, WL : WL + 128] = packed
    inv_out[...] = inv[more]


def after_kernel(sc, keep, r1, r2, r3, cz, inv, gain, first, second, up_gain, update, grad, rows):
    ctx, doc_len, z = sc[0], sc[1], sc[2]
    mask = byte_mask(ctx, doc_len)
    body = slice(0, WL)
    out = keep[0:CL, body]
    gn = keep[CL : CL + ROWS, body]
    dots = keep[CL : CL + ROWS, WL : WL + 1]
    for r in (r1, r2, r3):
        out = out + r[0:CL, body].astype(F32)
        gn = gn + r[CL : CL + ROWS, body].astype(F32)
        dots = dots + jnp.sum(r[CL : CL + ROWS, WL : WL + 128].astype(F32), axis=1, keepdims=True)
    update[...] = ((out[:, None, :] * up_gain[...][None]) * mask).reshape(SEG, WL).astype(BF16)
    i = inv[:, 0:1]
    gained = gn * gain[0:1, pl.ds(pl.multiple_of(z * WL, WL), WL)]
    full = i * gained - cz[...].astype(F32) * (i * i * i) * dots * (1.0 / D)
    exists = lax.broadcasted_iota(jnp.int32, (ROWS, WL), 0) + ctx * CL < LC
    rows[...] = jnp.where(exists, full, 0.0)
    taps = tap_weights(first[...], second[...])
    u = lax.broadcasted_iota(jnp.int32, (CL, 16, WL), 1)
    picked = jnp.where(u == 0, rows[0:CL][:, None, :], rows[1 : CL + 1][:, None, :])
    grad[...] = (picked * taps[None] * mask).reshape(SEG, WL).astype(BF16)


def call(kernel, outs, n_in, scratch=(), smem=(0,), flops=0, size=0, vmem=48 * 2**20):
    return pl.pallas_call(
        kernel,
        out_shape=[jax.ShapeDtypeStruct(s, d) for s, d in outs],
        in_specs=[pl.BlockSpec(memory_space=SM if i in smem else VM) for i in range(n_in)],
        out_specs=[pl.BlockSpec(memory_space=VM)] * len(outs),
        scratch_shapes=list(scratch),
        compiler_params=pltpu.CompilerParams(vmem_limit_bytes=vmem),
        cost_estimate=pl.CostEstimate(flops=flops, bytes_accessed=size, transcendentals=0),
    )


def shifted(x, axis, steps):
    n = lax.axis_size(axis)
    return lax.ppermute(x, axis, [(i, (i + steps) % n) for i in range(n)])


def local(
    tokens, lengths, conv_first, conv_second, norm_gain, w_query, w_key, w_value, w_out,
    bias_table, buckets, up_gain, grad_out,
):
    x, y, core = lax.axis_index("x"), lax.axis_index("y"), lax.axis_index("core")
    dp, z = lax.axis_index("dp"), lax.axis_index("tensor")
    ctx = (x * 2 + y) * 2 + core
    doc_len = lengths[0]
    small = jnp.stack([ctx, doc_len, z]).astype(jnp.int32)
    part, last, gco = call(
        before_kernel,
        [((CL, WL), F32), ((8, WL), F32), ((CL, WL), BF16)],
        6,
        [pltpu.VMEM((CL + 8, WL), F32)],
    )(small, tokens[0], grad_out[0], conv_first, conv_second, up_gain)
    rim = lax.ppermute(last, ("x", "y", "core"), [(i, i + 1) for i in range(15)])
    is_first = (jnp.arange(CL) == 0)[:, None]
    coarse = (part + jnp.where(is_first, rim[0:1], 0.0)).astype(BF16)
    payload = jnp.concatenate([coarse, gco], axis=0)
    own = lax.all_to_all(
        jnp.broadcast_to(payload[None], (32, 2 * CL, WL)), ("x", "y", "tensor"), 0, 0, tiled=True
    )
    rec = shifted(own, "core", 1)
    n = 640
    near = jnp.concatenate(
        [
            jnp.flip(buckets[:385]),
            jnp.full((n - LC,), bias_table.shape[0], jnp.int32),
            jnp.flip(buckets[385:]),
        ]
    )
    (strip,) = call(bias_kernel, [((NH, 128, LC), F32)], 2, smem=(1,))(
        jnp.broadcast_to(near[None], (8, n)), bias_table
    )
    gain = norm_gain[None]
    msg = (CL + ROWS, WL + 128)
    big = lambda rows: pltpu.VMEM((rows, WL), BF16)
    m1, m2, m3, keep, cz, inv, dw_own, dw_send = call(
        middle_kernel,
        [
            (msg, BF16), (msg, BF16), (msg, BF16), (msg, F32), ((ROWS, WL), BF16), ((ROWS, 128), F32),
            ((4, 64, WL), F32), ((4, 64, WL), BF16),
        ],
        9,
        [
            pltpu.VMEM((LC, D), BF16), pltpu.VMEM((LC, D), BF16),
            big(LC), big(LC), big(LC), big(LC), big(LC), big(LC + 16), big(LC + 16), big(LC + 16),
            pltpu.VMEM((LC + 16, 128), F32), pltpu.VMEM((LC, HD), F32), pltpu.VMEM((LC, HD), F32),
            pltpu.VMEM((128, WL), F32),
        ],
        flops=10**10,
        size=2 * 10**7,
    )(
        jnp.stack([core, ctx, dp, z, doc_len]).astype(jnp.int32),
        own, rec, gain, w_query, w_key, w_value, w_out, strip,
    )
    r1, r2, r3 = shifted(m1, "tensor", 1), shifted(m2, "tensor", 2), shifted(m3, "tensor", 3)
    other = shifted(dw_send, "dp", 1)
    update, grad_tokens = call(
        after_kernel,
        [((SEG, WL), BF16), ((SEG, WL), BF16)],
        11,
        [pltpu.VMEM((ROWS, WL), F32)],
    )(small, keep, r1, r2, r3, cz, inv, gain, conv_first, conv_second, up_gain)
    dw = dw_own + other.astype(F32)
    return (update[None], grad_tokens[None], dw[0], dw[1], dw[2], dw[3])


def solution(mesh):
    ctx = ("x", "y", "core")
    fine = Mesh(
        np.asarray(mesh.devices).reshape(2, 4, 2, 2, 4), ("dp", "x", "y", "core", "tensor")
    )
    tok = P("dp", ctx, "tensor")
    col = P(None, "tensor")
    in_specs = (tok, P("dp"), col, col, P(), col, col, col, col, col, P(), col, tok)
    dw = P(("dp",) + ctx, "tensor")
    return jax.shard_map(
        local, mesh=fine, in_specs=in_specs, out_specs=(tok, tok, dw, dw, dw, dw), check_vma=False
    )
```

time: 845 us -> 92.7 us (0.11)
  waiting for transfers between devices: 635 us -> 6.58 us
  local copies, waits for them, and re-layouts: 66 us -> 5.81 us
  blocking collectives: 66.2 us -> 34.6 us
  Pallas kernels: 0 us -> 27.8 us
  matrix products: 26.5 us -> 0 us
  other arithmetic: 20.1 us -> 0.33 us
  between operations: 15.4 us -> 1.39 us
    reduce_scatter x5 -> x0, waiting for transfers between devices: 533 us -> none  [the longest x1 132 us: local(): lax.psum_scatter(grad_wv.astype(jnp.bfloat16), ('dp', 'ctx'), scatter_dim...]
    all_gather x4 -> x0, blocking collectives: 66.2 us -> none  [the longest x1 25.8 us: local(): lax.all_gather(keys_loc, 'ctx', axis=0, tiled=True)]
    unnamed x8 -> x0, waiting for transfers between devices: 66.1 us -> none
    gather x2 -> x0, local copies, waits for them, and re-layouts: 59.8 us -> none  [local(): lookup = jnp.take(dist_bias, jnp.clip(distance, 0, total_keys - 1), axis=0)]
    all_to_all x0 -> x1, blocking collectives: none -> 34.6 us  [local(): lax.all_to_all(jnp.broadcast_to(payload[None], (32, 2 * CL, WL)), ('x', '...]
    psum x1 -> x0, waiting for transfers between devices: 31.6 us -> none  [local(): lax.psum(grad_normed_part.astype(jnp.bfloat16), 'tensor')]
    pallas_call x0 -> x4, Pallas kernels: none -> 27.8 us  [the longest x1 23.1 us: local(): call(middle_kernel, [(msg, BF16), (msg, BF16), (msg, BF16), (msg, F32), (...]
    dot_general x19 -> x0, matrix products: 26.5 us -> none  [the longest x1 2.46 us: local(): jnp.einsum('ic,dc->id', grad_keys, w_key, preferred_element_type=jnp.floa...]
  transfers between devices with their start and end apart: 9 -> 6, of which waited for: 8 -> 5; matrix products, arithmetic and copies ran while one was open for 10% -> 1% of each run, Pallas kernels for 0% -> 4%
where the time goes in v1:
time: 92.7 us; the launch traced here: 91.9 us
  blocking collectives  34.6 us (37%)
  Pallas kernels  27.8 us (30%)
  starting transfers between devices  15.4 us (17%)
  waiting for transfers between devices  6.58 us (7%)
  local copies, waits for them, and re-layouts  5.81 us (6%)
  between operations  1.39 us (1%)
    all_to_all x1, blocking collectives, local(): lax.all_to_all(jnp.broadcast_to(payload[None], (32, 2 * CL, WL)), ('x', '...  34.6 us
    pallas_call x1, Pallas kernels, local(): call(middle_kernel, [(msg, BF16), (msg, BF16), (msg, BF16), (msg, F32), (...  23.1 us
    ppermute x5, starting transfers between devices, shifted(): return lax.ppermute(x, axis, [(i, (i + steps) % n) for i in range(n)])  9.14 us
    ppermute x1, starting transfers between devices, local(): lax.ppermute(last, ('x', 'y', 'core'), [(i, i + 1) for i in range(15)])  6.21 us
    ppermute x5, waiting for transfers between devices, shifted(): return lax.ppermute(x, axis, [(i, (i + steps) % n) for i in range(n)])  5.74 us
    unnamed x25, local copies, waits for them, and re-layouts  4.52 us
    pallas_call x1, Pallas kernels, local(): call(after_kernel, [((SEG, WL), BF16), ((SEG, WL), BF16)], 11, [pltpu.VME...  2 us
  transfers between devices with their start and end apart: 6, of which 5 were waited for; matrix products, arithmetic and copies ran while one was open for 1% of the time, Pallas kernels for 4%

profile of v1, /device:TPU:1, one launch (start us, length us, event | category | flops | bytes accessed | tf_op | source)
XLA Modules:
  0.0 91.9 jit_solution(2010253481016540133)
XLA Ops:
  1.3 0.1 pad_add_fusion.1.sc
  1.4 1.0 %copy-done = bf16[1,512,512]{2,1,0:T(8,128)(2,1)S(1)} copy-done((bf16[1,512,512]{2,1,0:T(8,128)(2,1)S(1)}, bf16[1,512,512]{2,1,0:T(8,128)(2,1)}, u32[]{:S(2)}) %copy-start) | copy-done | bytes 524312
  2.4 1.0 %copy-done.1 = bf16[1,512,512]{2,1,0:T(8,128)(2,1)S(1)} copy-done((bf16[1,512,512]{2,1,0:T(8,128)(2,1)S(1)}, bf16[1,512,512]{2,1,0:T(8,128)(2,1)}, u32[]{:S(2)}) %copy-start.1) | copy-done | bytes 524312
  3.5 0.8 copy-done.2
  4.2 0.7 copy-done.4
  4.9 0.7 copy-done.6
  5.6 1.5 %shard_map.172 = (f32[32,512]{1,0:T(8,128)S(1)}, f32[8,512]{1,0:T(8,128)S(1)}, bf16[32,512]{1,0:T(8,128)(2,1)S(1)}) custom-call(s32[3]{0:T(128)S(1)} %pad_add_fusion.1.sc, bf16[512,512]{1,0:T(8,128)(2,1)S(1)} %bitcast.20, bf16[512,512]{1,0:T(8,128)(2,1)S(1)} %bitcast.21, f32[4,512]{1,0:T(4,128)S(1)} %copy-done.4, f32[4,512]{1,0:T(4,128)S(1)} %copy-done.6, ...), custom_call_target="tpu_custom_call" | custom-call | tf_op jit(solution)/shard_map/pallas_call | solution.py:226
  7.1 6.2 %collective-permute-start = (f32[8,512]{1,0:T(8,128)S(1)}, f32[8,512]{1,0:T(8,128)S(1)}, u32[]{:S(2)}, u32[]{:S(2)}) collective-permute-start(f32[8,512]{1,0:T(8,128)S(1)} %get-tuple-element.20), channel_id=1, source_target_pairs={{0,4},{4,8},{8,12},{12,16},{16,20},{20,24},{24,28},{28,32},{32,36}... | collective-permute-start | bytes 49160 | tf_op jit(solution)/shard_map/ppermute | solution.py:232
  13.3 0.8 collective-permute-done
  14.1 0.1 add_convert_fusion
  14.2 0.2 broadcast_in_dim.51
  14.5 34.6 %all_to_all.5.own = bf16[32,64,512]{2,1,0:T(8,128)(2,1)S(1)} all-to-all(bf16[32,64,512]{2,1,0:T(8,128)(2,1)S(1)} %broadcast_in_dim.51), channel_id=1, replica_groups=mesh['dp'=2,'x'=4,'y'=2,'core'=2,'tensor'=4] {'x','y','tensor'}, dimensions={0} | all-to-all | bytes 4194304 | tf_op jit(solution)/shard_map/all_to_all | solution.py:236
  49.1 4.0 %collective-permute-start.1 = (bf16[32,64,512]{2,1,0:T(8,128)(2,1)S(1)}, bf16[32,64,512]{2,1,0:T(8,128)(2,1)}, u32[]{:S(2)}, u32[]{:S(2)}) collective-permute-start(bf16[32,64,512]{2,1,0:T(8,128)(2,1)S(1)} %all_to_all.5.own), channel_id=1, source_target_pairs={{0,4},{4,0},{1,5},{5,1},{2,6},{6,2},{3,7},{7,3},{8,12},{12,8},{9,1... | collective-permute-start | bytes 6291464 | tf_op jit(solution)/shard_map/ppermute | solution.py:214
  53.2 0.1 rev.9
  53.3 0.1 reverse
  53.4 0.1 slice.37
  53.4 0.1 copy.19.table
  53.5 0.1 stack.25.sc
  53.6 0.1 pad_add_fusion
  53.7 1.2 %shard_map.173.strip = f32[4,128,512]{2,1,0:T(8,128)S(1)} custom-call(s32[8,640]{1,0:T(8,128)S(1)} %broadcast_in_dim.54.near, f32[32,4]{1,0:T(8,128)S(1)} %copy.19.table), custom_call_target="tpu_custom_call" | custom-call | tf_op jit(solution)/shard_map/pallas_call | solution.py:248
  54.9 2.1 %collective-permute-done.1.rec = bf16[32,64,512]{2,1,0:T(8,128)(2,1)} collective-permute-done((bf16[32,64,512]{2,1,0:T(8,128)(2,1)S(1)}, bf16[32,64,512]{2,1,0:T(8,128)(2,1)}, u32[]{:S(2)}, u32[]{:S(2)}) %collective-permute-start.1) | collective-permute-done | bytes 2097184 | tf_op jit(solution)/shard_map/ppermute | solution.py:214
  57.0 23.1 %shard_map.174 = (bf16[80,640]{1,0:T(8,128)(2,1)S(1)}, bf16[80,640]{1,0:T(8,128)(2,1)S(1)}, bf16[80,640]{1,0:T(8,128)(2,1)S(1)}, f32[80,640]{1,0:T(8,128)S(1)}, ...) custom-call(s32[5]{0:T(128)S(1)} %stack.25.sc, ...), custom_call_target="tpu_custom_call" | custom-call | flops 10000000000 | bytes 20000000 | tf_op jit(solution)/shard_map/pallas_call | solution.py:254
  80.2 1.4 %collective-permute-start.5 = (bf16[4,64,512]{2,1,0:T(8,128)(2,1)S(1)}, bf16[4,64,512]{2,1,0:T(8,128)(2,1)S(1)}, u32[]{:S(2)}, u32[]{:S(2)}) collective-permute-start(bf16[4,64,512]{2,1,0:T(8,128)(2,1)S(1)} %get-tuple-element.31), channel_id=1, source_target_pairs={{0,64},{64,0},{1,65},{65,1},{2,66},{66,2},{3,67},{67,3},{4,68},{68... | collective-permute-start | bytes 786440 | tf_op jit(solution)/shard_map/ppermute | solution.py:214
  81.5 0.5 collective-permute-start.2
  82.0 1.4 %collective-permute-start.3 = (bf16[80,640]{1,0:T(8,128)(2,1)S(1)}, bf16[80,640]{1,0:T(8,128)(2,1)S(1)}, u32[]{:S(2)}, u32[]{:S(2)}) collective-permute-start(bf16[80,640]{1,0:T(8,128)(2,1)S(1)} %get-tuple-element.24), channel_id=1, source_target_pairs={{0,2},{1,3},{2,0},{3,1},{4,6},{5,7},{6,4},{7,5},{8,10},{9,11},{10,... | collective-permute-start | bytes 307208 | tf_op jit(solution)/shard_map/ppermute | solution.py:214
  83.5 1.9 %collective-permute-start.4 = (bf16[80,640]{1,0:T(8,128)(2,1)S(1)}, bf16[80,640]{1,0:T(8,128)(2,1)S(1)}, u32[]{:S(2)}, u32[]{:S(2)}) collective-permute-start(bf16[80,640]{1,0:T(8,128)(2,1)S(1)} %get-tuple-element.25), channel_id=1, source_target_pairs={{0,3},{1,0},{2,1},{3,2},{4,7},{5,4},{6,5},{7,6},{8,11},{9,8},{10,9... | collective-permute-start | bytes 307208 | tf_op jit(solution)/shard_map/ppermute | solution.py:214
  85.3 2.0 %collective-permute-done.2.r1 = bf16[80,640]{1,0:T(8,128)(2,1)S(1)} collective-permute-done((bf16[80,640]{1,0:T(8,128)(2,1)S(1)}, bf16[80,640]{1,0:T(8,128)(2,1)S(1)}, u32[]{:S(2)}, u32[]{:S(2)}) %collective-permute-start.2) | collective-permute-done | bytes 102432 | tf_op jit(solution)/shard_map/ppermute | solution.py:214
  87.3 1.1 %collective-permute-done.3.r2 = bf16[80,640]{1,0:T(8,128)(2,1)S(1)} collective-permute-done((bf16[80,640]{1,0:T(8,128)(2,1)S(1)}, bf16[80,640]{1,0:T(8,128)(2,1)S(1)}, u32[]{:S(2)}, u32[]{:S(2)}) %collective-permute-start.3) | collective-permute-done | bytes 102432 | tf_op jit(solution)/shard_map/ppermute | solution.py:214
  88.4 0.6 collective-permute-done.4.r3
  89.0 2.0 %shard_map.175 = (bf16[512,512]{1,0:T(8,128)(2,1)}, bf16[512,512]{1,0:T(8,128)(2,1)}) custom-call(s32[3]{0:T(128)S(1)} %pad_add_fusion.1.sc, f32[80,640]{1,0:T(8,128)S(1)} %get-tuple-element.22.keep, bf16[80,640]{1,0:T(8,128)(2,1)S(1)} %collective-permute-done.2.r1, bf16[80,640]{1,0:T(8,128)(2,1)S(1)} %collective-permute-done.3.r2, ...), custom_call_target="tpu_custom_call" | custom-call | tf_op jit(solution)/shard_map/pallas_call | solution.py:275
  91.0 0.1 convert_add_fusion
  91.1 0.8 slice_bitcast_fusion
  (24 shorter events, 0.1 us)
Async XLA Ops:
  1.4 1.0 %copy-start = (bf16[1,512,512]{2,1,0:T(8,128)(2,1)S(1)}, bf16[1,512,512]{2,1,0:T(8,128)(2,1)}, u32[]{:S(2)}) copy-start(bf16[1,512,512]{2,1,0:T(8,128)(2,1)} %param.13) | copy-start | bytes 1572868
  2.4 1.0 %copy-start.1 = (bf16[1,512,512]{2,1,0:T(8,128)(2,1)S(1)}, bf16[1,512,512]{2,1,0:T(8,128)(2,1)}, u32[]{:S(2)}) copy-start(bf16[1,512,512]{2,1,0:T(8,128)(2,1)} %param.25) | copy-start | bytes 1572868
  3.4 0.8 copy-start.2
  4.2 0.7 copy-start.4
  4.9 0.7 copy-start.6
  7.1 7.1 %collective-permute-start = (f32[8,512]{1,0:T(8,128)S(1)}, f32[8,512]{1,0:T(8,128)S(1)}, u32[]{:S(2)}, u32[]{:S(2)}) collective-permute-start(f32[8,512]{1,0:T(8,128)S(1)} %get-tuple-element.20), channel_id=1, source_target_pairs={{0,4},{4,8},{8,12},{12,16},{16,20},{20,24},{24,28},{28,32},{32,36}... | collective-permute-start | bytes 49160 | tf_op jit(solution)/shard_map/ppermute | solution.py:232
  14.5 38.6 %copy-start.10 = (s32[512]{0:T(512)S(1)}, s32[512]{0:T(512)}, u32[]{:S(2)}) copy-start(s32[512]{0:T(512)} %param.23) | copy-start | bytes 6148
  14.5 39.0 %copy-start.9 = (f32[32,4]{0,1:T(4,128)S(1)}, f32[32,4]{0,1:T(4,128)}, u32[]{:S(2)}) copy-start(f32[32,4]{0,1:T(4,128)} %param.22) | copy-start | bytes 1540
  14.5 42.5 %copy-start.8 = (f32[2048]{0:T(1024)S(1)}, f32[2048]{0:T(1024)}, u32[]{:S(2)}) copy-start(f32[2048]{0:T(1024)} %param.17) | copy-start | bytes 24580
  49.1 7.9 %collective-permute-start.1 = (bf16[32,64,512]{2,1,0:T(8,128)(2,1)S(1)}, bf16[32,64,512]{2,1,0:T(8,128)(2,1)}, u32[]{:S(2)}, u32[]{:S(2)}) collective-permute-start(bf16[32,64,512]{2,1,0:T(8,128)(2,1)S(1)} %all_to_all.5.own), channel_id=1, source_target_pairs={{0,4},{4,0},{1,5},{5,1},{2,6},{6,2},{3,7},{7,3},{8,12},{12,8},{9,1... | collective-permute-start | bytes 6291464 | tf_op jit(solution)/shard_map/ppermute | solution.py:214
  57.0 32.0 %copy-start.3 = (f32[16,512]{1,0:T(8,128)S(1)}, f32[16,512]{1,0:T(8,128)}, u32[]{:S(2)}) copy-start(f32[16,512]{1,0:T(8,128)} %up_gain.3) | copy-start | bytes 98308
  57.0 32.0 %copy-start.5 = (f32[4,512]{1,0:T(4,128)S(1)}, f32[4,512]{1,0:T(4,128)}, u32[]{:S(2)}) copy-start(f32[4,512]{1,0:T(4,128)} %first.3) | copy-start | bytes 24580
  57.0 32.0 %copy-start.7 = (f32[4,512]{1,0:T(4,128)S(1)}, f32[4,512]{1,0:T(4,128)}, u32[]{:S(2)}) copy-start(f32[4,512]{1,0:T(4,128)} %second.3) | copy-start | bytes 24580
  80.2 10.8 %collective-permute-start.5 = (bf16[4,64,512]{2,1,0:T(8,128)(2,1)S(1)}, bf16[4,64,512]{2,1,0:T(8,128)(2,1)S(1)}, u32[]{:S(2)}, u32[]{:S(2)}) collective-permute-start(bf16[4,64,512]{2,1,0:T(8,128)(2,1)S(1)} %get-tuple-element.31), channel_id=1, source_target_pairs={{0,64},{64,0},{1,65},{65,1},{2,66},{66,2},{3,67},{67,3},{4,68},{68... | collective-permute-start | bytes 786440 | tf_op jit(solution)/shard_map/ppermute | solution.py:214
  81.5 5.8 %collective-permute-start.2 = (bf16[80,640]{1,0:T(8,128)(2,1)S(1)}, bf16[80,640]{1,0:T(8,128)(2,1)S(1)}, u32[]{:S(2)}, u32[]{:S(2)}) collective-permute-start(bf16[80,640]{1,0:T(8,128)(2,1)S(1)} %get-tuple-element.23), channel_id=1, source_target_pairs={{0,1},{1,2},{2,3},{3,0},{4,5},{5,6},{6,7},{7,4},{8,9},{9,10},{10,1... | collective-permute-start | bytes 307208 | tf_op jit(solution)/shard_map/ppermute | solution.py:214
  82.0 6.3 %collective-permute-start.3 = (bf16[80,640]{1,0:T(8,128)(2,1)S(1)}, bf16[80,640]{1,0:T(8,128)(2,1)S(1)}, u32[]{:S(2)}, u32[]{:S(2)}) collective-permute-start(bf16[80,640]{1,0:T(8,128)(2,1)S(1)} %get-tuple-element.24), channel_id=1, source_target_pairs={{0,2},{1,3},{2,0},{3,1},{4,6},{5,7},{6,4},{7,5},{8,10},{9,11},{10,... | collective-permute-start | bytes 307208 | tf_op jit(solution)/shard_map/ppermute | solution.py:214
  83.5 5.5 %collective-permute-start.4 = (bf16[80,640]{1,0:T(8,128)(2,1)S(1)}, bf16[80,640]{1,0:T(8,128)(2,1)S(1)}, u32[]{:S(2)}, u32[]{:S(2)}) collective-permute-start(bf16[80,640]{1,0:T(8,128)(2,1)S(1)} %get-tuple-element.25), channel_id=1, source_target_pairs={{0,3},{1,0},{2,1},{3,2},{4,7},{5,4},{6,5},{7,6},{8,11},{9,8},{10,9... | collective-permute-start | bytes 307208 | tf_op jit(solution)/shard_map/ppermute | solution.py:214

commit v2 on v1

v2 whole, which is shorter than its diff:
```python
import math

import jax
import jax.numpy as jnp
import numpy as np
from jax import lax
from jax.experimental import pallas as pl
from jax.experimental.pallas import tpu as pltpu
from jax.sharding import Mesh, PartitionSpec as P

F32 = jnp.float32
BF16 = jnp.bfloat16
NEG = float("-inf")
D = 2048
WL = 512
LC = 512
CL = 32
SEG = 512
HD = 128
NH = 2
HW = NH * HD
SCALE = 1.0 / math.sqrt(HD)
ROWS = CL + 16
VM = pltpu.VMEM
SM = pltpu.SMEM


def dg(a, b, ca, cb):
    return lax.dot_general(a, b, (((ca,), (cb,)), ((), ())), preferred_element_type=F32)


def tap_weights(first, second):
    taps = jnp.concatenate([second[a : a + 1] * first for a in range(4)], axis=0)
    return jnp.concatenate([taps[15:16], taps[:15]], axis=0)


def byte_mask(ctx, doc_len):
    pos = ctx * SEG + 16 * lax.broadcasted_iota(jnp.int32, (CL, 16, WL), 0)
    pos = pos + lax.broadcasted_iota(jnp.int32, (CL, 16, WL), 1)
    return (pos < doc_len).astype(F32)


def before_kernel(sc, tokens, grad_out, first, second, up_gain, part, last, gco, shift):
    mask = byte_mask(sc[0], sc[1])
    taps = tap_weights(first[...], second[...])
    u = lax.broadcasted_iota(jnp.int32, (CL, 16, WL), 1)
    prod = tokens[...].astype(F32).reshape(CL, 16, WL) * mask * taps[None]
    own = jnp.sum(jnp.where(u == 0, prod, 0.0), axis=1)
    onward = jnp.sum(jnp.where(u == 0, 0.0, prod), axis=1)
    shift[0:8] = jnp.zeros((8, WL), F32)
    shift[8 : 8 + CL] = onward
    part[...] = own + shift[7 : 7 + CL]
    last[...] = jnp.broadcast_to(shift[7 + CL : 8 + CL], (8, WL))
    weighted = grad_out[...].astype(F32).reshape(CL, 16, WL) * mask * up_gain[...][None]
    gco[...] = jnp.sum(weighted, axis=1).astype(BF16)


def bias_kernel(sc, near, table, strip):
    n = near.shape[1]
    which = near[0:1]
    for h in range(NH):
        row = jnp.full((1, n), NEG, F32)
        for b in range(table.shape[0]):
            row = jnp.where(which == b, table[b, sc[3] * NH + h], row)
        rolled = pltpu.roll(jnp.broadcast_to(row, (128, n)), 0, 1, stride=1, stride_axis=0)
        strip[h] = rolled[:, :LC]


def project_kernel(
    sc, p0, r1, r2, r3, gain, wq, wk, wv, wo, keep, send, blocks, craw, first, nrm, gco, both
):
    z, core = sc[2], sc[3]
    for s, src in enumerate((p0, r1, r2, r3)):
        cols = pl.ds(pl.multiple_of(lax.rem(z + 4 - s, 4) * WL, WL), WL)
        craw[:, cols] = src[0:CL]
        gco[:, cols] = src[CL : 2 * CL]
    first[...] = craw[0:16]
    c = craw[...].astype(F32)
    r = lax.rsqrt(jnp.sum(c * c, axis=1, keepdims=True) * (1.0 / D) + 1e-6)
    nrm[...] = (c * r * gain[...]).astype(BF16)
    for i, (src, w) in enumerate(((nrm, wq), (nrm, wk), (nrm, wv), (gco, wo))):
        y = jnp.dot(src[...], w[...], preferred_element_type=F32).astype(BF16)
        for half in range(2):
            both[half, :, i * HW : i * HW + HW] = y[:, half * HW : half * HW + HW]
    keep[...] = both[core]
    send[...] = both[1 - core]
    for chip in range(8):
        for d in range(2):
            cols = slice((d * 8 + chip) * 128, (d * 8 + chip) * 128 + 128)
            for part in range(2):
                rows = slice(part * 16, part * 16 + 16)
                at = part * 512 + d * 128
                blocks[chip, :, at : at + 128] = nrm[rows, cols]
                blocks[chip, :, at + 256 : at + 384] = gco[rows, cols]


def attend_kernel(sc, got, strip, res, keep, send, q, k, v, ga, acck, accv):
    ctx, doc_len, core = sc[0], sc[1], sc[3]
    for i, dst in enumerate((q, k, v, ga)):
        dst[...] = got[:, 0:64, i * HW : i * HW + HW].reshape(LC, HW)
    key_pos = lax.broadcasted_iota(jnp.int32, (1, LC), 1)
    key_mask = jnp.where(16 * key_pos < doc_len, 0.0, NEG)
    for h in range(NH):
        cols = slice(h * HD, h * HD + HD)
        for b in (3, 2, 1, 0):
            rows = slice(b * 128, b * 128 + 128)
            n = b * 128 + 128
            qb, gb, kb, vb = q[rows, cols], ga[rows, cols], k[0:n, cols], v[0:n, cols]
            s = dg(qb, kb, 1, 1) * SCALE + strip[h, :, LC - n :] + key_mask[:, :n]
            e = jnp.exp(s - jnp.max(s, axis=1, keepdims=True))
            p = e * (1.0 / jnp.sum(e, axis=1, keepdims=True))
            pb = p.astype(BF16)
            ab = jnp.dot(pb, vb, preferred_element_type=F32).astype(BF16)
            res[3, rows, cols] = ab
            dot = jnp.sum(gb.astype(F32) * ab.astype(F32), axis=1, keepdims=True)
            sg = (p * (dg(gb, vb, 1, 1) - dot)).astype(BF16)
            res[0, rows, cols] = (jnp.dot(sg, kb, preferred_element_type=F32) * SCALE).astype(BF16)
            tk = dg(sg, qb, 0, 0)
            tv = dg(pb, gb, 0, 0)
            if b == 3:
                acck[h] = tk
                accv[h] = tv
            else:
                acck[h, 0:n] += tk
                accv[h, 0:n] += tv
        res[1, 0:LC, cols] = (acck[h] * SCALE).astype(BF16)
        res[2, 0:LC, cols] = accv[h].astype(BF16)
    res[:, LC : LC + 16] = jnp.zeros((4, 16, HW), BF16)
    peer = ctx + 1 - 2 * core
    keep[...] = res[:, pl.ds(pl.multiple_of(ctx * CL, CL), ROWS)]
    send[...] = res[:, pl.ds(pl.multiple_of(peer * CL, CL), ROWS)]


def weights_kernel(sc, res, mine, other, keep, send, nb, gb, tile):
    core = sc[3]
    for chip in range(8):
        for src, c in ((mine, core), (other, 1 - core)):
            for part in range(2):
                rows = pl.ds(pl.multiple_of(chip * 64 + c * CL + part * 16, 16), 16)
                nb[rows] = src[chip, :, part * 512 : part * 512 + 256]
                gb[rows] = src[chip, :, part * 512 + 256 : part * 512 + 512]
    for w in range(4):
        tile[...] = dg((gb if w == 3 else nb)[...], res[w, 0:LC], 0, 0)
        for d in range(2):
            keep[w, d] = tile[pl.ds(pl.multiple_of(d * 128 + core * 64, 64), 64)]
            send[w, d] = tile[pl.ds(pl.multiple_of(d * 128 + 64 - core * 64, 64), 64)].astype(BF16)


def join_kernel(sc, keep, got, own, send):
    core, dp = sc[3], sc[4]
    a = pl.ds(pl.multiple_of(core * HW, HW), HW)
    b = pl.ds(pl.multiple_of((1 - core) * HW, HW), HW)
    own[:, :, a] = keep[:, dp]
    own[:, :, b] = got[:, dp].astype(F32)
    send[:, :, a] = keep[:, 1 - dp].astype(BF16)
    send[:, :, b] = got[:, 1 - dp]


def partial_kernel(
    sc, keep_r, got_r, craw, nxt, gain, wq, wk, wv, wo, msg1, msg2, msg3, keep, cz, inv_out, g, c
):
    z, core = sc[2], sc[3]
    g[:, :, pl.ds(pl.multiple_of(core * HW, HW), HW)] = keep_r[...]
    g[:, :, pl.ds(pl.multiple_of((1 - core) * HW, HW), HW)] = got_r[...]
    c[0:CL] = craw[...]
    c[CL:ROWS] = nxt[...]
    cf = c[...].astype(F32)
    r = lax.rsqrt(jnp.sum(cf * cf, axis=1, keepdims=True) * (1.0 / D) + 1e-6)
    inv_out[...] = jnp.broadcast_to(r, (ROWS, 128))
    lane = lax.broadcasted_iota(jnp.int32, (ROWS, 128), 1)
    dots = jnp.zeros((ROWS, 1), F32)
    for shift, msg in ((1, msg1), (2, msg2), (3, msg3), (0, keep)):
        t = lax.rem(z + shift, 4)
        part = pl.ds(pl.multiple_of(t * WL, WL), WL)
        gn = dg(g[0], wq[part], 1, 1) + dg(g[1], wk[part], 1, 1) + dg(g[2], wv[part], 1, 1)
        cb = c[:, part]
        dots = dots + jnp.sum(gn * gain[0:1, part] * cb.astype(F32), axis=1, keepdims=True)
        msg[0:CL, 0:WL] = dg(g[3, 0:CL], wo[part], 1, 1).astype(msg.dtype)
        msg[CL : CL + ROWS, 0:WL] = gn.astype(msg.dtype)
        msg[0:CL, WL : WL + 128] = jnp.zeros((CL, 128), msg.dtype)
        if shift == 0:
            cz[...] = cb
    keep[CL : CL + ROWS, WL : WL + 128] = jnp.broadcast_to(dots, (ROWS, 128))
    hi = dots.astype(BF16)
    lo = (dots - hi.astype(F32)).astype(BF16)
    lo2 = (dots - hi.astype(F32) - lo.astype(F32)).astype(BF16)
    packed = jnp.where(lane == 0, hi.astype(F32), jnp.where(lane == 1, lo.astype(F32), lo2.astype(F32)))
    packed = jnp.where(lane < 3, packed, 0.0).astype(BF16)
    for msg in (msg1, msg2, msg3):
        msg[CL : CL + ROWS, WL : WL + 128] = packed


def after_kernel(
    sc, keep, r1, r2, r3, cz, inv, gain, first, second, up_gain, dw, other,
    update, grad, o0, o1, o2, o3, rows,
):
    ctx, doc_len, z = sc[0], sc[1], sc[2]
    mask = byte_mask(ctx, doc_len)
    body = slice(0, WL)
    out = keep[0:CL, body]
    gn = keep[CL : CL + ROWS, body]
    dots = keep[CL : CL + ROWS, WL : WL + 1]
    for r in (r1, r2, r3):
        out = out + r[0:CL, body].astype(F32)
        gn = gn + r[CL : CL + ROWS, body].astype(F32)
        dots = dots + jnp.sum(r[CL : CL + ROWS, WL : WL + 128].astype(F32), axis=1, keepdims=True)
    update[...] = ((out[:, None, :] * up_gain[...][None]) * mask).reshape(SEG, WL).astype(BF16)
    i = inv[:, 0:1]
    gained = gn * gain[0:1, pl.ds(pl.multiple_of(z * WL, WL), WL)]
    full = i * gained - cz[...].astype(F32) * (i * i * i) * dots * (1.0 / D)
    exists = lax.broadcasted_iota(jnp.int32, (ROWS, WL), 0) + ctx * CL < LC
    rows[...] = jnp.where(exists, full, 0.0)
    taps = tap_weights(first[...], second[...])
    u = lax.broadcasted_iota(jnp.int32, (CL, 16, WL), 1)
    picked = jnp.where(u == 0, rows[0:CL][:, None, :], rows[1 : CL + 1][:, None, :])
    grad[...] = (picked * taps[None] * mask).reshape(SEG, WL).astype(BF16)
    for w, o in enumerate((o0, o1, o2, o3)):
        o[...] = dw[w] + other[w].astype(F32)


def call(kernel, outs, args, scratch=(), smem=(0,), flops=0, size=0, vmem=48 * 2**20, loads=False):
    def spec(i, a):
        if i in smem:
            return pl.BlockSpec(memory_space=SM)
        if loads:
            return pl.BlockSpec(a.shape, lambda i, n=a.ndim: (0,) * n)
        return pl.BlockSpec(memory_space=VM)

    return pl.pallas_call(
        kernel,
        grid=(1,) if loads else (),
        out_shape=[jax.ShapeDtypeStruct(s, d) for s, d in outs],
        in_specs=[spec(i, a) for i, a in enumerate(args)],
        out_specs=[pl.BlockSpec(memory_space=VM)] * len(outs),
        scratch_shapes=[pltpu.VMEM(s, d) for s, d in scratch],
        compiler_params=pltpu.CompilerParams(vmem_limit_bytes=vmem),
        cost_estimate=pl.CostEstimate(flops=flops, bytes_accessed=size, transcendentals=0),
    )(*args)


def shifted(x, axis, steps):
    n = lax.axis_size(axis)
    return lax.ppermute(x, axis, [(i, (i + steps) % n) for i in range(n)])


def local(
    tokens, lengths, conv_first, conv_second, norm_gain, w_query, w_key, w_value, w_out,
    bias_table, buckets, up_gain, grad_out,
):
    x, y, core = lax.axis_index("x"), lax.axis_index("y"), lax.axis_index("core")
    dp, z = lax.axis_index("dp"), lax.axis_index("tensor")
    ctx = (x * 2 + y) * 2 + core
    sc = jnp.stack([ctx, lengths[0], z, core, dp]).astype(jnp.int32)
    gain = norm_gain[None]
    weights = (w_query, w_key, w_value, w_out)
    part, last, gco = call(
        before_kernel,
        [((CL, WL), F32), ((8, WL), F32), ((CL, WL), BF16)],
        (sc, tokens[0], grad_out[0], conv_first, conv_second, up_gain),
        [((CL + 8, WL), F32)],
        loads=True,
    )
    rim = lax.ppermute(last, ("x", "y", "core"), [(i, i + 1) for i in range(15)])
    is_first = (jnp.arange(CL) == 0)[:, None]
    coarse = (part + jnp.where(is_first, rim[0:1], 0.0)).astype(BF16)
    piece = jnp.concatenate([coarse, gco], axis=0)
    n = 640
    near = jnp.concatenate(
        [
            jnp.flip(buckets[:385]),
            jnp.full((n - LC,), bias_table.shape[0], jnp.int32),
            jnp.flip(buckets[385:]),
        ]
    )
    (strip,) = call(
        bias_kernel,
        [((NH, 128, LC), F32)],
        (sc, jnp.broadcast_to(near[None], (8, n)), bias_table),
        smem=(0, 2),
    )
    pieces = [piece] + [shifted(piece, "tensor", s) for s in (1, 2, 3)]
    keep, send, blocks, craw, first = call(
        project_kernel,
        [((CL, 4 * HW), BF16), ((CL, 4 * HW), BF16), ((8, 16, 4 * HW), BF16), ((CL, D), BF16), ((16, D), BF16)],
        (sc, *pieces, gain, *weights),
        [((CL, D), BF16), ((CL, D), BF16), ((2, CL, 4 * HW), BF16)],
    )
    swapped = shifted(send, "core", 1)
    low = core == 0
    pair = jnp.concatenate([jnp.where(low, keep, swapped), jnp.where(low, swapped, keep)], axis=0)
    bundle = jnp.concatenate([jnp.broadcast_to(pair[None], (8,) + pair.shape), blocks], axis=1)
    got = lax.all_to_all(bundle, ("x", "y"), 0, 0, tiled=True)
    nxt = lax.ppermute(first, ("x", "y", "core"), [(i + 1, i) for i in range(15)])
    mine = got[:, 64:80]
    other_rows = shifted(mine, "core", 1)
    res, keep_r, send_r = call(
        attend_kernel,
        [((4, LC + 16, HW), BF16), ((4, ROWS, HW), BF16), ((4, ROWS, HW), BF16)],
        (sc, got, strip),
        [((LC, HW), BF16)] * 4 + [((NH, LC, HD), F32)] * 2,
        flops=6 * 10**9,
    )
    got_r = shifted(send_r, "core", 1)
    dw_keep, dw_send = call(
        weights_kernel,
        [((4, 2, 64, HW), F32), ((4, 2, 64, HW), BF16)],
        (sc, res, mine, other_rows),
        [((LC, 256), BF16), ((LC, 256), BF16), ((256, HW), F32)],
        flops=10**9,
    )
    dw_got = shifted(dw_send, "core", 1)
    dw_own, dw_other = call(
        join_kernel, [((4, 64, WL), F32), ((4, 64, WL), BF16)], (sc, dw_keep, dw_got)
    )
    dw_other = shifted(dw_other, "dp", 1)
    msg = (CL + ROWS, WL + 128)
    m1, m2, m3, own, cz, inv = call(
        partial_kernel,
        [(msg, BF16), (msg, BF16), (msg, BF16), (msg, F32), ((ROWS, WL), BF16), ((ROWS, 128), F32)],
        (sc, keep_r, got_r, craw, nxt, gain, *weights),
        [((4, ROWS, WL), BF16), ((ROWS, D), BF16)],
        flops=10**9,
    )
    r1, r2, r3 = shifted(m1, "tensor", 1), shifted(m2, "tensor", 2), shifted(m3, "tensor", 3)
    update, grad_tokens, *dw = call(
        after_kernel,
        [((SEG, WL), BF16)] * 2 + [((64, WL), F32)] * 4,
        (sc, own, r1, r2, r3, cz, inv, gain, conv_first, conv_second, up_gain, dw_own, dw_other),
        [((ROWS, WL), F32)],
    )
    return (update[None], grad_tokens[None], *dw)


def solution(mesh):
    ctx = ("x", "y", "core")
    fine = Mesh(
        np.asarray(mesh.devices).reshape(2, 4, 2, 2, 4), ("dp", "x", "y", "core", "tensor")
    )
    tok = P("dp", ctx, "tensor")
    col = P(None, "tensor")
    in_specs = (tok, P("dp"), col, col, P(), col, col, col, col, col, P(), col, tok)
    dw = P(("dp",) + ctx, "tensor")
    return jax.shard_map(
        local, mesh=fine, in_specs=in_specs, out_specs=(tok, tok, dw, dw, dw, dw), check_vma=False
    )
```

time: 92.7 us -> 92.4 us (level)
  blocking collectives: 34.6 us -> 0 us
  waiting for transfers between devices: 6.58 us -> 30.6 us
  starting transfers between devices: 15.4 us -> 29 us
  Pallas kernels: 27.8 us -> 20.4 us
  local copies, waits for them, and re-layouts: 5.81 us -> 8.82 us
  other arithmetic: 0.33 us -> 1.42 us
    all_to_all x1 -> x0, blocking collectives: 34.6 us -> none  [local(): lax.all_to_all(jnp.broadcast_to(payload[None], (32, 2 * CL, WL)), ('x', '...]
    all_to_all x0 -> x1, waiting for transfers between devices: none -> 18.1 us  [local(): got = lax.all_to_all(bundle, ('x', 'y'), 0, 0, tiled=True)]
    all_to_all x0 -> x1, starting transfers between devices: none -> 9.01 us  [local(): got = lax.all_to_all(bundle, ('x', 'y'), 0, 0, tiled=True)]
    pallas_call x4 -> x8, Pallas kernels: 27.8 us -> 20.4 us  [call(): pl.pallas_call(kernel, grid=(1,) if loads else (), out_shape=[jax.ShapeDt...]
    ppermute x0 -> x1, waiting for transfers between devices: none -> 4.68 us  [local(): lax.ppermute(first, ('x', 'y', 'core'), [(i + 1, i) for i in range(15)])]
    unnamed x25 -> x35, local copies, waits for them, and re-layouts: 4.52 us -> 8.42 us
    ppermute x5 -> x11, starting transfers between devices: 9.14 us -> 11.8 us  [shifted(): return lax.ppermute(x, axis, [(i, (i + steps) % n) for i in range(n)])]
    ppermute x0 -> x1, starting transfers between devices: none -> 1.99 us  [local(): lax.ppermute(first, ('x', 'y', 'core'), [(i + 1, i) for i in range(15)])]
  transfers between devices with their start and end apart: 6 -> 14, of which waited for: 5 -> 9; matrix products, arithmetic and copies ran while one was open for 1% -> 1% of each run, Pallas kernels for 4% -> 13%
where the time goes in v2:
time: 92.4 us; the launch traced here: 91.8 us
  waiting for transfers between devices  30.6 us (33%)
  starting transfers between devices  29 us (31%)
  Pallas kernels  20.4 us (22%)
  local copies, waits for them, and re-layouts  8.82 us (10%)
  between operations  1.53 us (2%)
  other arithmetic  1.42 us (2%)
    pallas_call x8, Pallas kernels, call(): pl.pallas_call(kernel, grid=(1,) if loads else (), out_shape=[jax.ShapeDt...  20.4 us
    all_to_all x1, waiting for transfers between devices, local(): got = lax.all_to_all(bundle, ('x', 'y'), 0, 0, tiled=True)  18.1 us
    ppermute x11, starting transfers between devices, shifted(): return lax.ppermute(x, axis, [(i, (i + steps) % n) for i in range(n)])  11.8 us
    all_to_all x1, starting transfers between devices, local(): got = lax.all_to_all(bundle, ('x', 'y'), 0, 0, tiled=True)  9.01 us
    unnamed x35, local copies, waits for them, and re-layouts  8.42 us
    ppermute x11, waiting for transfers between devices, shifted(): return lax.ppermute(x, axis, [(i, (i + steps) % n) for i in range(n)])  6.96 us
    ppermute x1, starting transfers between devices, local(): lax.ppermute(last, ('x', 'y', 'core'), [(i, i + 1) for i in range(15)])  6.21 us
    ppermute x1, waiting for transfers between devices, local(): lax.ppermute(first, ('x', 'y', 'core'), [(i + 1, i) for i in range(15)])  4.68 us
  transfers between devices with their start and end apart: 14, of which 9 were waited for; matrix products, arithmetic and copies ran while one was open for 1% of the time, Pallas kernels for 13%

profile of v2, /device:TPU:1, one launch (start us, length us, event | category | flops | bytes accessed | tf_op | source)
XLA Modules:
  0.0 91.8 jit_solution(1124246170726769254)
XLA Ops:
  1.4 1.0 %copy-done.4 = bf16[1,512,512]{2,1,0:T(8,128)(2,1)S(1)} copy-done((bf16[1,512,512]{2,1,0:T(8,128)(2,1)S(1)}, bf16[1,512,512]{2,1,0:T(8,128)(2,1)}, u32[]{:S(2)}) %copy-start.4) | copy-done | bytes 524312
  2.4 1.0 %copy-done.5 = bf16[1,512,512]{2,1,0:T(8,128)(2,1)S(1)} copy-done((bf16[1,512,512]{2,1,0:T(8,128)(2,1)S(1)}, bf16[1,512,512]{2,1,0:T(8,128)(2,1)}, u32[]{:S(2)}) %copy-start.5) | copy-done | bytes 524312
  3.5 0.8 copy-done.6
  4.2 0.7 copy-done.10
  4.9 0.7 copy-done.12
  5.6 1.5 %shard_map.172 = (f32[32,512]{1,0:T(8,128)S(1)}, f32[8,512]{1,0:T(8,128)S(1)}, bf16[32,512]{1,0:T(8,128)(2,1)S(1)}) custom-call(s32[5]{0:T(128)S(1)} %stack.19.sc, bf16[512,512]{1,0:T(8,128)(2,1)S(1)} %bitcast.12, bf16[512,512]{1,0:T(8,128)(2,1)S(1)} %bitcast.13, f32[4,512]{1,0:T(4,128)S(1)} %copy-done.10, f32[4,512]{1,0:T(4,128)S(1)} %copy-done.12, ...), custom_call_target="tpu_custom_call" | custom-call | tf_op jit(solution)/shard_map/pallas_call | solution.py:229
  7.1 6.2 %collective-permute-start = (f32[8,512]{1,0:T(8,128)S(1)}, f32[8,512]{1,0:T(8,128)S(1)}, u32[]{:S(2)}, u32[]{:S(2)}) collective-permute-start(f32[8,512]{1,0:T(8,128)S(1)} %get-tuple-element.34), channel_id=1, source_target_pairs={{0,4},{4,8},{8,12},{12,16},{16,20},{20,24},{24,28},{28,32},{32,36}... | collective-permute-start | bytes 49160 | tf_op jit(solution)/shard_map/ppermute | solution.py:263
  13.3 0.8 collective-permute-done
  14.2 1.7 %collective-permute-start.1 = (bf16[64,512]{1,0:T(8,128)(2,1)S(1)}, bf16[64,512]{1,0:T(8,128)(2,1)S(1)}, u32[]{:S(2)}, u32[]{:S(2)}) collective-permute-start(bf16[64,512]{1,0:T(8,128)(2,1)S(1)} %pad_maximum_fusion.2.p0), channel_id=1, source_target_pairs={{0,1},{1,2},{2,3},{3,0},{4,5},{5,6},{6,7},{7,4},{8,9},{9,10},{10,1... | collective-permute-start | bytes 196616 | tf_op jit(solution)/shard_map/ppermute | solution.py:243
  15.9 3.3 %collective-permute-start.2 = (bf16[64,512]{1,0:T(8,128)(2,1)S(1)}, bf16[64,512]{1,0:T(8,128)(2,1)S(1)}, u32[]{:S(2)}, u32[]{:S(2)}) collective-permute-start(bf16[64,512]{1,0:T(8,128)(2,1)S(1)} %pad_maximum_fusion.2.p0), channel_id=1, source_target_pairs={{0,2},{1,3},{2,0},{3,1},{4,6},{5,7},{6,4},{7,5},{8,10},{9,11},{10,... | collective-permute-start | bytes 196616 | tf_op jit(solution)/shard_map/ppermute | solution.py:243
  19.2 0.7 collective-permute-start.3
  20.0 1.6 %collective-permute-done.2.r2 = bf16[64,512]{1,0:T(8,128)(2,1)S(1)} collective-permute-done((bf16[64,512]{1,0:T(8,128)(2,1)S(1)}, bf16[64,512]{1,0:T(8,128)(2,1)S(1)}, u32[]{:S(2)}, u32[]{:S(2)}) %collective-permute-start.2) | collective-permute-done | bytes 65568 | tf_op jit(solution)/shard_map/ppermute | solution.py:243
  21.6 0.8 collective-permute-done.3.r3
  22.4 1.6 %copy-done = bf16[2048,512]{1,0:T(8,128)(2,1)S(1)} copy-done((bf16[2048,512]{1,0:T(8,128)(2,1)S(1)}, bf16[2048,512]{1,0:T(8,128)(2,1)}, u32[]{:S(2)}) %copy-start) | copy-done | bytes 2097176
  24.0 1.6 %copy-done.2 = bf16[2048,512]{1,0:T(8,128)(2,1)S(1)} copy-done((bf16[2048,512]{1,0:T(8,128)(2,1)S(1)}, bf16[2048,512]{1,0:T(8,128)(2,1)}, u32[]{:S(2)}) %copy-start.2) | copy-done | bytes 2097176
  25.6 0.7 copy-done.8
  26.2 3.9 %shard_map.173 = (bf16[32,1024]{1,0:T(8,128)(2,1)S(1)}, bf16[32,1024]{1,0:T(8,128)(2,1)S(1)}, bf16[8,16,1024]{2,1,0:T(8,128)(2,1)S(1)}, bf16[32,2048]{1,0:T(8,128)(2,1)S(1)}, bf16[16,2048]{1,0:T(8,128)(2,1)S(1)}) custom-call(s32[5]{0:T(128)S(1)} %stack.19.sc, bf16[64,512]{1,0:T(8,128)(2,1)S(1)} %pad_maximum_fusion.2.p0, ...), custom_call_target="tpu_custom_call" | custom-call | tf_op jit(solution)/shard_map/pallas_call | solution.py:229
  30.3 1.2 %collective-permute-done.4 = bf16[32,1024]{1,0:T(8,128)(2,1)S(1)} collective-permute-done((bf16[32,1024]{1,0:T(8,128)(2,1)S(1)}, bf16[32,1024]{1,0:T(8,128)(2,1)S(1)}, u32[]{:S(2)}, u32[]{:S(2)}) %collective-permute-start.4) | collective-permute-done | bytes 65568 | tf_op jit(solution)/shard_map/ppermute | solution.py:243
  31.7 1.2 %pad_maximum_fusion = bf16[8,80,1024]{2,1,0:T(8,128)(2,1)} fusion(bf16[8,16,1024]{2,1,0:T(8,128)(2,1)S(1)} %get-tuple-element.38, bf16[8,64,1024]{2,1,0:T(8,128)(2,1)S(1)} %broadcast_in_dim.52), kind=kLoop, calls=%fused_computation | loop fusion | flops 2621440 | bytes 2621440 | tf_op jit(solution)/shard_map/concatenate | solution.py:291
  32.9 9.0 %all-to-all-start = ((bf16[8,80,1024]{2,1,0:T(8,128)(2,1)}), bf16[8,80,1024]{2,1,0:T(8,128)(2,1)S(1)}, u32[]{:S(2)}, u32[]{:S(2)}) async-start(bf16[8,80,1024]{2,1,0:T(8,128)(2,1)} %pad_maximum_fusion), calls=%async_computation | async-start | bytes 2621440 | tf_op jit(solution)/shard_map/all_to_all | solution.py:292
  42.4 1.1 %shard_map.174.strip = f32[2,128,512]{2,1,0:T(8,128)S(1)} custom-call(s32[5]{0:T(128)S(1)} %stack.19.sc, s32[8,640]{1,0:T(8,128)S(1)} %broadcast_in_dim.54.near, f32[32,4]{1,0:T(8,128)S(1)} %copy.19.table), custom_call_target="tpu_custom_call" | custom-call | tf_op jit(solution)/shard_map/pallas_call | solution.py:229
  43.5 18.1 %all-to-all-done.got = bf16[8,80,1024]{2,1,0:T(8,128)(2,1)S(1)} async-done(((bf16[8,80,1024]{2,1,0:T(8,128)(2,1)}), bf16[8,80,1024]{2,1,0:T(8,128)(2,1)S(1)}, u32[]{:S(2)}, u32[]{:S(2)}) %all-to-all-start) | async-done | bytes 1310752 | tf_op jit(solution)/shard_map/all_to_all | solution.py:292
  61.7 1.5 %collective-permute-start.10 = (bf16[8,16,1024]{2,1,0:T(8,128)(2,1)S(1)}, bf16[8,16,1024]{2,1,0:T(8,128)(2,1)S(1)}, u32[]{:S(2)}, u32[]{:S(2)}) collective-permute-start(bf16[8,16,1024]{2,1,0:T(8,128)(2,1)S(1)} %slice.17.mine), channel_id=1, source_target_pairs={{0,4},{4,0},{1,5},{5,1},{2,6},{6,2},{3,7},{7,3},{8,12},{12,8},{9,1... | collective-permute-start | bytes 786440 | tf_op jit(solution)/shard_map/ppermute | solution.py:243
  63.2 5.3 %shard_map.175 = (bf16[4,528,256]{2,1,0:T(8,128)(2,1)S(1)}, bf16[4,48,256]{2,1,0:T(8,128)(2,1)S(1)}, bf16[4,48,256]{2,1,0:T(8,128)(2,1)S(1)}) custom-call(s32[5]{0:T(128)S(1)} %stack.19.sc, bf16[8,80,1024]{2,1,0:T(8,128)(2,1)S(1)} %all-to-all-done.got, f32[2,128,512]{2,1,0:T(8,128)S(1)} %shard_map.174.strip), custom_call_target="tpu_custom_call" | custom-call | flops 6000000000 | tf_op jit(solution)/shard_map/pallas_call | solution.py:229
  68.6 1.1 %shard_map.177 = (f32[4,2,64,256]{3,2,1,0:T(8,128)S(1)}, bf16[4,2,64,256]{3,2,1,0:T(8,128)(2,1)S(1)}) custom-call(s32[5]{0:T(128)S(1)} %stack.19.sc, bf16[4,528,256]{2,1,0:T(8,128)(2,1)S(1)} %get-tuple-element.49.res, bf16[8,16,1024]{2,1,0:T(8,128)(2,1)S(1)} %slice.17.mine, bf16[8,16,1024]{2,1,0:T(8,128)(2,1)S(1)} %collective-permute-done.10.other), custom_call_target="tpu_custom_call" | custom-call | flops 1000000000 | tf_op jit(solution)/shard_map/pallas_call | solution.py:229
  70.3 2.0 %collective-permute-start.6 = (bf16[16,2048]{1,0:T(8,128)(2,1)S(1)}, bf16[16,2048]{1,0:T(8,128)(2,1)S(1)}, u32[]{:S(2)}, u32[]{:S(2)}) collective-permute-start(bf16[16,2048]{1,0:T(8,128)(2,1)S(1)} %get-tuple-element.42), channel_id=1, source_target_pairs={{4,0},{8,4},{12,8},{16,12},{20,16},{24,20},{28,24},{32,28},{36,32}... | collective-permute-start | bytes 196616 | tf_op jit(solution)/shard_map/ppermute | solution.py:293
  73.4 4.7 %collective-permute-done.6.nxt = bf16[16,2048]{1,0:T(8,128)(2,1)S(1)} collective-permute-done((bf16[16,2048]{1,0:T(8,128)(2,1)S(1)}, bf16[16,2048]{1,0:T(8,128)(2,1)S(1)}, u32[]{:S(2)}, u32[]{:S(2)}) %collective-permute-start.6) | collective-permute-done | bytes 65568 | tf_op jit(solution)/shard_map/ppermute | solution.py:293
  78.1 4.8 %shard_map.176 = (bf16[80,640]{1,0:T(8,128)(2,1)S(1)}, bf16[80,640]{1,0:T(8,128)(2,1)S(1)}, bf16[80,640]{1,0:T(8,128)(2,1)S(1)}, f32[80,640]{1,0:T(8,128)S(1)}, ...) custom-call(s32[5]{0:T(128)S(1)} %stack.19.sc, bf16[4,48,256]{2,1,0:T(8,128)(2,1)S(1)} %get-tuple-element.39.keep_r, ...), custom_call_target="tpu_custom_call" | custom-call | flops 1000000000 | tf_op jit(solution)/shard_map/pallas_call | solution.py:229
  83.0 3.1 %collective-permute-start.8 = (bf16[80,640]{1,0:T(8,128)(2,1)S(1)}, bf16[80,640]{1,0:T(8,128)(2,1)S(1)}, u32[]{:S(2)}, u32[]{:S(2)}) collective-permute-start(bf16[80,640]{1,0:T(8,128)(2,1)S(1)} %get-tuple-element.45), channel_id=1, source_target_pairs={{0,2},{1,3},{2,0},{3,1},{4,6},{5,7},{6,4},{7,5},{8,10},{9,11},{10,... | collective-permute-start | bytes 307208 | tf_op jit(solution)/shard_map/ppermute | solution.py:243
  86.3 1.4 %collective-permute-done.7.r1 = bf16[80,640]{1,0:T(8,128)(2,1)S(1)} collective-permute-done((bf16[80,640]{1,0:T(8,128)(2,1)S(1)}, bf16[80,640]{1,0:T(8,128)(2,1)S(1)}, u32[]{:S(2)}, u32[]{:S(2)}) %collective-permute-start.7) | collective-permute-done | bytes 102432 | tf_op jit(solution)/shard_map/ppermute | solution.py:243
  87.7 1.5 %collective-permute-done.8.r2 = bf16[80,640]{1,0:T(8,128)(2,1)S(1)} collective-permute-done((bf16[80,640]{1,0:T(8,128)(2,1)S(1)}, bf16[80,640]{1,0:T(8,128)(2,1)S(1)}, u32[]{:S(2)}, u32[]{:S(2)}) %collective-permute-start.8) | collective-permute-done | bytes 102432 | tf_op jit(solution)/shard_map/ppermute | solution.py:243
  89.6 2.2 %shard_map.179 = (bf16[512,512]{1,0:T(8,128)(2,1)}, bf16[512,512]{1,0:T(8,128)(2,1)}, f32[64,512]{1,0:T(8,128)}, f32[64,512]{1,0:T(8,128)}, f32[64,512]{1,0:T(8,128)}, /*index=5*/f32[64,512]{1,0:T(8,128)}) custom-call(s32[5]{0:T(128)S(1)} %stack.19.sc, f32[80,640]{1,0:T(8,128)S(1)} %get-tuple-element.43.keep, bf16[80,640]{1,0:T(8,128)(2,1)S(1)} %collective-permute-done.7.r1, ...), custom_call_target="tpu_custom_call" | custom-call | tf_op jit(solution)/shard_map/pallas_call | solution.py:229
  (54 shorter events, 3.3 us)
Async XLA Ops:
  1.4 1.0 %copy-start.4 = (bf16[1,512,512]{2,1,0:T(8,128)(2,1)S(1)}, bf16[1,512,512]{2,1,0:T(8,128)(2,1)}, u32[]{:S(2)}) copy-start(bf16[1,512,512]{2,1,0:T(8,128)(2,1)} %param.13) | copy-start | bytes 1572868
  2.4 1.0 %copy-start.5 = (bf16[1,512,512]{2,1,0:T(8,128)(2,1)S(1)}, bf16[1,512,512]{2,1,0:T(8,128)(2,1)}, u32[]{:S(2)}) copy-start(bf16[1,512,512]{2,1,0:T(8,128)(2,1)} %param.25) | copy-start | bytes 1572868
  3.5 0.8 copy-start.6
  4.2 0.7 copy-start.10
  4.9 0.7 copy-start.12
  7.1 7.1 %collective-permute-start = (f32[8,512]{1,0:T(8,128)S(1)}, f32[8,512]{1,0:T(8,128)S(1)}, u32[]{:S(2)}, u32[]{:S(2)}) collective-permute-start(f32[8,512]{1,0:T(8,128)S(1)} %get-tuple-element.34), channel_id=1, source_target_pairs={{0,4},{4,8},{8,12},{12,16},{16,20},{20,24},{24,28},{28,32},{32,36}... | collective-permute-start | bytes 49160 | tf_op jit(solution)/shard_map/ppermute | solution.py:263
  14.2 5.7 %collective-permute-start.1 = (bf16[64,512]{1,0:T(8,128)(2,1)S(1)}, bf16[64,512]{1,0:T(8,128)(2,1)S(1)}, u32[]{:S(2)}, u32[]{:S(2)}) collective-permute-start(bf16[64,512]{1,0:T(8,128)(2,1)S(1)} %pad_maximum_fusion.2.p0), channel_id=1, source_target_pairs={{0,1},{1,2},{2,3},{3,0},{4,5},{5,6},{6,7},{7,4},{8,9},{9,10},{10,1... | collective-permute-start | bytes 196616 | tf_op jit(solution)/shard_map/ppermute | solution.py:243
  15.9 5.7 %collective-permute-start.2 = (bf16[64,512]{1,0:T(8,128)(2,1)S(1)}, bf16[64,512]{1,0:T(8,128)(2,1)S(1)}, u32[]{:S(2)}, u32[]{:S(2)}) collective-permute-start(bf16[64,512]{1,0:T(8,128)(2,1)S(1)} %pad_maximum_fusion.2.p0), channel_id=1, source_target_pairs={{0,2},{1,3},{2,0},{3,1},{4,6},{5,7},{6,4},{7,5},{8,10},{9,11},{10,... | collective-permute-start | bytes 196616 | tf_op jit(solution)/shard_map/ppermute | solution.py:243
  19.2 3.1 %collective-permute-start.3 = (bf16[64,512]{1,0:T(8,128)(2,1)S(1)}, bf16[64,512]{1,0:T(8,128)(2,1)S(1)}, u32[]{:S(2)}, u32[]{:S(2)}) collective-permute-start(bf16[64,512]{1,0:T(8,128)(2,1)S(1)} %pad_maximum_fusion.2.p0), channel_id=1, source_target_pairs={{0,3},{1,0},{2,1},{3,2},{4,7},{5,4},{6,5},{7,6},{8,11},{9,8},{10,9... | collective-permute-start | bytes 196616 | tf_op jit(solution)/shard_map/ppermute | solution.py:243
  22.4 1.6 %copy-start = (bf16[2048,512]{1,0:T(8,128)(2,1)S(1)}, bf16[2048,512]{1,0:T(8,128)(2,1)}, u32[]{:S(2)}) copy-start(bf16[2048,512]{1,0:T(8,128)(2,1)} %wq.3) | copy-start | bytes 6291460
  24.0 1.6 %copy-start.2 = (bf16[2048,512]{1,0:T(8,128)(2,1)S(1)}, bf16[2048,512]{1,0:T(8,128)(2,1)}, u32[]{:S(2)}) copy-start(bf16[2048,512]{1,0:T(8,128)(2,1)} %wk.3) | copy-start | bytes 6291460
  25.5 0.7 copy-start.8
  30.2 1.3 %collective-permute-start.4 = (bf16[32,1024]{1,0:T(8,128)(2,1)S(1)}, bf16[32,1024]{1,0:T(8,128)(2,1)S(1)}, u32[]{:S(2)}, u32[]{:S(2)}) collective-permute-start(bf16[32,1024]{1,0:T(8,128)(2,1)S(1)} %get-tuple-element.37), channel_id=1, source_target_pairs={{0,4},{4,0},{1,5},{5,1},{2,6},{6,2},{3,7},{7,3},{8,12},{12,8},{9,1... | collective-permute-start | bytes 196616 | tf_op jit(solution)/shard_map/ppermute | solution.py:243
  31.7 10.3 %copy-start.15 = (s32[512]{0:T(512)S(1)}, s32[512]{0:T(512)}, u32[]{:S(2)}) copy-start(s32[512]{0:T(512)} %param.23) | copy-start | bytes 6148
  31.7 10.6 %copy-start.14 = (f32[32,4]{0,1:T(4,128)S(1)}, f32[32,4]{0,1:T(4,128)}, u32[]{:S(2)}) copy-start(f32[32,4]{0,1:T(4,128)} %param.22) | copy-start | bytes 1540
  32.9 28.7 %all-to-all-start = ((bf16[8,80,1024]{2,1,0:T(8,128)(2,1)}), bf16[8,80,1024]{2,1,0:T(8,128)(2,1)S(1)}, u32[]{:S(2)}, u32[]{:S(2)}) async-start(bf16[8,80,1024]{2,1,0:T(8,128)(2,1)} %pad_maximum_fusion), calls=%async_computation | async-start | bytes 2621440 | tf_op jit(solution)/shard_map/all_to_all | solution.py:292
  61.7 6.9 %collective-permute-start.10 = (bf16[8,16,1024]{2,1,0:T(8,128)(2,1)S(1)}, bf16[8,16,1024]{2,1,0:T(8,128)(2,1)S(1)}, u32[]{:S(2)}, u32[]{:S(2)}) collective-permute-start(bf16[8,16,1024]{2,1,0:T(8,128)(2,1)S(1)} %slice.17.mine), channel_id=1, source_target_pairs={{0,4},{4,0},{1,5},{5,1},{2,6},{6,2},{3,7},{7,3},{8,12},{12,8},{9,1... | collective-permute-start | bytes 786440 | tf_op jit(solution)/shard_map/ppermute | solution.py:243
  68.5 9.5 %copy-start.1 = (bf16[2048,512]{1,0:T(8,128)(2,1)S(1)}, bf16[2048,512]{1,0:T(8,128)(2,1)}, u32[]{:S(2)}) copy-start(bf16[2048,512]{1,0:T(8,128)(2,1)} %wq.3) | copy-start | bytes 6291460
  68.6 9.5 %copy-start.3 = (bf16[2048,512]{1,0:T(8,128)(2,1)S(1)}, bf16[2048,512]{1,0:T(8,128)(2,1)}, u32[]{:S(2)}) copy-start(bf16[2048,512]{1,0:T(8,128)(2,1)} %wk.3) | copy-start | bytes 6291460
  68.6 9.5 %copy-start.9 = (f32[2048]{0:T(1024)S(1)}, f32[2048]{0:T(1024)}, u32[]{:S(2)}) copy-start(f32[2048]{0:T(1024)} %param.17) | copy-start | bytes 24580
  69.7 2.6 %collective-permute-start.11 = (bf16[4,2,64,256]{3,2,1,0:T(8,128)(2,1)S(1)}, bf16[4,2,64,256]{3,2,1,0:T(8,128)(2,1)S(1)}, u32[]{:S(2)}, u32[]{:S(2)}) collective-permute-start(bf16[4,2,64,256]{3,2,1,0:T(8,128)(2,1)S(1)} %get-tuple-element.51), channel_id=1, source_target_pairs={{0,4},{4,0},{1,5},{5,1},{2,6},{6,2},{3,7},{7,3},{8,12},{12,8},{9,1... | collective-permute-start | bytes 786440 | tf_op jit(solution)/shard_map/ppermute | solution.py:243
  69.8 8.3 %collective-permute-start.5 = (bf16[4,48,256]{2,1,0:T(8,128)(2,1)S(1)}, bf16[4,48,256]{2,1,0:T(8,128)(2,1)S(1)}, u32[]{:S(2)}, u32[]{:S(2)}) collective-permute-start(bf16[4,48,256]{2,1,0:T(8,128)(2,1)S(1)} %get-tuple-element.40), channel_id=1, source_target_pairs={{0,4},{4,0},{1,5},{5,1},{2,6},{6,2},{3,7},{7,3},{8,12},{12,8},{9,1... | collective-permute-start | bytes 294920 | tf_op jit(solution)/shard_map/ppermute | solution.py:243
  70.3 7.8 %collective-permute-start.6 = (bf16[16,2048]{1,0:T(8,128)(2,1)S(1)}, bf16[16,2048]{1,0:T(8,128)(2,1)S(1)}, u32[]{:S(2)}, u32[]{:S(2)}) collective-permute-start(bf16[16,2048]{1,0:T(8,128)(2,1)S(1)} %get-tuple-element.42), channel_id=1, source_target_pairs={{4,0},{8,4},{12,8},{16,12},{20,16},{24,20},{28,24},{32,28},{36,32}... | collective-permute-start | bytes 196616 | tf_op jit(solution)/shard_map/ppermute | solution.py:293
  72.9 16.7 %collective-permute-start.12 = (bf16[4,64,512]{2,1,0:T(8,128)(2,1)S(1)}, bf16[4,64,512]{2,1,0:T(8,128)(2,1)S(1)}, u32[]{:S(2)}, u32[]{:S(2)}) collective-permute-start(bf16[4,64,512]{2,1,0:T(8,128)(2,1)S(1)} %get-tuple-element.53), channel_id=1, source_target_pairs={{0,64},{64,0},{1,65},{65,1},{2,66},{66,2},{3,67},{67,3},{4,68},{68... | collective-permute-start | bytes 786440 | tf_op jit(solution)/shard_map/ppermute | solution.py:243
  78.1 11.5 %copy-start.7 = (f32[16,512]{1,0:T(8,128)S(1)}, f32[16,512]{1,0:T(8,128)}, u32[]{:S(2)}) copy-start(f32[16,512]{1,0:T(8,128)} %up_gain.3) | copy-start | bytes 98308
  78.1 11.5 %copy-start.11 = (f32[4,512]{1,0:T(4,128)S(1)}, f32[4,512]{1,0:T(4,128)}, u32[]{:S(2)}) copy-start(f32[4,512]{1,0:T(4,128)} %first.3) | copy-start | bytes 24580
  78.1 11.5 %copy-start.13 = (f32[4,512]{1,0:T(4,128)S(1)}, f32[4,512]{1,0:T(4,128)}, u32[]{:S(2)}) copy-start(f32[4,512]{1,0:T(4,128)} %second.3) | copy-start | bytes 24580
  82.9 4.8 %collective-permute-start.7 = (bf16[80,640]{1,0:T(8,128)(2,1)S(1)}, bf16[80,640]{1,0:T(8,128)(2,1)S(1)}, u32[]{:S(2)}, u32[]{:S(2)}) collective-permute-start(bf16[80,640]{1,0:T(8,128)(2,1)S(1)} %get-tuple-element.44), channel_id=1, source_target_pairs={{0,1},{1,2},{2,3},{3,0},{4,5},{5,6},{6,7},{7,4},{8,9},{9,10},{10,1... | collective-permute-start | bytes 307208 | tf_op jit(solution)/shard_map/ppermute | solution.py:243
  83.0 6.3 %collective-permute-start.8 = (bf16[80,640]{1,0:T(8,128)(2,1)S(1)}, bf16[80,640]{1,0:T(8,128)(2,1)S(1)}, u32[]{:S(2)}, u32[]{:S(2)}) collective-permute-start(bf16[80,640]{1,0:T(8,128)(2,1)S(1)} %get-tuple-element.45), channel_id=1, source_target_pairs={{0,2},{1,3},{2,0},{3,1},{4,6},{5,7},{6,4},{7,5},{8,10},{9,11},{10,... | collective-permute-start | bytes 307208 | tf_op jit(solution)/shard_map/ppermute | solution.py:243
  86.1 3.5 %collective-permute-start.9 = (bf16[80,640]{1,0:T(8,128)(2,1)S(1)}, bf16[80,640]{1,0:T(8,128)(2,1)S(1)}, u32[]{:S(2)}, u32[]{:S(2)}) collective-permute-start(bf16[80,640]{1,0:T(8,128)(2,1)S(1)} %get-tuple-element.46), channel_id=1, source_target_pairs={{0,3},{1,0},{2,1},{3,2},{4,7},{5,4},{6,5},{7,6},{8,11},{9,8},{10,9... | collective-permute-start | bytes 307208 | tf_op jit(solution)/shard_map/ppermute | solution.py:243

commit v3 on v2

--- a/solution.py
+++ b/solution.py
@@ -22,7 +22,9 @@
 SCALE = 1.0 / math.sqrt(HD)
 ROWS = CL + 16
 VM = pltpu.VMEM
+BIG = 63 * 2**20
 SM = pltpu.SMEM
+PIECE = 4 * CL + 16
 
 
 def dg(a, b, ca, cb):
@@ -40,10 +42,19 @@
     return (pos < doc_len).astype(F32)
 
 
-def before_kernel(sc, tokens, grad_out, first, second, up_gain, part, last, gco, shift):
+def before_kernel(
+    sc, tokens_h, grad_h, first_h, second_h, up_h, gain_h, part, last, ahead, gco, gain,
+    tokens, grad_out, first, second, up_gain, shift, sems,
+):
+    pairs = ((tokens_h, tokens), (first_h, first), (second_h, second), (grad_h, grad_out), (up_h, up_gain), (gain_h, gain))
+    copies = [pltpu.make_async_copy(a, b, sems.at[i]) for i, (a, b) in enumerate(pairs)]
+    for c in copies:
+        c.start()
     mask = byte_mask(sc[0], sc[1])
+    u = lax.broadcasted_iota(jnp.int32, (CL, 16, WL), 1)
+    for c in copies[:3]:
+        c.wait()
     taps = tap_weights(first[...], second[...])
-    u = lax.broadcasted_iota(jnp.int32, (CL, 16, WL), 1)
     prod = tokens[...].astype(F32).reshape(CL, 16, WL) * mask * taps[None]
     own = jnp.sum(jnp.where(u == 0, prod, 0.0), axis=1)
     onward = jnp.sum(jnp.where(u == 0, 0.0, prod), axis=1)
@@ -51,6 +62,9 @@
     shift[8 : 8 + CL] = onward
     part[...] = own + shift[7 : 7 + CL]
     last[...] = jnp.broadcast_to(shift[7 + CL : 8 + CL], (8, WL))
+    ahead[...] = jnp.broadcast_to(own[0:1], (8, WL))
+    for c in copies[3:]:
+        c.wait()
     weighted = grad_out[...].astype(F32).reshape(CL, 16, WL) * mask * up_gain[...][None]
     gco[...] = jnp.sum(weighted, axis=1).astype(BF16)
 
@@ -67,37 +81,57 @@
 
 
 def project_kernel(
-    sc, p0, r1, r2, r3, gain, wq, wk, wv, wo, keep, send, blocks, craw, first, nrm, gco, both
-):
-    z, core = sc[2], sc[3]
+    sc, p0, r1, r2, r3, gain, wq, wk, wv, wo, keep, send, blocks, c48, craw, nrm, gco, both, ws, sems
+):
+    copies = [pltpu.make_async_copy(w, ws.at[i], sems.at[i]) for i, w in enumerate((wo, wq, wk, wv))]
+    for cp in copies:
+        cp.start()
+    z, core, x, y = sc[2], sc[3], sc[5], sc[6]
     for s, src in enumerate((p0, r1, r2, r3)):
         cols = pl.ds(pl.multiple_of(lax.rem(z + 4 - s, 4) * WL, WL), WL)
-        craw[:, cols] = src[0:CL]
-        gco[:, cols] = src[CL : 2 * CL]
-    first[...] = craw[0:16]
+        for i in range(2):
+            rows = slice(i * CL, i * CL + CL)
+            craw[rows, cols] = src[2 * i * CL : 2 * i * CL + CL]
+            gco[rows, cols] = src[2 * i * CL + CL : 2 * i * CL + 2 * CL]
+        c48[CL:ROWS, cols] = src[4 * CL : PIECE]
+    c48[0:CL] = craw[pl.ds(pl.multiple_of(y * CL, CL), CL)]
     c = craw[...].astype(F32)
     r = lax.rsqrt(jnp.sum(c * c, axis=1, keepdims=True) * (1.0 / D) + 1e-6)
     nrm[...] = (c * r * gain[...]).astype(BF16)
-    for i, (src, w) in enumerate(((nrm, wq), (nrm, wk), (nrm, wv), (gco, wo))):
-        y = jnp.dot(src[...], w[...], preferred_element_type=F32).astype(BF16)
+    for i, (src, slot) in enumerate(((gco, 3), (nrm, 0), (nrm, 1), (nrm, 2))):
+        copies[i].wait()
+        v = jnp.dot(src[...], ws[i], preferred_element_type=F32).astype(BF16)
         for half in range(2):
-            both[half, :, i * HW : i * HW + HW] = y[:, half * HW : half * HW + HW]
+            both[half, :, slot * HW : slot * HW + HW] = v[:, half * HW : half * HW + HW]
     keep[...] = both[core]
     send[...] = both[1 - core]
-    for chip in range(8):
+    for s in range(4):
         for d in range(2):
-            cols = slice((d * 8 + chip) * 128, (d * 8 + chip) * 128 + 128)
-            for part in range(2):
-                rows = slice(part * 16, part * 16 + 16)
-                at = part * 512 + d * 128
-                blocks[chip, :, at : at + 128] = nrm[rows, cols]
-                blocks[chip, :, at + 256 : at + 384] = gco[rows, cols]
-
-
-def attend_kernel(sc, got, strip, res, keep, send, q, k, v, ga, acck, accv):
-    ctx, doc_len, core = sc[0], sc[1], sc[3]
-    for i, dst in enumerate((q, k, v, ga)):
-        dst[...] = got[:, 0:64, i * HW : i * HW + HW].reshape(LC, HW)
+            chip = lax.rem(x + s, 4) * 2 + y
+            cols = pl.ds(pl.multiple_of((d * 8 + chip) * 128, 128), 128)
+            for i in range(2):
+                rows = slice(i * CL, i * CL + CL)
+                at = i * 512 + d * 128
+                blocks[s, :, at : at + 128] = nrm[rows, cols]
+                blocks[s, :, at + 256 : at + 384] = gco[rows, cols]
+
+
+def pack_kernel(sc, keep, swapped, blocks, b0, b1, b2, b3):
+    core = sc[3]
+    for s, b in enumerate((b0, b1, b2, b3)):
+        for i in range(2):
+            for src, c in ((keep, core), (swapped, 1 - core)):
+                rows = pl.ds(pl.multiple_of(i * 64 + c * CL, CL), CL)
+                b[rows] = src[i * CL : i * CL + CL]
+        b[128:160] = blocks[s]
+
+
+def attend_kernel(sc, b0, r1, r2, r3, strip, res, keep, send, q, k, v, ga, acck, accv):
+    ctx, doc_len, core, x = sc[0], sc[1], sc[3], sc[5]
+    for s, src in enumerate((b0, r1, r2, r3)):
+        rows = pl.ds(pl.multiple_of(lax.rem(x + 4 - s, 4) * 128, 128), 128)
+        for i, dst in enumerate((q, k, v, ga)):
+            dst[rows] = src[0:128, i * HW : i * HW + HW]
     key_pos = lax.broadcasted_iota(jnp.int32, (1, LC), 1)
     key_mask = jnp.where(16 * key_pos < doc_len, 0.0, NEG)
     for h in range(NH):
@@ -132,13 +166,14 @@
 
 
 def weights_kernel(sc, res, mine, other, keep, send, nb, gb, tile):
-    core = sc[3]
-    for chip in range(8):
+    core, x = sc[3], sc[5]
+    for s in range(4):
         for src, c in ((mine, core), (other, 1 - core)):
-            for part in range(2):
-                rows = pl.ds(pl.multiple_of(chip * 64 + c * CL + part * 16, 16), 16)
-                nb[rows] = src[chip, :, part * 512 : part * 512 + 256]
-                gb[rows] = src[chip, :, part * 512 + 256 : part * 512 + 512]
+            for i in range(2):
+                at = (lax.rem(x + 4 - s, 4) * 4 + i * 2 + c) * CL
+                rows = pl.ds(pl.multiple_of(at, CL), CL)
+                nb[rows] = src[s, :, i * 512 : i * 512 + 256]
+                gb[rows] = src[s, :, i * 512 + 256 : i * 512 + 512]
     for w in range(4):
         tile[...] = dg((gb if w == 3 else nb)[...], res[w, 0:LC], 0, 0)
         for d in range(2):
@@ -146,7 +181,7 @@
             send[w, d] = tile[pl.ds(pl.multiple_of(d * 128 + 64 - core * 64, 64), 64)].astype(BF16)
 
 
-def join_kernel(sc, keep, got, own, send):
+def join_kernel(sc, keep, got, after, own, send):
     core, dp = sc[3], sc[4]
     a = pl.ds(pl.multiple_of(core * HW, HW), HW)
     b = pl.ds(pl.multiple_of((1 - core) * HW, HW), HW)
@@ -157,13 +192,11 @@
 
 
 def partial_kernel(
-    sc, keep_r, got_r, craw, nxt, gain, wq, wk, wv, wo, msg1, msg2, msg3, keep, cz, inv_out, g, c
+    sc, keep_r, got_r, c, gain, wq, wk, wv, wo, msg1, msg2, msg3, keep, cz, inv_out, g
 ):
     z, core = sc[2], sc[3]
     g[:, :, pl.ds(pl.multiple_of(core * HW, HW), HW)] = keep_r[...]
     g[:, :, pl.ds(pl.multiple_of((1 - core) * HW, HW), HW)] = got_r[...]
-    c[0:CL] = craw[...]
-    c[CL:ROWS] = nxt[...]
     cf = c[...].astype(F32)
     r = lax.rsqrt(jnp.sum(cf * cf, axis=1, keepdims=True) * (1.0 / D) + 1e-6)
     inv_out[...] = jnp.broadcast_to(r, (ROWS, 128))
@@ -218,21 +251,16 @@
         o[...] = dw[w] + other[w].astype(F32)
 
 
-def call(kernel, outs, args, scratch=(), smem=(0,), flops=0, size=0, vmem=48 * 2**20, loads=False):
-    def spec(i, a):
-        if i in smem:
-            return pl.BlockSpec(memory_space=SM)
-        if loads:
-            return pl.BlockSpec(a.shape, lambda i, n=a.ndim: (0,) * n)
-        return pl.BlockSpec(memory_space=VM)
+def call(kernel, outs, args, scratch=(), smem=(0,), flops=0, size=0, vmem=8 * 2**20, hbm=()):
+    def spec(i):
+        return pl.BlockSpec(memory_space=SM if i in smem else pltpu.HBM if i in hbm else VM)
 
     return pl.pallas_call(
         kernel,
-        grid=(1,) if loads else (),
         out_shape=[jax.ShapeDtypeStruct(s, d) for s, d in outs],
-        in_specs=[spec(i, a) for i, a in enumerate(args)],
+        in_specs=[spec(i) for i in range(len(args))],
         out_specs=[pl.BlockSpec(memory_space=VM)] * len(outs),
-        scratch_shapes=[pltpu.VMEM(s, d) for s, d in scratch],
+        scratch_shapes=[pltpu.VMEM(*s) if isinstance(s, tuple) else s for s in scratch],
         compiler_params=pltpu.CompilerParams(vmem_limit_bytes=vmem),
         cost_estimate=pl.CostEstimate(flops=flops, bytes_accessed=size, transcendentals=0),
     )(*args)
@@ -250,20 +278,31 @@
     x, y, core = lax.axis_index("x"), lax.axis_index("y"), lax.axis_index("core")
     dp, z = lax.axis_index("dp"), lax.axis_index("tensor")
     ctx = (x * 2 + y) * 2 + core
-    sc = jnp.stack([ctx, lengths[0], z, core, dp]).astype(jnp.int32)
-    gain = norm_gain[None]
+    sc = jnp.stack([ctx, lengths[0], z, core, dp, x, y]).astype(jnp.int32)
     weights = (w_query, w_key, w_value, w_out)
-    part, last, gco = call(
+    part, last, ahead, gco, gain = call(
         before_kernel,
-        [((CL, WL), F32), ((8, WL), F32), ((CL, WL), BF16)],
-        (sc, tokens[0], grad_out[0], conv_first, conv_second, up_gain),
-        [((CL + 8, WL), F32)],
-        loads=True,
-    )
-    rim = lax.ppermute(last, ("x", "y", "core"), [(i, i + 1) for i in range(15)])
+        [((CL, WL), F32), ((8, WL), F32), ((8, WL), F32), ((CL, WL), BF16), ((1, D), F32)],
+        (sc, tokens[0], grad_out[0], conv_first, conv_second, up_gain, norm_gain[None]),
+        [
+            ((SEG, WL), BF16), ((SEG, WL), BF16), ((4, WL), F32), ((4, WL), F32), ((16, WL), F32),
+            ((CL + 8, WL), F32), pltpu.SemaphoreType.DMA((6,)),
+        ],
+        hbm=(1, 2, 3, 4, 5, 6),
+        vmem=BIG,
+    )
+    line = ("x", "y", "core")
+    rim = lax.ppermute(last, line, [(i, i + 1) for i in range(15)])
+    lead = lax.ppermute(ahead, line, [(i + 1, i) for i in range(15)])
     is_first = (jnp.arange(CL) == 0)[:, None]
     coarse = (part + jnp.where(is_first, rim[0:1], 0.0)).astype(BF16)
     piece = jnp.concatenate([coarse, gco], axis=0)
+    across = shifted(piece, "y", 1)
+    nxt = jnp.where(is_first[:16], lead[0:1] + last[0:1], 0.0).astype(BF16)
+    low_y = y == 0
+    piece = jnp.concatenate(
+        [jnp.where(low_y, piece, across), jnp.where(low_y, across, piece), nxt], axis=0
+    )
     n = 640
     near = jnp.concatenate(
         [
@@ -279,24 +318,29 @@
         smem=(0, 2),
     )
     pieces = [piece] + [shifted(piece, "tensor", s) for s in (1, 2, 3)]
-    keep, send, blocks, craw, first = call(
+    keep, send, blocks, c48 = call(
         project_kernel,
-        [((CL, 4 * HW), BF16), ((CL, 4 * HW), BF16), ((8, 16, 4 * HW), BF16), ((CL, D), BF16), ((16, D), BF16)],
+        [((2 * CL, 4 * HW), BF16), ((2 * CL, 4 * HW), BF16), ((4, CL, 4 * HW), BF16), ((ROWS, D), BF16)],
         (sc, *pieces, gain, *weights),
-        [((CL, D), BF16), ((CL, D), BF16), ((2, CL, 4 * HW), BF16)],
+        [
+            ((2 * CL, D), BF16), ((2 * CL, D), BF16), ((2 * CL, D), BF16), ((2, 2 * CL, 4 * HW), BF16),
+            ((4, D, WL), BF16), pltpu.SemaphoreType.DMA((4,)),
+        ],
+        flops=10**9,
+        hbm=(6, 7, 8, 9),
+        vmem=BIG - 10 * 2**20,
     )
     swapped = shifted(send, "core", 1)
-    low = core == 0
-    pair = jnp.concatenate([jnp.where(low, keep, swapped), jnp.where(low, swapped, keep)], axis=0)
-    bundle = jnp.concatenate([jnp.broadcast_to(pair[None], (8,) + pair.shape), blocks], axis=1)
-    got = lax.all_to_all(bundle, ("x", "y"), 0, 0, tiled=True)
-    nxt = lax.ppermute(first, ("x", "y", "core"), [(i + 1, i) for i in range(15)])
-    mine = got[:, 64:80]
+    b0, b1, b2, b3 = call(
+        pack_kernel, [((5 * CL, 4 * HW), BF16)] * 4, (sc, keep, swapped, blocks)
+    )
+    bundles = [b0, shifted(b1, "x", 1), shifted(b2, "x", 2), shifted(b3, "x", 3)]
+    mine = jnp.stack([b[4 * CL :] for b in bundles])
     other_rows = shifted(mine, "core", 1)
     res, keep_r, send_r = call(
         attend_kernel,
         [((4, LC + 16, HW), BF16), ((4, ROWS, HW), BF16), ((4, ROWS, HW), BF16)],
-        (sc, got, strip),
+        (sc, *bundles, strip),
         [((LC, HW), BF16)] * 4 + [((NH, LC, HD), F32)] * 2,
         flops=6 * 10**9,
     )
@@ -309,19 +353,19 @@
         flops=10**9,
     )
     dw_got = shifted(dw_send, "core", 1)
-    dw_own, dw_other = call(
-        join_kernel, [((4, 64, WL), F32), ((4, 64, WL), BF16)], (sc, dw_keep, dw_got)
-    )
-    dw_other = shifted(dw_other, "dp", 1)
     msg = (CL + ROWS, WL + 128)
     m1, m2, m3, own, cz, inv = call(
         partial_kernel,
         [(msg, BF16), (msg, BF16), (msg, BF16), (msg, F32), ((ROWS, WL), BF16), ((ROWS, 128), F32)],
-        (sc, keep_r, got_r, craw, nxt, gain, *weights),
-        [((4, ROWS, WL), BF16), ((ROWS, D), BF16)],
+        (sc, keep_r, got_r, c48, gain, *weights),
+        [((4, ROWS, WL), BF16)],
         flops=10**9,
     )
     r1, r2, r3 = shifted(m1, "tensor", 1), shifted(m2, "tensor", 2), shifted(m3, "tensor", 3)
+    dw_own, dw_other = call(
+        join_kernel, [((4, 64, WL), F32), ((4, 64, WL), BF16)], (sc, dw_keep, dw_got, inv)
+    )
+    dw_other = shifted(dw_other, "dp", 1)
     update, grad_tokens, *dw = call(
         after_kernel,
         [((SEG, WL), BF16)] * 2 + [((64, WL), F32)] * 4,

time: 92.4 us -> 92.8 us (level)
  local copies, waits for them, and re-layouts: 8.82 us -> 3.42 us
  starting transfers between devices: 29 us -> 32.4 us
  Pallas kernels: 20.4 us -> 22.4 us
  other arithmetic: 1.42 us -> 3.39 us
  waiting for transfers between devices: 30.6 us -> 29.2 us
    ppermute x11 -> x15, waiting for transfers between devices: 6.96 us -> 28.2 us  [shifted(): return lax.ppermute(x, axis, [(i, (i + steps) % n) for i in range(n)])]
    all_to_all x1 -> x0, waiting for transfers between devices: 18.1 us -> none  [local(): got = lax.all_to_all(bundle, ('x', 'y'), 0, 0, tiled=True)]
    ppermute x11 -> x15, starting transfers between devices: 11.8 us -> 24.2 us  [shifted(): return lax.ppermute(x, axis, [(i, (i + steps) % n) for i in range(n)])]
    all_to_all x1 -> x0, starting transfers between devices: 9.01 us -> none  [local(): got = lax.all_to_all(bundle, ('x', 'y'), 0, 0, tiled=True)]
    unnamed x35 -> x33, local copies, waits for them, and re-layouts: 8.42 us -> 2.59 us
    ppermute x2, waiting for transfers between devices: 5.52 us -> 1.04 us  [the longest x1 1.04 us: local(): rim = lax.ppermute(last, line, [(i, i + 1) for i in range(15)])]
    pallas_call x8 -> x9, Pallas kernels: 20.4 us -> 22.4 us  [call(): pl.pallas_call(kernel, out_shape=[jax.ShapeDtypeStruct(s, d) for s, d in...]
    concatenate x2 -> x1, other arithmetic: 1.24 us -> 0.01 us  [local(): jnp.concatenate([jnp.where(low_y, piece, across), jnp.where(low_y, across...]
  transfers between devices with their start and end apart: 14 -> 17, of which waited for: 9 -> 12; matrix products, arithmetic and copies ran while one was open for 1% -> 3% of each run, Pallas kernels for 13% -> 10%
where the time goes in v3:
time: 92.8 us; the launch traced here: 92.3 us
  starting transfers between devices  32.4 us (35%)
  waiting for transfers between devices  29.2 us (31%)
  Pallas kernels  22.4 us (24%)
  local copies, waits for them, and re-layouts  3.42 us (4%)
  other arithmetic  3.39 us (4%)
  between operations  1.52 us (2%)
    ppermute x15, waiting for transfers between devices, shifted(): return lax.ppermute(x, axis, [(i, (i + steps) % n) for i in range(n)])  28.2 us
    ppermute x15, starting transfers between devices, shifted(): return lax.ppermute(x, axis, [(i, (i + steps) % n) for i in range(n)])  24.2 us
    pallas_call x9, Pallas kernels, call(): pl.pallas_call(kernel, out_shape=[jax.ShapeDtypeStruct(s, d) for s, d in...  22.4 us
    ppermute x1, starting transfers between devices, local(): rim = lax.ppermute(last, line, [(i, i + 1) for i in range(15)])  4.8 us
    ppermute x1, starting transfers between devices, local(): lead = lax.ppermute(ahead, line, [(i + 1, i) for i in range(15)])  3.33 us
    unnamed x33, local copies, waits for them, and re-layouts  2.59 us
  transfers between devices with their start and end apart: 17, of which 12 were waited for; matrix products, arithmetic and copies ran while one was open for 3% of the time, Pallas kernels for 10%

profile of v3, /device:TPU:1, one launch (start us, length us, event | category | flops | bytes accessed | tf_op | source)
XLA Modules:
  0.0 92.3 jit_solution(5407890658224026310)
XLA Ops:
  1.9 3.2 %shard_map.172 = (f32[32,512]{1,0:T(8,128)}, f32[8,512]{1,0:T(8,128)}, f32[8,512]{1,0:T(8,128)}, bf16[32,512]{1,0:T(8,128)(2,1)}, f32[1,2048]{1,0:T(1,128)}) custom-call(s32[7]{0:T(128)} %stack.42.sc, bf16[512,512]{1,0:T(8,128)(2,1)} %bitcast.24, bf16[512,512]{1,0:T(8,128)(2,1)} %bitcast.25, f32[4,512]{1,0:T(4,128)} %first.1, f32[4,512]{1,0:T(4,128)} %second.1, ...), custom_call_target="tpu_custom_call" | custom-call | tf_op jit(solution)/shard_map/pallas_call | solution.py:258
  5.1 3.3 %collective-permute-start.2 = (f32[8,512]{1,0:T(8,128)}, f32[8,512]{1,0:T(8,128)S(1)}, u32[]{:S(2)}, u32[]{:S(2)}) collective-permute-start(f32[8,512]{1,0:T(8,128)} %get-tuple-element.41), channel_id=1, source_target_pairs={{4,0},{8,4},{12,8},{16,12},{20,16},{24,20},{28,24},{32,28},{36,32}... | collective-permute-start | bytes 49160 | tf_op jit(solution)/shard_map/ppermute | solution.py:296
  8.4 4.8 %collective-permute-start = (f32[8,512]{1,0:T(8,128)}, f32[8,512]{1,0:T(8,128)S(1)}, u32[]{:S(2)}, u32[]{:S(2)}) collective-permute-start(f32[8,512]{1,0:T(8,128)} %get-tuple-element.39), channel_id=1, source_target_pairs={{0,4},{4,8},{8,12},{12,16},{16,20},{20,24},{24,28},{28,32},{32,36}... | collective-permute-start | bytes 49160 | tf_op jit(solution)/shard_map/ppermute | solution.py:295
  13.3 1.0 %collective-permute-done = f32[8,512]{1,0:T(8,128)S(1)} collective-permute-done((f32[8,512]{1,0:T(8,128)}, f32[8,512]{1,0:T(8,128)S(1)}, u32[]{:S(2)}, u32[]{:S(2)}) %collective-permute-start) | collective-permute-done | bytes 16416 | tf_op jit(solution)/shard_map/ppermute | solution.py:295
  14.3 0.9 add_convert_fusion
  15.2 0.8 pad_maximum_fusion.2
  16.0 3.6 %collective-permute-start.1 = (bf16[64,512]{1,0:T(8,128)(2,1)S(1)}, bf16[64,512]{1,0:T(8,128)(2,1)S(1)}, u32[]{:S(2)}, u32[]{:S(2)}) collective-permute-start(bf16[64,512]{1,0:T(8,128)(2,1)S(1)} %pad_maximum_fusion.2), channel_id=1, source_target_pairs={{0,8},{8,0},{1,9},{9,1},{2,10},{10,2},{3,11},{11,3},{4,12},{12,4},... | collective-permute-start | bytes 196616 | tf_op jit(solution)/shard_map/ppermute | solution.py:271
  20.4 1.4 %collective-permute-done.1 = bf16[64,512]{1,0:T(8,128)(2,1)S(1)} collective-permute-done((bf16[64,512]{1,0:T(8,128)(2,1)S(1)}, bf16[64,512]{1,0:T(8,128)(2,1)S(1)}, u32[]{:S(2)}, u32[]{:S(2)}) %collective-permute-start.1) | collective-permute-done | bytes 65568 | tf_op jit(solution)/shard_map/ppermute | solution.py:271
  21.8 0.8 broadcast_select_fusion.1
  22.6 1.7 %collective-permute-start.3 = (bf16[144,512]{1,0:T(8,128)(2,1)S(1)}, bf16[144,512]{1,0:T(8,128)(2,1)S(1)}, u32[]{:S(2)}, u32[]{:S(2)}) collective-permute-start(bf16[144,512]{1,0:T(8,128)(2,1)S(1)} %pad_maximum_fusion.1.p0), channel_id=1, source_target_pairs={{0,1},{1,2},{2,3},{3,0},{4,5},{5,6},{6,7},{7,4},{8,9},{9,10},{10,1... | collective-permute-start | bytes 442376 | tf_op jit(solution)/shard_map/ppermute | solution.py:271
  24.3 3.3 %collective-permute-start.4 = (bf16[144,512]{1,0:T(8,128)(2,1)S(1)}, bf16[144,512]{1,0:T(8,128)(2,1)S(1)}, u32[]{:S(2)}, u32[]{:S(2)}) collective-permute-start(bf16[144,512]{1,0:T(8,128)(2,1)S(1)} %pad_maximum_fusion.1.p0), channel_id=1, source_target_pairs={{0,2},{1,3},{2,0},{3,1},{4,6},{5,7},{6,4},{7,5},{8,10},{9,11},{10,... | collective-permute-start | bytes 442376 | tf_op jit(solution)/shard_map/ppermute | solution.py:271
  28.3 1.5 %collective-permute-done.3.r1 = bf16[144,512]{1,0:T(8,128)(2,1)S(1)} collective-permute-done((bf16[144,512]{1,0:T(8,128)(2,1)S(1)}, bf16[144,512]{1,0:T(8,128)(2,1)S(1)}, u32[]{:S(2)}, u32[]{:S(2)}) %collective-permute-start.3) | collective-permute-done | bytes 147488 | tf_op jit(solution)/shard_map/ppermute | solution.py:271
  29.8 4.0 %collective-permute-done.4.r2 = bf16[144,512]{1,0:T(8,128)(2,1)S(1)} collective-permute-done((bf16[144,512]{1,0:T(8,128)(2,1)S(1)}, bf16[144,512]{1,0:T(8,128)(2,1)S(1)}, u32[]{:S(2)}, u32[]{:S(2)}) %collective-permute-start.4) | collective-permute-done | bytes 147488 | tf_op jit(solution)/shard_map/ppermute | solution.py:271
  35.1 5.2 %shard_map.173 = (bf16[64,1024]{1,0:T(8,128)(2,1)S(1)}, bf16[64,1024]{1,0:T(8,128)(2,1)S(1)}, bf16[4,32,1024]{2,1,0:T(8,128)(2,1)}, bf16[48,2048]{1,0:T(8,128)(2,1)}) custom-call(s32[7]{0:T(128)S(1)} %copy-done.11, bf16[144,512]{1,0:T(8,128)(2,1)S(1)} %pad_maximum_fusion.1.p0, bf16[144,512]{1,0:T(8,128)(2,1)S(1)} %collective-permute-done.3.r1, ...), custom_call_target="tpu_custom_call" | custom-call | flops 1000000000 | tf_op jit(solution)/shard_map/pallas_call | solution.py:258
  40.4 1.8 %collective-permute-start.6 = (bf16[64,1024]{1,0:T(8,128)(2,1)S(1)}, bf16[64,1024]{1,0:T(8,128)(2,1)S(1)}, u32[]{:S(2)}, u32[]{:S(2)}) collective-permute-start(bf16[64,1024]{1,0:T(8,128)(2,1)S(1)} %get-tuple-element.44), channel_id=1, source_target_pairs={{0,4},{4,0},{1,5},{5,1},{2,6},{6,2},{3,7},{7,3},{8,12},{12,8},{9,1... | collective-permute-start | bytes 393224 | tf_op jit(solution)/shard_map/ppermute | solution.py:271
  43.2 0.9 %copy-done.4 = bf16[4,32,1024]{2,1,0:T(8,128)(2,1)S(1)} copy-done((bf16[4,32,1024]{2,1,0:T(8,128)(2,1)S(1)}, bf16[4,32,1024]{2,1,0:T(8,128)(2,1)}, u32[]{:S(2)}) %copy-start.4) | copy-done | bytes 262168
  44.8 5.1 %collective-permute-start.9 = (bf16[160,1024]{1,0:T(8,128)(2,1)S(1)}, bf16[160,1024]{1,0:T(8,128)(2,1)S(1)}, u32[]{:S(2)}, u32[]{:S(2)}) collective-permute-start(bf16[160,1024]{1,0:T(8,128)(2,1)S(1)} %get-tuple-element.49), channel_id=1, source_target_pairs={{0,48},{16,0},{32,16},{48,32},{1,49},{17,1},{33,17},{49,33},{2,50}... | collective-permute-start | bytes 983048 | tf_op jit(solution)/shard_map/ppermute | solution.py:271
  49.9 1.1 %shard_map.175.strip = f32[2,128,512]{2,1,0:T(8,128)S(1)} custom-call(s32[7]{0:T(128)S(1)} %copy-done.12, s32[8,640]{1,0:T(8,128)S(1)} %broadcast_in_dim.73.near, f32[32,4]{1,0:T(8,128)S(1)} %copy.19.table), custom_call_target="tpu_custom_call" | custom-call | tf_op jit(solution)/shard_map/pallas_call | solution.py:258
  51.1 1.4 %collective-permute-start.8 = (bf16[160,1024]{1,0:T(8,128)(2,1)S(1)}, bf16[160,1024]{1,0:T(8,128)(2,1)S(1)}, u32[]{:S(2)}, u32[]{:S(2)}) collective-permute-start(bf16[160,1024]{1,0:T(8,128)(2,1)S(1)} %get-tuple-element.48), channel_id=1, source_target_pairs={{0,32},{16,48},{32,0},{48,16},{1,33},{17,49},{33,1},{49,17},{2,34}... | collective-permute-start | bytes 983048 | tf_op jit(solution)/shard_map/ppermute | solution.py:271
  52.5 10.9 %collective-permute-done.9.r3 = bf16[160,1024]{1,0:T(8,128)(2,1)S(1)} collective-permute-done((bf16[160,1024]{1,0:T(8,128)(2,1)S(1)}, bf16[160,1024]{1,0:T(8,128)(2,1)S(1)}, u32[]{:S(2)}, u32[]{:S(2)}) %collective-permute-start.9) | collective-permute-done | bytes 327712 | tf_op jit(solution)/shard_map/ppermute | solution.py:271
  63.5 3.3 %collective-permute-done.8.r2 = bf16[160,1024]{1,0:T(8,128)(2,1)S(1)} collective-permute-done((bf16[160,1024]{1,0:T(8,128)(2,1)S(1)}, bf16[160,1024]{1,0:T(8,128)(2,1)S(1)}, u32[]{:S(2)}, u32[]{:S(2)}) %collective-permute-start.8) | collective-permute-done | bytes 327712 | tf_op jit(solution)/shard_map/ppermute | solution.py:271
  66.7 1.2 %collective-permute-done.7.r1 = bf16[160,1024]{1,0:T(8,128)(2,1)S(1)} collective-permute-done((bf16[160,1024]{1,0:T(8,128)(2,1)S(1)}, bf16[160,1024]{1,0:T(8,128)(2,1)S(1)}, u32[]{:S(2)}, u32[]{:S(2)}) %collective-permute-start.7) | collective-permute-done | bytes 327712 | tf_op jit(solution)/shard_map/ppermute | solution.py:271
  68.0 1.6 %collective-permute-start.14 = (bf16[4,32,1024]{2,1,0:T(8,128)(2,1)S(1)}, bf16[4,32,1024]{2,1,0:T(8,128)(2,1)S(1)}, u32[]{:S(2)}, u32[]{:S(2)}) collective-permute-start(bf16[4,32,1024]{2,1,0:T(8,128)(2,1)S(1)} %pad_maximum_fusion.mine), channel_id=1, source_target_pairs={{0,4},{4,0},{1,5},{5,1},{2,6},{6,2},{3,7},{7,3},{8,12},{12,8},{9,1... | collective-permute-start | bytes 786440 | tf_op jit(solution)/shard_map/ppermute | solution.py:271
  69.6 5.3 %shard_map.176 = (bf16[4,528,256]{2,1,0:T(8,128)(2,1)S(1)}, bf16[4,48,256]{2,1,0:T(8,128)(2,1)S(1)}, bf16[4,48,256]{2,1,0:T(8,128)(2,1)S(1)}) custom-call(s32[7]{0:T(128)S(1)} %copy-done.12, bf16[160,1024]{1,0:T(8,128)(2,1)S(1)} %get-tuple-element.46.b0, bf16[160,1024]{1,0:T(8,128)(2,1)S(1)} %collective-permute-done.7.r1, ...), custom_call_target="tpu_custom_call" | custom-call | flops 6000000000 | tf_op jit(solution)/shard_map/pallas_call | solution.py:258
  75.0 1.1 %shard_map.178 = (f32[4,2,64,256]{3,2,1,0:T(8,128)S(1)}, bf16[4,2,64,256]{3,2,1,0:T(8,128)(2,1)S(1)}) custom-call(s32[7]{0:T(128)S(1)} %copy-done.12, bf16[4,528,256]{2,1,0:T(8,128)(2,1)S(1)} %get-tuple-element.59.res, bf16[4,32,1024]{2,1,0:T(8,128)(2,1)S(1)} %pad_maximum_fusion.mine, bf16[4,32,1024]{2,1,0:T(8,128)(2,1)S(1)} %collective-permute-done.14.other), custom_call_target="tpu_custom_call" | custom-call | flops 1000000000 | tf_op jit(solution)/shard_map/pallas_call | solution.py:258
  76.6 1.2 %collective-permute-done.10.got_r = bf16[4,48,256]{2,1,0:T(8,128)(2,1)S(1)} collective-permute-done((bf16[4,48,256]{2,1,0:T(8,128)(2,1)S(1)}, bf16[4,48,256]{2,1,0:T(8,128)(2,1)S(1)}, u32[]{:S(2)}, u32[]{:S(2)}) %collective-permute-start.10) | collective-permute-done | bytes 98336 | tf_op jit(solution)/shard_map/ppermute | solution.py:271
  77.9 3.1 %shard_map.177 = (bf16[80,640]{1,0:T(8,128)(2,1)S(1)}, bf16[80,640]{1,0:T(8,128)(2,1)S(1)}, bf16[80,640]{1,0:T(8,128)(2,1)S(1)}, f32[80,640]{1,0:T(8,128)S(1)}, ...) custom-call(s32[7]{0:T(128)S(1)} %copy-done.12, bf16[4,48,256]{2,1,0:T(8,128)(2,1)S(1)} %get-tuple-element.50.keep_r, ...), custom_call_target="tpu_custom_call" | custom-call | flops 1000000000 | tf_op jit(solution)/shard_map/pallas_call | solution.py:258
  82.1 0.8 collective-permute-start.11
  82.9 2.3 %collective-permute-start.12 = (bf16[80,640]{1,0:T(8,128)(2,1)S(1)}, bf16[80,640]{1,0:T(8,128)(2,1)S(1)}, u32[]{:S(2)}, u32[]{:S(2)}) collective-permute-start(bf16[80,640]{1,0:T(8,128)(2,1)S(1)} %get-tuple-element.55), channel_id=1, source_target_pairs={{0,2},{1,3},{2,0},{3,1},{4,6},{5,7},{6,4},{7,5},{8,10},{9,11},{10,... | collective-permute-start | bytes 307208 | tf_op jit(solution)/shard_map/ppermute | solution.py:271
  86.0 1.4 %collective-permute-done.11.r1 = bf16[80,640]{1,0:T(8,128)(2,1)S(1)} collective-permute-done((bf16[80,640]{1,0:T(8,128)(2,1)S(1)}, bf16[80,640]{1,0:T(8,128)(2,1)S(1)}, u32[]{:S(2)}, u32[]{:S(2)}) %collective-permute-start.11) | collective-permute-done | bytes 102432 | tf_op jit(solution)/shard_map/ppermute | solution.py:271
  87.3 2.6 %collective-permute-done.12.r2 = bf16[80,640]{1,0:T(8,128)(2,1)S(1)} collective-permute-done((bf16[80,640]{1,0:T(8,128)(2,1)S(1)}, bf16[80,640]{1,0:T(8,128)(2,1)S(1)}, u32[]{:S(2)}, u32[]{:S(2)}) %collective-permute-start.12) | collective-permute-done | bytes 102432 | tf_op jit(solution)/shard_map/ppermute | solution.py:271
  90.1 2.2 %shard_map.180 = (bf16[512,512]{1,0:T(8,128)(2,1)}, bf16[512,512]{1,0:T(8,128)(2,1)}, f32[64,512]{1,0:T(8,128)}, f32[64,512]{1,0:T(8,128)}, f32[64,512]{1,0:T(8,128)}, /*index=5*/f32[64,512]{1,0:T(8,128)}) custom-call(s32[7]{0:T(128)S(1)} %copy-done.12, f32[80,640]{1,0:T(8,128)S(1)} %get-tuple-element.53.keep, ...), custom_call_target="tpu_custom_call" | custom-call | tf_op jit(solution)/shard_map/pallas_call | solution.py:258
  (63 shorter events, 8.0 us)
Async XLA Ops:
  5.1 14.5 %collective-permute-start.2 = (f32[8,512]{1,0:T(8,128)}, f32[8,512]{1,0:T(8,128)S(1)}, u32[]{:S(2)}, u32[]{:S(2)}) collective-permute-start(f32[8,512]{1,0:T(8,128)} %get-tuple-element.41), channel_id=1, source_target_pairs={{4,0},{8,4},{12,8},{16,12},{20,16},{24,20},{28,24},{32,28},{36,32}... | collective-permute-start | bytes 49160 | tf_op jit(solution)/shard_map/ppermute | solution.py:296
  8.4 5.9 %collective-permute-start = (f32[8,512]{1,0:T(8,128)}, f32[8,512]{1,0:T(8,128)S(1)}, u32[]{:S(2)}, u32[]{:S(2)}) collective-permute-start(f32[8,512]{1,0:T(8,128)} %get-tuple-element.39), channel_id=1, source_target_pairs={{0,4},{4,8},{8,12},{12,16},{16,20},{20,24},{24,28},{28,32},{32,36}... | collective-permute-start | bytes 49160 | tf_op jit(solution)/shard_map/ppermute | solution.py:295
  16.0 5.8 %collective-permute-start.1 = (bf16[64,512]{1,0:T(8,128)(2,1)S(1)}, bf16[64,512]{1,0:T(8,128)(2,1)S(1)}, u32[]{:S(2)}, u32[]{:S(2)}) collective-permute-start(bf16[64,512]{1,0:T(8,128)(2,1)S(1)} %pad_maximum_fusion.2), channel_id=1, source_target_pairs={{0,8},{8,0},{1,9},{9,1},{2,10},{10,2},{3,11},{11,3},{4,12},{12,4},... | collective-permute-start | bytes 196616 | tf_op jit(solution)/shard_map/ppermute | solution.py:271
  22.6 7.2 %collective-permute-start.3 = (bf16[144,512]{1,0:T(8,128)(2,1)S(1)}, bf16[144,512]{1,0:T(8,128)(2,1)S(1)}, u32[]{:S(2)}, u32[]{:S(2)}) collective-permute-start(bf16[144,512]{1,0:T(8,128)(2,1)S(1)} %pad_maximum_fusion.1.p0), channel_id=1, source_target_pairs={{0,1},{1,2},{2,3},{3,0},{4,5},{5,6},{6,7},{7,4},{8,9},{9,10},{10,1... | collective-permute-start | bytes 442376 | tf_op jit(solution)/shard_map/ppermute | solution.py:271
  24.3 9.5 %collective-permute-start.4 = (bf16[144,512]{1,0:T(8,128)(2,1)S(1)}, bf16[144,512]{1,0:T(8,128)(2,1)S(1)}, u32[]{:S(2)}, u32[]{:S(2)}) collective-permute-start(bf16[144,512]{1,0:T(8,128)(2,1)S(1)} %pad_maximum_fusion.1.p0), channel_id=1, source_target_pairs={{0,2},{1,3},{2,0},{3,1},{4,6},{5,7},{6,4},{7,5},{8,10},{9,11},{10,... | collective-permute-start | bytes 442376 | tf_op jit(solution)/shard_map/ppermute | solution.py:271
  27.6 6.2 %collective-permute-start.5 = (bf16[144,512]{1,0:T(8,128)(2,1)S(1)}, bf16[144,512]{1,0:T(8,128)(2,1)S(1)}, u32[]{:S(2)}, u32[]{:S(2)}) collective-permute-start(bf16[144,512]{1,0:T(8,128)(2,1)S(1)} %pad_maximum_fusion.1.p0), channel_id=1, source_target_pairs={{0,3},{1,0},{2,1},{3,2},{4,7},{5,4},{6,5},{7,6},{8,11},{9,8},{10,9... | collective-permute-start | bytes 442376 | tf_op jit(solution)/shard_map/ppermute | solution.py:271
  33.8 0.7 copy-start.7
  34.5 0.6 copy-start.11
  35.1 7.1 %copy-start.14 = (s32[512]{0:T(512)S(1)}, s32[512]{0:T(512)}, u32[]{:S(2)}) copy-start(s32[512]{0:T(512)} %param.23) | copy-start | bytes 6148
  35.1 7.4 %copy-start.13 = (f32[32,4]{0,1:T(4,128)S(1)}, f32[32,4]{0,1:T(4,128)}, u32[]{:S(2)}) copy-start(f32[32,4]{0,1:T(4,128)} %param.22) | copy-start | bytes 1540
  35.1 8.1 %copy-start.12 = (s32[7]{0:T(128)S(1)}, s32[7]{0:T(128)}, u32[]{:S(2)}) copy-start(s32[7]{0:T(128)} %stack.42.sc) | copy-start | bytes 88
  40.4 2.8 %collective-permute-start.6 = (bf16[64,1024]{1,0:T(8,128)(2,1)S(1)}, bf16[64,1024]{1,0:T(8,128)(2,1)S(1)}, u32[]{:S(2)}, u32[]{:S(2)}) collective-permute-start(bf16[64,1024]{1,0:T(8,128)(2,1)S(1)} %get-tuple-element.44), channel_id=1, source_target_pairs={{0,4},{4,0},{1,5},{5,1},{2,6},{6,2},{3,7},{7,3},{8,12},{12,8},{9,1... | collective-permute-start | bytes 393224 | tf_op jit(solution)/shard_map/ppermute | solution.py:271
  43.2 1.0 %copy-start.4 = (bf16[4,32,1024]{2,1,0:T(8,128)(2,1)S(1)}, bf16[4,32,1024]{2,1,0:T(8,128)(2,1)}, u32[]{:S(2)}) copy-start(bf16[4,32,1024]{2,1,0:T(8,128)(2,1)} %get-tuple-element.45.blocks) | copy-start | bytes 786436
  44.8 18.7 %collective-permute-start.9 = (bf16[160,1024]{1,0:T(8,128)(2,1)S(1)}, bf16[160,1024]{1,0:T(8,128)(2,1)S(1)}, u32[]{:S(2)}, u32[]{:S(2)}) collective-permute-start(bf16[160,1024]{1,0:T(8,128)(2,1)S(1)} %get-tuple-element.49), channel_id=1, source_target_pairs={{0,48},{16,0},{32,16},{48,32},{1,49},{17,1},{33,17},{49,33},{2,50}... | collective-permute-start | bytes 983048 | tf_op jit(solution)/shard_map/ppermute | solution.py:271
  51.0 16.9 %collective-permute-start.7 = (bf16[160,1024]{1,0:T(8,128)(2,1)S(1)}, bf16[160,1024]{1,0:T(8,128)(2,1)S(1)}, u32[]{:S(2)}, u32[]{:S(2)}) collective-permute-start(bf16[160,1024]{1,0:T(8,128)(2,1)S(1)} %get-tuple-element.47), channel_id=1, source_target_pairs={{0,16},{16,32},{32,48},{48,0},{1,17},{17,33},{33,49},{49,1},{2,18}... | collective-permute-start | bytes 983048 | tf_op jit(solution)/shard_map/ppermute | solution.py:271
  51.1 15.6 %collective-permute-start.8 = (bf16[160,1024]{1,0:T(8,128)(2,1)S(1)}, bf16[160,1024]{1,0:T(8,128)(2,1)S(1)}, u32[]{:S(2)}, u32[]{:S(2)}) collective-permute-start(bf16[160,1024]{1,0:T(8,128)(2,1)S(1)} %get-tuple-element.48), channel_id=1, source_target_pairs={{0,32},{16,48},{32,0},{48,16},{1,33},{17,49},{33,1},{49,17},{2,34}... | collective-permute-start | bytes 983048 | tf_op jit(solution)/shard_map/ppermute | solution.py:271
  68.0 7.0 %collective-permute-start.14 = (bf16[4,32,1024]{2,1,0:T(8,128)(2,1)S(1)}, bf16[4,32,1024]{2,1,0:T(8,128)(2,1)S(1)}, u32[]{:S(2)}, u32[]{:S(2)}) collective-permute-start(bf16[4,32,1024]{2,1,0:T(8,128)(2,1)S(1)} %pad_maximum_fusion.mine), channel_id=1, source_target_pairs={{0,4},{4,0},{1,5},{5,1},{2,6},{6,2},{3,7},{7,3},{8,12},{12,8},{9,1... | collective-permute-start | bytes 786440 | tf_op jit(solution)/shard_map/ppermute | solution.py:271
  69.6 8.2 %copy-start.1 = (bf16[2048,512]{1,0:T(8,128)(2,1)S(1)}, bf16[2048,512]{1,0:T(8,128)(2,1)}, u32[]{:S(2)}) copy-start(bf16[2048,512]{1,0:T(8,128)(2,1)} %wk.3) | copy-start | bytes 6291460
  69.6 8.3 %copy-start.2 = (bf16[2048,512]{1,0:T(8,128)(2,1)S(1)}, bf16[2048,512]{1,0:T(8,128)(2,1)}, u32[]{:S(2)}) copy-start(bf16[2048,512]{1,0:T(8,128)(2,1)} %wv.3) | copy-start | bytes 6291460
  69.6 8.3 %copy-start.3 = (bf16[2048,512]{1,0:T(8,128)(2,1)S(1)}, bf16[2048,512]{1,0:T(8,128)(2,1)}, u32[]{:S(2)}) copy-start(bf16[2048,512]{1,0:T(8,128)(2,1)} %wo.3) | copy-start | bytes 6291460
  74.9 2.9 %copy-start = (bf16[2048,512]{1,0:T(8,128)(2,1)S(1)}, bf16[2048,512]{1,0:T(8,128)(2,1)}, u32[]{:S(2)}) copy-start(bf16[2048,512]{1,0:T(8,128)(2,1)} %wq.3) | copy-start | bytes 6291460
  74.9 2.9 %copy-start.5 = (bf16[48,2048]{1,0:T(8,128)(2,1)S(1)}, bf16[48,2048]{1,0:T(8,128)(2,1)}, u32[]{:S(2)}) copy-start(bf16[48,2048]{1,0:T(8,128)(2,1)} %get-tuple-element.52.c) | copy-start | bytes 589828
  74.9 2.9 %copy-start.8 = (f32[1,2048]{1,0:T(1,128)S(1)}, f32[1,2048]{1,0:T(1,128)}, u32[]{:S(2)}) copy-start(f32[1,2048]{1,0:T(1,128)} %get-tuple-element.42.gain) | copy-start | bytes 24580
  76.0 5.0 %collective-permute-start.15 = (bf16[4,2,64,256]{3,2,1,0:T(8,128)(2,1)S(1)}, bf16[4,2,64,256]{3,2,1,0:T(8,128)(2,1)S(1)}, u32[]{:S(2)}, u32[]{:S(2)}) collective-permute-start(bf16[4,2,64,256]{3,2,1,0:T(8,128)(2,1)S(1)} %get-tuple-element.61), channel_id=1, source_target_pairs={{0,4},{4,0},{1,5},{5,1},{2,6},{6,2},{3,7},{7,3},{8,12},{12,8},{9,1... | collective-permute-start | bytes 786440 | tf_op jit(solution)/shard_map/ppermute | solution.py:271
  76.2 1.6 %collective-permute-start.10 = (bf16[4,48,256]{2,1,0:T(8,128)(2,1)S(1)}, bf16[4,48,256]{2,1,0:T(8,128)(2,1)S(1)}, u32[]{:S(2)}, u32[]{:S(2)}) collective-permute-start(bf16[4,48,256]{2,1,0:T(8,128)(2,1)S(1)} %get-tuple-element.51), channel_id=1, source_target_pairs={{0,4},{4,0},{1,5},{5,1},{2,6},{6,2},{3,7},{7,3},{8,12},{12,8},{9,1... | collective-permute-start | bytes 294920 | tf_op jit(solution)/shard_map/ppermute | solution.py:271
  77.8 12.3 %copy-start.6 = (f32[16,512]{1,0:T(8,128)S(1)}, f32[16,512]{1,0:T(8,128)}, u32[]{:S(2)}) copy-start(f32[16,512]{1,0:T(8,128)} %up_gain.1) | copy-start | bytes 98308
  77.9 12.3 %copy-start.9 = (f32[4,512]{1,0:T(4,128)S(1)}, f32[4,512]{1,0:T(4,128)}, u32[]{:S(2)}) copy-start(f32[4,512]{1,0:T(4,128)} %first.1) | copy-start | bytes 24580
  77.9 12.3 %copy-start.10 = (f32[4,512]{1,0:T(4,128)S(1)}, f32[4,512]{1,0:T(4,128)}, u32[]{:S(2)}) copy-start(f32[4,512]{1,0:T(4,128)} %second.1) | copy-start | bytes 24580
  81.6 8.5 %collective-permute-start.16 = (bf16[4,64,512]{2,1,0:T(8,128)(2,1)S(1)}, bf16[4,64,512]{2,1,0:T(8,128)(2,1)S(1)}, u32[]{:S(2)}, u32[]{:S(2)}) collective-permute-start(bf16[4,64,512]{2,1,0:T(8,128)(2,1)S(1)} %get-tuple-element.63), channel_id=1, source_target_pairs={{0,64},{64,0},{1,65},{65,1},{2,66},{66,2},{3,67},{67,3},{4,68},{68... | collective-permute-start | bytes 786440 | tf_op jit(solution)/shard_map/ppermute | solution.py:271
  82.1 5.2 %collective-permute-start.11 = (bf16[80,640]{1,0:T(8,128)(2,1)S(1)}, bf16[80,640]{1,0:T(8,128)(2,1)S(1)}, u32[]{:S(2)}, u32[]{:S(2)}) collective-permute-start(bf16[80,640]{1,0:T(8,128)(2,1)S(1)} %get-tuple-element.54), channel_id=1, source_target_pairs={{0,1},{1,2},{2,3},{3,0},{4,5},{5,6},{6,7},{7,4},{8,9},{9,10},{10,1... | collective-permute-start | bytes 307208 | tf_op jit(solution)/shard_map/ppermute | solution.py:271
  82.9 7.1 %collective-permute-start.12 = (bf16[80,640]{1,0:T(8,128)(2,1)S(1)}, bf16[80,640]{1,0:T(8,128)(2,1)S(1)}, u32[]{:S(2)}, u32[]{:S(2)}) collective-permute-start(bf16[80,640]{1,0:T(8,128)(2,1)S(1)} %get-tuple-element.55), channel_id=1, source_target_pairs={{0,2},{1,3},{2,0},{3,1},{4,6},{5,7},{6,4},{7,5},{8,10},{9,11},{10,... | collective-permute-start | bytes 307208 | tf_op jit(solution)/shard_map/ppermute | solution.py:271
  85.2 4.9 %collective-permute-start.13 = (bf16[80,640]{1,0:T(8,128)(2,1)S(1)}, bf16[80,640]{1,0:T(8,128)(2,1)S(1)}, u32[]{:S(2)}, u32[]{:S(2)}) collective-permute-start(bf16[80,640]{1,0:T(8,128)(2,1)S(1)} %get-tuple-element.56), channel_id=1, source_target_pairs={{0,3},{1,0},{2,1},{3,2},{4,7},{5,4},{6,5},{7,6},{8,11},{9,8},{10,9... | collective-permute-start | bytes 307208 | tf_op jit(solution)/shard_map/ppermute | solution.py:271

commit v4 on v3

--- a/solution.py
+++ b/solution.py
@@ -31,6 +31,13 @@
     return lax.dot_general(a, b, (((ca,), (cb,)), ((), ())), preferred_element_type=F32)
 
 
+class Place:
+    def __init__(self):
+        self.x, self.y, self.core = (lax.axis_index(a) for a in ("x", "y", "core"))
+        self.dp, self.z = lax.axis_index("dp"), lax.axis_index("tensor")
+        self.ctx = (self.x * 2 + self.y) * 2 + self.core
+
+
 def tap_weights(first, second):
     taps = jnp.concatenate([second[a : a + 1] * first for a in range(4)], axis=0)
     return jnp.concatenate([taps[15:16], taps[:15]], axis=0)
@@ -43,14 +50,14 @@
 
 
 def before_kernel(
-    sc, tokens_h, grad_h, first_h, second_h, up_h, gain_h, part, last, ahead, gco, gain,
+    lens, tokens_h, grad_h, first_h, second_h, up_h, gain_h, part, last, ahead, gco, gain,
     tokens, grad_out, first, second, up_gain, shift, sems,
 ):
     pairs = ((tokens_h, tokens), (first_h, first), (second_h, second), (grad_h, grad_out), (up_h, up_gain), (gain_h, gain))
     copies = [pltpu.make_async_copy(a, b, sems.at[i]) for i, (a, b) in enumerate(pairs)]
     for c in copies:
         c.start()
-    mask = byte_mask(sc[0], sc[1])
+    mask = byte_mask(Place().ctx, lens[0])
     u = lax.broadcasted_iota(jnp.int32, (CL, 16, WL), 1)
     for c in copies[:3]:
         c.wait()
@@ -69,24 +76,37 @@
     gco[...] = jnp.sum(weighted, axis=1).astype(BF16)
 
 
-def bias_kernel(sc, near, table, strip):
+def piece_kernel(part, gco, rim, piece):
+    first = lax.broadcasted_iota(jnp.int32, (CL, WL), 0) == 0
+    piece[0:CL] = (part[...] + jnp.where(first, rim[0:1], 0.0)).astype(BF16)
+    piece[CL : 2 * CL] = gco[...]
+
+
+def pile_kernel(piece, across, lead, last, out):
+    y = Place().y
+    out[pl.ds(pl.multiple_of(y * 64, 64), 64)] = piece[...]
+    out[pl.ds(pl.multiple_of(64 - y * 64, 64), 64)] = across[...]
+    first = lax.broadcasted_iota(jnp.int32, (16, WL), 0) == 0
+    out[128:144] = jnp.where(first, lead[0:1] + last[0:1], 0.0).astype(BF16)
+
+
+def bias_kernel(near, table, strip):
+    core = Place().core
     n = near.shape[1]
     which = near[0:1]
     for h in range(NH):
         row = jnp.full((1, n), NEG, F32)
         for b in range(table.shape[0]):
-            row = jnp.where(which == b, table[b, sc[3] * NH + h], row)
+            row = jnp.where(which == b, table[b, core * NH + h], row)
         rolled = pltpu.roll(jnp.broadcast_to(row, (128, n)), 0, 1, stride=1, stride_axis=0)
         strip[h] = rolled[:, :LC]
 
 
 def project_kernel(
-    sc, p0, r1, r2, r3, gain, wq, wk, wv, wo, keep, send, blocks, c48, craw, nrm, gco, both, ws, sems
-):
-    copies = [pltpu.make_async_copy(w, ws.at[i], sems.at[i]) for i, w in enumerate((wo, wq, wk, wv))]
-    for cp in copies:
-        cp.start()
-    z, core, x, y = sc[2], sc[3], sc[5], sc[6]
+    p0, r1, r2, r3, gain, wq, wk, wv, wo, keep, send, blocks, c48, craw, nrm, gco, both
+):
+    at = Place()
+    z, core, x, y = at.z, at.core, at.x, at.y
     for s, src in enumerate((p0, r1, r2, r3)):
         cols = pl.ds(pl.multiple_of(lax.rem(z + 4 - s, 4) * WL, WL), WL)
         for i in range(2):
@@ -98,9 +118,8 @@
     c = craw[...].astype(F32)
     r = lax.rsqrt(jnp.sum(c * c, axis=1, keepdims=True) * (1.0 / D) + 1e-6)
     nrm[...] = (c * r * gain[...]).astype(BF16)
-    for i, (src, slot) in enumerate(((gco, 3), (nrm, 0), (nrm, 1), (nrm, 2))):
-        copies[i].wait()
-        v = jnp.dot(src[...], ws[i], preferred_element_type=F32).astype(BF16)
+    for src, w, slot in ((gco, wo, 3), (nrm, wq, 0), (nrm, wk, 1), (nrm, wv, 2)):
+        v = jnp.dot(src[...], w[...], preferred_element_type=F32).astype(BF16)
         for half in range(2):
             both[half, :, slot * HW : slot * HW + HW] = v[:, half * HW : half * HW + HW]
     keep[...] = both[core]
@@ -116,22 +135,43 @@
                 blocks[s, :, at + 256 : at + 384] = gco[rows, cols]
 
 
-def pack_kernel(sc, keep, swapped, blocks, b0, b1, b2, b3):
-    core = sc[3]
-    for s, b in enumerate((b0, b1, b2, b3)):
-        for i in range(2):
-            for src, c in ((keep, core), (swapped, 1 - core)):
-                rows = pl.ds(pl.multiple_of(i * 64 + c * CL, CL), CL)
-                b[rows] = src[i * CL : i * CL + CL]
-        b[128:160] = blocks[s]
-
-
-def attend_kernel(sc, b0, r1, r2, r3, strip, res, keep, send, q, k, v, ga, acck, accv):
-    ctx, doc_len, core, x = sc[0], sc[1], sc[3], sc[5]
-    for s, src in enumerate((b0, r1, r2, r3)):
-        rows = pl.ds(pl.multiple_of(lax.rem(x + 4 - s, 4) * 128, 128), 128)
+def pack_kernel(keep, swapped, blocks, b0, up, down):
+    core = Place().core
+    for i in range(2):
+        for src, c in ((keep, core), (swapped, 1 - core)):
+            row = i * 64 + c * CL
+            new = src[i * CL : i * CL + CL]
+            b0[pl.ds(pl.multiple_of(row, CL), CL)] = new
+            up[pl.ds(pl.multiple_of((96 if i == 0 else -32) + row, CL), CL)] = new
+            down[pl.ds(pl.multiple_of(32 + row, CL), CL)] = new
+    b0[128:160] = blocks[0]
+    up[0:32] = blocks[1]
+    down[0:32] = blocks[3]
+    up[160:176] = blocks[2, 0:16]
+    down[160:176] = blocks[2, 16:32]
+
+
+def attend_kernel(
+    lens, b0, low, high, far_low, far_high, strip, res, keep, send, mine, q, k, v, ga, acck, accv
+):
+    at = Place()
+    ctx, core, x, doc_len = at.ctx, at.core, at.x, lens[0]
+    for src, first, n, s, row in (
+        (b0, 0, 128, 0, 0),
+        (low, 96, 64, 1, 0),
+        (low, 32, 64, 1, 64),
+        (far_low, 0, 64, 2, 0),
+        (far_high, 0, 64, 2, 64),
+        (high, 32, 128, 3, 0),
+    ):
+        rows = pl.ds(pl.multiple_of(lax.rem(x + 4 - s, 4) * 128 + row, 64), n)
         for i, dst in enumerate((q, k, v, ga)):
-            dst[rows] = src[0:128, i * HW : i * HW + HW]
+            dst[rows] = src[first : first + n, i * HW : i * HW + HW]
+    mine[0] = b0[128:160]
+    mine[1] = low[0:32]
+    mine[2, 0:16] = far_low[64:80]
+    mine[2, 16:32] = far_high[64:80]
+    mine[3] = high[0:32]
     key_pos = lax.broadcasted_iota(jnp.int32, (1, LC), 1)
     key_mask = jnp.where(16 * key_pos < doc_len, 0.0, NEG)
     for h in range(NH):
@@ -165,36 +205,36 @@
     send[...] = res[:, pl.ds(pl.multiple_of(peer * CL, CL), ROWS)]
 
 
-def weights_kernel(sc, res, mine, other, keep, send, nb, gb, tile):
-    core, x = sc[3], sc[5]
+def weights_kernel(res, mine, other, keep, send, nb, gb):
+    at = Place()
+    core, x, dp = at.core, at.x, at.dp
     for s in range(4):
         for src, c in ((mine, core), (other, 1 - core)):
             for i in range(2):
-                at = (lax.rem(x + 4 - s, 4) * 4 + i * 2 + c) * CL
-                rows = pl.ds(pl.multiple_of(at, CL), CL)
+                row = (lax.rem(x + 4 - s, 4) * 4 + i * 2 + c) * CL
+                rows = pl.ds(pl.multiple_of(row, CL), CL)
                 nb[rows] = src[s, :, i * 512 : i * 512 + 256]
                 gb[rows] = src[s, :, i * 512 + 256 : i * 512 + 512]
     for w in range(4):
-        tile[...] = dg((gb if w == 3 else nb)[...], res[w, 0:LC], 0, 0)
-        for d in range(2):
-            keep[w, d] = tile[pl.ds(pl.multiple_of(d * 128 + core * 64, 64), 64)]
-            send[w, d] = tile[pl.ds(pl.multiple_of(d * 128 + 64 - core * 64, 64), 64)].astype(BF16)
-
-
-def join_kernel(sc, keep, got, after, own, send):
-    core, dp = sc[3], sc[4]
-    a = pl.ds(pl.multiple_of(core * HW, HW), HW)
-    b = pl.ds(pl.multiple_of((1 - core) * HW, HW), HW)
-    own[:, :, a] = keep[:, dp]
-    own[:, :, b] = got[:, dp].astype(F32)
-    send[:, :, a] = keep[:, 1 - dp].astype(BF16)
-    send[:, :, b] = got[:, 1 - dp]
+        src = gb if w == 3 else nb
+        for d, out in ((dp, keep), (1 - dp, send)):
+            cols = pl.ds(pl.multiple_of(d * 128, 128), 128)
+            out[w] = dg(src[:, cols], res[w, 0:LC], 0, 0).astype(out.dtype)
+
+
+def total_kernel(keep, got, after, own, send):
+    core = Place().core
+    for w in range(4):
+        for c, out in ((core, own), (1 - core, send)):
+            rows = pl.ds(pl.multiple_of(c * 64, 64), 64)
+            out[w] = (keep[w, rows] + got[w, rows].astype(F32)).astype(out.dtype)
 
 
 def partial_kernel(
-    sc, keep_r, got_r, c, gain, wq, wk, wv, wo, msg1, msg2, msg3, keep, cz, inv_out, g
-):
-    z, core = sc[2], sc[3]
+    keep_r, got_r, c, gain, wq, wk, wv, wo, msg1, msg2, msg3, keep, cz, inv_out, g
+):
+    at = Place()
+    z, core = at.z, at.core
     g[:, :, pl.ds(pl.multiple_of(core * HW, HW), HW)] = keep_r[...]
     g[:, :, pl.ds(pl.multiple_of((1 - core) * HW, HW), HW)] = got_r[...]
     cf = c[...].astype(F32)
@@ -224,10 +264,11 @@
 
 
 def after_kernel(
-    sc, keep, r1, r2, r3, cz, inv, gain, first, second, up_gain, dw, other,
+    lens, keep, r1, r2, r3, cz, inv, gain, first, second, up_gain, dw, other,
     update, grad, o0, o1, o2, o3, rows,
 ):
-    ctx, doc_len, z = sc[0], sc[1], sc[2]
+    at = Place()
+    ctx, doc_len, z, core = at.ctx, lens[0], at.z, at.core
     mask = byte_mask(ctx, doc_len)
     body = slice(0, WL)
     out = keep[0:CL, body]
@@ -248,7 +289,8 @@
     picked = jnp.where(u == 0, rows[0:CL][:, None, :], rows[1 : CL + 1][:, None, :])
     grad[...] = (picked * taps[None] * mask).reshape(SEG, WL).astype(BF16)
     for w, o in enumerate((o0, o1, o2, o3)):
-        o[...] = dw[w] + other[w].astype(F32)
+        o[:, pl.ds(pl.multiple_of(core * HW, HW), HW)] = dw[w]
+        o[:, pl.ds(pl.multiple_of((1 - core) * HW, HW), HW)] = other[w].astype(F32)
 
 
 def call(kernel, outs, args, scratch=(), smem=(0,), flops=0, size=0, vmem=8 * 2**20, hbm=()):
@@ -275,15 +317,11 @@
     tokens, lengths, conv_first, conv_second, norm_gain, w_query, w_key, w_value, w_out,
     bias_table, buckets, up_gain, grad_out,
 ):
-    x, y, core = lax.axis_index("x"), lax.axis_index("y"), lax.axis_index("core")
-    dp, z = lax.axis_index("dp"), lax.axis_index("tensor")
-    ctx = (x * 2 + y) * 2 + core
-    sc = jnp.stack([ctx, lengths[0], z, core, dp, x, y]).astype(jnp.int32)
     weights = (w_query, w_key, w_value, w_out)
     part, last, ahead, gco, gain = call(
         before_kernel,
         [((CL, WL), F32), ((8, WL), F32), ((8, WL), F32), ((CL, WL), BF16), ((1, D), F32)],
-        (sc, tokens[0], grad_out[0], conv_first, conv_second, up_gain, norm_gain[None]),
+        (lengths, tokens[0], grad_out[0], conv_first, conv_second, up_gain, norm_gain[None]),
         [
             ((SEG, WL), BF16), ((SEG, WL), BF16), ((4, WL), F32), ((4, WL), F32), ((16, WL), F32),
             ((CL + 8, WL), F32), pltpu.SemaphoreType.DMA((6,)),
@@ -293,15 +331,16 @@
     )
     line = ("x", "y", "core")
     rim = lax.ppermute(last, line, [(i, i + 1) for i in range(15)])
+    (piece,) = call(piece_kernel, [((2 * CL, WL), BF16)], (part, gco, rim), smem=())
+    ahead, piece = lax.optimization_barrier((ahead, piece))
     lead = lax.ppermute(ahead, line, [(i + 1, i) for i in range(15)])
-    is_first = (jnp.arange(CL) == 0)[:, None]
-    coarse = (part + jnp.where(is_first, rim[0:1], 0.0)).astype(BF16)
-    piece = jnp.concatenate([coarse, gco], axis=0)
     across = shifted(piece, "y", 1)
-    nxt = jnp.where(is_first[:16], lead[0:1] + last[0:1], 0.0).astype(BF16)
-    low_y = y == 0
-    piece = jnp.concatenate(
-        [jnp.where(low_y, piece, across), jnp.where(low_y, across, piece), nxt], axis=0
+    (piece,) = call(
+        pile_kernel,
+        [((PIECE, WL), BF16)],
+        (piece, across, lead, last),
+        smem=(),
+        flops=6 * 10**9,
     )
     n = 640
     near = jnp.concatenate(
@@ -314,62 +353,69 @@
     (strip,) = call(
         bias_kernel,
         [((NH, 128, LC), F32)],
-        (sc, jnp.broadcast_to(near[None], (8, n)), bias_table),
-        smem=(0, 2),
+        (jnp.broadcast_to(near[None], (8, n)), bias_table),
+        smem=(1,),
     )
     pieces = [piece] + [shifted(piece, "tensor", s) for s in (1, 2, 3)]
     keep, send, blocks, c48 = call(
         project_kernel,
         [((2 * CL, 4 * HW), BF16), ((2 * CL, 4 * HW), BF16), ((4, CL, 4 * HW), BF16), ((ROWS, D), BF16)],
-        (sc, *pieces, gain, *weights),
+        (*pieces, gain, *weights),
+        [((2 * CL, D), BF16), ((2 * CL, D), BF16), ((2 * CL, D), BF16), ((2, 2 * CL, 4 * HW), BF16)],
+        smem=(),
+        flops=10**9,
+    )
+    swapped = shifted(send, "core", 1)
+    b0, up, down = call(
+        pack_kernel,
+        [((5 * CL, 4 * HW), BF16), ((176, 4 * HW), BF16), ((176, 4 * HW), BF16)],
+        (keep, swapped, blocks),
+        smem=(),
+    )
+    low, high = shifted(up, "x", 1), shifted(down, "x", -1)
+    far_low, far_high = shifted(low[96:], "x", 1), shifted(high[96:], "x", -1)
+    res, keep_r, send_r, mine = call(
+        attend_kernel,
         [
-            ((2 * CL, D), BF16), ((2 * CL, D), BF16), ((2 * CL, D), BF16), ((2, 2 * CL, 4 * HW), BF16),
-            ((4, D, WL), BF16), pltpu.SemaphoreType.DMA((4,)),
+            ((4, LC + 16, HW), BF16), ((4, ROWS, HW), BF16), ((4, ROWS, HW), BF16),
+            ((4, CL, 4 * HW), BF16),
         ],
-        flops=10**9,
-        hbm=(6, 7, 8, 9),
-        vmem=BIG - 10 * 2**20,
-    )
-    swapped = shifted(send, "core", 1)
-    b0, b1, b2, b3 = call(
-        pack_kernel, [((5 * CL, 4 * HW), BF16)] * 4, (sc, keep, swapped, blocks)
-    )
-    bundles = [b0, shifted(b1, "x", 1), shifted(b2, "x", 2), shifted(b3, "x", 3)]
-    mine = jnp.stack([b[4 * CL :] for b in bundles])
-    other_rows = shifted(mine, "core", 1)
-    res, keep_r, send_r = call(
-        attend_kernel,
-        [((4, LC + 16, HW), BF16), ((4, ROWS, HW), BF16), ((4, ROWS, HW), BF16)],
-        (sc, *bundles, strip),
+        (lengths, b0, low, high, far_low, far_high, strip),
         [((LC, HW), BF16)] * 4 + [((NH, LC, HD), F32)] * 2,
         flops=6 * 10**9,
     )
+    other_rows = shifted(mine, "core", 1)
     got_r = shifted(send_r, "core", 1)
     dw_keep, dw_send = call(
         weights_kernel,
-        [((4, 2, 64, HW), F32), ((4, 2, 64, HW), BF16)],
-        (sc, res, mine, other_rows),
-        [((LC, 256), BF16), ((LC, 256), BF16), ((256, HW), F32)],
+        [((4, 128, HW), F32), ((4, 128, HW), BF16)],
+        (res, mine, other_rows),
+        [((LC, 256), BF16), ((LC, 256), BF16)],
+        smem=(),
         flops=10**9,
     )
-    dw_got = shifted(dw_send, "core", 1)
+    dw_got = shifted(dw_send, "dp", 1)
     msg = (CL + ROWS, WL + 128)
     m1, m2, m3, own, cz, inv = call(
         partial_kernel,
         [(msg, BF16), (msg, BF16), (msg, BF16), (msg, F32), ((ROWS, WL), BF16), ((ROWS, 128), F32)],
-        (sc, keep_r, got_r, c48, gain, *weights),
+        (keep_r, got_r, c48, gain, *weights),
         [((4, ROWS, WL), BF16)],
+        smem=(),
         flops=10**9,
     )
     r1, r2, r3 = shifted(m1, "tensor", 1), shifted(m2, "tensor", 2), shifted(m3, "tensor", 3)
     dw_own, dw_other = call(
-        join_kernel, [((4, 64, WL), F32), ((4, 64, WL), BF16)], (sc, dw_keep, dw_got, inv)
-    )
-    dw_other = shifted(dw_other, "dp", 1)
+        total_kernel,
+        [((4, 64, HW), F32), ((4, 64, HW), BF16)],
+        (dw_keep, dw_got, r1),
+        smem=(),
+    )
+    dw_other = shifted(dw_other, "core", 1)
     update, grad_tokens, *dw = call(
         after_kernel,
         [((SEG, WL), BF16)] * 2 + [((64, WL), F32)] * 4,
-        (sc, own, r1, r2, r3, cz, inv, gain, conv_first, conv_second, up_gain, dw_own, dw_other),
+        (lengths, own, r1, r2, r3, cz, inv, gain, conv_first, conv_second, up_gain, dw_own, dw_other),
         [((ROWS, WL), F32)],
     )
     return (update[None], grad_tokens[None], *dw)

time: 92.8 us -> 85.3 us (0.919)
  Pallas kernels: 22.4 us -> 15.8 us
  waiting for transfers between devices: 29.2 us -> 33.3 us
  other arithmetic: 3.39 us -> 0.08 us
  starting transfers between devices: 32.4 us -> 29.7 us
    pallas_call x9 -> x11, Pallas kernels: 22.4 us -> 15.8 us  [call(): pl.pallas_call(kernel, out_shape=[jax.ShapeDtypeStruct(s, d) for s, d in...]
    ppermute x15 -> x16, starting transfers between devices: 24.2 us -> 18.4 us  [shifted(): return lax.ppermute(x, axis, [(i, (i + steps) % n) for i in range(n)])]
    ppermute x1, waiting for transfers between devices: 0.01 us -> 2.04 us  [local(): lead = lax.ppermute(ahead, line, [(i + 1, i) for i in range(15)])]
    ppermute x15 -> x16, waiting for transfers between devices: 28.2 us -> 30.2 us  [shifted(): return lax.ppermute(x, axis, [(i, (i + steps) % n) for i in range(n)])]
    ppermute x1, starting transfers between devices: 3.33 us -> 5.11 us  [local(): lead = lax.ppermute(ahead, line, [(i + 1, i) for i in range(15)])]
    ppermute x1, starting transfers between devices: 4.8 us -> 6.21 us  [local(): rim = lax.ppermute(last, line, [(i, i + 1) for i in range(15)])]
    slice x1 -> x2, local copies, waits for them, and re-layouts: 0.01 us -> 1.36 us  [local(): far_low, far_high = (shifted(low[96:], 'x', 1), shifted(high[96:], 'x', -1))]
    convert_element_type x2 -> x0, other arithmetic: 0.99 us -> none  [the longest x1 0.92 us: local(): coarse = (part + jnp.where(is_first, rim[0:1], 0.0)).astype(BF16)]
  transfers between devices with their start and end apart: 17 -> 18, of which waited for: 12 -> 11; matrix products, arithmetic and copies ran while one was open for 3% -> 2% of each run, Pallas kernels for 10% -> 5%
where the time goes in v4:
time: 85.3 us; the launch traced here: 84.7 us
  waiting for transfers between devices  33.3 us (39%)
  starting transfers between devices  29.7 us (35%)
  Pallas kernels  15.8 us (19%)
  local copies, waits for them, and re-layouts  4.18 us (5%)
  between operations  1.51 us (2%)
    ppermute x16, waiting for transfers between devices, shifted(): return lax.ppermute(x, axis, [(i, (i + steps) % n) for i in range(n)])  30.2 us
    ppermute x16, starting transfers between devices, shifted(): return lax.ppermute(x, axis, [(i, (i + steps) % n) for i in range(n)])  18.4 us
    pallas_call x11, Pallas kernels, call(): pl.pallas_call(kernel, out_shape=[jax.ShapeDtypeStruct(s, d) for s, d in...  15.8 us
    ppermute x1, starting transfers between devices, local(): rim = lax.ppermute(last, line, [(i, i + 1) for i in range(15)])  6.21 us
    ppermute x1, starting transfers between devices, local(): lead = lax.ppermute(ahead, line, [(i + 1, i) for i in range(15)])  5.11 us
    unnamed x35, local copies, waits for them, and re-layouts  2.65 us
    ppermute x1, waiting for transfers between devices, local(): lead = lax.ppermute(ahead, line, [(i + 1, i) for i in range(15)])  2.04 us
  transfers between devices with their start and end apart: 18, of which 11 were waited for; matrix products, arithmetic and copies ran while one was open for 2% of the time, Pallas kernels for 5%

profile of v4, /device:TPU:1, one launch (start us, length us, event | category | flops | bytes accessed | tf_op | source)
XLA Modules:
  0.0 84.7 jit_solution(4169808963900187692)
XLA Ops:
  1.3 2.5 %shard_map.172 = (f32[32,512]{1,0:T(8,128)}, f32[8,512]{1,0:T(8,128)}, f32[8,512]{1,0:T(8,128)}, bf16[32,512]{1,0:T(8,128)(2,1)}, f32[1,2048]{1,0:T(1,128)}) custom-call(s32[1]{0:T(128)S(6)} %copy.20.lens, bf16[512,512]{1,0:T(8,128)(2,1)} %bitcast.7, bf16[512,512]{1,0:T(8,128)(2,1)} %bitcast.8, f32[4,512]{1,0:T(4,128)} %first.1, f32[4,512]{1,0:T(4,128)} %second.1, ...), custom_call_target="tpu_custom_call" | custom-call | tf_op jit(solution)/shard_map/pallas_call | solution.py:300
  3.8 6.2 %collective-permute-start = (f32[8,512]{1,0:T(8,128)}, f32[8,512]{1,0:T(8,128)S(1)}, u32[]{:S(2)}, u32[]{:S(2)}) collective-permute-start(f32[8,512]{1,0:T(8,128)} %get-tuple-element.43.last), channel_id=1, source_target_pairs={{0,4},{4,8},{8,12},{12,16},{16,20},{20,24},{24,28},{28,32},{32,36}... | collective-permute-start | bytes 49160 | tf_op jit(solution)/shard_map/ppermute | solution.py:333
  10.0 1.1 %collective-permute-done.rim = f32[8,512]{1,0:T(8,128)S(1)} collective-permute-done((f32[8,512]{1,0:T(8,128)}, f32[8,512]{1,0:T(8,128)S(1)}, u32[]{:S(2)}, u32[]{:S(2)}) %collective-permute-start) | collective-permute-done | bytes 16416 | tf_op jit(solution)/shard_map/ppermute | solution.py:333
  11.1 0.8 copy-done.9
  11.9 0.8 copy-done.12
  12.8 1.1 %collective-permute-start.1 = (bf16[64,512]{1,0:T(8,128)(2,1)S(1)}, bf16[64,512]{1,0:T(8,128)(2,1)S(1)}, u32[]{:S(2)}, u32[]{:S(2)}) collective-permute-start(bf16[64,512]{1,0:T(8,128)(2,1)S(1)} %shard_map.173.piece), channel_id=1, source_target_pairs={{0,8},{8,0},{1,9},{9,1},{2,10},{10,2},{3,11},{11,3},{4,12},{12,4},... | collective-permute-start | bytes 196616 | tf_op jit(solution)/shard_map/ppermute | solution.py:313
  13.8 5.1 %collective-permute-start.2 = (f32[8,512]{1,0:T(8,128)}, f32[8,512]{1,0:T(8,128)S(1)}, u32[]{:S(2)}, u32[]{:S(2)}) collective-permute-start(f32[8,512]{1,0:T(8,128)} %get-tuple-element.45), channel_id=1, source_target_pairs={{4,0},{8,4},{12,8},{16,12},{20,16},{24,20},{28,24},{32,28},{36,32}... | collective-permute-start | bytes 49160 | tf_op jit(solution)/shard_map/ppermute | solution.py:336
  18.9 2.0 %collective-permute-done.2.lead = f32[8,512]{1,0:T(8,128)S(1)} collective-permute-done((f32[8,512]{1,0:T(8,128)}, f32[8,512]{1,0:T(8,128)S(1)}, u32[]{:S(2)}, u32[]{:S(2)}) %collective-permute-start.2) | collective-permute-done | bytes 16416 | tf_op jit(solution)/shard_map/ppermute | solution.py:336
  21.0 0.7 copy-done.13
  21.7 3.8 %collective-permute-start.5 = (bf16[144,512]{1,0:T(8,128)(2,1)S(1)}, bf16[144,512]{1,0:T(8,128)(2,1)S(1)}, u32[]{:S(2)}, u32[]{:S(2)}) collective-permute-start(bf16[144,512]{1,0:T(8,128)(2,1)S(1)} %shard_map.174.p0), channel_id=1, source_target_pairs={{0,3},{1,0},{2,1},{3,2},{4,7},{5,4},{6,5},{7,6},{8,11},{9,8},{10,9... | collective-permute-start | bytes 442376 | tf_op jit(solution)/shard_map/ppermute | solution.py:313
  25.5 0.7 collective-permute-start.3
  26.2 5.9 %collective-permute-done.5.r3 = bf16[144,512]{1,0:T(8,128)(2,1)S(1)} collective-permute-done((bf16[144,512]{1,0:T(8,128)(2,1)S(1)}, bf16[144,512]{1,0:T(8,128)(2,1)S(1)}, u32[]{:S(2)}, u32[]{:S(2)}) %collective-permute-start.5) | collective-permute-done | bytes 147488 | tf_op jit(solution)/shard_map/ppermute | solution.py:313
  32.2 0.7 collective-permute-done.4.r2
  32.9 2.8 %collective-permute-done.3.r1 = bf16[144,512]{1,0:T(8,128)(2,1)S(1)} collective-permute-done((bf16[144,512]{1,0:T(8,128)(2,1)S(1)}, bf16[144,512]{1,0:T(8,128)(2,1)S(1)}, u32[]{:S(2)}, u32[]{:S(2)}) %collective-permute-start.3) | collective-permute-done | bytes 147488 | tf_op jit(solution)/shard_map/ppermute | solution.py:313
  35.8 1.6 %shard_map.175 = (bf16[64,1024]{1,0:T(8,128)(2,1)S(1)}, bf16[64,1024]{1,0:T(8,128)(2,1)S(1)}, bf16[4,32,1024]{2,1,0:T(8,128)(2,1)S(1)}, bf16[48,2048]{1,0:T(8,128)(2,1)S(1)}) custom-call(bf16[144,512]{1,0:T(8,128)(2,1)S(1)} %shard_map.174.p0, bf16[144,512]{1,0:T(8,128)(2,1)S(1)} %collective-permute-done.3.r1, ...), custom_call_target="tpu_custom_call" | custom-call | flops 1000000000 | tf_op jit(solution)/shard_map/pallas_call | solution.py:300
  37.9 1.0 %collective-permute-done.6.swapped = bf16[64,1024]{1,0:T(8,128)(2,1)S(1)} collective-permute-done((bf16[64,1024]{1,0:T(8,128)(2,1)S(1)}, bf16[64,1024]{1,0:T(8,128)(2,1)S(1)}, u32[]{:S(2)}, u32[]{:S(2)}) %collective-permute-start.6) | collective-permute-done | bytes 131104 | tf_op jit(solution)/shard_map/ppermute | solution.py:313
  39.0 1.5 %collective-permute-start.7 = (bf16[176,1024]{1,0:T(8,128)(2,1)S(1)}, bf16[176,1024]{1,0:T(8,128)(2,1)S(1)}, u32[]{:S(2)}, u32[]{:S(2)}) collective-permute-start(bf16[176,1024]{1,0:T(8,128)(2,1)S(1)} %get-tuple-element.51), channel_id=1, source_target_pairs={{0,16},{16,32},{32,48},{48,0},{1,17},{17,33},{33,49},{49,1},{2,18}... | collective-permute-start | bytes 1081352 | tf_op jit(solution)/shard_map/ppermute | solution.py:313
  40.5 1.3 %collective-permute-start.8 = (bf16[176,1024]{1,0:T(8,128)(2,1)S(1)}, bf16[176,1024]{1,0:T(8,128)(2,1)S(1)}, u32[]{:S(2)}, u32[]{:S(2)}) collective-permute-start(bf16[176,1024]{1,0:T(8,128)(2,1)S(1)} %get-tuple-element.52), channel_id=1, source_target_pairs={{0,48},{16,0},{32,16},{48,32},{1,49},{17,1},{33,17},{49,33},{2,50}... | collective-permute-start | bytes 1081352 | tf_op jit(solution)/shard_map/ppermute | solution.py:313
  41.9 8.2 %collective-permute-done.7.low = bf16[176,1024]{1,0:T(8,128)(2,1)S(1)} collective-permute-done((bf16[176,1024]{1,0:T(8,128)(2,1)S(1)}, bf16[176,1024]{1,0:T(8,128)(2,1)S(1)}, u32[]{:S(2)}, u32[]{:S(2)}) %collective-permute-start.7) | collective-permute-done | bytes 360480 | tf_op jit(solution)/shard_map/ppermute | solution.py:313
  51.5 2.6 %collective-permute-start.10 = (bf16[80,1024]{1,0:T(8,128)(2,1)}, bf16[80,1024]{1,0:T(8,128)(2,1)}, u32[]{:S(2)}, u32[]{:S(2)}) collective-permute-start(bf16[80,1024]{1,0:T(8,128)(2,1)} %slice.17), channel_id=1, source_target_pairs={{0,48},{16,0},{32,16},{48,32},{1,49},{17,1},{33,17},{49,33},{2,50}... | collective-permute-start | bytes 491528 | tf_op jit(solution)/shard_map/ppermute | solution.py:313
  54.6 1.1 %shard_map.177.strip = f32[2,128,512]{2,1,0:T(8,128)S(1)} custom-call(s32[8,640]{1,0:T(8,128)S(1)} %broadcast_in_dim.20.near, f32[32,4]{1,0:T(8,128)S(1)} %copy.19.table), custom_call_target="tpu_custom_call" | custom-call | tf_op jit(solution)/shard_map/pallas_call | solution.py:300
  55.7 1.0 %collective-permute-done.9.far_low = bf16[80,1024]{1,0:T(8,128)(2,1)S(1)} collective-permute-done((bf16[80,1024]{1,0:T(8,128)(2,1)}, bf16[80,1024]{1,0:T(8,128)(2,1)S(1)}, u32[]{:S(2)}, u32[]{:S(2)}) %collective-permute-start.9) | collective-permute-done | bytes 163872 | tf_op jit(solution)/shard_map/ppermute | solution.py:313
  56.7 5.9 %shard_map.178 = (bf16[4,528,256]{2,1,0:T(8,128)(2,1)S(1)}, bf16[4,48,256]{2,1,0:T(8,128)(2,1)S(1)}, bf16[4,48,256]{2,1,0:T(8,128)(2,1)S(1)}, bf16[4,32,1024]{2,1,0:T(8,128)(2,1)S(1)}) custom-call(s32[1]{0:T(128)S(6)} %copy.20.lens, bf16[160,1024]{1,0:T(8,128)(2,1)S(1)} %get-tuple-element.50.b0, bf16[176,1024]{1,0:T(8,128)(2,1)S(1)} %collective-permute-done.7.low, ...), custom_call_target="tpu_custom_call" | custom-call | flops 6000000000 | tf_op jit(solution)/shard_map/pallas_call | solution.py:300
  62.6 2.3 %collective-permute-start.15 = (bf16[4,32,1024]{2,1,0:T(8,128)(2,1)S(1)}, bf16[4,32,1024]{2,1,0:T(8,128)(2,1)S(1)}, u32[]{:S(2)}, u32[]{:S(2)}) collective-permute-start(bf16[4,32,1024]{2,1,0:T(8,128)(2,1)S(1)} %get-tuple-element.63.mine), channel_id=1, source_target_pairs={{0,4},{4,0},{1,5},{5,1},{2,6},{6,2},{3,7},{7,3},{8,12},{12,8},{9,1... | collective-permute-start | bytes 786440 | tf_op jit(solution)/shard_map/ppermute | solution.py:313
  65.0 1.1 %collective-permute-done.15.other = bf16[4,32,1024]{2,1,0:T(8,128)(2,1)S(1)} collective-permute-done((bf16[4,32,1024]{2,1,0:T(8,128)(2,1)S(1)}, bf16[4,32,1024]{2,1,0:T(8,128)(2,1)S(1)}, u32[]{:S(2)}, u32[]{:S(2)}) %collective-permute-start.15) | collective-permute-done | bytes 262176 | tf_op jit(solution)/shard_map/ppermute | solution.py:313
  66.6 1.2 %collective-permute-start.16 = (bf16[4,128,256]{2,1,0:T(8,128)(2,1)S(1)}, bf16[4,128,256]{2,1,0:T(8,128)(2,1)S(1)}, u32[]{:S(2)}, u32[]{:S(2)}) collective-permute-start(bf16[4,128,256]{2,1,0:T(8,128)(2,1)S(1)} %get-tuple-element.65), channel_id=1, source_target_pairs={{0,64},{64,0},{1,65},{65,1},{2,66},{66,2},{3,67},{67,3},{4,68},{68... | collective-permute-start | bytes 786440 | tf_op jit(solution)/shard_map/ppermute | solution.py:313
  67.9 2.6 %shard_map.179 = (bf16[80,640]{1,0:T(8,128)(2,1)S(1)}, bf16[80,640]{1,0:T(8,128)(2,1)S(1)}, bf16[80,640]{1,0:T(8,128)(2,1)S(1)}, f32[80,640]{1,0:T(8,128)S(1)}, ...) custom-call(bf16[4,48,256]{2,1,0:T(8,128)(2,1)S(1)} %get-tuple-element.53.keep_r, ...), custom_call_target="tpu_custom_call" | custom-call | flops 1000000000 | tf_op jit(solution)/shard_map/pallas_call | solution.py:300
  70.5 4.7 %collective-permute-done.12.after.r1 = bf16[80,640]{1,0:T(8,128)(2,1)S(1)} collective-permute-done((bf16[80,640]{1,0:T(8,128)(2,1)S(1)}, bf16[80,640]{1,0:T(8,128)(2,1)S(1)}, u32[]{:S(2)}, u32[]{:S(2)}) %collective-permute-start.12) | collective-permute-done | bytes 102432 | tf_op jit(solution)/shard_map/ppermute | solution.py:313
  75.3 1.9 %collective-permute-start.17 = (bf16[4,64,256]{2,1,0:T(8,128)(2,1)S(1)}, bf16[4,64,256]{2,1,0:T(8,128)(2,1)S(1)}, u32[]{:S(2)}, u32[]{:S(2)}) collective-permute-start(bf16[4,64,256]{2,1,0:T(8,128)(2,1)S(1)} %get-tuple-element.67), channel_id=1, source_target_pairs={{0,4},{4,0},{1,5},{5,1},{2,6},{6,2},{3,7},{7,3},{8,12},{12,8},{9,1... | collective-permute-start | bytes 393224 | tf_op jit(solution)/shard_map/ppermute | solution.py:313
  77.2 1.2 %collective-permute-start.14 = (bf16[80,640]{1,0:T(8,128)(2,1)S(1)}, bf16[80,640]{1,0:T(8,128)(2,1)S(1)}, u32[]{:S(2)}, u32[]{:S(2)}) collective-permute-start(bf16[80,640]{1,0:T(8,128)(2,1)S(1)} %get-tuple-element.59), channel_id=1, source_target_pairs={{0,3},{1,0},{2,1},{3,2},{4,7},{5,4},{6,5},{7,6},{8,11},{9,8},{10,9... | collective-permute-start | bytes 307208 | tf_op jit(solution)/shard_map/ppermute | solution.py:313
  78.3 4.7 %collective-permute-done.13.r2 = bf16[80,640]{1,0:T(8,128)(2,1)S(1)} collective-permute-done((bf16[80,640]{1,0:T(8,128)(2,1)S(1)}, bf16[80,640]{1,0:T(8,128)(2,1)S(1)}, u32[]{:S(2)}, u32[]{:S(2)}) %collective-permute-start.13) | collective-permute-done | bytes 102432 | tf_op jit(solution)/shard_map/ppermute | solution.py:313
  83.1 1.5 %shard_map.182 = (bf16[512,512]{1,0:T(8,128)(2,1)}, bf16[512,512]{1,0:T(8,128)(2,1)}, f32[64,512]{1,0:T(8,128)}, f32[64,512]{1,0:T(8,128)}, f32[64,512]{1,0:T(8,128)}, /*index=5*/f32[64,512]{1,0:T(8,128)}) custom-call(s32[1]{0:T(128)S(6)} %copy.20.lens, f32[80,640]{1,0:T(8,128)S(1)} %get-tuple-element.56.keep, ...), custom_call_target="tpu_custom_call" | custom-call | tf_op jit(solution)/shard_map/pallas_call | solution.py:300
  (57 shorter events, 3.5 us)
Async XLA Ops:
  3.8 7.3 %collective-permute-start = (f32[8,512]{1,0:T(8,128)}, f32[8,512]{1,0:T(8,128)S(1)}, u32[]{:S(2)}, u32[]{:S(2)}) collective-permute-start(f32[8,512]{1,0:T(8,128)} %get-tuple-element.43.last), channel_id=1, source_target_pairs={{0,4},{4,8},{8,12},{12,16},{16,20},{20,24},{24,28},{28,32},{32,36}... | collective-permute-start | bytes 49160 | tf_op jit(solution)/shard_map/ppermute | solution.py:333
  11.1 0.8 copy-start.9
  12.7 23.0 %copy-start = (bf16[2048,512]{1,0:T(8,128)(2,1)S(1)}, bf16[2048,512]{1,0:T(8,128)(2,1)}, u32[]{:S(2)}) copy-start(bf16[2048,512]{1,0:T(8,128)(2,1)} %wq.3) | copy-start | bytes 6291460
  12.7 23.0 %copy-start.1 = (bf16[2048,512]{1,0:T(8,128)(2,1)S(1)}, bf16[2048,512]{1,0:T(8,128)(2,1)}, u32[]{:S(2)}) copy-start(bf16[2048,512]{1,0:T(8,128)(2,1)} %wk.3) | copy-start | bytes 6291460
  12.7 23.0 %copy-start.3 = (bf16[2048,512]{1,0:T(8,128)(2,1)S(1)}, bf16[2048,512]{1,0:T(8,128)(2,1)}, u32[]{:S(2)}) copy-start(bf16[2048,512]{1,0:T(8,128)(2,1)} %wv.3) | copy-start | bytes 6291460
  12.7 23.0 %copy-start.5 = (bf16[2048,512]{1,0:T(8,128)(2,1)S(1)}, bf16[2048,512]{1,0:T(8,128)(2,1)}, u32[]{:S(2)}) copy-start(bf16[2048,512]{1,0:T(8,128)(2,1)} %wo.3) | copy-start | bytes 6291460
  12.7 23.0 %copy-start.8 = (f32[1,2048]{1,0:T(1,128)S(1)}, f32[1,2048]{1,0:T(1,128)}, u32[]{:S(2)}) copy-start(f32[1,2048]{1,0:T(1,128)} %get-tuple-element.46.gain) | copy-start | bytes 24580
  12.8 8.2 %collective-permute-start.1 = (bf16[64,512]{1,0:T(8,128)(2,1)S(1)}, bf16[64,512]{1,0:T(8,128)(2,1)S(1)}, u32[]{:S(2)}, u32[]{:S(2)}) collective-permute-start(bf16[64,512]{1,0:T(8,128)(2,1)S(1)} %shard_map.173.piece), channel_id=1, source_target_pairs={{0,8},{8,0},{1,9},{9,1},{2,10},{10,2},{3,11},{11,3},{4,12},{12,4},... | collective-permute-start | bytes 196616 | tf_op jit(solution)/shard_map/ppermute | solution.py:313
  13.8 7.2 %collective-permute-start.2 = (f32[8,512]{1,0:T(8,128)}, f32[8,512]{1,0:T(8,128)S(1)}, u32[]{:S(2)}, u32[]{:S(2)}) collective-permute-start(f32[8,512]{1,0:T(8,128)} %get-tuple-element.45), channel_id=1, source_target_pairs={{4,0},{8,4},{12,8},{16,12},{20,16},{24,20},{28,24},{32,28},{36,32}... | collective-permute-start | bytes 49160 | tf_op jit(solution)/shard_map/ppermute | solution.py:336
  21.7 10.4 %collective-permute-start.5 = (bf16[144,512]{1,0:T(8,128)(2,1)S(1)}, bf16[144,512]{1,0:T(8,128)(2,1)S(1)}, u32[]{:S(2)}, u32[]{:S(2)}) collective-permute-start(bf16[144,512]{1,0:T(8,128)(2,1)S(1)} %shard_map.174.p0), channel_id=1, source_target_pairs={{0,3},{1,0},{2,1},{3,2},{4,7},{5,4},{6,5},{7,6},{8,11},{9,8},{10,9... | collective-permute-start | bytes 442376 | tf_op jit(solution)/shard_map/ppermute | solution.py:313
  25.5 7.3 %collective-permute-start.4 = (bf16[144,512]{1,0:T(8,128)(2,1)S(1)}, bf16[144,512]{1,0:T(8,128)(2,1)S(1)}, u32[]{:S(2)}, u32[]{:S(2)}) collective-permute-start(bf16[144,512]{1,0:T(8,128)(2,1)S(1)} %shard_map.174.p0), channel_id=1, source_target_pairs={{0,2},{1,3},{2,0},{3,1},{4,6},{5,7},{6,4},{7,5},{8,10},{9,11},{10,... | collective-permute-start | bytes 442376 | tf_op jit(solution)/shard_map/ppermute | solution.py:313
  25.5 10.2 %collective-permute-start.3 = (bf16[144,512]{1,0:T(8,128)(2,1)S(1)}, bf16[144,512]{1,0:T(8,128)(2,1)S(1)}, u32[]{:S(2)}, u32[]{:S(2)}) collective-permute-start(bf16[144,512]{1,0:T(8,128)(2,1)S(1)} %shard_map.174.p0), channel_id=1, source_target_pairs={{0,1},{1,2},{2,3},{3,0},{4,5},{5,6},{6,7},{7,4},{8,9},{9,10},{10,1... | collective-permute-start | bytes 442376 | tf_op jit(solution)/shard_map/ppermute | solution.py:313
  35.7 18.4 %copy-start.15 = (s32[512]{0:T(512)S(1)}, s32[512]{0:T(512)}, u32[]{:S(2)}) copy-start(s32[512]{0:T(512)} %param.23) | copy-start | bytes 6148
  35.8 18.7 %copy-start.14 = (f32[32,4]{0,1:T(4,128)S(1)}, f32[32,4]{0,1:T(4,128)}, u32[]{:S(2)}) copy-start(f32[32,4]{0,1:T(4,128)} %param.22) | copy-start | bytes 1540
  37.4 1.5 %collective-permute-start.6 = (bf16[64,1024]{1,0:T(8,128)(2,1)S(1)}, bf16[64,1024]{1,0:T(8,128)(2,1)S(1)}, u32[]{:S(2)}, u32[]{:S(2)}) collective-permute-start(bf16[64,1024]{1,0:T(8,128)(2,1)S(1)} %get-tuple-element.48), channel_id=1, source_target_pairs={{0,4},{4,0},{1,5},{5,1},{2,6},{6,2},{3,7},{7,3},{8,12},{12,8},{9,1... | collective-permute-start | bytes 393224 | tf_op jit(solution)/shard_map/ppermute | solution.py:313
  39.0 11.1 %collective-permute-start.7 = (bf16[176,1024]{1,0:T(8,128)(2,1)S(1)}, bf16[176,1024]{1,0:T(8,128)(2,1)S(1)}, u32[]{:S(2)}, u32[]{:S(2)}) collective-permute-start(bf16[176,1024]{1,0:T(8,128)(2,1)S(1)} %get-tuple-element.51), channel_id=1, source_target_pairs={{0,16},{16,32},{32,48},{48,0},{1,17},{17,33},{33,49},{49,1},{2,18}... | collective-permute-start | bytes 1081352 | tf_op jit(solution)/shard_map/ppermute | solution.py:313
  40.5 10.3 %collective-permute-start.8 = (bf16[176,1024]{1,0:T(8,128)(2,1)S(1)}, bf16[176,1024]{1,0:T(8,128)(2,1)S(1)}, u32[]{:S(2)}, u32[]{:S(2)}) collective-permute-start(bf16[176,1024]{1,0:T(8,128)(2,1)S(1)} %get-tuple-element.52), channel_id=1, source_target_pairs={{0,48},{16,0},{32,16},{48,32},{1,49},{17,1},{33,17},{49,33},{2,50}... | collective-permute-start | bytes 1081352 | tf_op jit(solution)/shard_map/ppermute | solution.py:313
  50.7 6.0 %collective-permute-start.9 = (bf16[80,1024]{1,0:T(8,128)(2,1)}, bf16[80,1024]{1,0:T(8,128)(2,1)S(1)}, u32[]{:S(2)}, u32[]{:S(2)}) collective-permute-start(bf16[80,1024]{1,0:T(8,128)(2,1)} %slice.16), channel_id=1, source_target_pairs={{0,16},{16,32},{32,48},{48,0},{1,17},{17,33},{33,49},{49,1},{2,18}... | collective-permute-start | bytes 491528 | tf_op jit(solution)/shard_map/ppermute | solution.py:313
  51.5 5.2 %collective-permute-start.10 = (bf16[80,1024]{1,0:T(8,128)(2,1)}, bf16[80,1024]{1,0:T(8,128)(2,1)}, u32[]{:S(2)}, u32[]{:S(2)}) collective-permute-start(bf16[80,1024]{1,0:T(8,128)(2,1)} %slice.17), channel_id=1, source_target_pairs={{0,48},{16,0},{32,16},{48,32},{1,49},{17,1},{33,17},{49,33},{2,50}... | collective-permute-start | bytes 491528 | tf_op jit(solution)/shard_map/ppermute | solution.py:313
  56.7 11.1 %copy-start.4 = (bf16[2048,512]{1,0:T(8,128)(2,1)S(1)}, bf16[2048,512]{1,0:T(8,128)(2,1)}, u32[]{:S(2)}) copy-start(bf16[2048,512]{1,0:T(8,128)(2,1)} %wv.3) | copy-start | bytes 6291460
  56.7 11.1 %copy-start.6 = (bf16[2048,512]{1,0:T(8,128)(2,1)S(1)}, bf16[2048,512]{1,0:T(8,128)(2,1)}, u32[]{:S(2)}) copy-start(bf16[2048,512]{1,0:T(8,128)(2,1)} %wo.3) | copy-start | bytes 6291460
  62.6 5.2 %copy-start.2 = (bf16[2048,512]{1,0:T(8,128)(2,1)S(1)}, bf16[2048,512]{1,0:T(8,128)(2,1)}, u32[]{:S(2)}) copy-start(bf16[2048,512]{1,0:T(8,128)(2,1)} %wk.3) | copy-start | bytes 6291460
  62.6 3.4 %collective-permute-start.15 = (bf16[4,32,1024]{2,1,0:T(8,128)(2,1)S(1)}, bf16[4,32,1024]{2,1,0:T(8,128)(2,1)S(1)}, u32[]{:S(2)}, u32[]{:S(2)}) collective-permute-start(bf16[4,32,1024]{2,1,0:T(8,128)(2,1)S(1)} %get-tuple-element.63.mine), channel_id=1, source_target_pairs={{0,4},{4,0},{1,5},{5,1},{2,6},{6,2},{3,7},{7,3},{8,12},{12,8},{9,1... | collective-permute-start | bytes 786440 | tf_op jit(solution)/shard_map/ppermute | solution.py:313
  64.9 2.9 %collective-permute-start.11 = (bf16[4,48,256]{2,1,0:T(8,128)(2,1)S(1)}, bf16[4,48,256]{2,1,0:T(8,128)(2,1)S(1)}, u32[]{:S(2)}, u32[]{:S(2)}) collective-permute-start(bf16[4,48,256]{2,1,0:T(8,128)(2,1)S(1)} %get-tuple-element.54), channel_id=1, source_target_pairs={{0,4},{4,0},{1,5},{5,1},{2,6},{6,2},{3,7},{7,3},{8,12},{12,8},{9,1... | collective-permute-start | bytes 294920 | tf_op jit(solution)/shard_map/ppermute | solution.py:313
  66.6 8.6 %collective-permute-start.16 = (bf16[4,128,256]{2,1,0:T(8,128)(2,1)S(1)}, bf16[4,128,256]{2,1,0:T(8,128)(2,1)S(1)}, u32[]{:S(2)}, u32[]{:S(2)}) collective-permute-start(bf16[4,128,256]{2,1,0:T(8,128)(2,1)S(1)} %get-tuple-element.65), channel_id=1, source_target_pairs={{0,64},{64,0},{1,65},{65,1},{2,66},{66,2},{3,67},{67,3},{4,68},{68... | collective-permute-start | bytes 786440 | tf_op jit(solution)/shard_map/ppermute | solution.py:313
  67.9 15.2 %copy-start.7 = (f32[16,512]{1,0:T(8,128)S(1)}, f32[16,512]{1,0:T(8,128)}, u32[]{:S(2)}) copy-start(f32[16,512]{1,0:T(8,128)} %up_gain.1) | copy-start | bytes 98308
  67.9 15.2 %copy-start.10 = (f32[4,512]{1,0:T(4,128)S(1)}, f32[4,512]{1,0:T(4,128)}, u32[]{:S(2)}) copy-start(f32[4,512]{1,0:T(4,128)} %first.1) | copy-start | bytes 24580
  67.9 15.2 %copy-start.11 = (f32[4,512]{1,0:T(4,128)S(1)}, f32[4,512]{1,0:T(4,128)}, u32[]{:S(2)}) copy-start(f32[4,512]{1,0:T(4,128)} %second.1) | copy-start | bytes 24580
  70.5 4.8 %collective-permute-start.12 = (bf16[80,640]{1,0:T(8,128)(2,1)S(1)}, bf16[80,640]{1,0:T(8,128)(2,1)S(1)}, u32[]{:S(2)}, u32[]{:S(2)}) collective-permute-start(bf16[80,640]{1,0:T(8,128)(2,1)S(1)} %get-tuple-element.57), channel_id=1, source_target_pairs={{0,1},{1,2},{2,3},{3,0},{4,5},{5,6},{6,7},{7,4},{8,9},{9,10},{10,1... | collective-permute-start | bytes 307208 | tf_op jit(solution)/shard_map/ppermute | solution.py:313
  75.3 7.8 %collective-permute-start.17 = (bf16[4,64,256]{2,1,0:T(8,128)(2,1)S(1)}, bf16[4,64,256]{2,1,0:T(8,128)(2,1)S(1)}, u32[]{:S(2)}, u32[]{:S(2)}) collective-permute-start(bf16[4,64,256]{2,1,0:T(8,128)(2,1)S(1)} %get-tuple-element.67), channel_id=1, source_target_pairs={{0,4},{4,0},{1,5},{5,1},{2,6},{6,2},{3,7},{7,3},{8,12},{12,8},{9,1... | collective-permute-start | bytes 393224 | tf_op jit(solution)/shard_map/ppermute | solution.py:313
  77.1 5.9 %collective-permute-start.13 = (bf16[80,640]{1,0:T(8,128)(2,1)S(1)}, bf16[80,640]{1,0:T(8,128)(2,1)S(1)}, u32[]{:S(2)}, u32[]{:S(2)}) collective-permute-start(bf16[80,640]{1,0:T(8,128)(2,1)S(1)} %get-tuple-element.58), channel_id=1, source_target_pairs={{0,2},{1,3},{2,0},{3,1},{4,6},{5,7},{6,4},{7,5},{8,10},{9,11},{10,... | collective-permute-start | bytes 307208 | tf_op jit(solution)/shard_map/ppermute | solution.py:313
  77.2 5.9 %collective-permute-start.14 = (bf16[80,640]{1,0:T(8,128)(2,1)S(1)}, bf16[80,640]{1,0:T(8,128)(2,1)S(1)}, u32[]{:S(2)}, u32[]{:S(2)}) collective-permute-start(bf16[80,640]{1,0:T(8,128)(2,1)S(1)} %get-tuple-element.59), channel_id=1, source_target_pairs={{0,3},{1,0},{2,1},{3,2},{4,7},{5,4},{6,5},{7,6},{8,11},{9,8},{10,9... | collective-permute-start | bytes 307208 | tf_op jit(solution)/shard_map/ppermute | solution.py:313
  (2 other events, 1.5 us)

commit v5 on v4

--- a/solution.py
+++ b/solution.py
@@ -24,7 +24,7 @@
 VM = pltpu.VMEM
 BIG = 63 * 2**20
 SM = pltpu.SMEM
-PIECE = 4 * CL + 16
+PIECE = 4 * CL
 
 
 def dg(a, b, ca, cb):
@@ -50,7 +50,7 @@
 
 
 def before_kernel(
-    lens, tokens_h, grad_h, first_h, second_h, up_h, gain_h, part, last, ahead, gco, gain,
+    lens, tokens_h, grad_h, first_h, second_h, up_h, gain_h, part, last, gco, gain,
     tokens, grad_out, first, second, up_gain, shift, sems,
 ):
     pairs = ((tokens_h, tokens), (first_h, first), (second_h, second), (grad_h, grad_out), (up_h, up_gain), (gain_h, gain))
@@ -69,7 +69,6 @@
     shift[8 : 8 + CL] = onward
     part[...] = own + shift[7 : 7 + CL]
     last[...] = jnp.broadcast_to(shift[7 + CL : 8 + CL], (8, WL))
-    ahead[...] = jnp.broadcast_to(own[0:1], (8, WL))
     for c in copies[3:]:
         c.wait()
     weighted = grad_out[...].astype(F32).reshape(CL, 16, WL) * mask * up_gain[...][None]
@@ -82,12 +81,10 @@
     piece[CL : 2 * CL] = gco[...]
 
 
-def pile_kernel(piece, across, lead, last, out):
+def pile_kernel(piece, across, out):
     y = Place().y
     out[pl.ds(pl.multiple_of(y * 64, 64), 64)] = piece[...]
     out[pl.ds(pl.multiple_of(64 - y * 64, 64), 64)] = across[...]
-    first = lax.broadcasted_iota(jnp.int32, (16, WL), 0) == 0
-    out[128:144] = jnp.where(first, lead[0:1] + last[0:1], 0.0).astype(BF16)
 
 
 def bias_kernel(near, table, strip):
@@ -103,7 +100,7 @@
 
 
 def project_kernel(
-    p0, r1, r2, r3, gain, wq, wk, wv, wo, keep, send, blocks, c48, craw, nrm, gco, both
+    p0, r1, r2, r3, gain, wq, wk, wv, wo, keep, send, blocks, mine, craw, nrm, gco, both
 ):
     at = Place()
     z, core, x, y = at.z, at.core, at.x, at.y
@@ -113,8 +110,7 @@
             rows = slice(i * CL, i * CL + CL)
             craw[rows, cols] = src[2 * i * CL : 2 * i * CL + CL]
             gco[rows, cols] = src[2 * i * CL + CL : 2 * i * CL + 2 * CL]
-        c48[CL:ROWS, cols] = src[4 * CL : PIECE]
-    c48[0:CL] = craw[pl.ds(pl.multiple_of(y * CL, CL), CL)]
+    mine[...] = craw[pl.ds(pl.multiple_of(y * CL, CL), CL)]
     c = craw[...].astype(F32)
     r = lax.rsqrt(jnp.sum(c * c, axis=1, keepdims=True) * (1.0 / D) + 1e-6)
     nrm[...] = (c * r * gain[...]).astype(BF16)
@@ -123,7 +119,9 @@
         for half in range(2):
             both[half, :, slot * HW : slot * HW + HW] = v[:, half * HW : half * HW + HW]
     keep[...] = both[core]
-    send[...] = both[1 - core]
+    send[0:64] = both[1 - core]
+    tops = [c[i * CL : i * CL + 1, j * 1024 : j * 1024 + 1024] for i in range(2) for j in range(2)]
+    send[64:80] = jnp.concatenate(tops + [jnp.zeros((12, 1024), F32)], axis=0).astype(BF16)
     for s in range(4):
         for d in range(2):
             chip = lax.rem(x + s, 4) * 2 + y
@@ -149,10 +147,30 @@
     down[0:32] = blocks[3]
     up[160:176] = blocks[2, 0:16]
     down[160:176] = blocks[2, 16:32]
+    down[176:192] = swapped[64:80]
+
+
+def onward_kernel(src, out):
+    out[...] = src[96:176]
+
+
+def gather_kernel(b0, low, high, far_low, far_high, swapped, mine, nxt):
+    mine[0] = b0[128:160]
+    mine[1] = low[0:32]
+    mine[2, 0:16] = far_low[64:80]
+    mine[2, 16:32] = far_high[64:80]
+    mine[3] = high[0:32]
+    at = Place()
+    wraps = jnp.logical_and(at.core == 1, at.y == 1)
+    tops = jnp.where(wraps, high[176:192].astype(F32), swapped[64:80].astype(F32))
+    upper = jnp.where(at.core == 0, at.y, 1 - at.y) == 1
+    for j in range(2):
+        row = jnp.where(upper, tops[2 + j : 3 + j], tops[j : j + 1])
+        nxt[:, j * 1024 : j * 1024 + 1024] = jnp.broadcast_to(row, (16, 1024)).astype(BF16)
 
 
 def attend_kernel(
-    lens, b0, low, high, far_low, far_high, strip, res, keep, send, mine, q, k, v, ga, acck, accv
+    lens, b0, low, high, far_low, far_high, strip, res, keep, send, q, k, v, ga, acck, accv
 ):
     at = Place()
     ctx, core, x, doc_len = at.ctx, at.core, at.x, lens[0]
@@ -167,11 +185,6 @@
         rows = pl.ds(pl.multiple_of(lax.rem(x + 4 - s, 4) * 128 + row, 64), n)
         for i, dst in enumerate((q, k, v, ga)):
             dst[rows] = src[first : first + n, i * HW : i * HW + HW]
-    mine[0] = b0[128:160]
-    mine[1] = low[0:32]
-    mine[2, 0:16] = far_low[64:80]
-    mine[2, 16:32] = far_high[64:80]
-    mine[3] = high[0:32]
     key_pos = lax.broadcasted_iota(jnp.int32, (1, LC), 1)
     key_mask = jnp.where(16 * key_pos < doc_len, 0.0, NEG)
     for h in range(NH):
@@ -205,7 +218,7 @@
     send[...] = res[:, pl.ds(pl.multiple_of(peer * CL, CL), ROWS)]
 
 
-def weights_kernel(res, mine, other, keep, send, nb, gb):
+def weights_kernel(res, mine, other, keep, to_core, to_dp, to_both, nb, gb, tile):
     at = Place()
     core, x, dp = at.core, at.x, at.dp
     for s in range(4):
@@ -217,26 +230,22 @@
                 gb[rows] = src[s, :, i * 512 + 256 : i * 512 + 512]
     for w in range(4):
         src = gb if w == 3 else nb
-        for d, out in ((dp, keep), (1 - dp, send)):
+        for d, a, b in ((dp, keep, to_core), (1 - dp, to_dp, to_both)):
             cols = pl.ds(pl.multiple_of(d * 128, 128), 128)
-            out[w] = dg(src[:, cols], res[w, 0:LC], 0, 0).astype(out.dtype)
-
-
-def total_kernel(keep, got, after, own, send):
-    core = Place().core
-    for w in range(4):
-        for c, out in ((core, own), (1 - core, send)):
-            rows = pl.ds(pl.multiple_of(c * 64, 64), 64)
-            out[w] = (keep[w, rows] + got[w, rows].astype(F32)).astype(out.dtype)
+            tile[...] = dg(src[:, cols], res[w, 0:LC], 0, 0)
+            a[w] = tile[pl.ds(pl.multiple_of(core * 64, 64), 64)].astype(a.dtype)
+            b[w] = tile[pl.ds(pl.multiple_of(64 - core * 64, 64), 64)].astype(BF16)
 
 
 def partial_kernel(
-    keep_r, got_r, c, gain, wq, wk, wv, wo, msg1, msg2, msg3, keep, cz, inv_out, g
+    keep_r, got_r, crow, nxt, after, gain, wq, wk, wv, wo, msg1, msg2, msg3, keep, cz, inv_out, g, c
 ):
     at = Place()
     z, core = at.z, at.core
     g[:, :, pl.ds(pl.multiple_of(core * HW, HW), HW)] = keep_r[...]
     g[:, :, pl.ds(pl.multiple_of((1 - core) * HW, HW), HW)] = got_r[...]
+    c[0:CL] = crow[...]
+    c[CL:ROWS] = nxt[...]
     cf = c[...].astype(F32)
     r = lax.rsqrt(jnp.sum(cf * cf, axis=1, keepdims=True) * (1.0 / D) + 1e-6)
     inv_out[...] = jnp.broadcast_to(r, (ROWS, 128))
@@ -263,12 +272,19 @@
         msg[CL : CL + ROWS, WL : WL + 128] = packed
 
 
+def total_kernel(dw, from_core, from_dp, from_both, o0, o1, o2, o3):
+    core = Place().core
+    for w, o in enumerate((o0, o1, o2, o3)):
+        o[:, pl.ds(pl.multiple_of(core * HW, HW), HW)] = dw[w] + from_dp[w].astype(F32)
+        there = from_core[w].astype(F32) + from_both[w].astype(F32)
+        o[:, pl.ds(pl.multiple_of((1 - core) * HW, HW), HW)] = there
+
+
 def after_kernel(
-    lens, keep, r1, r2, r3, cz, inv, gain, first, second, up_gain, dw, other,
-    update, grad, o0, o1, o2, o3, rows,
-):
-    at = Place()
-    ctx, doc_len, z, core = at.ctx, lens[0], at.z, at.core
+    lens, keep, r1, r2, r3, cz, inv, gain, first, second, up_gain, update, grad, rows
+):
+    at = Place()
+    ctx, doc_len, z = at.ctx, lens[0], at.z
     mask = byte_mask(ctx, doc_len)
     body = slice(0, WL)
     out = keep[0:CL, body]
@@ -288,18 +304,15 @@
     u = lax.broadcasted_iota(jnp.int32, (CL, 16, WL), 1)
     picked = jnp.where(u == 0, rows[0:CL][:, None, :], rows[1 : CL + 1][:, None, :])
     grad[...] = (picked * taps[None] * mask).reshape(SEG, WL).astype(BF16)
-    for w, o in enumerate((o0, o1, o2, o3)):
-        o[:, pl.ds(pl.multiple_of(core * HW, HW), HW)] = dw[w]
-        o[:, pl.ds(pl.multiple_of((1 - core) * HW, HW), HW)] = other[w].astype(F32)
-
-
-def call(kernel, outs, args, scratch=(), smem=(0,), flops=0, size=0, vmem=8 * 2**20, hbm=()):
+
+
+def call(kernel, outs, args, scratch=(), smem=(0,), flops=0, size=0, vmem=8 * 2**20, hbm=(), typed=True):
     def spec(i):
         return pl.BlockSpec(memory_space=SM if i in smem else pltpu.HBM if i in hbm else VM)
 
     return pl.pallas_call(
         kernel,
-        out_shape=[jax.ShapeDtypeStruct(s, d) for s, d in outs],
+        out_shape=[pltpu.VMEM(s, d) if typed else jax.ShapeDtypeStruct(s, d) for s, d in outs],
         in_specs=[spec(i) for i in range(len(args))],
         out_specs=[pl.BlockSpec(memory_space=VM)] * len(outs),
         scratch_shapes=[pltpu.VMEM(*s) if isinstance(s, tuple) else s for s in scratch],
@@ -318,9 +331,9 @@
     bias_table, buckets, up_gain, grad_out,
 ):
     weights = (w_query, w_key, w_value, w_out)
-    part, last, ahead, gco, gain = call(
+    part, last, gco, gain = call(
         before_kernel,
-        [((CL, WL), F32), ((8, WL), F32), ((8, WL), F32), ((CL, WL), BF16), ((1, D), F32)],
+        [((CL, WL), F32), ((8, WL), F32), ((CL, WL), BF16), ((1, D), F32)],
         (lengths, tokens[0], grad_out[0], conv_first, conv_second, up_gain, norm_gain[None]),
         [
             ((SEG, WL), BF16), ((SEG, WL), BF16), ((4, WL), F32), ((4, WL), F32), ((16, WL), F32),
@@ -332,13 +345,11 @@
     line = ("x", "y", "core")
     rim = lax.ppermute(last, line, [(i, i + 1) for i in range(15)])
     (piece,) = call(piece_kernel, [((2 * CL, WL), BF16)], (part, gco, rim), smem=())
-    ahead, piece = lax.optimization_barrier((ahead, piece))
-    lead = lax.ppermute(ahead, line, [(i + 1, i) for i in range(15)])
     across = shifted(piece, "y", 1)
     (piece,) = call(
         pile_kernel,
         [((PIECE, WL), BF16)],
-        (piece, across, lead, last),
+        (piece, across),
         smem=(),
         flops=6 * 10**9,
     )
@@ -357,9 +368,9 @@
         smem=(1,),
     )
     pieces = [piece] + [shifted(piece, "tensor", s) for s in (1, 2, 3)]
-    keep, send, blocks, c48 = call(
+    keep, send, blocks, crow = call(
         project_kernel,
-        [((2 * CL, 4 * HW), BF16), ((2 * CL, 4 * HW), BF16), ((4, CL, 4 * HW), BF16), ((ROWS, D), BF16)],
+        [((64, 4 * HW), BF16), ((80, 4 * HW), BF16), ((4, CL, 4 * HW), BF16), ((CL, D), BF16)],
         (*pieces, gain, *weights),
         [((2 * CL, D), BF16), ((2 * CL, D), BF16), ((2 * CL, D), BF16), ((2, 2 * CL, 4 * HW), BF16)],
         smem=(),
@@ -368,55 +379,63 @@
     swapped = shifted(send, "core", 1)
     b0, up, down = call(
         pack_kernel,
-        [((5 * CL, 4 * HW), BF16), ((176, 4 * HW), BF16), ((176, 4 * HW), BF16)],
+        [((160, 4 * HW), BF16), ((176, 4 * HW), BF16), ((192, 4 * HW), BF16)],
         (keep, swapped, blocks),
         smem=(),
     )
     low, high = shifted(up, "x", 1), shifted(down, "x", -1)
-    far_low, far_high = shifted(low[96:], "x", 1), shifted(high[96:], "x", -1)
-    res, keep_r, send_r, mine = call(
+    far = [((80, 4 * HW), BF16)]
+    far_low = shifted(call(onward_kernel, far, (low,), smem=())[0], "x", 1)
+    far_high = shifted(call(onward_kernel, far, (high,), smem=())[0], "x", -1)
+    mine, nxt = call(
+        gather_kernel,
+        [((4, CL, 4 * HW), BF16), ((16, D), BF16)],
+        (b0, low, high, far_low, far_high, swapped),
+        smem=(),
+    )
+    other_rows = shifted(mine, "core", 1)
+    res, keep_r, send_r = call(
         attend_kernel,
-        [
-            ((4, LC + 16, HW), BF16), ((4, ROWS, HW), BF16), ((4, ROWS, HW), BF16),
-            ((4, CL, 4 * HW), BF16),
-        ],
+        [((4, LC + 16, HW), BF16), ((4, ROWS, HW), BF16), ((4, ROWS, HW), BF16)],
         (lengths, b0, low, high, far_low, far_high, strip),
         [((LC, HW), BF16)] * 4 + [((NH, LC, HD), F32)] * 2,
         flops=6 * 10**9,
     )
-    other_rows = shifted(mine, "core", 1)
     got_r = shifted(send_r, "core", 1)
-    dw_keep, dw_send = call(
+    dw_keep, to_core, to_dp, to_both = call(
         weights_kernel,
-        [((4, 128, HW), F32), ((4, 128, HW), BF16)],
+        [((4, 64, HW), F32)] + [((4, 64, HW), BF16)] * 3,
         (res, mine, other_rows),
-        [((LC, 256), BF16), ((LC, 256), BF16)],
+        [((LC, 256), BF16), ((LC, 256), BF16), ((128, HW), F32)],
         smem=(),
         flops=10**9,
     )
-    dw_got = shifted(dw_send, "dp", 1)
+    from_core, from_dp = shifted(to_core, "core", 1), shifted(to_dp, "dp", 1)
+    from_both = lax.ppermute(to_both, ("dp", "core"), [(i, 3 - i) for i in range(4)])
     msg = (CL + ROWS, WL + 128)
     m1, m2, m3, own, cz, inv = call(
         partial_kernel,
         [(msg, BF16), (msg, BF16), (msg, BF16), (msg, F32), ((ROWS, WL), BF16), ((ROWS, 128), F32)],
-        (keep_r, got_r, c48, gain, *weights),
-        [((4, ROWS, WL), BF16)],
+        (keep_r, got_r, crow, nxt, dw_keep, gain, *weights),
+        [((4, ROWS, WL), BF16), ((ROWS, D), BF16)],
         smem=(),
         flops=10**9,
     )
     r1, r2, r3 = shifted(m1, "tensor", 1), shifted(m2, "tensor", 2), shifted(m3, "tensor", 3)
-    dw_own, dw_other = call(
+    dw = call(
         total_kernel,
-        [((4, 64, HW), F32), ((4, 64, HW), BF16)],
-        (dw_keep, dw_got, r1),
-        smem=(),
-    )
-    dw_other = shifted(dw_other, "core", 1)
-    update, grad_tokens, *dw = call(
+        [((64, WL), F32)] * 4,
+        (dw_keep, from_core, from_dp, from_both),
+        smem=(),
+        flops=6 * 10**9,
+        typed=False,
+    )
+    update, grad_tokens = call(
         after_kernel,
-        [((SEG, WL), BF16)] * 2 + [((64, WL), F32)] * 4,
-        (lengths, own, r1, r2, r3, cz, inv, gain, conv_first, conv_second, up_gain, dw_own, dw_other),
+        [((SEG, WL), BF16)] * 2,
+        (lengths, own, r1, r2, r3, cz, inv, gain, conv_first, conv_second, up_gain),
         [((ROWS, WL), F32)],
+        typed=False,
     )
     return (update[None], grad_tokens[None], *dw)
 

time: 85.3 us -> 78.3 us (0.918)
  waiting for transfers between devices: 33.3 us -> 25.9 us
  local copies, waits for them, and re-layouts: 4.18 us -> 0.69 us
  Pallas kernels: 15.8 us -> 18.4 us
  starting transfers between devices: 29.7 us -> 30.8 us
    ppermute x16, starting transfers between devices: 18.4 us -> 24.1 us  [shifted(): return lax.ppermute(x, axis, [(i, (i + steps) % n) for i in range(n)])]
    ppermute x16, waiting for transfers between devices: 30.2 us -> 25 us  [shifted(): return lax.ppermute(x, axis, [(i, (i + steps) % n) for i in range(n)])]
    ppermute x1, starting transfers between devices: 5.11 us -> 0.52 us  [local(): lax.ppermute(to_both, ('dp', 'core'), [(i, 3 - i) for i in range(4)])]
    pallas_call x11 -> x14, Pallas kernels: 15.8 us -> 18.4 us  [call(): pl.pallas_call(kernel, out_shape=[pltpu.VMEM(s, d) if typed else jax.Shap...]
    unnamed x35 -> x31, local copies, waits for them, and re-layouts: 2.65 us -> 0.51 us
    ppermute x1, waiting for transfers between devices: 2.04 us -> 0.01 us  [local(): lax.ppermute(to_both, ('dp', 'core'), [(i, 3 - i) for i in range(4)])]
    slice x2 -> x0, local copies, waits for them, and re-layouts: 1.36 us -> none  [local(): far_low, far_high = (shifted(low[96:], 'x', 1), shifted(high[96:], 'x', -1))]
  transfers between devices with their start and end apart: 18 -> 18, of which waited for: 11 -> 13; matrix products, arithmetic and copies ran while one was open for 2% -> 1% of each run, Pallas kernels for 5% -> 13%
where the time goes in v5:
time: 78.3 us; the launch traced here: 77.4 us
  starting transfers between devices  30.8 us (39%)
  waiting for transfers between devices  25.9 us (33%)
  Pallas kernels  18.4 us (23%)
  between operations  1.45 us (2%)
    ppermute x16, waiting for transfers between devices, shifted(): return lax.ppermute(x, axis, [(i, (i + steps) % n) for i in range(n)])  25 us
    ppermute x16, starting transfers between devices, shifted(): return lax.ppermute(x, axis, [(i, (i + steps) % n) for i in range(n)])  24.1 us
    pallas_call x14, Pallas kernels, call(): pl.pallas_call(kernel, out_shape=[pltpu.VMEM(s, d) if typed else jax.Shap...  18.4 us
    ppermute x1, starting transfers between devices, local(): rim = lax.ppermute(last, line, [(i, i + 1) for i in range(15)])  6.21 us
  transfers between devices with their start and end apart: 18, of which 13 were waited for; matrix products, arithmetic and copies ran while one was open for 1% of the time, Pallas kernels for 13%

profile of v5, /device:TPU:1, one launch (start us, length us, event | category | flops | bytes accessed | tf_op | source)
XLA Modules:
  0.0 77.4 jit_solution(1136604336371940265)
XLA Ops:
  1.3 1.9 %shard_map.172 = (f32[32,512]{1,0:T(8,128)S(1)}, f32[8,512]{1,0:T(8,128)S(1)}, bf16[32,512]{1,0:T(8,128)(2,1)S(1)}, f32[1,2048]{1,0:T(1,128)S(1)}) custom-call(s32[1]{0:T(128)S(6)} %copy.20.lens, bf16[512,512]{1,0:T(8,128)(2,1)} %bitcast.7, bf16[512,512]{1,0:T(8,128)(2,1)} %bitcast.8, f32[4,512]{1,0:T(4,128)} %first.1, f32[4,512]{1,0:T(4,128)} %second.1, ...), custom_call_target="tpu_custom_call" | custom-call | tf_op jit(solution)/shard_map/pallas_call | solution.py:313
  3.2 6.2 %collective-permute-start = (f32[8,512]{1,0:T(8,128)S(1)}, f32[8,512]{1,0:T(8,128)S(1)}, u32[]{:S(2)}, u32[]{:S(2)}) collective-permute-start(f32[8,512]{1,0:T(8,128)S(1)} %get-tuple-element.40), channel_id=1, source_target_pairs={{0,4},{4,8},{8,12},{12,16},{16,20},{20,24},{24,28},{28,32},{32,36}... | collective-permute-start | bytes 49160 | tf_op jit(solution)/shard_map/ppermute | solution.py:346
  9.4 0.8 %collective-permute-done.rim = f32[8,512]{1,0:T(8,128)S(1)} collective-permute-done((f32[8,512]{1,0:T(8,128)S(1)}, f32[8,512]{1,0:T(8,128)S(1)}, u32[]{:S(2)}, u32[]{:S(2)}) %collective-permute-start) | collective-permute-done | bytes 16416 | tf_op jit(solution)/shard_map/ppermute | solution.py:346
  10.3 1.1 %collective-permute-start.1 = (bf16[64,512]{1,0:T(8,128)(2,1)S(1)}, bf16[64,512]{1,0:T(8,128)(2,1)S(1)}, u32[]{:S(2)}, u32[]{:S(2)}) collective-permute-start(bf16[64,512]{1,0:T(8,128)(2,1)S(1)} %shard_map.173.piece), channel_id=1, source_target_pairs={{0,8},{8,0},{1,9},{9,1},{2,10},{10,2},{3,11},{11,3},{4,12},{12,4},... | collective-permute-start | bytes 196616 | tf_op jit(solution)/shard_map/ppermute | solution.py:326
  11.4 3.6 %collective-permute-done.1.across = bf16[64,512]{1,0:T(8,128)(2,1)S(1)} collective-permute-done((bf16[64,512]{1,0:T(8,128)(2,1)S(1)}, bf16[64,512]{1,0:T(8,128)(2,1)S(1)}, u32[]{:S(2)}, u32[]{:S(2)}) %collective-permute-start.1) | collective-permute-done | bytes 65568 | tf_op jit(solution)/shard_map/ppermute | solution.py:326
  15.0 1.7 %collective-permute-start.2 = (bf16[128,512]{1,0:T(8,128)(2,1)S(1)}, bf16[128,512]{1,0:T(8,128)(2,1)S(1)}, u32[]{:S(2)}, u32[]{:S(2)}) collective-permute-start(bf16[128,512]{1,0:T(8,128)(2,1)S(1)} %shard_map.174.p0), channel_id=1, source_target_pairs={{0,1},{1,2},{2,3},{3,0},{4,5},{5,6},{6,7},{7,4},{8,9},{9,10},{10,1... | collective-permute-start | bytes 393224 | tf_op jit(solution)/shard_map/ppermute | solution.py:326
  16.7 3.3 %collective-permute-start.3 = (bf16[128,512]{1,0:T(8,128)(2,1)S(1)}, bf16[128,512]{1,0:T(8,128)(2,1)S(1)}, u32[]{:S(2)}, u32[]{:S(2)}) collective-permute-start(bf16[128,512]{1,0:T(8,128)(2,1)S(1)} %shard_map.174.p0), channel_id=1, source_target_pairs={{0,2},{1,3},{2,0},{3,1},{4,6},{5,7},{6,4},{7,5},{8,10},{9,11},{10,... | collective-permute-start | bytes 393224 | tf_op jit(solution)/shard_map/ppermute | solution.py:326
  20.0 0.7 collective-permute-start.4
  21.2 3.1 %collective-permute-done.3.r2 = bf16[128,512]{1,0:T(8,128)(2,1)S(1)} collective-permute-done((bf16[128,512]{1,0:T(8,128)(2,1)S(1)}, bf16[128,512]{1,0:T(8,128)(2,1)S(1)}, u32[]{:S(2)}, u32[]{:S(2)}) %collective-permute-start.3) | collective-permute-done | bytes 131104 | tf_op jit(solution)/shard_map/ppermute | solution.py:326
  24.3 0.7 collective-permute-done.4.r3
  25.0 1.6 %shard_map.175 = (bf16[64,1024]{1,0:T(8,128)(2,1)S(1)}, bf16[80,1024]{1,0:T(8,128)(2,1)S(1)}, bf16[4,32,1024]{2,1,0:T(8,128)(2,1)S(1)}, bf16[32,2048]{1,0:T(8,128)(2,1)S(1)}) custom-call(bf16[128,512]{1,0:T(8,128)(2,1)S(1)} %shard_map.174.p0, bf16[128,512]{1,0:T(8,128)(2,1)S(1)} %collective-permute-done.2.r1, ...), custom_call_target="tpu_custom_call" | custom-call | flops 1000000000 | tf_op jit(solution)/shard_map/pallas_call | solution.py:313
  26.6 2.5 %collective-permute-start.5 = (bf16[80,1024]{1,0:T(8,128)(2,1)S(1)}, bf16[80,1024]{1,0:T(8,128)(2,1)S(1)}, u32[]{:S(2)}, u32[]{:S(2)}) collective-permute-start(bf16[80,1024]{1,0:T(8,128)(2,1)S(1)} %get-tuple-element.43), channel_id=1, source_target_pairs={{0,4},{4,0},{1,5},{5,1},{2,6},{6,2},{3,7},{7,3},{8,12},{12,8},{9,1... | collective-permute-start | bytes 491528 | tf_op jit(solution)/shard_map/ppermute | solution.py:326
  29.1 1.0 %collective-permute-done.5.swapped = bf16[80,1024]{1,0:T(8,128)(2,1)S(1)} collective-permute-done((bf16[80,1024]{1,0:T(8,128)(2,1)S(1)}, bf16[80,1024]{1,0:T(8,128)(2,1)S(1)}, u32[]{:S(2)}, u32[]{:S(2)}) %collective-permute-start.5) | collective-permute-done | bytes 163872 | tf_op jit(solution)/shard_map/ppermute | solution.py:326
  30.2 3.8 %collective-permute-start.7 = (bf16[192,1024]{1,0:T(8,128)(2,1)S(1)}, bf16[192,1024]{1,0:T(8,128)(2,1)S(1)}, u32[]{:S(2)}, u32[]{:S(2)}) collective-permute-start(bf16[192,1024]{1,0:T(8,128)(2,1)S(1)} %get-tuple-element.47), channel_id=1, source_target_pairs={{0,48},{16,0},{32,16},{48,32},{1,49},{17,1},{33,17},{49,33},{2,50}... | collective-permute-start | bytes 1179656 | tf_op jit(solution)/shard_map/ppermute | solution.py:326
  34.0 10.5 %collective-permute-done.6.src.low = bf16[176,1024]{1,0:T(8,128)(2,1)S(1)} collective-permute-done((bf16[176,1024]{1,0:T(8,128)(2,1)S(1)}, bf16[176,1024]{1,0:T(8,128)(2,1)S(1)}, u32[]{:S(2)}, u32[]{:S(2)}) %collective-permute-start.6) | collective-permute-done | bytes 360480 | tf_op jit(solution)/shard_map/ppermute | solution.py:326
  44.5 0.7 shard_map.177
  45.2 0.7 shard_map.178
  45.9 2.7 %collective-permute-start.9 = (bf16[80,1024]{1,0:T(8,128)(2,1)}, bf16[80,1024]{1,0:T(8,128)(2,1)}, u32[]{:S(2)}, u32[]{:S(2)}) collective-permute-start(bf16[80,1024]{1,0:T(8,128)(2,1)} %shard_map.178), channel_id=1, source_target_pairs={{0,48},{16,0},{32,16},{48,32},{1,49},{17,1},{33,17},{49,33},{2,50}... | collective-permute-start | bytes 491528 | tf_op jit(solution)/shard_map/ppermute | solution.py:326
  49.1 1.1 %shard_map.179.strip = f32[2,128,512]{2,1,0:T(8,128)S(1)} custom-call(s32[8,640]{1,0:T(8,128)S(1)} %broadcast_in_dim.20.near, f32[32,4]{1,0:T(8,128)S(1)} %copy.19.table), custom_call_target="tpu_custom_call" | custom-call | tf_op jit(solution)/shard_map/pallas_call | solution.py:313
  51.2 0.9 %shard_map.181 = (bf16[4,32,1024]{2,1,0:T(8,128)(2,1)S(1)}, bf16[16,2048]{1,0:T(8,128)(2,1)S(1)}) custom-call(bf16[160,1024]{1,0:T(8,128)(2,1)S(1)} %get-tuple-element.45.b0, bf16[176,1024]{1,0:T(8,128)(2,1)S(1)} %collective-permute-done.6.src.low, bf16[192,1024]{1,0:T(8,128)(2,1)S(1)} %collective-permute-done.7.src.high, ...), custom_call_target="tpu_custom_call" | custom-call | tf_op jit(solution)/shard_map/pallas_call | solution.py:313
  52.1 2.7 %collective-permute-start.11 = (bf16[4,32,1024]{2,1,0:T(8,128)(2,1)S(1)}, bf16[4,32,1024]{2,1,0:T(8,128)(2,1)S(1)}, u32[]{:S(2)}, u32[]{:S(2)}) collective-permute-start(bf16[4,32,1024]{2,1,0:T(8,128)(2,1)S(1)} %get-tuple-element.53.mine), channel_id=1, source_target_pairs={{0,4},{4,0},{1,5},{5,1},{2,6},{6,2},{3,7},{7,3},{8,12},{12,8},{9,1... | collective-permute-start | bytes 786440 | tf_op jit(solution)/shard_map/ppermute | solution.py:326
  54.8 5.9 %shard_map.180 = (bf16[4,528,256]{2,1,0:T(8,128)(2,1)S(1)}, bf16[4,48,256]{2,1,0:T(8,128)(2,1)S(1)}, bf16[4,48,256]{2,1,0:T(8,128)(2,1)S(1)}) custom-call(s32[1]{0:T(128)S(6)} %copy.20.lens, bf16[160,1024]{1,0:T(8,128)(2,1)S(1)} %get-tuple-element.45.b0, bf16[176,1024]{1,0:T(8,128)(2,1)S(1)} %collective-permute-done.6.src.low, ...), custom_call_target="tpu_custom_call" | custom-call | flops 6000000000 | tf_op jit(solution)/shard_map/pallas_call | solution.py:313
  60.9 0.7 shard_map.182
  62.3 2.6 %shard_map.183 = (bf16[80,640]{1,0:T(8,128)(2,1)S(1)}, bf16[80,640]{1,0:T(8,128)(2,1)S(1)}, bf16[80,640]{1,0:T(8,128)(2,1)S(1)}, f32[80,640]{1,0:T(8,128)S(1)}, ...) custom-call(bf16[4,48,256]{2,1,0:T(8,128)(2,1)S(1)} %get-tuple-element.48.keep_r, ...), custom_call_target="tpu_custom_call" | custom-call | flops 1000000000 | tf_op jit(solution)/shard_map/pallas_call | solution.py:313
  64.9 0.6 collective-permute-start.12
  65.9 1.3 %collective-permute-start.16 = (bf16[4,64,256]{2,1,0:T(8,128)(2,1)S(1)}, bf16[4,64,256]{2,1,0:T(8,128)(2,1)S(1)}, u32[]{:S(2)}, u32[]{:S(2)}) collective-permute-start(bf16[4,64,256]{2,1,0:T(8,128)(2,1)S(1)} %get-tuple-element.64), channel_id=1, source_target_pairs={{0,64},{64,0},{1,65},{65,1},{2,66},{66,2},{3,67},{67,3},{4,68},{68... | collective-permute-start | bytes 393224 | tf_op jit(solution)/shard_map/ppermute | solution.py:326
  67.7 2.5 %collective-permute-start.13 = (bf16[80,640]{1,0:T(8,128)(2,1)S(1)}, bf16[80,640]{1,0:T(8,128)(2,1)S(1)}, u32[]{:S(2)}, u32[]{:S(2)}) collective-permute-start(bf16[80,640]{1,0:T(8,128)(2,1)S(1)} %get-tuple-element.57), channel_id=1, source_target_pairs={{0,2},{1,3},{2,0},{3,1},{4,6},{5,7},{6,4},{7,5},{8,10},{9,11},{10,... | collective-permute-start | bytes 307208 | tf_op jit(solution)/shard_map/ppermute | solution.py:326
  70.6 0.7 collective-permute-start.14
  71.3 2.3 %collective-permute-done.13.r2 = bf16[80,640]{1,0:T(8,128)(2,1)S(1)} collective-permute-done((bf16[80,640]{1,0:T(8,128)(2,1)S(1)}, bf16[80,640]{1,0:T(8,128)(2,1)S(1)}, u32[]{:S(2)}, u32[]{:S(2)}) %collective-permute-start.13) | collective-permute-done | bytes 102432 | tf_op jit(solution)/shard_map/ppermute | solution.py:326
  73.7 1.4 %collective-permute-done.14.r3 = bf16[80,640]{1,0:T(8,128)(2,1)S(1)} collective-permute-done((bf16[80,640]{1,0:T(8,128)(2,1)S(1)}, bf16[80,640]{1,0:T(8,128)(2,1)S(1)}, u32[]{:S(2)}, u32[]{:S(2)}) %collective-permute-start.14) | collective-permute-done | bytes 102432 | tf_op jit(solution)/shard_map/ppermute | solution.py:326
  75.1 1.4 %shard_map.184 = (bf16[512,512]{1,0:T(8,128)(2,1)}, bf16[512,512]{1,0:T(8,128)(2,1)}) custom-call(s32[1]{0:T(128)S(6)} %copy.20.lens, f32[80,640]{1,0:T(8,128)S(1)} %get-tuple-element.55.keep, bf16[80,640]{1,0:T(8,128)(2,1)S(1)} %collective-permute-done.12.r1, bf16[80,640]{1,0:T(8,128)(2,1)S(1)} %collective-permute-done.13.r2, ...), custom_call_target="tpu_custom_call" | custom-call | tf_op jit(solution)/shard_map/pallas_call | solution.py:313
  76.5 0.8 %shard_map.185 = (f32[64,512]{1,0:T(8,128)}, f32[64,512]{1,0:T(8,128)}, f32[64,512]{1,0:T(8,128)}, f32[64,512]{1,0:T(8,128)}) custom-call(f32[4,64,256]{2,1,0:T(8,128)S(1)} %get-tuple-element.54.after.dw, bf16[4,64,256]{2,1,0:T(8,128)(2,1)S(1)} %collective-permute-done.15.from_core, bf16[4,64,256]{2,1,0:T(8,128)(2,1)S(1)} %collective-permute-done.16.from_dp, ...), custom_call_target="tpu_custom_call" | custom-call | flops 6000000000 | tf_op jit(solution)/shard_map/pallas_call | solution.py:313
  (54 shorter events, 4.2 us)
Async XLA Ops:
  3.2 7.1 %collective-permute-start = (f32[8,512]{1,0:T(8,128)S(1)}, f32[8,512]{1,0:T(8,128)S(1)}, u32[]{:S(2)}, u32[]{:S(2)}) collective-permute-start(f32[8,512]{1,0:T(8,128)S(1)} %get-tuple-element.40), channel_id=1, source_target_pairs={{0,4},{4,8},{8,12},{12,16},{16,20},{20,24},{24,28},{28,32},{32,36}... | collective-permute-start | bytes 49160 | tf_op jit(solution)/shard_map/ppermute | solution.py:346
  10.3 14.7 %copy-start = (bf16[2048,512]{1,0:T(8,128)(2,1)S(1)}, bf16[2048,512]{1,0:T(8,128)(2,1)}, u32[]{:S(2)}) copy-start(bf16[2048,512]{1,0:T(8,128)(2,1)} %wq.3) | copy-start | bytes 6291460
  10.3 14.7 %copy-start.1 = (bf16[2048,512]{1,0:T(8,128)(2,1)S(1)}, bf16[2048,512]{1,0:T(8,128)(2,1)}, u32[]{:S(2)}) copy-start(bf16[2048,512]{1,0:T(8,128)(2,1)} %wk.3) | copy-start | bytes 6291460
  10.3 14.7 %copy-start.3 = (bf16[2048,512]{1,0:T(8,128)(2,1)S(1)}, bf16[2048,512]{1,0:T(8,128)(2,1)}, u32[]{:S(2)}) copy-start(bf16[2048,512]{1,0:T(8,128)(2,1)} %wv.3) | copy-start | bytes 6291460
  10.3 14.7 %copy-start.5 = (bf16[2048,512]{1,0:T(8,128)(2,1)S(1)}, bf16[2048,512]{1,0:T(8,128)(2,1)}, u32[]{:S(2)}) copy-start(bf16[2048,512]{1,0:T(8,128)(2,1)} %wo.3) | copy-start | bytes 6291460
  10.3 4.7 %collective-permute-start.1 = (bf16[64,512]{1,0:T(8,128)(2,1)S(1)}, bf16[64,512]{1,0:T(8,128)(2,1)S(1)}, u32[]{:S(2)}, u32[]{:S(2)}) collective-permute-start(bf16[64,512]{1,0:T(8,128)(2,1)S(1)} %shard_map.173.piece), channel_id=1, source_target_pairs={{0,8},{8,0},{1,9},{9,1},{2,10},{10,2},{3,11},{11,3},{4,12},{12,4},... | collective-permute-start | bytes 196616 | tf_op jit(solution)/shard_map/ppermute | solution.py:326
  15.0 6.2 %collective-permute-start.2 = (bf16[128,512]{1,0:T(8,128)(2,1)S(1)}, bf16[128,512]{1,0:T(8,128)(2,1)S(1)}, u32[]{:S(2)}, u32[]{:S(2)}) collective-permute-start(bf16[128,512]{1,0:T(8,128)(2,1)S(1)} %shard_map.174.p0), channel_id=1, source_target_pairs={{0,1},{1,2},{2,3},{3,0},{4,5},{5,6},{6,7},{7,4},{8,9},{9,10},{10,1... | collective-permute-start | bytes 393224 | tf_op jit(solution)/shard_map/ppermute | solution.py:326
  16.7 7.5 %collective-permute-start.3 = (bf16[128,512]{1,0:T(8,128)(2,1)S(1)}, bf16[128,512]{1,0:T(8,128)(2,1)S(1)}, u32[]{:S(2)}, u32[]{:S(2)}) collective-permute-start(bf16[128,512]{1,0:T(8,128)(2,1)S(1)} %shard_map.174.p0), channel_id=1, source_target_pairs={{0,2},{1,3},{2,0},{3,1},{4,6},{5,7},{6,4},{7,5},{8,10},{9,11},{10,... | collective-permute-start | bytes 393224 | tf_op jit(solution)/shard_map/ppermute | solution.py:326
  20.0 4.9 %collective-permute-start.4 = (bf16[128,512]{1,0:T(8,128)(2,1)S(1)}, bf16[128,512]{1,0:T(8,128)(2,1)S(1)}, u32[]{:S(2)}, u32[]{:S(2)}) collective-permute-start(bf16[128,512]{1,0:T(8,128)(2,1)S(1)} %shard_map.174.p0), channel_id=1, source_target_pairs={{0,3},{1,0},{2,1},{3,2},{4,7},{5,4},{6,5},{7,6},{8,11},{9,8},{10,9... | collective-permute-start | bytes 393224 | tf_op jit(solution)/shard_map/ppermute | solution.py:326
  25.0 23.6 %copy-start.13 = (s32[512]{0:T(512)S(1)}, s32[512]{0:T(512)}, u32[]{:S(2)}) copy-start(s32[512]{0:T(512)} %param.23) | copy-start | bytes 6148
  25.0 23.9 %copy-start.12 = (f32[32,4]{0,1:T(4,128)S(1)}, f32[32,4]{0,1:T(4,128)}, u32[]{:S(2)}) copy-start(f32[32,4]{0,1:T(4,128)} %param.22) | copy-start | bytes 1540
  26.6 18.6 %copy-start.7 = (bf16[32,2048]{1,0:T(8,128)(2,1)}, bf16[32,2048]{1,0:T(8,128)(2,1)S(1)}, u32[]{:S(2)}) copy-start(bf16[32,2048]{1,0:T(8,128)(2,1)S(1)} %get-tuple-element.50.crow) | copy-start | bytes 393220
  26.6 3.5 %collective-permute-start.5 = (bf16[80,1024]{1,0:T(8,128)(2,1)S(1)}, bf16[80,1024]{1,0:T(8,128)(2,1)S(1)}, u32[]{:S(2)}, u32[]{:S(2)}) collective-permute-start(bf16[80,1024]{1,0:T(8,128)(2,1)S(1)} %get-tuple-element.43), channel_id=1, source_target_pairs={{0,4},{4,0},{1,5},{5,1},{2,6},{6,2},{3,7},{7,3},{8,12},{12,8},{9,1... | collective-permute-start | bytes 491528 | tf_op jit(solution)/shard_map/ppermute | solution.py:326
  30.2 15.0 %collective-permute-start.7 = (bf16[192,1024]{1,0:T(8,128)(2,1)S(1)}, bf16[192,1024]{1,0:T(8,128)(2,1)S(1)}, u32[]{:S(2)}, u32[]{:S(2)}) collective-permute-start(bf16[192,1024]{1,0:T(8,128)(2,1)S(1)} %get-tuple-element.47), channel_id=1, source_target_pairs={{0,48},{16,0},{32,16},{48,32},{1,49},{17,1},{33,17},{49,33},{2,50}... | collective-permute-start | bytes 1179656 | tf_op jit(solution)/shard_map/ppermute | solution.py:326
  34.0 10.5 %collective-permute-start.6 = (bf16[176,1024]{1,0:T(8,128)(2,1)S(1)}, bf16[176,1024]{1,0:T(8,128)(2,1)S(1)}, u32[]{:S(2)}, u32[]{:S(2)}) collective-permute-start(bf16[176,1024]{1,0:T(8,128)(2,1)S(1)} %get-tuple-element.46), channel_id=1, source_target_pairs={{0,16},{16,32},{32,48},{48,0},{1,17},{17,33},{33,49},{49,1},{2,18}... | collective-permute-start | bytes 1081352 | tf_op jit(solution)/shard_map/ppermute | solution.py:326
  45.2 5.6 %collective-permute-start.8 = (bf16[80,1024]{1,0:T(8,128)(2,1)}, bf16[80,1024]{1,0:T(8,128)(2,1)S(1)}, u32[]{:S(2)}, u32[]{:S(2)}) collective-permute-start(bf16[80,1024]{1,0:T(8,128)(2,1)} %shard_map.177), channel_id=1, source_target_pairs={{0,16},{16,32},{32,48},{48,0},{1,17},{17,33},{33,49},{49,1},{2,18}... | collective-permute-start | bytes 491528 | tf_op jit(solution)/shard_map/ppermute | solution.py:326
  45.9 5.3 %collective-permute-start.9 = (bf16[80,1024]{1,0:T(8,128)(2,1)}, bf16[80,1024]{1,0:T(8,128)(2,1)}, u32[]{:S(2)}, u32[]{:S(2)}) collective-permute-start(bf16[80,1024]{1,0:T(8,128)(2,1)} %shard_map.178), channel_id=1, source_target_pairs={{0,48},{16,0},{32,16},{48,32},{1,49},{17,1},{33,17},{49,33},{2,50}... | collective-permute-start | bytes 491528 | tf_op jit(solution)/shard_map/ppermute | solution.py:326
  52.1 8.8 %collective-permute-start.11 = (bf16[4,32,1024]{2,1,0:T(8,128)(2,1)S(1)}, bf16[4,32,1024]{2,1,0:T(8,128)(2,1)S(1)}, u32[]{:S(2)}, u32[]{:S(2)}) collective-permute-start(bf16[4,32,1024]{2,1,0:T(8,128)(2,1)S(1)} %get-tuple-element.53.mine), channel_id=1, source_target_pairs={{0,4},{4,0},{1,5},{5,1},{2,6},{6,2},{3,7},{7,3},{8,12},{12,8},{9,1... | collective-permute-start | bytes 786440 | tf_op jit(solution)/shard_map/ppermute | solution.py:326
  54.8 7.3 %copy-start.4 = (bf16[2048,512]{1,0:T(8,128)(2,1)S(1)}, bf16[2048,512]{1,0:T(8,128)(2,1)}, u32[]{:S(2)}) copy-start(bf16[2048,512]{1,0:T(8,128)(2,1)} %wv.3) | copy-start | bytes 6291460
  54.8 7.3 %copy-start.6 = (bf16[2048,512]{1,0:T(8,128)(2,1)S(1)}, bf16[2048,512]{1,0:T(8,128)(2,1)}, u32[]{:S(2)}) copy-start(bf16[2048,512]{1,0:T(8,128)(2,1)} %wo.3) | copy-start | bytes 6291460
  60.7 1.6 %copy-start.2 = (bf16[2048,512]{1,0:T(8,128)(2,1)S(1)}, bf16[2048,512]{1,0:T(8,128)(2,1)}, u32[]{:S(2)}) copy-start(bf16[2048,512]{1,0:T(8,128)(2,1)} %wk.3) | copy-start | bytes 6291460
  60.7 1.6 %copy-start.8 = (bf16[32,2048]{1,0:T(8,128)(2,1)S(1)}, bf16[32,2048]{1,0:T(8,128)(2,1)}, u32[]{:S(2)}) copy-start(bf16[32,2048]{1,0:T(8,128)(2,1)} %copy-done.7) | copy-start | bytes 393220
  60.7 1.4 %collective-permute-start.10 = (bf16[4,48,256]{2,1,0:T(8,128)(2,1)S(1)}, bf16[4,48,256]{2,1,0:T(8,128)(2,1)S(1)}, u32[]{:S(2)}, u32[]{:S(2)}) collective-permute-start(bf16[4,48,256]{2,1,0:T(8,128)(2,1)S(1)} %get-tuple-element.49), channel_id=1, source_target_pairs={{0,4},{4,0},{1,5},{5,1},{2,6},{6,2},{3,7},{7,3},{8,12},{12,8},{9,1... | collective-permute-start | bytes 294920 | tf_op jit(solution)/shard_map/ppermute | solution.py:326
  62.3 12.8 %copy-start.9 = (f32[16,512]{1,0:T(8,128)S(1)}, f32[16,512]{1,0:T(8,128)}, u32[]{:S(2)}) copy-start(f32[16,512]{1,0:T(8,128)} %up_gain.1) | copy-start | bytes 98308
  62.3 12.8 %copy-start.10 = (f32[4,512]{1,0:T(4,128)S(1)}, f32[4,512]{1,0:T(4,128)}, u32[]{:S(2)}) copy-start(f32[4,512]{1,0:T(4,128)} %first.1) | copy-start | bytes 24580
  62.3 12.8 %copy-start.11 = (f32[4,512]{1,0:T(4,128)S(1)}, f32[4,512]{1,0:T(4,128)}, u32[]{:S(2)}) copy-start(f32[4,512]{1,0:T(4,128)} %second.1) | copy-start | bytes 24580
  64.9 5.7 %collective-permute-start.12 = (bf16[80,640]{1,0:T(8,128)(2,1)S(1)}, bf16[80,640]{1,0:T(8,128)(2,1)S(1)}, u32[]{:S(2)}, u32[]{:S(2)}) collective-permute-start(bf16[80,640]{1,0:T(8,128)(2,1)S(1)} %get-tuple-element.56), channel_id=1, source_target_pairs={{0,1},{1,2},{2,3},{3,0},{4,5},{5,6},{6,7},{7,4},{8,9},{9,10},{10,1... | collective-permute-start | bytes 307208 | tf_op jit(solution)/shard_map/ppermute | solution.py:326
  65.5 11.0 %collective-permute-start.15 = (bf16[4,64,256]{2,1,0:T(8,128)(2,1)S(1)}, bf16[4,64,256]{2,1,0:T(8,128)(2,1)S(1)}, u32[]{:S(2)}, u32[]{:S(2)}) collective-permute-start(bf16[4,64,256]{2,1,0:T(8,128)(2,1)S(1)} %get-tuple-element.63), channel_id=1, source_target_pairs={{0,4},{4,0},{1,5},{5,1},{2,6},{6,2},{3,7},{7,3},{8,12},{12,8},{9,1... | collective-permute-start | bytes 393224 | tf_op jit(solution)/shard_map/ppermute | solution.py:326
  65.9 10.7 %collective-permute-start.16 = (bf16[4,64,256]{2,1,0:T(8,128)(2,1)S(1)}, bf16[4,64,256]{2,1,0:T(8,128)(2,1)S(1)}, u32[]{:S(2)}, u32[]{:S(2)}) collective-permute-start(bf16[4,64,256]{2,1,0:T(8,128)(2,1)S(1)} %get-tuple-element.64), channel_id=1, source_target_pairs={{0,64},{64,0},{1,65},{65,1},{2,66},{66,2},{3,67},{67,3},{4,68},{68... | collective-permute-start | bytes 393224 | tf_op jit(solution)/shard_map/ppermute | solution.py:326
  67.2 9.4 %collective-permute-start.17 = (bf16[4,64,256]{2,1,0:T(8,128)(2,1)S(1)}, bf16[4,64,256]{2,1,0:T(8,128)(2,1)S(1)}, u32[]{:S(2)}, u32[]{:S(2)}) collective-permute-start(bf16[4,64,256]{2,1,0:T(8,128)(2,1)S(1)} %get-tuple-element.65), channel_id=1, source_target_pairs={{0,68},{4,64},{64,4},{68,0},{1,69},{5,65},{65,5},{69,1},{2,70},{6,... | collective-permute-start | bytes 393224 | tf_op jit(solution)/shard_map/ppermute | solution.py:414
  67.7 6.0 %collective-permute-start.13 = (bf16[80,640]{1,0:T(8,128)(2,1)S(1)}, bf16[80,640]{1,0:T(8,128)(2,1)S(1)}, u32[]{:S(2)}, u32[]{:S(2)}) collective-permute-start(bf16[80,640]{1,0:T(8,128)(2,1)S(1)} %get-tuple-element.57), channel_id=1, source_target_pairs={{0,2},{1,3},{2,0},{3,1},{4,6},{5,7},{6,4},{7,5},{8,10},{9,11},{10,... | collective-permute-start | bytes 307208 | tf_op jit(solution)/shard_map/ppermute | solution.py:326
  70.6 4.4 %collective-permute-start.14 = (bf16[80,640]{1,0:T(8,128)(2,1)S(1)}, bf16[80,640]{1,0:T(8,128)(2,1)S(1)}, u32[]{:S(2)}, u32[]{:S(2)}) collective-permute-start(bf16[80,640]{1,0:T(8,128)(2,1)S(1)} %get-tuple-element.58), channel_id=1, source_target_pairs={{0,3},{1,0},{2,1},{3,2},{4,7},{5,4},{6,5},{7,6},{8,11},{9,8},{10,9... | collective-permute-start | bytes 307208 | tf_op jit(solution)/shard_map/ppermute | solution.py:326

commit v6 on v5

--- a/solution.py
+++ b/solution.py
@@ -133,36 +133,33 @@
                 blocks[s, :, at + 256 : at + 384] = gco[rows, cols]
 
 
-def pack_kernel(keep, swapped, blocks, b0, up, down):
+def pack_kernel(keep, swapped, blocks, b0, up_far, up_near, down_far, down_near):
     core = Place().core
     for i in range(2):
         for src, c in ((keep, core), (swapped, 1 - core)):
-            row = i * 64 + c * CL
             new = src[i * CL : i * CL + CL]
-            b0[pl.ds(pl.multiple_of(row, CL), CL)] = new
-            up[pl.ds(pl.multiple_of((96 if i == 0 else -32) + row, CL), CL)] = new
-            down[pl.ds(pl.multiple_of(32 + row, CL), CL)] = new
+            row = pl.multiple_of(c * CL, CL)
+            b0[pl.ds(pl.multiple_of(i * 64 + row, CL), CL)] = new
+            up, down, a, b = ((up_far, down_near, 0, 32), (up_near, down_far, 32, 0))[i]
+            up[pl.ds(pl.multiple_of(a + row, CL), CL)] = new
+            down[pl.ds(pl.multiple_of(b + row, CL), CL)] = new
     b0[128:160] = blocks[0]
-    up[0:32] = blocks[1]
-    down[0:32] = blocks[3]
-    up[160:176] = blocks[2, 0:16]
-    down[160:176] = blocks[2, 16:32]
-    down[176:192] = swapped[64:80]
-
-
-def onward_kernel(src, out):
-    out[...] = src[96:176]
-
-
-def gather_kernel(b0, low, high, far_low, far_high, swapped, mine, nxt):
+    up_near[0:32] = blocks[1]
+    down_near[0:32] = blocks[3]
+    up_far[64:80] = blocks[2, 0:16]
+    down_far[64:80] = blocks[2, 16:32]
+    down_near[96:112] = swapped[64:80]
+
+
+def gather_kernel(b0, low_near, high_near, far_low, far_high, swapped, mine, nxt):
     mine[0] = b0[128:160]
-    mine[1] = low[0:32]
+    mine[1] = low_near[0:32]
     mine[2, 0:16] = far_low[64:80]
     mine[2, 16:32] = far_high[64:80]
-    mine[3] = high[0:32]
+    mine[3] = high_near[0:32]
     at = Place()
     wraps = jnp.logical_and(at.core == 1, at.y == 1)
-    tops = jnp.where(wraps, high[176:192].astype(F32), swapped[64:80].astype(F32))
+    tops = jnp.where(wraps, high_near[96:112].astype(F32), swapped[64:80].astype(F32))
     upper = jnp.where(at.core == 0, at.y, 1 - at.y) == 1
     for j in range(2):
         row = jnp.where(upper, tops[2 + j : 3 + j], tops[j : j + 1])
@@ -170,55 +167,61 @@
 
 
 def attend_kernel(
-    lens, b0, low, high, far_low, far_high, strip, res, keep, send, q, k, v, ga, acck, accv
+    lens, b0, low_far, low_near, high_far, high_near, far_low, far_high, strip,
+    res, keep, send, q, k, v, ga, acck, accv,
 ):
     at = Place()
     ctx, core, x, doc_len = at.ctx, at.core, at.x, lens[0]
     for src, first, n, s, row in (
         (b0, 0, 128, 0, 0),
-        (low, 96, 64, 1, 0),
-        (low, 32, 64, 1, 64),
+        (low_far, 0, 64, 1, 0),
+        (low_near, 32, 64, 1, 64),
         (far_low, 0, 64, 2, 0),
         (far_high, 0, 64, 2, 64),
-        (high, 32, 128, 3, 0),
+        (high_near, 32, 64, 3, 0),
+        (high_far, 0, 64, 3, 64),
     ):
         rows = pl.ds(pl.multiple_of(lax.rem(x + 4 - s, 4) * 128 + row, 64), n)
         for i, dst in enumerate((q, k, v, ga)):
             dst[rows] = src[first : first + n, i * HW : i * HW + HW]
     key_pos = lax.broadcasted_iota(jnp.int32, (1, LC), 1)
     key_mask = jnp.where(16 * key_pos < doc_len, 0.0, NEG)
-    for h in range(NH):
-        cols = slice(h * HD, h * HD + HD)
-        for b in (3, 2, 1, 0):
-            rows = slice(b * 128, b * 128 + 128)
-            n = b * 128 + 128
-            qb, gb, kb, vb = q[rows, cols], ga[rows, cols], k[0:n, cols], v[0:n, cols]
-            s = dg(qb, kb, 1, 1) * SCALE + strip[h, :, LC - n :] + key_mask[:, :n]
-            e = jnp.exp(s - jnp.max(s, axis=1, keepdims=True))
-            p = e * (1.0 / jnp.sum(e, axis=1, keepdims=True))
-            pb = p.astype(BF16)
-            ab = jnp.dot(pb, vb, preferred_element_type=F32).astype(BF16)
-            res[3, rows, cols] = ab
-            dot = jnp.sum(gb.astype(F32) * ab.astype(F32), axis=1, keepdims=True)
-            sg = (p * (dg(gb, vb, 1, 1) - dot)).astype(BF16)
-            res[0, rows, cols] = (jnp.dot(sg, kb, preferred_element_type=F32) * SCALE).astype(BF16)
-            tk = dg(sg, qb, 0, 0)
-            tv = dg(pb, gb, 0, 0)
+    heads = [(h, slice(h * HD, h * HD + HD)) for h in range(NH)]
+    for b in (3, 2, 1, 0):
+        rows = slice(b * 128, b * 128 + 128)
+        n = b * 128 + 128
+        qb, gb = [[r[rows, c] for _, c in heads] for r in (q, ga)]
+        kb, vb = [[r[0:n, c] for _, c in heads] for r in (k, v)]
+        s = [dg(qb[h], kb[h], 1, 1) for h, _ in heads]
+        dp = [dg(gb[h], vb[h], 1, 1) for h, _ in heads]
+        s = [s[h] * SCALE + strip[h, :, LC - n :] + key_mask[:, :n] for h, _ in heads]
+        e = [jnp.exp(a - jnp.max(a, axis=1, keepdims=True)) for a in s]
+        p = [a * (1.0 / jnp.sum(a, axis=1, keepdims=True)) for a in e]
+        dot = [jnp.sum(p[h] * dp[h], axis=1, keepdims=True) for h, _ in heads]
+        sg = [(p[h] * (dp[h] - dot[h])).astype(BF16) for h, _ in heads]
+        pb = [a.astype(BF16) for a in p]
+        for h, c in heads:
+            tk = dg(sg[h], qb[h], 0, 0)
+            tv = dg(pb[h], gb[h], 0, 0)
             if b == 3:
                 acck[h] = tk
                 accv[h] = tv
             else:
                 acck[h, 0:n] += tk
                 accv[h, 0:n] += tv
-        res[1, 0:LC, cols] = (acck[h] * SCALE).astype(BF16)
-        res[2, 0:LC, cols] = accv[h].astype(BF16)
+            gq = jnp.dot(sg[h], kb[h], preferred_element_type=F32) * SCALE
+            res[0, rows, c] = gq.astype(BF16)
+            res[3, rows, c] = jnp.dot(pb[h], vb[h], preferred_element_type=F32).astype(BF16)
+    for h, c in heads:
+        res[1, 0:LC, c] = (acck[h] * SCALE).astype(BF16)
+        res[2, 0:LC, c] = accv[h].astype(BF16)
     res[:, LC : LC + 16] = jnp.zeros((4, 16, HW), BF16)
     peer = ctx + 1 - 2 * core
     keep[...] = res[:, pl.ds(pl.multiple_of(ctx * CL, CL), ROWS)]
     send[...] = res[:, pl.ds(pl.multiple_of(peer * CL, CL), ROWS)]
 
 
-def weights_kernel(res, mine, other, keep, to_core, to_dp, to_both, nb, gb, tile):
+def weights_kernel(res, mine, other, keep, send, nb, gb):
     at = Place()
     core, x, dp = at.core, at.x, at.dp
     for s in range(4):
@@ -230,11 +233,17 @@
                 gb[rows] = src[s, :, i * 512 + 256 : i * 512 + 512]
     for w in range(4):
         src = gb if w == 3 else nb
-        for d, a, b in ((dp, keep, to_core), (1 - dp, to_dp, to_both)):
+        for d, out in ((dp, keep), (1 - dp, send)):
             cols = pl.ds(pl.multiple_of(d * 128, 128), 128)
-            tile[...] = dg(src[:, cols], res[w, 0:LC], 0, 0)
-            a[w] = tile[pl.ds(pl.multiple_of(core * 64, 64), 64)].astype(a.dtype)
-            b[w] = tile[pl.ds(pl.multiple_of(64 - core * 64, 64), 64)].astype(BF16)
+            out[w] = dg(src[:, cols], res[w, 0:LC], 0, 0).astype(out.dtype)
+
+
+def sum_kernel(keep, got, r1, r2, r3, own, send):
+    core = Place().core
+    for w in range(4):
+        for c, out in ((core, own), (1 - core, send)):
+            rows = pl.ds(pl.multiple_of(c * 64, 64), 64)
+            out[w] = (keep[w, rows] + got[w, rows].astype(F32)).astype(out.dtype)
 
 
 def partial_kernel(
@@ -272,12 +281,11 @@
         msg[CL : CL + ROWS, WL : WL + 128] = packed
 
 
-def total_kernel(dw, from_core, from_dp, from_both, o0, o1, o2, o3):
+def total_kernel(own, other, o0, o1, o2, o3):
     core = Place().core
     for w, o in enumerate((o0, o1, o2, o3)):
-        o[:, pl.ds(pl.multiple_of(core * HW, HW), HW)] = dw[w] + from_dp[w].astype(F32)
-        there = from_core[w].astype(F32) + from_both[w].astype(F32)
-        o[:, pl.ds(pl.multiple_of((1 - core) * HW, HW), HW)] = there
+        o[:, pl.ds(pl.multiple_of(core * HW, HW), HW)] = own[w]
+        o[:, pl.ds(pl.multiple_of((1 - core) * HW, HW), HW)] = other[w].astype(F32)
 
 
 def after_kernel(
@@ -377,41 +385,39 @@
         flops=10**9,
     )
     swapped = shifted(send, "core", 1)
-    b0, up, down = call(
+    b0, up_far, up_near, down_far, down_near = call(
         pack_kernel,
-        [((160, 4 * HW), BF16), ((176, 4 * HW), BF16), ((192, 4 * HW), BF16)],
+        [((n, 4 * HW), BF16) for n in (160, 80, 96, 80, 112)],
         (keep, swapped, blocks),
         smem=(),
     )
-    low, high = shifted(up, "x", 1), shifted(down, "x", -1)
-    far = [((80, 4 * HW), BF16)]
-    far_low = shifted(call(onward_kernel, far, (low,), smem=())[0], "x", 1)
-    far_high = shifted(call(onward_kernel, far, (high,), smem=())[0], "x", -1)
+    low_far, high_far = shifted(up_far, "x", 1), shifted(down_far, "x", -1)
+    low_near, high_near = shifted(up_near, "x", 1), shifted(down_near, "x", -1)
+    far_low, far_high = shifted(low_far, "x", 1), shifted(high_far, "x", -1)
     mine, nxt = call(
         gather_kernel,
         [((4, CL, 4 * HW), BF16), ((16, D), BF16)],
-        (b0, low, high, far_low, far_high, swapped),
+        (b0, low_near, high_near, far_low, far_high, swapped),
         smem=(),
     )
     other_rows = shifted(mine, "core", 1)
     res, keep_r, send_r = call(
         attend_kernel,
         [((4, LC + 16, HW), BF16), ((4, ROWS, HW), BF16), ((4, ROWS, HW), BF16)],
-        (lengths, b0, low, high, far_low, far_high, strip),
+        (lengths, b0, low_far, low_near, high_far, high_near, far_low, far_high, strip),
         [((LC, HW), BF16)] * 4 + [((NH, LC, HD), F32)] * 2,
         flops=6 * 10**9,
     )
     got_r = shifted(send_r, "core", 1)
-    dw_keep, to_core, to_dp, to_both = call(
+    dw_keep, dw_send = call(
         weights_kernel,
-        [((4, 64, HW), F32)] + [((4, 64, HW), BF16)] * 3,
+        [((4, 128, HW), F32), ((4, 128, HW), BF16)],
         (res, mine, other_rows),
-        [((LC, 256), BF16), ((LC, 256), BF16), ((128, HW), F32)],
+        [((LC, 256), BF16), ((LC, 256), BF16)],
         smem=(),
         flops=10**9,
     )
-    from_core, from_dp = shifted(to_core, "core", 1), shifted(to_dp, "dp", 1)
-    from_both = lax.ppermute(to_both, ("dp", "core"), [(i, 3 - i) for i in range(4)])
+    dw_got = shifted(dw_send, "dp", 1)
     msg = (CL + ROWS, WL + 128)
     m1, m2, m3, own, cz, inv = call(
         partial_kernel,
@@ -422,10 +428,17 @@
         flops=10**9,
     )
     r1, r2, r3 = shifted(m1, "tensor", 1), shifted(m2, "tensor", 2), shifted(m3, "tensor", 3)
+    dw_own, dw_other = call(
+        sum_kernel,
+        [((4, 64, HW), F32), ((4, 64, HW), BF16)],
+        (dw_keep, dw_got, r1, r2, r3),
+        smem=(),
+    )
+    dw_other = shifted(dw_other, "core", 1)
     dw = call(
         total_kernel,
         [((64, WL), F32)] * 4,
-        (dw_keep, from_core, from_dp, from_both),
+        (dw_own, dw_other),
         smem=(),
         flops=6 * 10**9,
         typed=False,

time: 78.3 us -> 69.6 us (0.89)
  waiting for transfers between devices: 25.9 us -> 20.4 us
  Pallas kernels: 18.4 us -> 15 us
  starting transfers between devices: 30.8 us -> 31.9 us
    ppermute x16 -> x18, waiting for transfers between devices: 25 us -> 19.6 us  [shifted(): return lax.ppermute(x, axis, [(i, (i + steps) % n) for i in range(n)])]
    pallas_call x14 -> x13, Pallas kernels: 18.4 us -> 15 us  [call(): pl.pallas_call(kernel, out_shape=[pltpu.VMEM(s, d) if typed else jax.Shap...]
    ppermute x16 -> x18, starting transfers between devices: 24.1 us -> 25.7 us  [shifted(): return lax.ppermute(x, axis, [(i, (i + steps) % n) for i in range(n)])]
  transfers between devices with their start and end apart: 18 -> 19, of which waited for: 13 -> 13; matrix products, arithmetic and copies ran while one was open for 1% -> 1% of each run, Pallas kernels for 13% -> 14%
where the time goes in v6:
time: 69.6 us; the launch traced here: 69.4 us
  starting transfers between devices  31.9 us (46%)
  waiting for transfers between devices  20.4 us (29%)
  Pallas kernels  15 us (22%)
  between operations  1.47 us (2%)
    ppermute x18, starting transfers between devices, shifted(): return lax.ppermute(x, axis, [(i, (i + steps) % n) for i in range(n)])  25.7 us
    ppermute x18, waiting for transfers between devices, shifted(): return lax.ppermute(x, axis, [(i, (i + steps) % n) for i in range(n)])  19.6 us
    pallas_call x13, Pallas kernels, call(): pl.pallas_call(kernel, out_shape=[pltpu.VMEM(s, d) if typed else jax.Shap...  15 us
    ppermute x1, starting transfers between devices, local(): rim = lax.ppermute(last, line, [(i, i + 1) for i in range(15)])  6.21 us
  transfers between devices with their start and end apart: 19, of which 13 were waited for; matrix products, arithmetic and copies ran while one was open for 1% of the time, Pallas kernels for 14%

profile of v6, /device:TPU:1, one launch (start us, length us, event | category | flops | bytes accessed | tf_op | source)
XLA Modules:
  0.0 69.4 jit_solution(14030561910384745739)
XLA Ops:
  1.3 1.9 %shard_map.172 = (f32[32,512]{1,0:T(8,128)S(1)}, f32[8,512]{1,0:T(8,128)S(1)}, bf16[32,512]{1,0:T(8,128)(2,1)S(1)}, f32[1,2048]{1,0:T(1,128)S(1)}) custom-call(s32[1]{0:T(128)S(6)} %copy.20.lens, bf16[512,512]{1,0:T(8,128)(2,1)} %bitcast.7, bf16[512,512]{1,0:T(8,128)(2,1)} %bitcast.8, f32[4,512]{1,0:T(4,128)} %first.1, f32[4,512]{1,0:T(4,128)} %second.1, ...), custom_call_target="tpu_custom_call" | custom-call | tf_op jit(solution)/shard_map/pallas_call | solution.py:321
  3.2 6.2 %collective-permute-start = (f32[8,512]{1,0:T(8,128)S(1)}, f32[8,512]{1,0:T(8,128)S(1)}, u32[]{:S(2)}, u32[]{:S(2)}) collective-permute-start(f32[8,512]{1,0:T(8,128)S(1)} %get-tuple-element.42), channel_id=1, source_target_pairs={{0,4},{4,8},{8,12},{12,16},{16,20},{20,24},{24,28},{28,32},{32,36}... | collective-permute-start | bytes 49160 | tf_op jit(solution)/shard_map/ppermute | solution.py:354
  9.4 0.8 %collective-permute-done.rim = f32[8,512]{1,0:T(8,128)S(1)} collective-permute-done((f32[8,512]{1,0:T(8,128)S(1)}, f32[8,512]{1,0:T(8,128)S(1)}, u32[]{:S(2)}, u32[]{:S(2)}) %collective-permute-start) | collective-permute-done | bytes 16416 | tf_op jit(solution)/shard_map/ppermute | solution.py:354
  10.3 1.1 %collective-permute-start.1 = (bf16[64,512]{1,0:T(8,128)(2,1)S(1)}, bf16[64,512]{1,0:T(8,128)(2,1)S(1)}, u32[]{:S(2)}, u32[]{:S(2)}) collective-permute-start(bf16[64,512]{1,0:T(8,128)(2,1)S(1)} %shard_map.173.piece), channel_id=1, source_target_pairs={{0,8},{8,0},{1,9},{9,1},{2,10},{10,2},{3,11},{11,3},{4,12},{12,4},... | collective-permute-start | bytes 196616 | tf_op jit(solution)/shard_map/ppermute | solution.py:334
  11.4 3.6 %collective-permute-done.1.across = bf16[64,512]{1,0:T(8,128)(2,1)S(1)} collective-permute-done((bf16[64,512]{1,0:T(8,128)(2,1)S(1)}, bf16[64,512]{1,0:T(8,128)(2,1)S(1)}, u32[]{:S(2)}, u32[]{:S(2)}) %collective-permute-start.1) | collective-permute-done | bytes 65568 | tf_op jit(solution)/shard_map/ppermute | solution.py:334
  15.0 1.7 %collective-permute-start.2 = (bf16[128,512]{1,0:T(8,128)(2,1)S(1)}, bf16[128,512]{1,0:T(8,128)(2,1)S(1)}, u32[]{:S(2)}, u32[]{:S(2)}) collective-permute-start(bf16[128,512]{1,0:T(8,128)(2,1)S(1)} %shard_map.174.p0), channel_id=1, source_target_pairs={{0,1},{1,2},{2,3},{3,0},{4,5},{5,6},{6,7},{7,4},{8,9},{9,10},{10,1... | collective-permute-start | bytes 393224 | tf_op jit(solution)/shard_map/ppermute | solution.py:334
  16.7 3.3 %collective-permute-start.3 = (bf16[128,512]{1,0:T(8,128)(2,1)S(1)}, bf16[128,512]{1,0:T(8,128)(2,1)S(1)}, u32[]{:S(2)}, u32[]{:S(2)}) collective-permute-start(bf16[128,512]{1,0:T(8,128)(2,1)S(1)} %shard_map.174.p0), channel_id=1, source_target_pairs={{0,2},{1,3},{2,0},{3,1},{4,6},{5,7},{6,4},{7,5},{8,10},{9,11},{10,... | collective-permute-start | bytes 393224 | tf_op jit(solution)/shard_map/ppermute | solution.py:334
  20.0 0.7 %collective-permute-start.4 = (bf16[128,512]{1,0:T(8,128)(2,1)S(1)}, bf16[128,512]{1,0:T(8,128)(2,1)S(1)}, u32[]{:S(2)}, u32[]{:S(2)}) collective-permute-start(bf16[128,512]{1,0:T(8,128)(2,1)S(1)} %shard_map.174.p0), channel_id=1, source_target_pairs={{0,3},{1,0},{2,1},{3,2},{4,7},{5,4},{6,5},{7,6},{8,11},{9,8},{10,9... | collective-permute-start | bytes 393224 | tf_op jit(solution)/shard_map/ppermute | solution.py:334
  21.2 3.1 %collective-permute-done.3.r2 = bf16[128,512]{1,0:T(8,128)(2,1)S(1)} collective-permute-done((bf16[128,512]{1,0:T(8,128)(2,1)S(1)}, bf16[128,512]{1,0:T(8,128)(2,1)S(1)}, u32[]{:S(2)}, u32[]{:S(2)}) %collective-permute-start.3) | collective-permute-done | bytes 131104 | tf_op jit(solution)/shard_map/ppermute | solution.py:334
  24.3 0.7 collective-permute-done.4.r3
  25.0 1.6 %shard_map.175 = (bf16[64,1024]{1,0:T(8,128)(2,1)S(1)}, bf16[80,1024]{1,0:T(8,128)(2,1)S(1)}, bf16[4,32,1024]{2,1,0:T(8,128)(2,1)S(1)}, bf16[32,2048]{1,0:T(8,128)(2,1)S(1)}) custom-call(bf16[128,512]{1,0:T(8,128)(2,1)S(1)} %shard_map.174.p0, bf16[128,512]{1,0:T(8,128)(2,1)S(1)} %collective-permute-done.2.r1, ...), custom_call_target="tpu_custom_call" | custom-call | flops 1000000000 | tf_op jit(solution)/shard_map/pallas_call | solution.py:321
  26.6 2.5 %collective-permute-start.5 = (bf16[80,1024]{1,0:T(8,128)(2,1)S(1)}, bf16[80,1024]{1,0:T(8,128)(2,1)S(1)}, u32[]{:S(2)}, u32[]{:S(2)}) collective-permute-start(bf16[80,1024]{1,0:T(8,128)(2,1)S(1)} %get-tuple-element.45), channel_id=1, source_target_pairs={{0,4},{4,0},{1,5},{5,1},{2,6},{6,2},{3,7},{7,3},{8,12},{12,8},{9,1... | collective-permute-start | bytes 491528 | tf_op jit(solution)/shard_map/ppermute | solution.py:334
  29.1 1.0 %collective-permute-done.5.swapped = bf16[80,1024]{1,0:T(8,128)(2,1)S(1)} collective-permute-done((bf16[80,1024]{1,0:T(8,128)(2,1)S(1)}, bf16[80,1024]{1,0:T(8,128)(2,1)S(1)}, u32[]{:S(2)}, u32[]{:S(2)}) %collective-permute-start.5) | collective-permute-done | bytes 163872 | tf_op jit(solution)/shard_map/ppermute | solution.py:334
  30.1 0.8 %shard_map.176 = (bf16[160,1024]{1,0:T(8,128)(2,1)S(1)}, bf16[80,1024]{1,0:T(8,128)(2,1)S(1)}, bf16[96,1024]{1,0:T(8,128)(2,1)}, bf16[80,1024]{1,0:T(8,128)(2,1)S(1)}, bf16[112,1024]{1,0:T(8,128)(2,1)}) custom-call(bf16[64,1024]{1,0:T(8,128)(2,1)S(1)} %get-tuple-element.44.keep, bf16[80,1024]{1,0:T(8,128)(2,1)S(1)} %collective-permute-done.5.swapped, ...), custom_call_target="tpu_custom_call" | custom-call | tf_op jit(solution)/shard_map/pallas_call | solution.py:321
  31.0 2.4 %collective-permute-start.6 = (bf16[80,1024]{1,0:T(8,128)(2,1)S(1)}, bf16[80,1024]{1,0:T(8,128)(2,1)}, u32[]{:S(2)}, u32[]{:S(2)}) collective-permute-start(bf16[80,1024]{1,0:T(8,128)(2,1)S(1)} %get-tuple-element.48), channel_id=1, source_target_pairs={{0,16},{16,32},{32,48},{48,0},{1,17},{17,33},{33,49},{49,1},{2,18}... | collective-permute-start | bytes 491528 | tf_op jit(solution)/shard_map/ppermute | solution.py:334
  33.4 1.3 %collective-permute-start.8 = (bf16[80,1024]{1,0:T(8,128)(2,1)S(1)}, bf16[80,1024]{1,0:T(8,128)(2,1)}, u32[]{:S(2)}, u32[]{:S(2)}) collective-permute-start(bf16[80,1024]{1,0:T(8,128)(2,1)S(1)} %get-tuple-element.50), channel_id=1, source_target_pairs={{0,48},{16,0},{32,16},{48,32},{1,49},{17,1},{33,17},{49,33},{2,50}... | collective-permute-start | bytes 491528 | tf_op jit(solution)/shard_map/ppermute | solution.py:334
  34.7 1.5 %collective-permute-start.9 = (bf16[112,1024]{1,0:T(8,128)(2,1)}, bf16[112,1024]{1,0:T(8,128)(2,1)S(1)}, u32[]{:S(2)}, u32[]{:S(2)}) collective-permute-start(bf16[112,1024]{1,0:T(8,128)(2,1)} %get-tuple-element.51), channel_id=1, source_target_pairs={{0,48},{16,0},{32,16},{48,32},{1,49},{17,1},{33,17},{49,33},{2,50}... | collective-permute-start | bytes 688136 | tf_op jit(solution)/shard_map/ppermute | solution.py:334
  36.1 2.9 %collective-permute-done.6.low_far = bf16[80,1024]{1,0:T(8,128)(2,1)} collective-permute-done((bf16[80,1024]{1,0:T(8,128)(2,1)S(1)}, bf16[80,1024]{1,0:T(8,128)(2,1)}, u32[]{:S(2)}, u32[]{:S(2)}) %collective-permute-start.6) | collective-permute-done | bytes 163872 | tf_op jit(solution)/shard_map/ppermute | solution.py:334
  39.1 2.7 %collective-permute-start.11 = (bf16[80,1024]{1,0:T(8,128)(2,1)}, bf16[80,1024]{1,0:T(8,128)(2,1)S(1)}, u32[]{:S(2)}, u32[]{:S(2)}) collective-permute-start(bf16[80,1024]{1,0:T(8,128)(2,1)} %collective-permute-done.8.high_far), channel_id=1, source_target_pairs={{0,48},{16,0},{32,16},{48,32},{1,49},{17,1},{33,17},{49,33},{2,50}... | collective-permute-start | bytes 491528 | tf_op jit(solution)/shard_map/ppermute | solution.py:334
  42.3 1.1 %shard_map.177.strip = f32[2,128,512]{2,1,0:T(8,128)S(1)} custom-call(s32[8,640]{1,0:T(8,128)S(1)} %broadcast_in_dim.20.near, f32[32,4]{1,0:T(8,128)S(1)} %copy.19.table), custom_call_target="tpu_custom_call" | custom-call | tf_op jit(solution)/shard_map/pallas_call | solution.py:321
  43.4 3.3 %collective-permute-done.10.far_low = bf16[80,1024]{1,0:T(8,128)(2,1)S(1)} collective-permute-done((bf16[80,1024]{1,0:T(8,128)(2,1)}, bf16[80,1024]{1,0:T(8,128)(2,1)S(1)}, u32[]{:S(2)}, u32[]{:S(2)}) %collective-permute-start.10) | collective-permute-done | bytes 163872 | tf_op jit(solution)/shard_map/ppermute | solution.py:334
  47.0 1.6 %collective-permute-start.13 = (bf16[4,32,1024]{2,1,0:T(8,128)(2,1)S(1)}, bf16[4,32,1024]{2,1,0:T(8,128)(2,1)S(1)}, u32[]{:S(2)}, u32[]{:S(2)}) collective-permute-start(bf16[4,32,1024]{2,1,0:T(8,128)(2,1)S(1)} %get-tuple-element.57.mine), channel_id=1, source_target_pairs={{0,4},{4,0},{1,5},{5,1},{2,6},{6,2},{3,7},{7,3},{8,12},{12,8},{9,1... | collective-permute-start | bytes 786440 | tf_op jit(solution)/shard_map/ppermute | solution.py:334
  48.6 4.2 %shard_map.178 = (bf16[4,528,256]{2,1,0:T(8,128)(2,1)S(1)}, bf16[4,48,256]{2,1,0:T(8,128)(2,1)S(1)}, bf16[4,48,256]{2,1,0:T(8,128)(2,1)S(1)}) custom-call(s32[1]{0:T(128)S(6)} %copy.20.lens, bf16[160,1024]{1,0:T(8,128)(2,1)S(1)} %get-tuple-element.47.b0, bf16[80,1024]{1,0:T(8,128)(2,1)} %collective-permute-done.6.low_far, ...), custom_call_target="tpu_custom_call" | custom-call | flops 6000000000 | tf_op jit(solution)/shard_map/pallas_call | solution.py:321
  53.4 1.4 %collective-permute-start.17 = (bf16[4,128,256]{2,1,0:T(8,128)(2,1)S(1)}, bf16[4,128,256]{2,1,0:T(8,128)(2,1)S(1)}, u32[]{:S(2)}, u32[]{:S(2)}) collective-permute-start(bf16[4,128,256]{2,1,0:T(8,128)(2,1)S(1)} %get-tuple-element.67), channel_id=1, source_target_pairs={{0,64},{64,0},{1,65},{65,1},{2,66},{66,2},{3,67},{67,3},{4,68},{68... | collective-permute-start | bytes 786440 | tf_op jit(solution)/shard_map/ppermute | solution.py:334
  54.8 2.6 %shard_map.181 = (bf16[80,640]{1,0:T(8,128)(2,1)S(1)}, bf16[80,640]{1,0:T(8,128)(2,1)S(1)}, bf16[80,640]{1,0:T(8,128)(2,1)S(1)}, f32[80,640]{1,0:T(8,128)S(1)}, ...) custom-call(bf16[4,48,256]{2,1,0:T(8,128)(2,1)S(1)} %get-tuple-element.52.keep_r, ...), custom_call_target="tpu_custom_call" | custom-call | flops 1000000000 | tf_op jit(solution)/shard_map/pallas_call | solution.py:321
  58.1 2.5 %collective-permute-start.15 = (bf16[80,640]{1,0:T(8,128)(2,1)S(1)}, bf16[80,640]{1,0:T(8,128)(2,1)S(1)}, u32[]{:S(2)}, u32[]{:S(2)}) collective-permute-start(bf16[80,640]{1,0:T(8,128)(2,1)S(1)} %get-tuple-element.61), channel_id=1, source_target_pairs={{0,2},{1,3},{2,0},{3,1},{4,6},{5,7},{6,4},{7,5},{8,10},{9,11},{10,... | collective-permute-start | bytes 307208 | tf_op jit(solution)/shard_map/ppermute | solution.py:334
  61.2 1.0 %collective-permute-done.14.r1 = bf16[80,640]{1,0:T(8,128)(2,1)S(1)} collective-permute-done((bf16[80,640]{1,0:T(8,128)(2,1)S(1)}, bf16[80,640]{1,0:T(8,128)(2,1)S(1)}, u32[]{:S(2)}, u32[]{:S(2)}) %collective-permute-start.14) | collective-permute-done | bytes 102432 | tf_op jit(solution)/shard_map/ppermute | solution.py:334
  62.2 2.5 %collective-permute-done.15.r2 = bf16[80,640]{1,0:T(8,128)(2,1)S(1)} collective-permute-done((bf16[80,640]{1,0:T(8,128)(2,1)S(1)}, bf16[80,640]{1,0:T(8,128)(2,1)S(1)}, u32[]{:S(2)}, u32[]{:S(2)}) %collective-permute-start.15) | collective-permute-done | bytes 102432 | tf_op jit(solution)/shard_map/ppermute | solution.py:334
  64.7 0.7 collective-permute-done.16.r3
  65.4 1.7 %collective-permute-start.18 = (bf16[4,64,256]{2,1,0:T(8,128)(2,1)S(1)}, bf16[4,64,256]{2,1,0:T(8,128)(2,1)S(1)}, u32[]{:S(2)}, u32[]{:S(2)}) collective-permute-start(bf16[4,64,256]{2,1,0:T(8,128)(2,1)S(1)} %get-tuple-element.69), channel_id=1, source_target_pairs={{0,4},{4,0},{1,5},{5,1},{2,6},{6,2},{3,7},{7,3},{8,12},{12,8},{9,1... | collective-permute-start | bytes 393224 | tf_op jit(solution)/shard_map/ppermute | solution.py:334
  67.1 1.4 %shard_map.182 = (bf16[512,512]{1,0:T(8,128)(2,1)}, bf16[512,512]{1,0:T(8,128)(2,1)}) custom-call(s32[1]{0:T(128)S(6)} %copy.20.lens, f32[80,640]{1,0:T(8,128)S(1)} %get-tuple-element.59.keep, bf16[80,640]{1,0:T(8,128)(2,1)S(1)} %collective-permute-done.14.r1, bf16[80,640]{1,0:T(8,128)(2,1)S(1)} %collective-permute-done.15.r2, ...), custom_call_target="tpu_custom_call" | custom-call | tf_op jit(solution)/shard_map/pallas_call | solution.py:321
  68.6 0.8 %shard_map.184 = (f32[64,512]{1,0:T(8,128)}, f32[64,512]{1,0:T(8,128)}, f32[64,512]{1,0:T(8,128)}, f32[64,512]{1,0:T(8,128)}) custom-call(f32[4,64,256]{2,1,0:T(8,128)S(1)} %get-tuple-element.68.own, bf16[4,64,256]{2,1,0:T(8,128)(2,1)S(1)} %collective-permute-done.18.other), custom_call_target="tpu_custom_call" | custom-call | flops 6000000000 | tf_op jit(solution)/shard_map/pallas_call | solution.py:321
  (51 shorter events, 3.3 us)
Async XLA Ops:
  3.2 7.1 %collective-permute-start = (f32[8,512]{1,0:T(8,128)S(1)}, f32[8,512]{1,0:T(8,128)S(1)}, u32[]{:S(2)}, u32[]{:S(2)}) collective-permute-start(f32[8,512]{1,0:T(8,128)S(1)} %get-tuple-element.42), channel_id=1, source_target_pairs={{0,4},{4,8},{8,12},{12,16},{16,20},{20,24},{24,28},{28,32},{32,36}... | collective-permute-start | bytes 49160 | tf_op jit(solution)/shard_map/ppermute | solution.py:354
  10.3 14.7 %copy-start = (bf16[2048,512]{1,0:T(8,128)(2,1)S(1)}, bf16[2048,512]{1,0:T(8,128)(2,1)}, u32[]{:S(2)}) copy-start(bf16[2048,512]{1,0:T(8,128)(2,1)} %wq.3) | copy-start | bytes 6291460
  10.3 14.7 %copy-start.1 = (bf16[2048,512]{1,0:T(8,128)(2,1)S(1)}, bf16[2048,512]{1,0:T(8,128)(2,1)}, u32[]{:S(2)}) copy-start(bf16[2048,512]{1,0:T(8,128)(2,1)} %wk.3) | copy-start | bytes 6291460
  10.3 14.7 %copy-start.3 = (bf16[2048,512]{1,0:T(8,128)(2,1)S(1)}, bf16[2048,512]{1,0:T(8,128)(2,1)}, u32[]{:S(2)}) copy-start(bf16[2048,512]{1,0:T(8,128)(2,1)} %wv.3) | copy-start | bytes 6291460
  10.3 14.7 %copy-start.5 = (bf16[2048,512]{1,0:T(8,128)(2,1)S(1)}, bf16[2048,512]{1,0:T(8,128)(2,1)}, u32[]{:S(2)}) copy-start(bf16[2048,512]{1,0:T(8,128)(2,1)} %wo.3) | copy-start | bytes 6291460
  10.3 4.7 %collective-permute-start.1 = (bf16[64,512]{1,0:T(8,128)(2,1)S(1)}, bf16[64,512]{1,0:T(8,128)(2,1)S(1)}, u32[]{:S(2)}, u32[]{:S(2)}) collective-permute-start(bf16[64,512]{1,0:T(8,128)(2,1)S(1)} %shard_map.173.piece), channel_id=1, source_target_pairs={{0,8},{8,0},{1,9},{9,1},{2,10},{10,2},{3,11},{11,3},{4,12},{12,4},... | collective-permute-start | bytes 196616 | tf_op jit(solution)/shard_map/ppermute | solution.py:334
  15.0 6.2 %collective-permute-start.2 = (bf16[128,512]{1,0:T(8,128)(2,1)S(1)}, bf16[128,512]{1,0:T(8,128)(2,1)S(1)}, u32[]{:S(2)}, u32[]{:S(2)}) collective-permute-start(bf16[128,512]{1,0:T(8,128)(2,1)S(1)} %shard_map.174.p0), channel_id=1, source_target_pairs={{0,1},{1,2},{2,3},{3,0},{4,5},{5,6},{6,7},{7,4},{8,9},{9,10},{10,1... | collective-permute-start | bytes 393224 | tf_op jit(solution)/shard_map/ppermute | solution.py:334
  16.7 7.5 %collective-permute-start.3 = (bf16[128,512]{1,0:T(8,128)(2,1)S(1)}, bf16[128,512]{1,0:T(8,128)(2,1)S(1)}, u32[]{:S(2)}, u32[]{:S(2)}) collective-permute-start(bf16[128,512]{1,0:T(8,128)(2,1)S(1)} %shard_map.174.p0), channel_id=1, source_target_pairs={{0,2},{1,3},{2,0},{3,1},{4,6},{5,7},{6,4},{7,5},{8,10},{9,11},{10,... | collective-permute-start | bytes 393224 | tf_op jit(solution)/shard_map/ppermute | solution.py:334
  20.0 4.9 %collective-permute-start.4 = (bf16[128,512]{1,0:T(8,128)(2,1)S(1)}, bf16[128,512]{1,0:T(8,128)(2,1)S(1)}, u32[]{:S(2)}, u32[]{:S(2)}) collective-permute-start(bf16[128,512]{1,0:T(8,128)(2,1)S(1)} %shard_map.174.p0), channel_id=1, source_target_pairs={{0,3},{1,0},{2,1},{3,2},{4,7},{5,4},{6,5},{7,6},{8,11},{9,8},{10,9... | collective-permute-start | bytes 393224 | tf_op jit(solution)/shard_map/ppermute | solution.py:334
  25.0 16.8 %copy-start.11 = (s32[512]{0:T(512)S(1)}, s32[512]{0:T(512)}, u32[]{:S(2)}) copy-start(s32[512]{0:T(512)} %param.23) | copy-start | bytes 6148
  25.0 17.1 %copy-start.10 = (f32[32,4]{0,1:T(4,128)S(1)}, f32[32,4]{0,1:T(4,128)}, u32[]{:S(2)}) copy-start(f32[32,4]{0,1:T(4,128)} %param.22) | copy-start | bytes 1540
  26.6 3.5 %collective-permute-start.5 = (bf16[80,1024]{1,0:T(8,128)(2,1)S(1)}, bf16[80,1024]{1,0:T(8,128)(2,1)S(1)}, u32[]{:S(2)}, u32[]{:S(2)}) collective-permute-start(bf16[80,1024]{1,0:T(8,128)(2,1)S(1)} %get-tuple-element.45), channel_id=1, source_target_pairs={{0,4},{4,0},{1,5},{5,1},{2,6},{6,2},{3,7},{7,3},{8,12},{12,8},{9,1... | collective-permute-start | bytes 491528 | tf_op jit(solution)/shard_map/ppermute | solution.py:334
  31.0 8.1 %collective-permute-start.6 = (bf16[80,1024]{1,0:T(8,128)(2,1)S(1)}, bf16[80,1024]{1,0:T(8,128)(2,1)}, u32[]{:S(2)}, u32[]{:S(2)}) collective-permute-start(bf16[80,1024]{1,0:T(8,128)(2,1)S(1)} %get-tuple-element.48), channel_id=1, source_target_pairs={{0,16},{16,32},{32,48},{48,0},{1,17},{17,33},{33,49},{49,1},{2,18}... | collective-permute-start | bytes 491528 | tf_op jit(solution)/shard_map/ppermute | solution.py:334
  33.4 5.7 %collective-permute-start.8 = (bf16[80,1024]{1,0:T(8,128)(2,1)S(1)}, bf16[80,1024]{1,0:T(8,128)(2,1)}, u32[]{:S(2)}, u32[]{:S(2)}) collective-permute-start(bf16[80,1024]{1,0:T(8,128)(2,1)S(1)} %get-tuple-element.50), channel_id=1, source_target_pairs={{0,48},{16,0},{32,16},{48,32},{1,49},{17,1},{33,17},{49,33},{2,50}... | collective-permute-start | bytes 491528 | tf_op jit(solution)/shard_map/ppermute | solution.py:334
  34.7 8.7 %collective-permute-start.9 = (bf16[112,1024]{1,0:T(8,128)(2,1)}, bf16[112,1024]{1,0:T(8,128)(2,1)S(1)}, u32[]{:S(2)}, u32[]{:S(2)}) collective-permute-start(bf16[112,1024]{1,0:T(8,128)(2,1)} %get-tuple-element.51), channel_id=1, source_target_pairs={{0,48},{16,0},{32,16},{48,32},{1,49},{17,1},{33,17},{49,33},{2,50}... | collective-permute-start | bytes 688136 | tf_op jit(solution)/shard_map/ppermute | solution.py:334
  36.1 7.2 %collective-permute-start.7 = (bf16[96,1024]{1,0:T(8,128)(2,1)}, bf16[96,1024]{1,0:T(8,128)(2,1)S(1)}, u32[]{:S(2)}, u32[]{:S(2)}) collective-permute-start(bf16[96,1024]{1,0:T(8,128)(2,1)} %get-tuple-element.49), channel_id=1, source_target_pairs={{0,16},{16,32},{32,48},{48,0},{1,17},{17,33},{33,49},{49,1},{2,18}... | collective-permute-start | bytes 589832 | tf_op jit(solution)/shard_map/ppermute | solution.py:334
  39.1 7.7 %collective-permute-start.10 = (bf16[80,1024]{1,0:T(8,128)(2,1)}, bf16[80,1024]{1,0:T(8,128)(2,1)S(1)}, u32[]{:S(2)}, u32[]{:S(2)}) collective-permute-start(bf16[80,1024]{1,0:T(8,128)(2,1)} %collective-permute-done.6.low_far), channel_id=1, source_target_pairs={{0,16},{16,32},{32,48},{48,0},{1,17},{17,33},{33,49},{49,1},{2,18}... | collective-permute-start | bytes 491528 | tf_op jit(solution)/shard_map/ppermute | solution.py:334
  39.1 7.9 %collective-permute-start.11 = (bf16[80,1024]{1,0:T(8,128)(2,1)}, bf16[80,1024]{1,0:T(8,128)(2,1)S(1)}, u32[]{:S(2)}, u32[]{:S(2)}) collective-permute-start(bf16[80,1024]{1,0:T(8,128)(2,1)} %collective-permute-done.8.high_far), channel_id=1, source_target_pairs={{0,48},{16,0},{32,16},{48,32},{1,49},{17,1},{33,17},{49,33},{2,50}... | collective-permute-start | bytes 491528 | tf_op jit(solution)/shard_map/ppermute | solution.py:334
  47.0 5.9 %collective-permute-start.13 = (bf16[4,32,1024]{2,1,0:T(8,128)(2,1)S(1)}, bf16[4,32,1024]{2,1,0:T(8,128)(2,1)S(1)}, u32[]{:S(2)}, u32[]{:S(2)}) collective-permute-start(bf16[4,32,1024]{2,1,0:T(8,128)(2,1)S(1)} %get-tuple-element.57.mine), channel_id=1, source_target_pairs={{0,4},{4,0},{1,5},{5,1},{2,6},{6,2},{3,7},{7,3},{8,12},{12,8},{9,1... | collective-permute-start | bytes 786440 | tf_op jit(solution)/shard_map/ppermute | solution.py:334
  48.6 6.2 %copy-start.4 = (bf16[2048,512]{1,0:T(8,128)(2,1)S(1)}, bf16[2048,512]{1,0:T(8,128)(2,1)}, u32[]{:S(2)}) copy-start(bf16[2048,512]{1,0:T(8,128)(2,1)} %wv.3) | copy-start | bytes 6291460
  48.6 6.2 %copy-start.6 = (bf16[2048,512]{1,0:T(8,128)(2,1)S(1)}, bf16[2048,512]{1,0:T(8,128)(2,1)}, u32[]{:S(2)}) copy-start(bf16[2048,512]{1,0:T(8,128)(2,1)} %wo.3) | copy-start | bytes 6291460
  52.7 2.1 %copy-start.2 = (bf16[2048,512]{1,0:T(8,128)(2,1)S(1)}, bf16[2048,512]{1,0:T(8,128)(2,1)}, u32[]{:S(2)}) copy-start(bf16[2048,512]{1,0:T(8,128)(2,1)} %wk.3) | copy-start | bytes 6291460
  52.8 2.0 %collective-permute-start.12 = (bf16[4,48,256]{2,1,0:T(8,128)(2,1)S(1)}, bf16[4,48,256]{2,1,0:T(8,128)(2,1)S(1)}, u32[]{:S(2)}, u32[]{:S(2)}) collective-permute-start(bf16[4,48,256]{2,1,0:T(8,128)(2,1)S(1)} %get-tuple-element.53), channel_id=1, source_target_pairs={{0,4},{4,0},{1,5},{5,1},{2,6},{6,2},{3,7},{7,3},{8,12},{12,8},{9,1... | collective-permute-start | bytes 294920 | tf_op jit(solution)/shard_map/ppermute | solution.py:334
  53.4 12.0 %collective-permute-start.17 = (bf16[4,128,256]{2,1,0:T(8,128)(2,1)S(1)}, bf16[4,128,256]{2,1,0:T(8,128)(2,1)S(1)}, u32[]{:S(2)}, u32[]{:S(2)}) collective-permute-start(bf16[4,128,256]{2,1,0:T(8,128)(2,1)S(1)} %get-tuple-element.67), channel_id=1, source_target_pairs={{0,64},{64,0},{1,65},{65,1},{2,66},{66,2},{3,67},{67,3},{4,68},{68... | collective-permute-start | bytes 786440 | tf_op jit(solution)/shard_map/ppermute | solution.py:334
  54.8 12.3 %copy-start.7 = (f32[16,512]{1,0:T(8,128)S(1)}, f32[16,512]{1,0:T(8,128)}, u32[]{:S(2)}) copy-start(f32[16,512]{1,0:T(8,128)} %up_gain.1) | copy-start | bytes 98308
  54.8 12.3 %copy-start.8 = (f32[4,512]{1,0:T(4,128)S(1)}, f32[4,512]{1,0:T(4,128)}, u32[]{:S(2)}) copy-start(f32[4,512]{1,0:T(4,128)} %first.1) | copy-start | bytes 24580
  54.8 12.3 %copy-start.9 = (f32[4,512]{1,0:T(4,128)S(1)}, f32[4,512]{1,0:T(4,128)}, u32[]{:S(2)}) copy-start(f32[4,512]{1,0:T(4,128)} %second.1) | copy-start | bytes 24580
  57.4 4.8 %collective-permute-start.14 = (bf16[80,640]{1,0:T(8,128)(2,1)S(1)}, bf16[80,640]{1,0:T(8,128)(2,1)S(1)}, u32[]{:S(2)}, u32[]{:S(2)}) collective-permute-start(bf16[80,640]{1,0:T(8,128)(2,1)S(1)} %get-tuple-element.60), channel_id=1, source_target_pairs={{0,1},{1,2},{2,3},{3,0},{4,5},{5,6},{6,7},{7,4},{8,9},{9,10},{10,1... | collective-permute-start | bytes 307208 | tf_op jit(solution)/shard_map/ppermute | solution.py:334
  58.1 6.6 %collective-permute-start.15 = (bf16[80,640]{1,0:T(8,128)(2,1)S(1)}, bf16[80,640]{1,0:T(8,128)(2,1)S(1)}, u32[]{:S(2)}, u32[]{:S(2)}) collective-permute-start(bf16[80,640]{1,0:T(8,128)(2,1)S(1)} %get-tuple-element.61), channel_id=1, source_target_pairs={{0,2},{1,3},{2,0},{3,1},{4,6},{5,7},{6,4},{7,5},{8,10},{9,11},{10,... | collective-permute-start | bytes 307208 | tf_op jit(solution)/shard_map/ppermute | solution.py:334
  60.6 4.8 %collective-permute-start.16 = (bf16[80,640]{1,0:T(8,128)(2,1)S(1)}, bf16[80,640]{1,0:T(8,128)(2,1)S(1)}, u32[]{:S(2)}, u32[]{:S(2)}) collective-permute-start(bf16[80,640]{1,0:T(8,128)(2,1)S(1)} %get-tuple-element.62), channel_id=1, source_target_pairs={{0,3},{1,0},{2,1},{3,2},{4,7},{5,4},{6,5},{7,6},{8,11},{9,8},{10,9... | collective-permute-start | bytes 307208 | tf_op jit(solution)/shard_map/ppermute | solution.py:334
  65.4 3.2 %collective-permute-start.18 = (bf16[4,64,256]{2,1,0:T(8,128)(2,1)S(1)}, bf16[4,64,256]{2,1,0:T(8,128)(2,1)S(1)}, u32[]{:S(2)}, u32[]{:S(2)}) collective-permute-start(bf16[4,64,256]{2,1,0:T(8,128)(2,1)S(1)} %get-tuple-element.69), channel_id=1, source_target_pairs={{0,4},{4,0},{1,5},{5,1},{2,6},{6,2},{3,7},{7,3},{8,12},{12,8},{9,1... | collective-permute-start | bytes 393224 | tf_op jit(solution)/shard_map/ppermute | solution.py:334

commit v7 on v6

--- a/solution.py
+++ b/solution.py
@@ -38,6 +38,12 @@
         self.ctx = (self.x * 2 + self.y) * 2 + self.core
 
 
+def in_three(a):
+    hi = a.astype(BF16).astype(F32)
+    lo = (a - hi).astype(BF16).astype(F32)
+    return hi, lo, (a - hi - lo).astype(BF16).astype(F32)
+
+
 def tap_weights(first, second):
     taps = jnp.concatenate([second[a : a + 1] * first for a in range(4)], axis=0)
     return jnp.concatenate([taps[15:16], taps[:15]], axis=0)
@@ -50,7 +56,7 @@
 
 
 def before_kernel(
-    lens, tokens_h, grad_h, first_h, second_h, up_h, gain_h, part, last, gco, gain,
+    lens, tokens_h, grad_h, first_h, second_h, up_h, gain_h, piece, row, last, gain,
     tokens, grad_out, first, second, up_gain, shift, sems,
 ):
     pairs = ((tokens_h, tokens), (first_h, first), (second_h, second), (grad_h, grad_out), (up_h, up_gain), (gain_h, gain))
@@ -67,24 +73,26 @@
     onward = jnp.sum(jnp.where(u == 0, 0.0, prod), axis=1)
     shift[0:8] = jnp.zeros((8, WL), F32)
     shift[8 : 8 + CL] = onward
-    part[...] = own + shift[7 : 7 + CL]
+    part = own + shift[7 : 7 + CL]
+    piece[0:CL] = part.astype(BF16)
+    row[...] = jnp.broadcast_to(part[0:1], (8, WL))
+    piece[64:80] = jnp.concatenate(list(in_three(part[0:1])) + [jnp.zeros((13, WL), F32)], axis=0).astype(BF16)
     last[...] = jnp.broadcast_to(shift[7 + CL : 8 + CL], (8, WL))
     for c in copies[3:]:
         c.wait()
     weighted = grad_out[...].astype(F32).reshape(CL, 16, WL) * mask * up_gain[...][None]
-    gco[...] = jnp.sum(weighted, axis=1).astype(BF16)
-
-
-def piece_kernel(part, gco, rim, piece):
-    first = lax.broadcasted_iota(jnp.int32, (CL, WL), 0) == 0
-    piece[0:CL] = (part[...] + jnp.where(first, rim[0:1], 0.0)).astype(BF16)
-    piece[CL : 2 * CL] = gco[...]
-
-
-def pile_kernel(piece, across, out):
+    piece[CL : 2 * CL] = jnp.sum(weighted, axis=1).astype(BF16)
+
+
+def pile_kernel(piece, row, across, rim, rim_across, out):
     y = Place().y
-    out[pl.ds(pl.multiple_of(y * 64, 64), 64)] = piece[...]
-    out[pl.ds(pl.multiple_of(64 - y * 64, 64), 64)] = across[...]
+    first = lax.broadcasted_iota(jnp.int32, (16, WL), 0) == 0
+    sent = across[64:80].astype(F32)
+    theirs = sent[0:1] + sent[1:2] + sent[2:3] + rim_across[0:1]
+    for src, at, top in ((piece, y * 64, row[0:1] + rim[0:1]), (across, 64 - y * 64, theirs)):
+        head = jnp.where(first, top, src[0:16].astype(F32))
+        out[pl.ds(pl.multiple_of(at, 64), 16)] = head.astype(BF16)
+        out[pl.ds(pl.multiple_of(at + 16, 16), 48)] = src[16:64]
 
 
 def bias_kernel(near, table, strip):
@@ -133,22 +141,28 @@
                 blocks[s, :, at + 256 : at + 384] = gco[rows, cols]
 
 
-def pack_kernel(keep, swapped, blocks, b0, up_far, up_near, down_far, down_near):
+def pack_far_kernel(keep, swapped, blocks, up, down):
     core = Place().core
+    for i, out in ((0, up), (1, down)):
+        for src, c in ((keep, core), (swapped, 1 - core)):
+            out[pl.ds(pl.multiple_of(c * CL, CL), CL)] = src[i * CL : i * CL + CL]
+    up[64:80] = blocks[2, 0:16]
+    down[64:80] = blocks[2, 16:32]
+
+
+def pack_near_kernel(keep, swapped, blocks, up, down, b0):
+    core = Place().core
+    for i, out in ((1, up), (0, down)):
+        for src, c in ((keep, core), (swapped, 1 - core)):
+            out[pl.ds(pl.multiple_of(32 + c * CL, CL), CL)] = src[i * CL : i * CL + CL]
     for i in range(2):
         for src, c in ((keep, core), (swapped, 1 - core)):
-            new = src[i * CL : i * CL + CL]
-            row = pl.multiple_of(c * CL, CL)
-            b0[pl.ds(pl.multiple_of(i * 64 + row, CL), CL)] = new
-            up, down, a, b = ((up_far, down_near, 0, 32), (up_near, down_far, 32, 0))[i]
-            up[pl.ds(pl.multiple_of(a + row, CL), CL)] = new
-            down[pl.ds(pl.multiple_of(b + row, CL), CL)] = new
+            row = pl.multiple_of(i * 64 + c * CL, CL)
+            b0[pl.ds(row, CL)] = src[i * CL : i * CL + CL]
+    up[0:32] = blocks[1]
+    down[0:32] = blocks[3]
+    down[96:112] = swapped[64:80]
     b0[128:160] = blocks[0]
-    up_near[0:32] = blocks[1]
-    down_near[0:32] = blocks[3]
-    up_far[64:80] = blocks[2, 0:16]
-    down_far[64:80] = blocks[2, 16:32]
-    down_near[96:112] = swapped[64:80]
 
 
 def gather_kernel(b0, low_near, high_near, far_low, far_high, swapped, mine, nxt):
@@ -168,7 +182,7 @@
 
 def attend_kernel(
     lens, b0, low_far, low_near, high_far, high_near, far_low, far_high, strip,
-    res, keep, send, q, k, v, ga, acck, accv,
+    res, keep, send, q, k, v, ga, score, dprob, sg, pb,
 ):
     at = Place()
     ctx, core, x, doc_len = at.ctx, at.core, at.x, lens[0]
@@ -186,35 +200,28 @@
             dst[rows] = src[first : first + n, i * HW : i * HW + HW]
     key_pos = lax.broadcasted_iota(jnp.int32, (1, LC), 1)
     key_mask = jnp.where(16 * key_pos < doc_len, 0.0, NEG)
-    heads = [(h, slice(h * HD, h * HD + HD)) for h in range(NH)]
-    for b in (3, 2, 1, 0):
-        rows = slice(b * 128, b * 128 + 128)
-        n = b * 128 + 128
-        qb, gb = [[r[rows, c] for _, c in heads] for r in (q, ga)]
-        kb, vb = [[r[0:n, c] for _, c in heads] for r in (k, v)]
-        s = [dg(qb[h], kb[h], 1, 1) for h, _ in heads]
-        dp = [dg(gb[h], vb[h], 1, 1) for h, _ in heads]
-        s = [s[h] * SCALE + strip[h, :, LC - n :] + key_mask[:, :n] for h, _ in heads]
-        e = [jnp.exp(a - jnp.max(a, axis=1, keepdims=True)) for a in s]
-        p = [a * (1.0 / jnp.sum(a, axis=1, keepdims=True)) for a in e]
-        dot = [jnp.sum(p[h] * dp[h], axis=1, keepdims=True) for h, _ in heads]
-        sg = [(p[h] * (dp[h] - dot[h])).astype(BF16) for h, _ in heads]
-        pb = [a.astype(BF16) for a in p]
-        for h, c in heads:
-            tk = dg(sg[h], qb[h], 0, 0)
-            tv = dg(pb[h], gb[h], 0, 0)
-            if b == 3:
-                acck[h] = tk
-                accv[h] = tv
-            else:
-                acck[h, 0:n] += tk
-                accv[h, 0:n] += tv
-            gq = jnp.dot(sg[h], kb[h], preferred_element_type=F32) * SCALE
-            res[0, rows, c] = gq.astype(BF16)
-            res[3, rows, c] = jnp.dot(pb[h], vb[h], preferred_element_type=F32).astype(BF16)
-    for h, c in heads:
-        res[1, 0:LC, c] = (acck[h] * SCALE).astype(BF16)
-        res[2, 0:LC, c] = accv[h].astype(BF16)
+    work = [(b, h, slice(h * HD, h * HD + HD)) for b in (3, 2, 1, 0) for h in range(NH)]
+    for b, h, c in work:
+        rows, n = slice(b * 128, b * 128 + 128), b * 128 + 128
+        score[h, rows, 0:n] = dg(q[rows, c], k[0:n, c], 1, 1)
+        dprob[h, rows, 0:n] = dg(ga[rows, c], v[0:n, c], 1, 1)
+    for b, h, c in work:
+        rows, n = slice(b * 128, b * 128 + 128), b * 128 + 128
+        s = score[h, rows, 0:n] * SCALE + strip[h, :, LC - n :] + key_mask[:, :n]
+        e = jnp.exp(s - jnp.max(s, axis=1, keepdims=True))
+        p = e * (1.0 / jnp.sum(e, axis=1, keepdims=True))
+        dp = dprob[h, rows, 0:n]
+        dot = jnp.sum(p * dp, axis=1, keepdims=True)
+        sg[h, rows, 0:n] = (p * (dp - dot)).astype(BF16)
+        pb[h, rows, 0:n] = p.astype(BF16)
+    for b, h, c in work:
+        rows, n = slice(b * 128, b * 128 + 128), b * 128 + 128
+        gq = jnp.dot(sg[h, rows, 0:n], k[0:n, c], preferred_element_type=F32)
+        res[0, rows, c] = (gq * SCALE).astype(BF16)
+        res[3, rows, c] = jnp.dot(pb[h, rows, 0:n], v[0:n, c], preferred_element_type=F32).astype(BF16)
+        tail = slice(b * 128, LC)
+        res[1, rows, c] = (dg(sg[h, tail, rows], q[tail, c], 0, 0) * SCALE).astype(BF16)
+        res[2, rows, c] = dg(pb[h, tail, rows], ga[tail, c], 0, 0).astype(BF16)
     res[:, LC : LC + 16] = jnp.zeros((4, 16, HW), BF16)
     peer = ctx + 1 - 2 * core
     keep[...] = res[:, pl.ds(pl.multiple_of(ctx * CL, CL), ROWS)]
@@ -238,7 +245,7 @@
             out[w] = dg(src[:, cols], res[w, 0:LC], 0, 0).astype(out.dtype)
 
 
-def sum_kernel(keep, got, r1, r2, r3, own, send):
+def sum_kernel(keep, got, r1, own, send):
     core = Place().core
     for w in range(4):
         for c, out in ((core, own), (1 - core, send)):
@@ -339,9 +346,9 @@
     bias_table, buckets, up_gain, grad_out,
 ):
     weights = (w_query, w_key, w_value, w_out)
-    part, last, gco, gain = call(
+    piece, row, last, gain = call(
         before_kernel,
-        [((CL, WL), F32), ((8, WL), F32), ((CL, WL), BF16), ((1, D), F32)],
+        [((80, WL), BF16), ((8, WL), F32), ((8, WL), F32), ((1, D), F32)],
         (lengths, tokens[0], grad_out[0], conv_first, conv_second, up_gain, norm_gain[None]),
         [
             ((SEG, WL), BF16), ((SEG, WL), BF16), ((4, WL), F32), ((4, WL), F32), ((16, WL), F32),
@@ -352,12 +359,13 @@
     )
     line = ("x", "y", "core")
     rim = lax.ppermute(last, line, [(i, i + 1) for i in range(15)])
-    (piece,) = call(piece_kernel, [((2 * CL, WL), BF16)], (part, gco, rim), smem=())
+    over = [(i, ((i + 1) ^ 2)) for i in range(15)]
     across = shifted(piece, "y", 1)
+    rim_across = lax.ppermute(last, line, over)
     (piece,) = call(
         pile_kernel,
         [((PIECE, WL), BF16)],
-        (piece, across),
+        (piece, row, across, rim, rim_across),
         smem=(),
         flops=6 * 10**9,
     )
@@ -385,9 +393,12 @@
         flops=10**9,
     )
     swapped = shifted(send, "core", 1)
-    b0, up_far, up_near, down_far, down_near = call(
-        pack_kernel,
-        [((n, 4 * HW), BF16) for n in (160, 80, 96, 80, 112)],
+    up_far, down_far = call(
+        pack_far_kernel, [((80, 4 * HW), BF16)] * 2, (keep, swapped, blocks), smem=()
+    )
+    up_near, down_near, b0 = call(
+        pack_near_kernel,
+        [((n, 4 * HW), BF16) for n in (96, 112, 160)],
         (keep, swapped, blocks),
         smem=(),
     )
@@ -405,8 +416,9 @@
         attend_kernel,
         [((4, LC + 16, HW), BF16), ((4, ROWS, HW), BF16), ((4, ROWS, HW), BF16)],
         (lengths, b0, low_far, low_near, high_far, high_near, far_low, far_high, strip),
-        [((LC, HW), BF16)] * 4 + [((NH, LC, HD), F32)] * 2,
+        [((LC, HW), BF16)] * 4 + [((NH, LC, LC), F32)] * 2 + [((NH, LC, LC), BF16)] * 2,
         flops=6 * 10**9,
+        vmem=16 * 2**20,
     )
     got_r = shifted(send_r, "core", 1)
     dw_keep, dw_send = call(
@@ -431,7 +443,7 @@
     dw_own, dw_other = call(
         sum_kernel,
         [((4, 64, HW), F32), ((4, 64, HW), BF16)],
-        (dw_keep, dw_got, r1, r2, r3),
+        (dw_keep, dw_got, r1),
         smem=(),
     )
     dw_other = shifted(dw_other, "core", 1)
@@ -448,6 +460,7 @@
         [((SEG, WL), BF16)] * 2,
         (lengths, own, r1, r2, r3, cz, inv, gain, conv_first, conv_second, up_gain),
         [((ROWS, WL), F32)],
+        flops=2 * 10**10,
         typed=False,
     )
     return (update[None], grad_tokens[None], *dw)

time: 69.6 us -> 66.3 us (0.953)
  waiting for transfers between devices: 20.4 us -> 16.5 us
  starting transfers between devices: 31.9 us -> 33.3 us
  Pallas kernels: 15 us -> 13.8 us
    ppermute x18, waiting for transfers between devices: 19.6 us -> 11.9 us  [shifted(): return lax.ppermute(x, axis, [(i, (i + steps) % n) for i in range(n)])]
    ppermute x0 -> x1, waiting for transfers between devices: none -> 4.62 us  [local(): rim_across = lax.ppermute(last, line, over)]
    ppermute x1, starting transfers between devices: 6.21 us -> 2.71 us  [local(): rim = lax.ppermute(last, line, [(i, i + 1) for i in range(15)])]
    ppermute x18, starting transfers between devices: 25.7 us -> 28.6 us  [shifted(): return lax.ppermute(x, axis, [(i, (i + steps) % n) for i in range(n)])]
    ppermute x0 -> x1, starting transfers between devices: none -> 1.92 us  [local(): rim_across = lax.ppermute(last, line, over)]
    pallas_call x13, Pallas kernels: 15 us -> 13.8 us  [call(): pl.pallas_call(kernel, out_shape=[pltpu.VMEM(s, d) if typed else jax.Shap...]
    ppermute x1, waiting for transfers between devices: 0.85 us -> 0.01 us  [local(): rim = lax.ppermute(last, line, [(i, i + 1) for i in range(15)])]
  transfers between devices with their start and end apart: 19 -> 20, of which waited for: 13 -> 10; matrix products, arithmetic and copies ran while one was open for 1% -> 1% of each run, Pallas kernels for 14% -> 14%
where the time goes in v7:
time: 66.3 us; the launch traced here: 65.7 us
  starting transfers between devices  33.3 us (50%)
  waiting for transfers between devices  16.5 us (25%)
  Pallas kernels  13.8 us (21%)
  between operations  1.47 us (2%)
    ppermute x18, starting transfers between devices, shifted(): return lax.ppermute(x, axis, [(i, (i + steps) % n) for i in range(n)])  28.6 us
    pallas_call x13, Pallas kernels, call(): pl.pallas_call(kernel, out_shape=[pltpu.VMEM(s, d) if typed else jax.Shap...  13.8 us
    ppermute x18, waiting for transfers between devices, shifted(): return lax.ppermute(x, axis, [(i, (i + steps) % n) for i in range(n)])  11.9 us
    ppermute x1, waiting for transfers between devices, local(): rim_across = lax.ppermute(last, line, over)  4.62 us
    ppermute x1, starting transfers between devices, local(): rim = lax.ppermute(last, line, [(i, i + 1) for i in range(15)])  2.71 us
    ppermute x1, starting transfers between devices, local(): rim_across = lax.ppermute(last, line, over)  1.92 us
  transfers between devices with their start and end apart: 20, of which 10 were waited for; matrix products, arithmetic and copies ran while one was open for 1% of the time, Pallas kernels for 14%

profile of v7, /device:TPU:1, one launch (start us, length us, event | category | flops | bytes accessed | tf_op | source)
XLA Modules:
  0.0 65.7 jit_solution(10799178840902005045)
XLA Ops:
  1.3 1.9 %shard_map.172 = (bf16[80,512]{1,0:T(8,128)(2,1)S(1)}, f32[8,512]{1,0:T(8,128)S(1)}, f32[8,512]{1,0:T(8,128)S(1)}, f32[1,2048]{1,0:T(1,128)S(1)}) custom-call(s32[1]{0:T(128)S(6)} %copy.20.lens, bf16[512,512]{1,0:T(8,128)(2,1)} %bitcast.7, bf16[512,512]{1,0:T(8,128)(2,1)} %bitcast.8, f32[4,512]{1,0:T(4,128)} %first.1, f32[4,512]{1,0:T(4,128)} %second.1, ...), custom_call_target="tpu_custom_call" | custom-call | tf_op jit(solution)/shard_map/pallas_call | solution.py:328
  3.2 3.8 %collective-permute-start = (bf16[80,512]{1,0:T(8,128)(2,1)S(1)}, bf16[80,512]{1,0:T(8,128)(2,1)S(1)}, u32[]{:S(2)}, u32[]{:S(2)}) collective-permute-start(bf16[80,512]{1,0:T(8,128)(2,1)S(1)} %get-tuple-element.40.piece), channel_id=1, source_target_pairs={{0,8},{8,0},{1,9},{9,1},{2,10},{10,2},{3,11},{11,3},{4,12},{12,4},... | collective-permute-start | bytes 245768 | tf_op jit(solution)/shard_map/ppermute | solution.py:341
  7.0 2.7 %collective-permute-start.1 = (f32[8,512]{1,0:T(8,128)S(1)}, f32[8,512]{1,0:T(8,128)S(1)}, u32[]{:S(2)}, u32[]{:S(2)}) collective-permute-start(f32[8,512]{1,0:T(8,128)S(1)} %get-tuple-element.42), channel_id=1, source_target_pairs={{0,4},{4,8},{8,12},{12,16},{16,20},{20,24},{24,28},{28,32},{32,36}... | collective-permute-start | bytes 49160 | tf_op jit(solution)/shard_map/ppermute | solution.py:361
  9.7 1.9 %collective-permute-start.2 = (f32[8,512]{1,0:T(8,128)S(1)}, f32[8,512]{1,0:T(8,128)S(1)}, u32[]{:S(2)}, u32[]{:S(2)}) collective-permute-start(f32[8,512]{1,0:T(8,128)S(1)} %get-tuple-element.42), channel_id=1, source_target_pairs={{0,12},{4,0},{8,4},{12,24},{16,28},{20,16},{24,20},{28,40},{32,44}... | collective-permute-start | bytes 49160 | tf_op jit(solution)/shard_map/ppermute | solution.py:364
  11.7 4.6 %collective-permute-done.2.rim_across = f32[8,512]{1,0:T(8,128)S(1)} collective-permute-done((f32[8,512]{1,0:T(8,128)S(1)}, f32[8,512]{1,0:T(8,128)S(1)}, u32[]{:S(2)}, u32[]{:S(2)}) %collective-permute-start.2) | collective-permute-done | bytes 16416 | tf_op jit(solution)/shard_map/ppermute | solution.py:364
  16.4 1.8 %collective-permute-start.3 = (bf16[128,512]{1,0:T(8,128)(2,1)S(1)}, bf16[128,512]{1,0:T(8,128)(2,1)S(1)}, u32[]{:S(2)}, u32[]{:S(2)}) collective-permute-start(bf16[128,512]{1,0:T(8,128)(2,1)S(1)} %shard_map.173.p0), channel_id=1, source_target_pairs={{0,1},{1,2},{2,3},{3,0},{4,5},{5,6},{6,7},{7,4},{8,9},{9,10},{10,1... | collective-permute-start | bytes 393224 | tf_op jit(solution)/shard_map/ppermute | solution.py:341
  18.2 3.3 %collective-permute-start.4 = (bf16[128,512]{1,0:T(8,128)(2,1)S(1)}, bf16[128,512]{1,0:T(8,128)(2,1)S(1)}, u32[]{:S(2)}, u32[]{:S(2)}) collective-permute-start(bf16[128,512]{1,0:T(8,128)(2,1)S(1)} %shard_map.173.p0), channel_id=1, source_target_pairs={{0,2},{1,3},{2,0},{3,1},{4,6},{5,7},{6,4},{7,5},{8,10},{9,11},{10,... | collective-permute-start | bytes 393224 | tf_op jit(solution)/shard_map/ppermute | solution.py:341
  21.5 0.7 %collective-permute-start.5 = (bf16[128,512]{1,0:T(8,128)(2,1)S(1)}, bf16[128,512]{1,0:T(8,128)(2,1)S(1)}, u32[]{:S(2)}, u32[]{:S(2)}) collective-permute-start(bf16[128,512]{1,0:T(8,128)(2,1)S(1)} %shard_map.173.p0), channel_id=1, source_target_pairs={{0,3},{1,0},{2,1},{3,2},{4,7},{5,4},{6,5},{7,6},{8,11},{9,8},{10,9... | collective-permute-start | bytes 393224 | tf_op jit(solution)/shard_map/ppermute | solution.py:341
  22.2 0.9 %collective-permute-done.3.r1 = bf16[128,512]{1,0:T(8,128)(2,1)S(1)} collective-permute-done((bf16[128,512]{1,0:T(8,128)(2,1)S(1)}, bf16[128,512]{1,0:T(8,128)(2,1)S(1)}, u32[]{:S(2)}, u32[]{:S(2)}) %collective-permute-start.3) | collective-permute-done | bytes 131104 | tf_op jit(solution)/shard_map/ppermute | solution.py:341
  23.1 3.4 %collective-permute-done.4.r2 = bf16[128,512]{1,0:T(8,128)(2,1)S(1)} collective-permute-done((bf16[128,512]{1,0:T(8,128)(2,1)S(1)}, bf16[128,512]{1,0:T(8,128)(2,1)S(1)}, u32[]{:S(2)}, u32[]{:S(2)}) %collective-permute-start.4) | collective-permute-done | bytes 131104 | tf_op jit(solution)/shard_map/ppermute | solution.py:341
  26.7 1.6 %shard_map.174 = (bf16[64,1024]{1,0:T(8,128)(2,1)S(1)}, bf16[80,1024]{1,0:T(8,128)(2,1)S(1)}, bf16[4,32,1024]{2,1,0:T(8,128)(2,1)S(1)}, bf16[32,2048]{1,0:T(8,128)(2,1)S(1)}) custom-call(bf16[128,512]{1,0:T(8,128)(2,1)S(1)} %shard_map.173.p0, bf16[128,512]{1,0:T(8,128)(2,1)S(1)} %collective-permute-done.3.r1, ...), custom_call_target="tpu_custom_call" | custom-call | flops 1000000000 | tf_op jit(solution)/shard_map/pallas_call | solution.py:328
  28.3 2.1 %collective-permute-start.6 = (bf16[80,1024]{1,0:T(8,128)(2,1)S(1)}, bf16[80,1024]{1,0:T(8,128)(2,1)S(1)}, u32[]{:S(2)}, u32[]{:S(2)}) collective-permute-start(bf16[80,1024]{1,0:T(8,128)(2,1)S(1)} %get-tuple-element.45), channel_id=1, source_target_pairs={{0,4},{4,0},{1,5},{5,1},{2,6},{6,2},{3,7},{7,3},{8,12},{12,8},{9,1... | collective-permute-start | bytes 491528 | tf_op jit(solution)/shard_map/ppermute | solution.py:341
  30.4 1.0 %collective-permute-done.6.swapped = bf16[80,1024]{1,0:T(8,128)(2,1)S(1)} collective-permute-done((bf16[80,1024]{1,0:T(8,128)(2,1)S(1)}, bf16[80,1024]{1,0:T(8,128)(2,1)S(1)}, u32[]{:S(2)}, u32[]{:S(2)}) %collective-permute-start.6) | collective-permute-done | bytes 163872 | tf_op jit(solution)/shard_map/ppermute | solution.py:341
  31.5 1.3 %collective-permute-start.7 = (bf16[80,1024]{1,0:T(8,128)(2,1)S(1)}, bf16[80,1024]{1,0:T(8,128)(2,1)}, u32[]{:S(2)}, u32[]{:S(2)}) collective-permute-start(bf16[80,1024]{1,0:T(8,128)(2,1)S(1)} %get-tuple-element.48), channel_id=1, source_target_pairs={{0,16},{16,32},{32,48},{48,0},{1,17},{17,33},{33,49},{49,1},{2,18}... | collective-permute-start | bytes 491528 | tf_op jit(solution)/shard_map/ppermute | solution.py:341
  32.8 1.5 %collective-permute-start.9 = (bf16[80,1024]{1,0:T(8,128)(2,1)S(1)}, bf16[80,1024]{1,0:T(8,128)(2,1)}, u32[]{:S(2)}, u32[]{:S(2)}) collective-permute-start(bf16[80,1024]{1,0:T(8,128)(2,1)S(1)} %get-tuple-element.50), channel_id=1, source_target_pairs={{0,48},{16,0},{32,16},{48,32},{1,49},{17,1},{33,17},{49,33},{2,50}... | collective-permute-start | bytes 491528 | tf_op jit(solution)/shard_map/ppermute | solution.py:341
  34.2 0.8 %shard_map.175 = (bf16[96,1024]{1,0:T(8,128)(2,1)}, bf16[112,1024]{1,0:T(8,128)(2,1)}, bf16[160,1024]{1,0:T(8,128)(2,1)S(1)}) custom-call(bf16[64,1024]{1,0:T(8,128)(2,1)S(1)} %get-tuple-element.44.keep, bf16[80,1024]{1,0:T(8,128)(2,1)S(1)} %collective-permute-done.6.swapped, bf16[4,32,1024]{2,1,0:T(8,128)(2,1)S(1)} %get-tuple-element.46.blocks), custom_call_target="tpu_custom_call" | custom-call | tf_op jit(solution)/shard_map/pallas_call | solution.py:328
  35.5 1.0 %collective-permute-start.8 = (bf16[96,1024]{1,0:T(8,128)(2,1)}, bf16[96,1024]{1,0:T(8,128)(2,1)S(1)}, u32[]{:S(2)}, u32[]{:S(2)}) collective-permute-start(bf16[96,1024]{1,0:T(8,128)(2,1)} %get-tuple-element.49), channel_id=1, source_target_pairs={{0,16},{16,32},{32,48},{48,0},{1,17},{17,33},{33,49},{49,1},{2,18}... | collective-permute-start | bytes 589832 | tf_op jit(solution)/shard_map/ppermute | solution.py:341
  36.5 1.8 %collective-permute-done.7.low_far = bf16[80,1024]{1,0:T(8,128)(2,1)} collective-permute-done((bf16[80,1024]{1,0:T(8,128)(2,1)S(1)}, bf16[80,1024]{1,0:T(8,128)(2,1)}, u32[]{:S(2)}, u32[]{:S(2)}) %collective-permute-start.7) | collective-permute-done | bytes 163872 | tf_op jit(solution)/shard_map/ppermute | solution.py:341
  38.3 2.7 %collective-permute-start.12 = (bf16[80,1024]{1,0:T(8,128)(2,1)}, bf16[80,1024]{1,0:T(8,128)(2,1)S(1)}, u32[]{:S(2)}, u32[]{:S(2)}) collective-permute-start(bf16[80,1024]{1,0:T(8,128)(2,1)} %collective-permute-done.9.high_far), channel_id=1, source_target_pairs={{0,48},{16,0},{32,16},{48,32},{1,49},{17,1},{33,17},{49,33},{2,50}... | collective-permute-start | bytes 491528 | tf_op jit(solution)/shard_map/ppermute | solution.py:341
  41.5 1.1 %shard_map.177.strip = f32[2,128,512]{2,1,0:T(8,128)S(1)} custom-call(s32[8,640]{1,0:T(8,128)S(1)} %broadcast_in_dim.20.near, f32[32,4]{1,0:T(8,128)S(1)} %copy.19.table), custom_call_target="tpu_custom_call" | custom-call | tf_op jit(solution)/shard_map/pallas_call | solution.py:328
  42.9 3.0 %collective-permute-done.11.far_low = bf16[80,1024]{1,0:T(8,128)(2,1)S(1)} collective-permute-done((bf16[80,1024]{1,0:T(8,128)(2,1)}, bf16[80,1024]{1,0:T(8,128)(2,1)S(1)}, u32[]{:S(2)}, u32[]{:S(2)}) %collective-permute-start.11) | collective-permute-done | bytes 163872 | tf_op jit(solution)/shard_map/ppermute | solution.py:341
  46.5 1.4 %collective-permute-start.14 = (bf16[4,32,1024]{2,1,0:T(8,128)(2,1)S(1)}, bf16[4,32,1024]{2,1,0:T(8,128)(2,1)S(1)}, u32[]{:S(2)}, u32[]{:S(2)}) collective-permute-start(bf16[4,32,1024]{2,1,0:T(8,128)(2,1)S(1)} %get-tuple-element.57.mine), channel_id=1, source_target_pairs={{0,4},{4,0},{1,5},{5,1},{2,6},{6,2},{3,7},{7,3},{8,12},{12,8},{9,1... | collective-permute-start | bytes 786440 | tf_op jit(solution)/shard_map/ppermute | solution.py:341
  47.9 2.9 %shard_map.178 = (bf16[4,528,256]{2,1,0:T(8,128)(2,1)S(1)}, bf16[4,48,256]{2,1,0:T(8,128)(2,1)S(1)}, bf16[4,48,256]{2,1,0:T(8,128)(2,1)S(1)}) custom-call(s32[1]{0:T(128)S(6)} %copy.20.lens, bf16[160,1024]{1,0:T(8,128)(2,1)S(1)} %get-tuple-element.47.b0, bf16[80,1024]{1,0:T(8,128)(2,1)} %collective-permute-done.7.low_far, ...), custom_call_target="tpu_custom_call" | custom-call | flops 6000000000 | tf_op jit(solution)/shard_map/pallas_call | solution.py:328
  51.5 1.4 %collective-permute-start.18 = (bf16[4,128,256]{2,1,0:T(8,128)(2,1)S(1)}, bf16[4,128,256]{2,1,0:T(8,128)(2,1)S(1)}, u32[]{:S(2)}, u32[]{:S(2)}) collective-permute-start(bf16[4,128,256]{2,1,0:T(8,128)(2,1)S(1)} %get-tuple-element.67), channel_id=1, source_target_pairs={{0,64},{64,0},{1,65},{65,1},{2,66},{66,2},{3,67},{67,3},{4,68},{68... | collective-permute-start | bytes 786440 | tf_op jit(solution)/shard_map/ppermute | solution.py:341
  53.0 2.6 %shard_map.181 = (bf16[80,640]{1,0:T(8,128)(2,1)S(1)}, bf16[80,640]{1,0:T(8,128)(2,1)S(1)}, bf16[80,640]{1,0:T(8,128)(2,1)S(1)}, f32[80,640]{1,0:T(8,128)S(1)}, ...) custom-call(bf16[4,48,256]{2,1,0:T(8,128)(2,1)S(1)} %get-tuple-element.52.keep_r, ...), custom_call_target="tpu_custom_call" | custom-call | flops 1000000000 | tf_op jit(solution)/shard_map/pallas_call | solution.py:328
  55.6 1.0 %collective-permute-start.15 = (bf16[80,640]{1,0:T(8,128)(2,1)S(1)}, bf16[80,640]{1,0:T(8,128)(2,1)S(1)}, u32[]{:S(2)}, u32[]{:S(2)}) collective-permute-start(bf16[80,640]{1,0:T(8,128)(2,1)S(1)} %get-tuple-element.60), channel_id=1, source_target_pairs={{0,1},{1,2},{2,3},{3,0},{4,5},{5,6},{6,7},{7,4},{8,9},{9,10},{10,1... | collective-permute-start | bytes 307208 | tf_op jit(solution)/shard_map/ppermute | solution.py:341
  56.6 2.1 %collective-permute-start.16 = (bf16[80,640]{1,0:T(8,128)(2,1)S(1)}, bf16[80,640]{1,0:T(8,128)(2,1)S(1)}, u32[]{:S(2)}, u32[]{:S(2)}) collective-permute-start(bf16[80,640]{1,0:T(8,128)(2,1)S(1)} %get-tuple-element.61), channel_id=1, source_target_pairs={{0,2},{1,3},{2,0},{3,1},{4,6},{5,7},{6,4},{7,5},{8,10},{9,11},{10,... | collective-permute-start | bytes 307208 | tf_op jit(solution)/shard_map/ppermute | solution.py:341
  58.7 1.0 %collective-permute-start.17 = (bf16[80,640]{1,0:T(8,128)(2,1)S(1)}, bf16[80,640]{1,0:T(8,128)(2,1)S(1)}, u32[]{:S(2)}, u32[]{:S(2)}) collective-permute-start(bf16[80,640]{1,0:T(8,128)(2,1)S(1)} %get-tuple-element.62), channel_id=1, source_target_pairs={{0,3},{1,0},{2,1},{3,2},{4,7},{5,4},{6,5},{7,6},{8,11},{9,8},{10,9... | collective-permute-start | bytes 307208 | tf_op jit(solution)/shard_map/ppermute | solution.py:341
  59.7 0.7 %collective-permute-done.15.r1 = bf16[80,640]{1,0:T(8,128)(2,1)S(1)} collective-permute-done((bf16[80,640]{1,0:T(8,128)(2,1)S(1)}, bf16[80,640]{1,0:T(8,128)(2,1)S(1)}, u32[]{:S(2)}, u32[]{:S(2)}) %collective-permute-start.15) | collective-permute-done | bytes 102432 | tf_op jit(solution)/shard_map/ppermute | solution.py:341
  60.4 2.9 %collective-permute-start.19 = (bf16[4,64,256]{2,1,0:T(8,128)(2,1)S(1)}, bf16[4,64,256]{2,1,0:T(8,128)(2,1)S(1)}, u32[]{:S(2)}, u32[]{:S(2)}) collective-permute-start(bf16[4,64,256]{2,1,0:T(8,128)(2,1)S(1)} %get-tuple-element.69), channel_id=1, source_target_pairs={{0,4},{4,0},{1,5},{5,1},{2,6},{6,2},{3,7},{7,3},{8,12},{12,8},{9,1... | collective-permute-start | bytes 393224 | tf_op jit(solution)/shard_map/ppermute | solution.py:341
  63.4 1.4 %shard_map.182 = (bf16[512,512]{1,0:T(8,128)(2,1)}, bf16[512,512]{1,0:T(8,128)(2,1)}) custom-call(s32[1]{0:T(128)S(6)} %copy.20.lens, f32[80,640]{1,0:T(8,128)S(1)} %get-tuple-element.59.keep, bf16[80,640]{1,0:T(8,128)(2,1)S(1)} %collective-permute-done.15.r1, bf16[80,640]{1,0:T(8,128)(2,1)S(1)} %collective-permute-done.16.r2, ...), custom_call_target="tpu_custom_call" | custom-call | flops 20000000000 | tf_op jit(solution)/shard_map/pallas_call | solution.py:328
  64.8 0.8 %shard_map.184 = (f32[64,512]{1,0:T(8,128)}, f32[64,512]{1,0:T(8,128)}, f32[64,512]{1,0:T(8,128)}, f32[64,512]{1,0:T(8,128)}) custom-call(f32[4,64,256]{2,1,0:T(8,128)S(1)} %get-tuple-element.68.own, bf16[4,64,256]{2,1,0:T(8,128)(2,1)S(1)} %collective-permute-done.19.other), custom_call_target="tpu_custom_call" | custom-call | flops 6000000000 | tf_op jit(solution)/shard_map/pallas_call | solution.py:328
  (53 shorter events, 2.9 us)
Async XLA Ops:
  3.2 13.1 %collective-permute-start = (bf16[80,512]{1,0:T(8,128)(2,1)S(1)}, bf16[80,512]{1,0:T(8,128)(2,1)S(1)}, u32[]{:S(2)}, u32[]{:S(2)}) collective-permute-start(bf16[80,512]{1,0:T(8,128)(2,1)S(1)} %get-tuple-element.40.piece), channel_id=1, source_target_pairs={{0,8},{8,0},{1,9},{9,1},{2,10},{10,2},{3,11},{11,3},{4,12},{12,4},... | collective-permute-start | bytes 245768 | tf_op jit(solution)/shard_map/ppermute | solution.py:341
  7.0 4.6 %collective-permute-start.1 = (f32[8,512]{1,0:T(8,128)S(1)}, f32[8,512]{1,0:T(8,128)S(1)}, u32[]{:S(2)}, u32[]{:S(2)}) collective-permute-start(f32[8,512]{1,0:T(8,128)S(1)} %get-tuple-element.42), channel_id=1, source_target_pairs={{0,4},{4,8},{8,12},{12,16},{16,20},{20,24},{24,28},{28,32},{32,36}... | collective-permute-start | bytes 49160 | tf_op jit(solution)/shard_map/ppermute | solution.py:361
  9.7 6.6 %collective-permute-start.2 = (f32[8,512]{1,0:T(8,128)S(1)}, f32[8,512]{1,0:T(8,128)S(1)}, u32[]{:S(2)}, u32[]{:S(2)}) collective-permute-start(f32[8,512]{1,0:T(8,128)S(1)} %get-tuple-element.42), channel_id=1, source_target_pairs={{0,12},{4,0},{8,4},{12,24},{16,28},{20,16},{24,20},{28,40},{32,44}... | collective-permute-start | bytes 49160 | tf_op jit(solution)/shard_map/ppermute | solution.py:364
  16.3 10.4 %copy-start = (bf16[2048,512]{1,0:T(8,128)(2,1)S(1)}, bf16[2048,512]{1,0:T(8,128)(2,1)}, u32[]{:S(2)}) copy-start(bf16[2048,512]{1,0:T(8,128)(2,1)} %wq.3) | copy-start | bytes 6291460
  16.3 10.4 %copy-start.1 = (bf16[2048,512]{1,0:T(8,128)(2,1)S(1)}, bf16[2048,512]{1,0:T(8,128)(2,1)}, u32[]{:S(2)}) copy-start(bf16[2048,512]{1,0:T(8,128)(2,1)} %wk.3) | copy-start | bytes 6291460
  16.3 10.4 %copy-start.3 = (bf16[2048,512]{1,0:T(8,128)(2,1)S(1)}, bf16[2048,512]{1,0:T(8,128)(2,1)}, u32[]{:S(2)}) copy-start(bf16[2048,512]{1,0:T(8,128)(2,1)} %wv.3) | copy-start | bytes 6291460
  16.3 10.4 %copy-start.5 = (bf16[2048,512]{1,0:T(8,128)(2,1)S(1)}, bf16[2048,512]{1,0:T(8,128)(2,1)}, u32[]{:S(2)}) copy-start(bf16[2048,512]{1,0:T(8,128)(2,1)} %wo.3) | copy-start | bytes 6291460
  16.4 6.8 %collective-permute-start.3 = (bf16[128,512]{1,0:T(8,128)(2,1)S(1)}, bf16[128,512]{1,0:T(8,128)(2,1)S(1)}, u32[]{:S(2)}, u32[]{:S(2)}) collective-permute-start(bf16[128,512]{1,0:T(8,128)(2,1)S(1)} %shard_map.173.p0), channel_id=1, source_target_pairs={{0,1},{1,2},{2,3},{3,0},{4,5},{5,6},{6,7},{7,4},{8,9},{9,10},{10,1... | collective-permute-start | bytes 393224 | tf_op jit(solution)/shard_map/ppermute | solution.py:341
  18.2 8.3 %collective-permute-start.4 = (bf16[128,512]{1,0:T(8,128)(2,1)S(1)}, bf16[128,512]{1,0:T(8,128)(2,1)S(1)}, u32[]{:S(2)}, u32[]{:S(2)}) collective-permute-start(bf16[128,512]{1,0:T(8,128)(2,1)S(1)} %shard_map.173.p0), channel_id=1, source_target_pairs={{0,2},{1,3},{2,0},{3,1},{4,6},{5,7},{6,4},{7,5},{8,10},{9,11},{10,... | collective-permute-start | bytes 393224 | tf_op jit(solution)/shard_map/ppermute | solution.py:341
  21.5 5.2 %collective-permute-start.5 = (bf16[128,512]{1,0:T(8,128)(2,1)S(1)}, bf16[128,512]{1,0:T(8,128)(2,1)S(1)}, u32[]{:S(2)}, u32[]{:S(2)}) collective-permute-start(bf16[128,512]{1,0:T(8,128)(2,1)S(1)} %shard_map.173.p0), channel_id=1, source_target_pairs={{0,3},{1,0},{2,1},{3,2},{4,7},{5,4},{6,5},{7,6},{8,11},{9,8},{10,9... | collective-permute-start | bytes 393224 | tf_op jit(solution)/shard_map/ppermute | solution.py:341
  26.7 14.3 %copy-start.11 = (s32[512]{0:T(512)S(1)}, s32[512]{0:T(512)}, u32[]{:S(2)}) copy-start(s32[512]{0:T(512)} %param.23) | copy-start | bytes 6148
  26.7 14.6 %copy-start.10 = (f32[32,4]{0,1:T(4,128)S(1)}, f32[32,4]{0,1:T(4,128)}, u32[]{:S(2)}) copy-start(f32[32,4]{0,1:T(4,128)} %param.22) | copy-start | bytes 1540
  28.3 3.2 %collective-permute-start.6 = (bf16[80,1024]{1,0:T(8,128)(2,1)S(1)}, bf16[80,1024]{1,0:T(8,128)(2,1)S(1)}, u32[]{:S(2)}, u32[]{:S(2)}) collective-permute-start(bf16[80,1024]{1,0:T(8,128)(2,1)S(1)} %get-tuple-element.45), channel_id=1, source_target_pairs={{0,4},{4,0},{1,5},{5,1},{2,6},{6,2},{3,7},{7,3},{8,12},{12,8},{9,1... | collective-permute-start | bytes 491528 | tf_op jit(solution)/shard_map/ppermute | solution.py:341
  31.5 6.8 %collective-permute-start.7 = (bf16[80,1024]{1,0:T(8,128)(2,1)S(1)}, bf16[80,1024]{1,0:T(8,128)(2,1)}, u32[]{:S(2)}, u32[]{:S(2)}) collective-permute-start(bf16[80,1024]{1,0:T(8,128)(2,1)S(1)} %get-tuple-element.48), channel_id=1, source_target_pairs={{0,16},{16,32},{32,48},{48,0},{1,17},{17,33},{33,49},{49,1},{2,18}... | collective-permute-start | bytes 491528 | tf_op jit(solution)/shard_map/ppermute | solution.py:341
  32.8 5.5 %collective-permute-start.9 = (bf16[80,1024]{1,0:T(8,128)(2,1)S(1)}, bf16[80,1024]{1,0:T(8,128)(2,1)}, u32[]{:S(2)}, u32[]{:S(2)}) collective-permute-start(bf16[80,1024]{1,0:T(8,128)(2,1)S(1)} %get-tuple-element.50), channel_id=1, source_target_pairs={{0,48},{16,0},{32,16},{48,32},{1,49},{17,1},{33,17},{49,33},{2,50}... | collective-permute-start | bytes 491528 | tf_op jit(solution)/shard_map/ppermute | solution.py:341
  35.1 7.9 %collective-permute-start.10 = (bf16[112,1024]{1,0:T(8,128)(2,1)}, bf16[112,1024]{1,0:T(8,128)(2,1)S(1)}, u32[]{:S(2)}, u32[]{:S(2)}) collective-permute-start(bf16[112,1024]{1,0:T(8,128)(2,1)} %get-tuple-element.51), channel_id=1, source_target_pairs={{0,48},{16,0},{32,16},{48,32},{1,49},{17,1},{33,17},{49,33},{2,50}... | collective-permute-start | bytes 688136 | tf_op jit(solution)/shard_map/ppermute | solution.py:341
  35.5 7.1 %collective-permute-start.8 = (bf16[96,1024]{1,0:T(8,128)(2,1)}, bf16[96,1024]{1,0:T(8,128)(2,1)S(1)}, u32[]{:S(2)}, u32[]{:S(2)}) collective-permute-start(bf16[96,1024]{1,0:T(8,128)(2,1)} %get-tuple-element.49), channel_id=1, source_target_pairs={{0,16},{16,32},{32,48},{48,0},{1,17},{17,33},{33,49},{49,1},{2,18}... | collective-permute-start | bytes 589832 | tf_op jit(solution)/shard_map/ppermute | solution.py:341
  38.3 7.7 %collective-permute-start.11 = (bf16[80,1024]{1,0:T(8,128)(2,1)}, bf16[80,1024]{1,0:T(8,128)(2,1)S(1)}, u32[]{:S(2)}, u32[]{:S(2)}) collective-permute-start(bf16[80,1024]{1,0:T(8,128)(2,1)} %collective-permute-done.7.low_far), channel_id=1, source_target_pairs={{0,16},{16,32},{32,48},{48,0},{1,17},{17,33},{33,49},{49,1},{2,18}... | collective-permute-start | bytes 491528 | tf_op jit(solution)/shard_map/ppermute | solution.py:341
  38.3 8.1 %collective-permute-start.12 = (bf16[80,1024]{1,0:T(8,128)(2,1)}, bf16[80,1024]{1,0:T(8,128)(2,1)S(1)}, u32[]{:S(2)}, u32[]{:S(2)}) collective-permute-start(bf16[80,1024]{1,0:T(8,128)(2,1)} %collective-permute-done.9.high_far), channel_id=1, source_target_pairs={{0,48},{16,0},{32,16},{48,32},{1,49},{17,1},{33,17},{49,33},{2,50}... | collective-permute-start | bytes 491528 | tf_op jit(solution)/shard_map/ppermute | solution.py:341
  46.5 4.5 %collective-permute-start.14 = (bf16[4,32,1024]{2,1,0:T(8,128)(2,1)S(1)}, bf16[4,32,1024]{2,1,0:T(8,128)(2,1)S(1)}, u32[]{:S(2)}, u32[]{:S(2)}) collective-permute-start(bf16[4,32,1024]{2,1,0:T(8,128)(2,1)S(1)} %get-tuple-element.57.mine), channel_id=1, source_target_pairs={{0,4},{4,0},{1,5},{5,1},{2,6},{6,2},{3,7},{7,3},{8,12},{12,8},{9,1... | collective-permute-start | bytes 786440 | tf_op jit(solution)/shard_map/ppermute | solution.py:341
  47.9 5.0 %copy-start.4 = (bf16[2048,512]{1,0:T(8,128)(2,1)S(1)}, bf16[2048,512]{1,0:T(8,128)(2,1)}, u32[]{:S(2)}) copy-start(bf16[2048,512]{1,0:T(8,128)(2,1)} %wv.3) | copy-start | bytes 6291460
  47.9 5.0 %copy-start.6 = (bf16[2048,512]{1,0:T(8,128)(2,1)S(1)}, bf16[2048,512]{1,0:T(8,128)(2,1)}, u32[]{:S(2)}) copy-start(bf16[2048,512]{1,0:T(8,128)(2,1)} %wo.3) | copy-start | bytes 6291460
  50.9 2.1 %copy-start.2 = (bf16[2048,512]{1,0:T(8,128)(2,1)S(1)}, bf16[2048,512]{1,0:T(8,128)(2,1)}, u32[]{:S(2)}) copy-start(bf16[2048,512]{1,0:T(8,128)(2,1)} %wk.3) | copy-start | bytes 6291460
  50.9 2.1 %collective-permute-start.13 = (bf16[4,48,256]{2,1,0:T(8,128)(2,1)S(1)}, bf16[4,48,256]{2,1,0:T(8,128)(2,1)S(1)}, u32[]{:S(2)}, u32[]{:S(2)}) collective-permute-start(bf16[4,48,256]{2,1,0:T(8,128)(2,1)S(1)} %get-tuple-element.53), channel_id=1, source_target_pairs={{0,4},{4,0},{1,5},{5,1},{2,6},{6,2},{3,7},{7,3},{8,12},{12,8},{9,1... | collective-permute-start | bytes 294920 | tf_op jit(solution)/shard_map/ppermute | solution.py:341
  51.5 8.8 %collective-permute-start.18 = (bf16[4,128,256]{2,1,0:T(8,128)(2,1)S(1)}, bf16[4,128,256]{2,1,0:T(8,128)(2,1)S(1)}, u32[]{:S(2)}, u32[]{:S(2)}) collective-permute-start(bf16[4,128,256]{2,1,0:T(8,128)(2,1)S(1)} %get-tuple-element.67), channel_id=1, source_target_pairs={{0,64},{64,0},{1,65},{65,1},{2,66},{66,2},{3,67},{67,3},{4,68},{68... | collective-permute-start | bytes 786440 | tf_op jit(solution)/shard_map/ppermute | solution.py:341
  53.0 10.4 %copy-start.7 = (f32[16,512]{1,0:T(8,128)S(1)}, f32[16,512]{1,0:T(8,128)}, u32[]{:S(2)}) copy-start(f32[16,512]{1,0:T(8,128)} %up_gain.1) | copy-start | bytes 98308
  53.0 10.4 %copy-start.8 = (f32[4,512]{1,0:T(4,128)S(1)}, f32[4,512]{1,0:T(4,128)}, u32[]{:S(2)}) copy-start(f32[4,512]{1,0:T(4,128)} %first.1) | copy-start | bytes 24580
  53.0 10.4 %copy-start.9 = (f32[4,512]{1,0:T(4,128)S(1)}, f32[4,512]{1,0:T(4,128)}, u32[]{:S(2)}) copy-start(f32[4,512]{1,0:T(4,128)} %second.1) | copy-start | bytes 24580
  55.6 4.8 %collective-permute-start.15 = (bf16[80,640]{1,0:T(8,128)(2,1)S(1)}, bf16[80,640]{1,0:T(8,128)(2,1)S(1)}, u32[]{:S(2)}, u32[]{:S(2)}) collective-permute-start(bf16[80,640]{1,0:T(8,128)(2,1)S(1)} %get-tuple-element.60), channel_id=1, source_target_pairs={{0,1},{1,2},{2,3},{3,0},{4,5},{5,6},{6,7},{7,4},{8,9},{9,10},{10,1... | collective-permute-start | bytes 307208 | tf_op jit(solution)/shard_map/ppermute | solution.py:341
  56.6 6.8 %collective-permute-start.16 = (bf16[80,640]{1,0:T(8,128)(2,1)S(1)}, bf16[80,640]{1,0:T(8,128)(2,1)S(1)}, u32[]{:S(2)}, u32[]{:S(2)}) collective-permute-start(bf16[80,640]{1,0:T(8,128)(2,1)S(1)} %get-tuple-element.61), channel_id=1, source_target_pairs={{0,2},{1,3},{2,0},{3,1},{4,6},{5,7},{6,4},{7,5},{8,10},{9,11},{10,... | collective-permute-start | bytes 307208 | tf_op jit(solution)/shard_map/ppermute | solution.py:341
  58.7 4.7 %collective-permute-start.17 = (bf16[80,640]{1,0:T(8,128)(2,1)S(1)}, bf16[80,640]{1,0:T(8,128)(2,1)S(1)}, u32[]{:S(2)}, u32[]{:S(2)}) collective-permute-start(bf16[80,640]{1,0:T(8,128)(2,1)S(1)} %get-tuple-element.62), channel_id=1, source_target_pairs={{0,3},{1,0},{2,1},{3,2},{4,7},{5,4},{6,5},{7,6},{8,11},{9,8},{10,9... | collective-permute-start | bytes 307208 | tf_op jit(solution)/shard_map/ppermute | solution.py:341
  60.4 4.4 %collective-permute-start.19 = (bf16[4,64,256]{2,1,0:T(8,128)(2,1)S(1)}, bf16[4,64,256]{2,1,0:T(8,128)(2,1)S(1)}, u32[]{:S(2)}, u32[]{:S(2)}) collective-permute-start(bf16[4,64,256]{2,1,0:T(8,128)(2,1)S(1)} %get-tuple-element.69), channel_id=1, source_target_pairs={{0,4},{4,0},{1,5},{5,1},{2,6},{6,2},{3,7},{7,3},{8,12},{12,8},{9,1... | collective-permute-start | bytes 393224 | tf_op jit(solution)/shard_map/ppermute | solution.py:341

commit v8 on v7

--- a/solution.py
+++ b/solution.py
@@ -38,12 +38,6 @@
         self.ctx = (self.x * 2 + self.y) * 2 + self.core
 
 
-def in_three(a):
-    hi = a.astype(BF16).astype(F32)
-    lo = (a - hi).astype(BF16).astype(F32)
-    return hi, lo, (a - hi - lo).astype(BF16).astype(F32)
-
-
 def tap_weights(first, second):
     taps = jnp.concatenate([second[a : a + 1] * first for a in range(4)], axis=0)
     return jnp.concatenate([taps[15:16], taps[:15]], axis=0)
@@ -56,7 +50,7 @@
 
 
 def before_kernel(
-    lens, tokens_h, grad_h, first_h, second_h, up_h, gain_h, piece, row, last, gain,
+    lens, tokens_h, grad_h, first_h, second_h, up_h, gain_h, part, last, gco, gain,
     tokens, grad_out, first, second, up_gain, shift, sems,
 ):
     pairs = ((tokens_h, tokens), (first_h, first), (second_h, second), (grad_h, grad_out), (up_h, up_gain), (gain_h, gain))
@@ -73,26 +67,24 @@
     onward = jnp.sum(jnp.where(u == 0, 0.0, prod), axis=1)
     shift[0:8] = jnp.zeros((8, WL), F32)
     shift[8 : 8 + CL] = onward
-    part = own + shift[7 : 7 + CL]
-    piece[0:CL] = part.astype(BF16)
-    row[...] = jnp.broadcast_to(part[0:1], (8, WL))
-    piece[64:80] = jnp.concatenate(list(in_three(part[0:1])) + [jnp.zeros((13, WL), F32)], axis=0).astype(BF16)
+    part[...] = own + shift[7 : 7 + CL]
     last[...] = jnp.broadcast_to(shift[7 + CL : 8 + CL], (8, WL))
     for c in copies[3:]:
         c.wait()
     weighted = grad_out[...].astype(F32).reshape(CL, 16, WL) * mask * up_gain[...][None]
-    piece[CL : 2 * CL] = jnp.sum(weighted, axis=1).astype(BF16)
-
-
-def pile_kernel(piece, row, across, rim, rim_across, out):
+    gco[...] = jnp.sum(weighted, axis=1).astype(BF16)
+
+
+def piece_kernel(part, gco, rim, piece):
+    first = lax.broadcasted_iota(jnp.int32, (CL, WL), 0) == 0
+    piece[0:CL] = (part[...] + jnp.where(first, rim[0:1], 0.0)).astype(BF16)
+    piece[CL : 2 * CL] = gco[...]
+
+
+def pile_kernel(piece, across, out):
     y = Place().y
-    first = lax.broadcasted_iota(jnp.int32, (16, WL), 0) == 0
-    sent = across[64:80].astype(F32)
-    theirs = sent[0:1] + sent[1:2] + sent[2:3] + rim_across[0:1]
-    for src, at, top in ((piece, y * 64, row[0:1] + rim[0:1]), (across, 64 - y * 64, theirs)):
-        head = jnp.where(first, top, src[0:16].astype(F32))
-        out[pl.ds(pl.multiple_of(at, 64), 16)] = head.astype(BF16)
-        out[pl.ds(pl.multiple_of(at + 16, 16), 48)] = src[16:64]
+    out[pl.ds(pl.multiple_of(y * 64, 64), 64)] = piece[...]
+    out[pl.ds(pl.multiple_of(64 - y * 64, 64), 64)] = across[...]
 
 
 def bias_kernel(near, table, strip):
@@ -108,7 +100,7 @@
 
 
 def project_kernel(
-    p0, r1, r2, r3, gain, wq, wk, wv, wo, keep, send, blocks, mine, craw, nrm, gco, both
+    p0, r2, r1, r3, gain, wq, wk, wv, wo, keep, send, blocks, mine, craw, nrm, gco, both
 ):
     at = Place()
     z, core, x, y = at.z, at.core, at.x, at.y
@@ -245,7 +237,7 @@
             out[w] = dg(src[:, cols], res[w, 0:LC], 0, 0).astype(out.dtype)
 
 
-def sum_kernel(keep, got, r1, own, send):
+def sum_kernel(keep, got, r2, own, send):
     core = Place().core
     for w in range(4):
         for c, out in ((core, own), (1 - core, send)):
@@ -296,7 +288,7 @@
 
 
 def after_kernel(
-    lens, keep, r1, r2, r3, cz, inv, gain, first, second, up_gain, update, grad, rows
+    lens, keep, r2, r1, r3, cz, inv, gain, first, second, up_gain, update, grad, rows
 ):
     at = Place()
     ctx, doc_len, z = at.ctx, lens[0], at.z
@@ -346,9 +338,9 @@
     bias_table, buckets, up_gain, grad_out,
 ):
     weights = (w_query, w_key, w_value, w_out)
-    piece, row, last, gain = call(
+    part, last, gco, gain = call(
         before_kernel,
-        [((80, WL), BF16), ((8, WL), F32), ((8, WL), F32), ((1, D), F32)],
+        [((CL, WL), F32), ((8, WL), F32), ((CL, WL), BF16), ((1, D), F32)],
         (lengths, tokens[0], grad_out[0], conv_first, conv_second, up_gain, norm_gain[None]),
         [
             ((SEG, WL), BF16), ((SEG, WL), BF16), ((4, WL), F32), ((4, WL), F32), ((16, WL), F32),
@@ -359,13 +351,12 @@
     )
     line = ("x", "y", "core")
     rim = lax.ppermute(last, line, [(i, i + 1) for i in range(15)])
-    over = [(i, ((i + 1) ^ 2)) for i in range(15)]
+    (piece,) = call(piece_kernel, [((2 * CL, WL), BF16)], (part, gco, rim), smem=())
     across = shifted(piece, "y", 1)
-    rim_across = lax.ppermute(last, line, over)
     (piece,) = call(
         pile_kernel,
         [((PIECE, WL), BF16)],
-        (piece, row, across, rim, rim_across),
+        (piece, across),
         smem=(),
         flops=6 * 10**9,
     )
@@ -383,7 +374,8 @@
         (jnp.broadcast_to(near[None], (8, n)), bias_table),
         smem=(1,),
     )
-    pieces = [piece] + [shifted(piece, "tensor", s) for s in (1, 2, 3)]
+    far = shifted(piece, "tensor", 2)
+    pieces = [piece, far, shifted(piece, "tensor", 1), shifted(piece, "tensor", 3)]
     keep, send, blocks, crow = call(
         project_kernel,
         [((64, 4 * HW), BF16), ((80, 4 * HW), BF16), ((4, CL, 4 * HW), BF16), ((CL, D), BF16)],
@@ -439,11 +431,11 @@
         smem=(),
         flops=10**9,
     )
-    r1, r2, r3 = shifted(m1, "tensor", 1), shifted(m2, "tensor", 2), shifted(m3, "tensor", 3)
+    r2, r1, r3 = shifted(m2, "tensor", 2), shifted(m1, "tensor", 1), shifted(m3, "tensor", 3)
     dw_own, dw_other = call(
         sum_kernel,
         [((4, 64, HW), F32), ((4, 64, HW), BF16)],
-        (dw_keep, dw_got, r1),
+        (dw_keep, dw_got, r2),
         smem=(),
     )
     dw_other = shifted(dw_other, "core", 1)
@@ -458,7 +450,7 @@
     update, grad_tokens = call(
         after_kernel,
         [((SEG, WL), BF16)] * 2,
-        (lengths, own, r1, r2, r3, cz, inv, gain, conv_first, conv_second, up_gain),
+        (lengths, own, r2, r1, r3, cz, inv, gain, conv_first, conv_second, up_gain),
         [((ROWS, WL), F32)],
         flops=2 * 10**10,
         typed=False,

time: 66.3 us -> 66.6 us (level)
  starting transfers between devices: 33.3 us -> 34.5 us
    ppermute x1 -> x0, waiting for transfers between devices: 4.62 us -> none  [local(): rim_across = lax.ppermute(last, line, over)]
    ppermute x1, starting transfers between devices: 2.71 us -> 6.21 us  [local(): rim = lax.ppermute(last, line, [(i, i + 1) for i in range(15)])]
    ppermute x18, waiting for transfers between devices: 11.9 us -> 15.2 us  [shifted(): return lax.ppermute(x, axis, [(i, (i + steps) % n) for i in range(n)])]
    ppermute x1 -> x0, starting transfers between devices: 1.92 us -> none  [local(): rim_across = lax.ppermute(last, line, over)]
    ppermute x1, waiting for transfers between devices: 0.01 us -> 0.85 us  [local(): rim = lax.ppermute(last, line, [(i, i + 1) for i in range(15)])]
    pallas_call x13 -> x14, Pallas kernels: 13.8 us -> 13.8 us  [call(): pl.pallas_call(kernel, out_shape=[pltpu.VMEM(s, d) if typed else jax.Shap...]
  transfers between devices with their start and end apart: 20 -> 19, of which waited for: 10 -> 9; matrix products, arithmetic and copies ran while one was open for 1% -> 1% of each run, Pallas kernels for 14% -> 14%
where the time goes in v8:
time: 66.6 us; the launch traced here: 66.4 us
  starting transfers between devices  34.5 us (52%)
  waiting for transfers between devices  16 us (24%)
  Pallas kernels  13.8 us (21%)
  between operations  1.47 us (2%)
    ppermute x18, starting transfers between devices, shifted(): return lax.ppermute(x, axis, [(i, (i + steps) % n) for i in range(n)])  28.3 us
    ppermute x18, waiting for transfers between devices, shifted(): return lax.ppermute(x, axis, [(i, (i + steps) % n) for i in range(n)])  15.2 us
    pallas_call x14, Pallas kernels, call(): pl.pallas_call(kernel, out_shape=[pltpu.VMEM(s, d) if typed else jax.Shap...  13.8 us
    ppermute x1, starting transfers between devices, local(): rim = lax.ppermute(last, line, [(i, i + 1) for i in range(15)])  6.21 us
  transfers between devices with their start and end apart: 19, of which 9 were waited for; matrix products, arithmetic and copies ran while one was open for 1% of the time, Pallas kernels for 14%

profile of v8, /device:TPU:1, one launch (start us, length us, event | category | flops | bytes accessed | tf_op | source)
XLA Modules:
  0.0 66.4 jit_solution(7591376233153501949)
XLA Ops:
  1.3 1.9 %shard_map.172 = (f32[32,512]{1,0:T(8,128)S(1)}, f32[8,512]{1,0:T(8,128)S(1)}, bf16[32,512]{1,0:T(8,128)(2,1)S(1)}, f32[1,2048]{1,0:T(1,128)S(1)}) custom-call(s32[1]{0:T(128)S(6)} %copy.20.lens, bf16[512,512]{1,0:T(8,128)(2,1)} %bitcast.7, bf16[512,512]{1,0:T(8,128)(2,1)} %bitcast.8, f32[4,512]{1,0:T(4,128)} %first.1, f32[4,512]{1,0:T(4,128)} %second.1, ...), custom_call_target="tpu_custom_call" | custom-call | tf_op jit(solution)/shard_map/pallas_call | solution.py:320
  3.2 6.2 %collective-permute-start = (f32[8,512]{1,0:T(8,128)S(1)}, f32[8,512]{1,0:T(8,128)S(1)}, u32[]{:S(2)}, u32[]{:S(2)}) collective-permute-start(f32[8,512]{1,0:T(8,128)S(1)} %get-tuple-element.42), channel_id=1, source_target_pairs={{0,4},{4,8},{8,12},{12,16},{16,20},{20,24},{24,28},{28,32},{32,36}... | collective-permute-start | bytes 49160 | tf_op jit(solution)/shard_map/ppermute | solution.py:353
  9.4 0.8 %collective-permute-done.rim = f32[8,512]{1,0:T(8,128)S(1)} collective-permute-done((f32[8,512]{1,0:T(8,128)S(1)}, f32[8,512]{1,0:T(8,128)S(1)}, u32[]{:S(2)}, u32[]{:S(2)}) %collective-permute-start) | collective-permute-done | bytes 16416 | tf_op jit(solution)/shard_map/ppermute | solution.py:353
  10.3 1.1 %collective-permute-start.1 = (bf16[64,512]{1,0:T(8,128)(2,1)S(1)}, bf16[64,512]{1,0:T(8,128)(2,1)S(1)}, u32[]{:S(2)}, u32[]{:S(2)}) collective-permute-start(bf16[64,512]{1,0:T(8,128)(2,1)S(1)} %shard_map.173.piece), channel_id=1, source_target_pairs={{0,8},{8,0},{1,9},{9,1},{2,10},{10,2},{3,11},{11,3},{4,12},{12,4},... | collective-permute-start | bytes 196616 | tf_op jit(solution)/shard_map/ppermute | solution.py:333
  11.4 3.6 %collective-permute-done.1.across = bf16[64,512]{1,0:T(8,128)(2,1)S(1)} collective-permute-done((bf16[64,512]{1,0:T(8,128)(2,1)S(1)}, bf16[64,512]{1,0:T(8,128)(2,1)S(1)}, u32[]{:S(2)}, u32[]{:S(2)}) %collective-permute-start.1) | collective-permute-done | bytes 65568 | tf_op jit(solution)/shard_map/ppermute | solution.py:333
  15.0 3.7 %collective-permute-start.2 = (bf16[128,512]{1,0:T(8,128)(2,1)S(1)}, bf16[128,512]{1,0:T(8,128)(2,1)S(1)}, u32[]{:S(2)}, u32[]{:S(2)}) collective-permute-start(bf16[128,512]{1,0:T(8,128)(2,1)S(1)} %shard_map.174.p0), channel_id=1, source_target_pairs={{0,2},{1,3},{2,0},{3,1},{4,6},{5,7},{6,4},{7,5},{8,10},{9,11},{10,... | collective-permute-start | bytes 393224 | tf_op jit(solution)/shard_map/ppermute | solution.py:333
  18.7 0.7 %collective-permute-start.3 = (bf16[128,512]{1,0:T(8,128)(2,1)S(1)}, bf16[128,512]{1,0:T(8,128)(2,1)S(1)}, u32[]{:S(2)}, u32[]{:S(2)}) collective-permute-start(bf16[128,512]{1,0:T(8,128)(2,1)S(1)} %shard_map.174.p0), channel_id=1, source_target_pairs={{0,1},{1,2},{2,3},{3,0},{4,5},{5,6},{6,7},{7,4},{8,9},{9,10},{10,1... | collective-permute-start | bytes 393224 | tf_op jit(solution)/shard_map/ppermute | solution.py:333
  19.5 1.9 %collective-permute-start.4 = (bf16[128,512]{1,0:T(8,128)(2,1)S(1)}, bf16[128,512]{1,0:T(8,128)(2,1)S(1)}, u32[]{:S(2)}, u32[]{:S(2)}) collective-permute-start(bf16[128,512]{1,0:T(8,128)(2,1)S(1)} %shard_map.174.p0), channel_id=1, source_target_pairs={{0,3},{1,0},{2,1},{3,2},{4,7},{5,4},{6,5},{7,6},{8,11},{9,8},{10,9... | collective-permute-start | bytes 393224 | tf_op jit(solution)/shard_map/ppermute | solution.py:333
  21.4 3.4 %collective-permute-done.3.r1 = bf16[128,512]{1,0:T(8,128)(2,1)S(1)} collective-permute-done((bf16[128,512]{1,0:T(8,128)(2,1)S(1)}, bf16[128,512]{1,0:T(8,128)(2,1)S(1)}, u32[]{:S(2)}, u32[]{:S(2)}) %collective-permute-start.3) | collective-permute-done | bytes 131104 | tf_op jit(solution)/shard_map/ppermute | solution.py:333
  24.8 1.6 %shard_map.175 = (bf16[64,1024]{1,0:T(8,128)(2,1)S(1)}, bf16[80,1024]{1,0:T(8,128)(2,1)S(1)}, bf16[4,32,1024]{2,1,0:T(8,128)(2,1)S(1)}, bf16[32,2048]{1,0:T(8,128)(2,1)S(1)}) custom-call(bf16[128,512]{1,0:T(8,128)(2,1)S(1)} %shard_map.174.p0, bf16[128,512]{1,0:T(8,128)(2,1)S(1)} %collective-permute-done.2.r2, ...), custom_call_target="tpu_custom_call" | custom-call | flops 1000000000 | tf_op jit(solution)/shard_map/pallas_call | solution.py:320
  26.4 2.3 %collective-permute-start.5 = (bf16[80,1024]{1,0:T(8,128)(2,1)S(1)}, bf16[80,1024]{1,0:T(8,128)(2,1)S(1)}, u32[]{:S(2)}, u32[]{:S(2)}) collective-permute-start(bf16[80,1024]{1,0:T(8,128)(2,1)S(1)} %get-tuple-element.45), channel_id=1, source_target_pairs={{0,4},{4,0},{1,5},{5,1},{2,6},{6,2},{3,7},{7,3},{8,12},{12,8},{9,1... | collective-permute-start | bytes 491528 | tf_op jit(solution)/shard_map/ppermute | solution.py:333
  28.7 1.0 %collective-permute-done.5.swapped = bf16[80,1024]{1,0:T(8,128)(2,1)S(1)} collective-permute-done((bf16[80,1024]{1,0:T(8,128)(2,1)S(1)}, bf16[80,1024]{1,0:T(8,128)(2,1)S(1)}, u32[]{:S(2)}, u32[]{:S(2)}) %collective-permute-start.5) | collective-permute-done | bytes 163872 | tf_op jit(solution)/shard_map/ppermute | solution.py:333
  29.8 2.5 %collective-permute-start.6 = (bf16[80,1024]{1,0:T(8,128)(2,1)S(1)}, bf16[80,1024]{1,0:T(8,128)(2,1)}, u32[]{:S(2)}, u32[]{:S(2)}) collective-permute-start(bf16[80,1024]{1,0:T(8,128)(2,1)S(1)} %get-tuple-element.48), channel_id=1, source_target_pairs={{0,16},{16,32},{32,48},{48,0},{1,17},{17,33},{33,49},{49,1},{2,18}... | collective-permute-start | bytes 491528 | tf_op jit(solution)/shard_map/ppermute | solution.py:333
  32.3 1.3 %collective-permute-start.8 = (bf16[80,1024]{1,0:T(8,128)(2,1)S(1)}, bf16[80,1024]{1,0:T(8,128)(2,1)}, u32[]{:S(2)}, u32[]{:S(2)}) collective-permute-start(bf16[80,1024]{1,0:T(8,128)(2,1)S(1)} %get-tuple-element.50), channel_id=1, source_target_pairs={{0,48},{16,0},{32,16},{48,32},{1,49},{17,1},{33,17},{49,33},{2,50}... | collective-permute-start | bytes 491528 | tf_op jit(solution)/shard_map/ppermute | solution.py:333
  33.6 0.8 %shard_map.176 = (bf16[96,1024]{1,0:T(8,128)(2,1)}, bf16[112,1024]{1,0:T(8,128)(2,1)}, bf16[160,1024]{1,0:T(8,128)(2,1)S(1)}) custom-call(bf16[64,1024]{1,0:T(8,128)(2,1)S(1)} %get-tuple-element.44.keep, bf16[80,1024]{1,0:T(8,128)(2,1)S(1)} %collective-permute-done.5.swapped, bf16[4,32,1024]{2,1,0:T(8,128)(2,1)S(1)} %get-tuple-element.46.blocks), custom_call_target="tpu_custom_call" | custom-call | tf_op jit(solution)/shard_map/pallas_call | solution.py:320
  34.5 1.4 %collective-permute-start.9 = (bf16[112,1024]{1,0:T(8,128)(2,1)}, bf16[112,1024]{1,0:T(8,128)(2,1)S(1)}, u32[]{:S(2)}, u32[]{:S(2)}) collective-permute-start(bf16[112,1024]{1,0:T(8,128)(2,1)} %get-tuple-element.51), channel_id=1, source_target_pairs={{0,48},{16,0},{32,16},{48,32},{1,49},{17,1},{33,17},{49,33},{2,50}... | collective-permute-start | bytes 688136 | tf_op jit(solution)/shard_map/ppermute | solution.py:333
  35.9 2.0 %collective-permute-done.6.low_far = bf16[80,1024]{1,0:T(8,128)(2,1)} collective-permute-done((bf16[80,1024]{1,0:T(8,128)(2,1)S(1)}, bf16[80,1024]{1,0:T(8,128)(2,1)}, u32[]{:S(2)}, u32[]{:S(2)}) %collective-permute-start.6) | collective-permute-done | bytes 163872 | tf_op jit(solution)/shard_map/ppermute | solution.py:333
  37.9 2.7 %collective-permute-start.11 = (bf16[80,1024]{1,0:T(8,128)(2,1)}, bf16[80,1024]{1,0:T(8,128)(2,1)S(1)}, u32[]{:S(2)}, u32[]{:S(2)}) collective-permute-start(bf16[80,1024]{1,0:T(8,128)(2,1)} %collective-permute-done.8.high_far), channel_id=1, source_target_pairs={{0,48},{16,0},{32,16},{48,32},{1,49},{17,1},{33,17},{49,33},{2,50}... | collective-permute-start | bytes 491528 | tf_op jit(solution)/shard_map/ppermute | solution.py:333
  41.1 1.1 %shard_map.178.strip = f32[2,128,512]{2,1,0:T(8,128)S(1)} custom-call(s32[8,640]{1,0:T(8,128)S(1)} %broadcast_in_dim.20.near, f32[32,4]{1,0:T(8,128)S(1)} %copy.19.table), custom_call_target="tpu_custom_call" | custom-call | tf_op jit(solution)/shard_map/pallas_call | solution.py:320
  42.5 3.5 %collective-permute-done.10.far_low = bf16[80,1024]{1,0:T(8,128)(2,1)S(1)} collective-permute-done((bf16[80,1024]{1,0:T(8,128)(2,1)}, bf16[80,1024]{1,0:T(8,128)(2,1)S(1)}, u32[]{:S(2)}, u32[]{:S(2)}) %collective-permute-start.10) | collective-permute-done | bytes 163872 | tf_op jit(solution)/shard_map/ppermute | solution.py:333
  46.0 2.2 %collective-permute-start.13 = (bf16[4,32,1024]{2,1,0:T(8,128)(2,1)S(1)}, bf16[4,32,1024]{2,1,0:T(8,128)(2,1)S(1)}, u32[]{:S(2)}, u32[]{:S(2)}) collective-permute-start(bf16[4,32,1024]{2,1,0:T(8,128)(2,1)S(1)} %get-tuple-element.57.mine), channel_id=1, source_target_pairs={{0,4},{4,0},{1,5},{5,1},{2,6},{6,2},{3,7},{7,3},{8,12},{12,8},{9,1... | collective-permute-start | bytes 786440 | tf_op jit(solution)/shard_map/ppermute | solution.py:333
  48.2 2.9 %shard_map.179 = (bf16[4,528,256]{2,1,0:T(8,128)(2,1)S(1)}, bf16[4,48,256]{2,1,0:T(8,128)(2,1)S(1)}, bf16[4,48,256]{2,1,0:T(8,128)(2,1)S(1)}) custom-call(s32[1]{0:T(128)S(6)} %copy.20.lens, bf16[160,1024]{1,0:T(8,128)(2,1)S(1)} %get-tuple-element.47.b0, bf16[80,1024]{1,0:T(8,128)(2,1)} %collective-permute-done.6.low_far, ...), custom_call_target="tpu_custom_call" | custom-call | flops 6000000000 | tf_op jit(solution)/shard_map/pallas_call | solution.py:320
  51.3 0.5 shard_map.181
  51.8 1.4 %collective-permute-start.17 = (bf16[4,128,256]{2,1,0:T(8,128)(2,1)S(1)}, bf16[4,128,256]{2,1,0:T(8,128)(2,1)S(1)}, u32[]{:S(2)}, u32[]{:S(2)}) collective-permute-start(bf16[4,128,256]{2,1,0:T(8,128)(2,1)S(1)} %get-tuple-element.67), channel_id=1, source_target_pairs={{0,64},{64,0},{1,65},{65,1},{2,66},{66,2},{3,67},{67,3},{4,68},{68... | collective-permute-start | bytes 786440 | tf_op jit(solution)/shard_map/ppermute | solution.py:333
  53.2 2.6 %shard_map.182 = (bf16[80,640]{1,0:T(8,128)(2,1)S(1)}, bf16[80,640]{1,0:T(8,128)(2,1)S(1)}, bf16[80,640]{1,0:T(8,128)(2,1)S(1)}, f32[80,640]{1,0:T(8,128)S(1)}, ...) custom-call(bf16[4,48,256]{2,1,0:T(8,128)(2,1)S(1)} %get-tuple-element.52.keep_r, ...), custom_call_target="tpu_custom_call" | custom-call | flops 1000000000 | tf_op jit(solution)/shard_map/pallas_call | solution.py:320
  55.8 1.2 %collective-permute-start.14 = (bf16[80,640]{1,0:T(8,128)(2,1)S(1)}, bf16[80,640]{1,0:T(8,128)(2,1)S(1)}, u32[]{:S(2)}, u32[]{:S(2)}) collective-permute-start(bf16[80,640]{1,0:T(8,128)(2,1)S(1)} %get-tuple-element.60), channel_id=1, source_target_pairs={{0,2},{1,3},{2,0},{3,1},{4,6},{5,7},{6,4},{7,5},{8,10},{9,11},{10,... | collective-permute-start | bytes 307208 | tf_op jit(solution)/shard_map/ppermute | solution.py:333
  57.1 2.4 %collective-permute-start.15 = (bf16[80,640]{1,0:T(8,128)(2,1)S(1)}, bf16[80,640]{1,0:T(8,128)(2,1)S(1)}, u32[]{:S(2)}, u32[]{:S(2)}) collective-permute-start(bf16[80,640]{1,0:T(8,128)(2,1)S(1)} %get-tuple-element.61), channel_id=1, source_target_pairs={{0,1},{1,2},{2,3},{3,0},{4,5},{5,6},{6,7},{7,4},{8,9},{9,10},{10,1... | collective-permute-start | bytes 307208 | tf_op jit(solution)/shard_map/ppermute | solution.py:333
  59.4 0.3 collective-permute-start.16
  59.7 1.2 %collective-permute-done.14.r2 = bf16[80,640]{1,0:T(8,128)(2,1)S(1)} collective-permute-done((bf16[80,640]{1,0:T(8,128)(2,1)S(1)}, bf16[80,640]{1,0:T(8,128)(2,1)S(1)}, u32[]{:S(2)}, u32[]{:S(2)}) %collective-permute-start.14) | collective-permute-done | bytes 102432 | tf_op jit(solution)/shard_map/ppermute | solution.py:333
  61.0 3.0 %collective-permute-start.18 = (bf16[4,64,256]{2,1,0:T(8,128)(2,1)S(1)}, bf16[4,64,256]{2,1,0:T(8,128)(2,1)S(1)}, u32[]{:S(2)}, u32[]{:S(2)}) collective-permute-start(bf16[4,64,256]{2,1,0:T(8,128)(2,1)S(1)} %get-tuple-element.69), channel_id=1, source_target_pairs={{0,4},{4,0},{1,5},{5,1},{2,6},{6,2},{3,7},{7,3},{8,12},{12,8},{9,1... | collective-permute-start | bytes 393224 | tf_op jit(solution)/shard_map/ppermute | solution.py:333
  64.2 1.4 %shard_map.183 = (bf16[512,512]{1,0:T(8,128)(2,1)}, bf16[512,512]{1,0:T(8,128)(2,1)}) custom-call(s32[1]{0:T(128)S(6)} %copy.20.lens, f32[80,640]{1,0:T(8,128)S(1)} %get-tuple-element.59.keep, bf16[80,640]{1,0:T(8,128)(2,1)S(1)} %collective-permute-done.14.r2, bf16[80,640]{1,0:T(8,128)(2,1)S(1)} %collective-permute-done.15.r1, ...), custom_call_target="tpu_custom_call" | custom-call | flops 20000000000 | tf_op jit(solution)/shard_map/pallas_call | solution.py:320
  65.6 0.8 %shard_map.185 = (f32[64,512]{1,0:T(8,128)}, f32[64,512]{1,0:T(8,128)}, f32[64,512]{1,0:T(8,128)}, f32[64,512]{1,0:T(8,128)}) custom-call(f32[4,64,256]{2,1,0:T(8,128)S(1)} %get-tuple-element.68.own, bf16[4,64,256]{2,1,0:T(8,128)(2,1)S(1)} %collective-permute-done.18.other), custom_call_target="tpu_custom_call" | custom-call | flops 6000000000 | tf_op jit(solution)/shard_map/pallas_call | solution.py:320
  (52 shorter events, 1.4 us)
Async XLA Ops:
  3.2 7.1 %collective-permute-start = (f32[8,512]{1,0:T(8,128)S(1)}, f32[8,512]{1,0:T(8,128)S(1)}, u32[]{:S(2)}, u32[]{:S(2)}) collective-permute-start(f32[8,512]{1,0:T(8,128)S(1)} %get-tuple-element.42), channel_id=1, source_target_pairs={{0,4},{4,8},{8,12},{12,16},{16,20},{20,24},{24,28},{28,32},{32,36}... | collective-permute-start | bytes 49160 | tf_op jit(solution)/shard_map/ppermute | solution.py:353
  10.3 14.5 %copy-start = (bf16[2048,512]{1,0:T(8,128)(2,1)S(1)}, bf16[2048,512]{1,0:T(8,128)(2,1)}, u32[]{:S(2)}) copy-start(bf16[2048,512]{1,0:T(8,128)(2,1)} %wq.3) | copy-start | bytes 6291460
  10.3 14.5 %copy-start.1 = (bf16[2048,512]{1,0:T(8,128)(2,1)S(1)}, bf16[2048,512]{1,0:T(8,128)(2,1)}, u32[]{:S(2)}) copy-start(bf16[2048,512]{1,0:T(8,128)(2,1)} %wk.3) | copy-start | bytes 6291460
  10.3 14.5 %copy-start.3 = (bf16[2048,512]{1,0:T(8,128)(2,1)S(1)}, bf16[2048,512]{1,0:T(8,128)(2,1)}, u32[]{:S(2)}) copy-start(bf16[2048,512]{1,0:T(8,128)(2,1)} %wv.3) | copy-start | bytes 6291460
  10.3 14.5 %copy-start.5 = (bf16[2048,512]{1,0:T(8,128)(2,1)S(1)}, bf16[2048,512]{1,0:T(8,128)(2,1)}, u32[]{:S(2)}) copy-start(bf16[2048,512]{1,0:T(8,128)(2,1)} %wo.3) | copy-start | bytes 6291460
  10.3 4.7 %collective-permute-start.1 = (bf16[64,512]{1,0:T(8,128)(2,1)S(1)}, bf16[64,512]{1,0:T(8,128)(2,1)S(1)}, u32[]{:S(2)}, u32[]{:S(2)}) collective-permute-start(bf16[64,512]{1,0:T(8,128)(2,1)S(1)} %shard_map.173.piece), channel_id=1, source_target_pairs={{0,8},{8,0},{1,9},{9,1},{2,10},{10,2},{3,11},{11,3},{4,12},{12,4},... | collective-permute-start | bytes 196616 | tf_op jit(solution)/shard_map/ppermute | solution.py:333
  15.0 6.4 %collective-permute-start.2 = (bf16[128,512]{1,0:T(8,128)(2,1)S(1)}, bf16[128,512]{1,0:T(8,128)(2,1)S(1)}, u32[]{:S(2)}, u32[]{:S(2)}) collective-permute-start(bf16[128,512]{1,0:T(8,128)(2,1)S(1)} %shard_map.174.p0), channel_id=1, source_target_pairs={{0,2},{1,3},{2,0},{3,1},{4,6},{5,7},{6,4},{7,5},{8,10},{9,11},{10,... | collective-permute-start | bytes 393224 | tf_op jit(solution)/shard_map/ppermute | solution.py:333
  18.7 6.1 %collective-permute-start.3 = (bf16[128,512]{1,0:T(8,128)(2,1)S(1)}, bf16[128,512]{1,0:T(8,128)(2,1)S(1)}, u32[]{:S(2)}, u32[]{:S(2)}) collective-permute-start(bf16[128,512]{1,0:T(8,128)(2,1)S(1)} %shard_map.174.p0), channel_id=1, source_target_pairs={{0,1},{1,2},{2,3},{3,0},{4,5},{5,6},{6,7},{7,4},{8,9},{9,10},{10,1... | collective-permute-start | bytes 393224 | tf_op jit(solution)/shard_map/ppermute | solution.py:333
  19.5 5.3 %collective-permute-start.4 = (bf16[128,512]{1,0:T(8,128)(2,1)S(1)}, bf16[128,512]{1,0:T(8,128)(2,1)S(1)}, u32[]{:S(2)}, u32[]{:S(2)}) collective-permute-start(bf16[128,512]{1,0:T(8,128)(2,1)S(1)} %shard_map.174.p0), channel_id=1, source_target_pairs={{0,3},{1,0},{2,1},{3,2},{4,7},{5,4},{6,5},{7,6},{8,11},{9,8},{10,9... | collective-permute-start | bytes 393224 | tf_op jit(solution)/shard_map/ppermute | solution.py:333
  24.8 15.8 %copy-start.11 = (s32[512]{0:T(512)S(1)}, s32[512]{0:T(512)}, u32[]{:S(2)}) copy-start(s32[512]{0:T(512)} %param.23) | copy-start | bytes 6148
  24.8 16.2 %copy-start.10 = (f32[32,4]{0,1:T(4,128)S(1)}, f32[32,4]{0,1:T(4,128)}, u32[]{:S(2)}) copy-start(f32[32,4]{0,1:T(4,128)} %param.22) | copy-start | bytes 1540
  26.4 3.3 %collective-permute-start.5 = (bf16[80,1024]{1,0:T(8,128)(2,1)S(1)}, bf16[80,1024]{1,0:T(8,128)(2,1)S(1)}, u32[]{:S(2)}, u32[]{:S(2)}) collective-permute-start(bf16[80,1024]{1,0:T(8,128)(2,1)S(1)} %get-tuple-element.45), channel_id=1, source_target_pairs={{0,4},{4,0},{1,5},{5,1},{2,6},{6,2},{3,7},{7,3},{8,12},{12,8},{9,1... | collective-permute-start | bytes 491528 | tf_op jit(solution)/shard_map/ppermute | solution.py:333
  29.8 8.2 %collective-permute-start.6 = (bf16[80,1024]{1,0:T(8,128)(2,1)S(1)}, bf16[80,1024]{1,0:T(8,128)(2,1)}, u32[]{:S(2)}, u32[]{:S(2)}) collective-permute-start(bf16[80,1024]{1,0:T(8,128)(2,1)S(1)} %get-tuple-element.48), channel_id=1, source_target_pairs={{0,16},{16,32},{32,48},{48,0},{1,17},{17,33},{33,49},{49,1},{2,18}... | collective-permute-start | bytes 491528 | tf_op jit(solution)/shard_map/ppermute | solution.py:333
  32.3 5.7 %collective-permute-start.8 = (bf16[80,1024]{1,0:T(8,128)(2,1)S(1)}, bf16[80,1024]{1,0:T(8,128)(2,1)}, u32[]{:S(2)}, u32[]{:S(2)}) collective-permute-start(bf16[80,1024]{1,0:T(8,128)(2,1)S(1)} %get-tuple-element.50), channel_id=1, source_target_pairs={{0,48},{16,0},{32,16},{48,32},{1,49},{17,1},{33,17},{49,33},{2,50}... | collective-permute-start | bytes 491528 | tf_op jit(solution)/shard_map/ppermute | solution.py:333
  34.5 8.0 %collective-permute-start.9 = (bf16[112,1024]{1,0:T(8,128)(2,1)}, bf16[112,1024]{1,0:T(8,128)(2,1)S(1)}, u32[]{:S(2)}, u32[]{:S(2)}) collective-permute-start(bf16[112,1024]{1,0:T(8,128)(2,1)} %get-tuple-element.51), channel_id=1, source_target_pairs={{0,48},{16,0},{32,16},{48,32},{1,49},{17,1},{33,17},{49,33},{2,50}... | collective-permute-start | bytes 688136 | tf_op jit(solution)/shard_map/ppermute | solution.py:333
  35.8 6.6 %collective-permute-start.7 = (bf16[96,1024]{1,0:T(8,128)(2,1)}, bf16[96,1024]{1,0:T(8,128)(2,1)S(1)}, u32[]{:S(2)}, u32[]{:S(2)}) collective-permute-start(bf16[96,1024]{1,0:T(8,128)(2,1)} %get-tuple-element.49), channel_id=1, source_target_pairs={{0,16},{16,32},{32,48},{48,0},{1,17},{17,33},{33,49},{49,1},{2,18}... | collective-permute-start | bytes 589832 | tf_op jit(solution)/shard_map/ppermute | solution.py:333
  37.9 8.0 %collective-permute-start.10 = (bf16[80,1024]{1,0:T(8,128)(2,1)}, bf16[80,1024]{1,0:T(8,128)(2,1)S(1)}, u32[]{:S(2)}, u32[]{:S(2)}) collective-permute-start(bf16[80,1024]{1,0:T(8,128)(2,1)} %collective-permute-done.6.low_far), channel_id=1, source_target_pairs={{0,16},{16,32},{32,48},{48,0},{1,17},{17,33},{33,49},{49,1},{2,18}... | collective-permute-start | bytes 491528 | tf_op jit(solution)/shard_map/ppermute | solution.py:333
  37.9 8.0 %collective-permute-start.11 = (bf16[80,1024]{1,0:T(8,128)(2,1)}, bf16[80,1024]{1,0:T(8,128)(2,1)S(1)}, u32[]{:S(2)}, u32[]{:S(2)}) collective-permute-start(bf16[80,1024]{1,0:T(8,128)(2,1)} %collective-permute-done.8.high_far), channel_id=1, source_target_pairs={{0,48},{16,0},{32,16},{48,32},{1,49},{17,1},{33,17},{49,33},{2,50}... | collective-permute-start | bytes 491528 | tf_op jit(solution)/shard_map/ppermute | solution.py:333
  46.0 5.3 %collective-permute-start.13 = (bf16[4,32,1024]{2,1,0:T(8,128)(2,1)S(1)}, bf16[4,32,1024]{2,1,0:T(8,128)(2,1)S(1)}, u32[]{:S(2)}, u32[]{:S(2)}) collective-permute-start(bf16[4,32,1024]{2,1,0:T(8,128)(2,1)S(1)} %get-tuple-element.57.mine), channel_id=1, source_target_pairs={{0,4},{4,0},{1,5},{5,1},{2,6},{6,2},{3,7},{7,3},{8,12},{12,8},{9,1... | collective-permute-start | bytes 786440 | tf_op jit(solution)/shard_map/ppermute | solution.py:333
  48.2 5.0 %copy-start.4 = (bf16[2048,512]{1,0:T(8,128)(2,1)S(1)}, bf16[2048,512]{1,0:T(8,128)(2,1)}, u32[]{:S(2)}) copy-start(bf16[2048,512]{1,0:T(8,128)(2,1)} %wv.3) | copy-start | bytes 6291460
  48.2 5.0 %copy-start.6 = (bf16[2048,512]{1,0:T(8,128)(2,1)S(1)}, bf16[2048,512]{1,0:T(8,128)(2,1)}, u32[]{:S(2)}) copy-start(bf16[2048,512]{1,0:T(8,128)(2,1)} %wo.3) | copy-start | bytes 6291460
  51.1 2.1 %copy-start.2 = (bf16[2048,512]{1,0:T(8,128)(2,1)S(1)}, bf16[2048,512]{1,0:T(8,128)(2,1)}, u32[]{:S(2)}) copy-start(bf16[2048,512]{1,0:T(8,128)(2,1)} %wk.3) | copy-start | bytes 6291460
  51.2 2.0 %collective-permute-start.12 = (bf16[4,48,256]{2,1,0:T(8,128)(2,1)S(1)}, bf16[4,48,256]{2,1,0:T(8,128)(2,1)S(1)}, u32[]{:S(2)}, u32[]{:S(2)}) collective-permute-start(bf16[4,48,256]{2,1,0:T(8,128)(2,1)S(1)} %get-tuple-element.53), channel_id=1, source_target_pairs={{0,4},{4,0},{1,5},{5,1},{2,6},{6,2},{3,7},{7,3},{8,12},{12,8},{9,1... | collective-permute-start | bytes 294920 | tf_op jit(solution)/shard_map/ppermute | solution.py:333
  51.8 9.1 %collective-permute-start.17 = (bf16[4,128,256]{2,1,0:T(8,128)(2,1)S(1)}, bf16[4,128,256]{2,1,0:T(8,128)(2,1)S(1)}, u32[]{:S(2)}, u32[]{:S(2)}) collective-permute-start(bf16[4,128,256]{2,1,0:T(8,128)(2,1)S(1)} %get-tuple-element.67), channel_id=1, source_target_pairs={{0,64},{64,0},{1,65},{65,1},{2,66},{66,2},{3,67},{67,3},{4,68},{68... | collective-permute-start | bytes 786440 | tf_op jit(solution)/shard_map/ppermute | solution.py:333
  53.2 11.0 %copy-start.7 = (f32[16,512]{1,0:T(8,128)S(1)}, f32[16,512]{1,0:T(8,128)}, u32[]{:S(2)}) copy-start(f32[16,512]{1,0:T(8,128)} %up_gain.1) | copy-start | bytes 98308
  53.2 10.9 %copy-start.8 = (f32[4,512]{1,0:T(4,128)S(1)}, f32[4,512]{1,0:T(4,128)}, u32[]{:S(2)}) copy-start(f32[4,512]{1,0:T(4,128)} %first.1) | copy-start | bytes 24580
  53.2 10.9 %copy-start.9 = (f32[4,512]{1,0:T(4,128)S(1)}, f32[4,512]{1,0:T(4,128)}, u32[]{:S(2)}) copy-start(f32[4,512]{1,0:T(4,128)} %second.1) | copy-start | bytes 24580
  55.8 5.1 %collective-permute-start.14 = (bf16[80,640]{1,0:T(8,128)(2,1)S(1)}, bf16[80,640]{1,0:T(8,128)(2,1)S(1)}, u32[]{:S(2)}, u32[]{:S(2)}) collective-permute-start(bf16[80,640]{1,0:T(8,128)(2,1)S(1)} %get-tuple-element.60), channel_id=1, source_target_pairs={{0,2},{1,3},{2,0},{3,1},{4,6},{5,7},{6,4},{7,5},{8,10},{9,11},{10,... | collective-permute-start | bytes 307208 | tf_op jit(solution)/shard_map/ppermute | solution.py:333
  57.1 6.9 %collective-permute-start.15 = (bf16[80,640]{1,0:T(8,128)(2,1)S(1)}, bf16[80,640]{1,0:T(8,128)(2,1)S(1)}, u32[]{:S(2)}, u32[]{:S(2)}) collective-permute-start(bf16[80,640]{1,0:T(8,128)(2,1)S(1)} %get-tuple-element.61), channel_id=1, source_target_pairs={{0,1},{1,2},{2,3},{3,0},{4,5},{5,6},{6,7},{7,4},{8,9},{9,10},{10,1... | collective-permute-start | bytes 307208 | tf_op jit(solution)/shard_map/ppermute | solution.py:333
  59.4 4.7 %collective-permute-start.16 = (bf16[80,640]{1,0:T(8,128)(2,1)S(1)}, bf16[80,640]{1,0:T(8,128)(2,1)S(1)}, u32[]{:S(2)}, u32[]{:S(2)}) collective-permute-start(bf16[80,640]{1,0:T(8,128)(2,1)S(1)} %get-tuple-element.62), channel_id=1, source_target_pairs={{0,3},{1,0},{2,1},{3,2},{4,7},{5,4},{6,5},{7,6},{8,11},{9,8},{10,9... | collective-permute-start | bytes 307208 | tf_op jit(solution)/shard_map/ppermute | solution.py:333
  61.0 4.6 %collective-permute-start.18 = (bf16[4,64,256]{2,1,0:T(8,128)(2,1)S(1)}, bf16[4,64,256]{2,1,0:T(8,128)(2,1)S(1)}, u32[]{:S(2)}, u32[]{:S(2)}) collective-permute-start(bf16[4,64,256]{2,1,0:T(8,128)(2,1)S(1)} %get-tuple-element.69), channel_id=1, source_target_pairs={{0,4},{4,0},{1,5},{5,1},{2,6},{6,2},{3,7},{7,3},{8,12},{12,8},{9,1... | collective-permute-start | bytes 393224 | tf_op jit(solution)/shard_map/ppermute | solution.py:333

commit v9 on v7

--- a/solution.py
+++ b/solution.py
@@ -108,7 +108,7 @@
 
 
 def project_kernel(
-    p0, r1, r2, r3, gain, wq, wk, wv, wo, keep, send, blocks, mine, craw, nrm, gco, both
+    p0, r2, r1, r3, gain, wq, wk, wv, wo, keep, send, blocks, mine, craw, nrm, gco, both
 ):
     at = Place()
     z, core, x, y = at.z, at.core, at.x, at.y
@@ -228,7 +228,7 @@
     send[...] = res[:, pl.ds(pl.multiple_of(peer * CL, CL), ROWS)]
 
 
-def weights_kernel(res, mine, other, keep, send, nb, gb):
+def weights_kernel(res, mine, other, send_r, keep, to_core, to_dp, to_both, nb, gb, tile):
     at = Place()
     core, x, dp = at.core, at.x, at.dp
     for s in range(4):
@@ -240,17 +240,12 @@
                 gb[rows] = src[s, :, i * 512 + 256 : i * 512 + 512]
     for w in range(4):
         src = gb if w == 3 else nb
-        for d, out in ((dp, keep), (1 - dp, send)):
+        for d, a, b in ((dp, keep.at[w], to_core.at[w, ROWS:]), (1 - dp, to_dp.at[w], to_both.at[w])):
             cols = pl.ds(pl.multiple_of(d * 128, 128), 128)
-            out[w] = dg(src[:, cols], res[w, 0:LC], 0, 0).astype(out.dtype)
-
-
-def sum_kernel(keep, got, r1, own, send):
-    core = Place().core
-    for w in range(4):
-        for c, out in ((core, own), (1 - core, send)):
-            rows = pl.ds(pl.multiple_of(c * 64, 64), 64)
-            out[w] = (keep[w, rows] + got[w, rows].astype(F32)).astype(out.dtype)
+            tile[...] = dg(src[:, cols], res[w, 0:LC], 0, 0)
+            a[...] = tile[pl.ds(pl.multiple_of(core * 64, 64), 64)].astype(a.dtype)
+            b[...] = tile[pl.ds(pl.multiple_of(64 - core * 64, 64), 64)].astype(BF16)
+    to_core[:, 0:ROWS] = send_r[...]
 
 
 def partial_kernel(
@@ -259,7 +254,7 @@
     at = Place()
     z, core = at.z, at.core
     g[:, :, pl.ds(pl.multiple_of(core * HW, HW), HW)] = keep_r[...]
-    g[:, :, pl.ds(pl.multiple_of((1 - core) * HW, HW), HW)] = got_r[...]
+    g[:, :, pl.ds(pl.multiple_of((1 - core) * HW, HW), HW)] = got_r[:, 0:ROWS]
     c[0:CL] = crow[...]
     c[CL:ROWS] = nxt[...]
     cf = c[...].astype(F32)
@@ -288,11 +283,12 @@
         msg[CL : CL + ROWS, WL : WL + 128] = packed
 
 
-def total_kernel(own, other, o0, o1, o2, o3):
+def total_kernel(keep, got, from_dp, from_both, after, o0, o1, o2, o3):
     core = Place().core
     for w, o in enumerate((o0, o1, o2, o3)):
-        o[:, pl.ds(pl.multiple_of(core * HW, HW), HW)] = own[w]
-        o[:, pl.ds(pl.multiple_of((1 - core) * HW, HW), HW)] = other[w].astype(F32)
+        o[:, pl.ds(pl.multiple_of(core * HW, HW), HW)] = keep[w] + from_dp[w].astype(F32)
+        there = got[w, ROWS:].astype(F32) + from_both[w].astype(F32)
+        o[:, pl.ds(pl.multiple_of((1 - core) * HW, HW), HW)] = there
 
 
 def after_kernel(
@@ -383,7 +379,7 @@
         (jnp.broadcast_to(near[None], (8, n)), bias_table),
         smem=(1,),
     )
-    pieces = [piece] + [shifted(piece, "tensor", s) for s in (1, 2, 3)]
+    pieces = [piece] + [shifted(piece, "tensor", s) for s in (2, 1, 3)]
     keep, send, blocks, crow = call(
         project_kernel,
         [((64, 4 * HW), BF16), ((80, 4 * HW), BF16), ((4, CL, 4 * HW), BF16), ((CL, D), BF16)],
@@ -420,16 +416,17 @@
         flops=6 * 10**9,
         vmem=16 * 2**20,
     )
-    got_r = shifted(send_r, "core", 1)
-    dw_keep, dw_send = call(
+    dw_keep, to_core, to_dp, to_both = call(
         weights_kernel,
-        [((4, 128, HW), F32), ((4, 128, HW), BF16)],
-        (res, mine, other_rows),
-        [((LC, 256), BF16), ((LC, 256), BF16)],
+        [((4, 64, HW), F32), ((4, ROWS + 64, HW), BF16), ((4, 64, HW), BF16), ((4, 64, HW), BF16)],
+        (res, mine, other_rows, send_r),
+        [((LC, 256), BF16), ((LC, 256), BF16), ((128, HW), F32)],
         smem=(),
         flops=10**9,
     )
-    dw_got = shifted(dw_send, "dp", 1)
+    got_r = shifted(to_core, "core", 1)
+    from_dp = shifted(to_dp, "dp", 1)
+    from_both = lax.ppermute(to_both, ("dp", "core"), [(i, 3 - i) for i in range(4)])
     msg = (CL + ROWS, WL + 128)
     m1, m2, m3, own, cz, inv = call(
         partial_kernel,
@@ -440,17 +437,10 @@
         flops=10**9,
     )
     r1, r2, r3 = shifted(m1, "tensor", 1), shifted(m2, "tensor", 2), shifted(m3, "tensor", 3)
-    dw_own, dw_other = call(
-        sum_kernel,
-        [((4, 64, HW), F32), ((4, 64, HW), BF16)],
-        (dw_keep, dw_got, r1),
-        smem=(),
-    )
-    dw_other = shifted(dw_other, "core", 1)
     dw = call(
         total_kernel,
         [((64, WL), F32)] * 4,
-        (dw_own, dw_other),
+        (dw_keep, got_r, from_dp, from_both, r1),
         smem=(),
         flops=6 * 10**9,
         typed=False,

time: 66.3 us -> 66.9 us (level)
  waiting for transfers between devices: 16.5 us -> 19.4 us
  starting transfers between devices: 33.3 us -> 31.3 us
    ppermute x18 -> x17, waiting for transfers between devices: 11.9 us -> 14.7 us  [shifted(): return lax.ppermute(x, axis, [(i, (i + steps) % n) for i in range(n)])]
    ppermute x18 -> x17, starting transfers between devices: 28.6 us -> 25.9 us  [shifted(): return lax.ppermute(x, axis, [(i, (i + steps) % n) for i in range(n)])]
    ppermute x0 -> x1, starting transfers between devices: none -> 0.79 us  [local(): lax.ppermute(to_both, ('dp', 'core'), [(i, 3 - i) for i in range(4)])]
    pallas_call x13 -> x12, Pallas kernels: 13.8 us -> 14 us  [call(): pl.pallas_call(kernel, out_shape=[pltpu.VMEM(s, d) if typed else jax.Shap...]
  transfers between devices with their start and end apart: 20 -> 20, of which waited for: 10 -> 10; matrix products, arithmetic and copies ran while one was open for 1% -> 1% of each run, Pallas kernels for 14% -> 12%
where the time goes in v9:
time: 66.9 us; the launch traced here: 66.8 us
  starting transfers between devices  31.3 us (47%)
  waiting for transfers between devices  19.4 us (29%)
  Pallas kernels  14 us (21%)
  between operations  1.49 us (2%)
    ppermute x17, starting transfers between devices, shifted(): return lax.ppermute(x, axis, [(i, (i + steps) % n) for i in range(n)])  25.9 us
    ppermute x17, waiting for transfers between devices, shifted(): return lax.ppermute(x, axis, [(i, (i + steps) % n) for i in range(n)])  14.7 us
    pallas_call x12, Pallas kernels, call(): pl.pallas_call(kernel, out_shape=[pltpu.VMEM(s, d) if typed else jax.Shap...  14 us
    ppermute x1, waiting for transfers between devices, local(): rim_across = lax.ppermute(last, line, over)  4.62 us
    ppermute x1, starting transfers between devices, local(): rim = lax.ppermute(last, line, [(i, i + 1) for i in range(15)])  2.71 us
    ppermute x1, starting transfers between devices, local(): rim_across = lax.ppermute(last, line, over)  1.92 us
  transfers between devices with their start and end apart: 20, of which 10 were waited for; matrix products, arithmetic and copies ran while one was open for 1% of the time, Pallas kernels for 12%

profile of v9, /device:TPU:1, one launch (start us, length us, event | category | flops | bytes accessed | tf_op | source)
XLA Modules:
  0.0 66.8 jit_solution(1284039190740688029)
XLA Ops:
  1.3 1.9 %shard_map.172 = (bf16[80,512]{1,0:T(8,128)(2,1)S(1)}, f32[8,512]{1,0:T(8,128)S(1)}, f32[8,512]{1,0:T(8,128)S(1)}, f32[1,2048]{1,0:T(1,128)S(1)}) custom-call(s32[1]{0:T(128)S(6)} %copy.20.lens, bf16[512,512]{1,0:T(8,128)(2,1)} %bitcast.7, bf16[512,512]{1,0:T(8,128)(2,1)} %bitcast.8, f32[4,512]{1,0:T(4,128)} %first.1, f32[4,512]{1,0:T(4,128)} %second.1, ...), custom_call_target="tpu_custom_call" | custom-call | tf_op jit(solution)/shard_map/pallas_call | solution.py:324
  3.2 3.8 %collective-permute-start = (bf16[80,512]{1,0:T(8,128)(2,1)S(1)}, bf16[80,512]{1,0:T(8,128)(2,1)S(1)}, u32[]{:S(2)}, u32[]{:S(2)}) collective-permute-start(bf16[80,512]{1,0:T(8,128)(2,1)S(1)} %get-tuple-element.40.piece), channel_id=1, source_target_pairs={{0,8},{8,0},{1,9},{9,1},{2,10},{10,2},{3,11},{11,3},{4,12},{12,4},... | collective-permute-start | bytes 245768 | tf_op jit(solution)/shard_map/ppermute | solution.py:337
  7.0 2.7 %collective-permute-start.1 = (f32[8,512]{1,0:T(8,128)S(1)}, f32[8,512]{1,0:T(8,128)S(1)}, u32[]{:S(2)}, u32[]{:S(2)}) collective-permute-start(f32[8,512]{1,0:T(8,128)S(1)} %get-tuple-element.42), channel_id=1, source_target_pairs={{0,4},{4,8},{8,12},{12,16},{16,20},{20,24},{24,28},{28,32},{32,36}... | collective-permute-start | bytes 49160 | tf_op jit(solution)/shard_map/ppermute | solution.py:357
  9.7 1.9 %collective-permute-start.2 = (f32[8,512]{1,0:T(8,128)S(1)}, f32[8,512]{1,0:T(8,128)S(1)}, u32[]{:S(2)}, u32[]{:S(2)}) collective-permute-start(f32[8,512]{1,0:T(8,128)S(1)} %get-tuple-element.42), channel_id=1, source_target_pairs={{0,12},{4,0},{8,4},{12,24},{16,28},{20,16},{24,20},{28,40},{32,44}... | collective-permute-start | bytes 49160 | tf_op jit(solution)/shard_map/ppermute | solution.py:360
  11.7 4.6 %collective-permute-done.2.rim_across = f32[8,512]{1,0:T(8,128)S(1)} collective-permute-done((f32[8,512]{1,0:T(8,128)S(1)}, f32[8,512]{1,0:T(8,128)S(1)}, u32[]{:S(2)}, u32[]{:S(2)}) %collective-permute-start.2) | collective-permute-done | bytes 16416 | tf_op jit(solution)/shard_map/ppermute | solution.py:360
  16.4 3.8 %collective-permute-start.3 = (bf16[128,512]{1,0:T(8,128)(2,1)S(1)}, bf16[128,512]{1,0:T(8,128)(2,1)S(1)}, u32[]{:S(2)}, u32[]{:S(2)}) collective-permute-start(bf16[128,512]{1,0:T(8,128)(2,1)S(1)} %shard_map.173.p0), channel_id=1, source_target_pairs={{0,2},{1,3},{2,0},{3,1},{4,6},{5,7},{6,4},{7,5},{8,10},{9,11},{10,... | collective-permute-start | bytes 393224 | tf_op jit(solution)/shard_map/ppermute | solution.py:337
  20.1 0.7 %collective-permute-start.4 = (bf16[128,512]{1,0:T(8,128)(2,1)S(1)}, bf16[128,512]{1,0:T(8,128)(2,1)S(1)}, u32[]{:S(2)}, u32[]{:S(2)}) collective-permute-start(bf16[128,512]{1,0:T(8,128)(2,1)S(1)} %shard_map.173.p0), channel_id=1, source_target_pairs={{0,1},{1,2},{2,3},{3,0},{4,5},{5,6},{6,7},{7,4},{8,9},{9,10},{10,1... | collective-permute-start | bytes 393224 | tf_op jit(solution)/shard_map/ppermute | solution.py:337
  20.9 1.9 %collective-permute-start.5 = (bf16[128,512]{1,0:T(8,128)(2,1)S(1)}, bf16[128,512]{1,0:T(8,128)(2,1)S(1)}, u32[]{:S(2)}, u32[]{:S(2)}) collective-permute-start(bf16[128,512]{1,0:T(8,128)(2,1)S(1)} %shard_map.173.p0), channel_id=1, source_target_pairs={{0,3},{1,0},{2,1},{3,2},{4,7},{5,4},{6,5},{7,6},{8,11},{9,8},{10,9... | collective-permute-start | bytes 393224 | tf_op jit(solution)/shard_map/ppermute | solution.py:337
  23.0 3.4 %collective-permute-done.4.r1 = bf16[128,512]{1,0:T(8,128)(2,1)S(1)} collective-permute-done((bf16[128,512]{1,0:T(8,128)(2,1)S(1)}, bf16[128,512]{1,0:T(8,128)(2,1)S(1)}, u32[]{:S(2)}, u32[]{:S(2)}) %collective-permute-start.4) | collective-permute-done | bytes 131104 | tf_op jit(solution)/shard_map/ppermute | solution.py:337
  26.4 1.6 %shard_map.174 = (bf16[64,1024]{1,0:T(8,128)(2,1)S(1)}, bf16[80,1024]{1,0:T(8,128)(2,1)S(1)}, bf16[4,32,1024]{2,1,0:T(8,128)(2,1)S(1)}, bf16[32,2048]{1,0:T(8,128)(2,1)S(1)}) custom-call(bf16[128,512]{1,0:T(8,128)(2,1)S(1)} %shard_map.173.p0, bf16[128,512]{1,0:T(8,128)(2,1)S(1)} %collective-permute-done.3.r2, ...), custom_call_target="tpu_custom_call" | custom-call | flops 1000000000 | tf_op jit(solution)/shard_map/pallas_call | solution.py:324
  28.0 1.9 %collective-permute-start.6 = (bf16[80,1024]{1,0:T(8,128)(2,1)S(1)}, bf16[80,1024]{1,0:T(8,128)(2,1)S(1)}, u32[]{:S(2)}, u32[]{:S(2)}) collective-permute-start(bf16[80,1024]{1,0:T(8,128)(2,1)S(1)} %get-tuple-element.45), channel_id=1, source_target_pairs={{0,4},{4,0},{1,5},{5,1},{2,6},{6,2},{3,7},{7,3},{8,12},{12,8},{9,1... | collective-permute-start | bytes 491528 | tf_op jit(solution)/shard_map/ppermute | solution.py:337
  29.9 1.0 %collective-permute-done.6.swapped = bf16[80,1024]{1,0:T(8,128)(2,1)S(1)} collective-permute-done((bf16[80,1024]{1,0:T(8,128)(2,1)S(1)}, bf16[80,1024]{1,0:T(8,128)(2,1)S(1)}, u32[]{:S(2)}, u32[]{:S(2)}) %collective-permute-start.6) | collective-permute-done | bytes 163872 | tf_op jit(solution)/shard_map/ppermute | solution.py:337
  31.0 1.3 %collective-permute-start.7 = (bf16[80,1024]{1,0:T(8,128)(2,1)S(1)}, bf16[80,1024]{1,0:T(8,128)(2,1)}, u32[]{:S(2)}, u32[]{:S(2)}) collective-permute-start(bf16[80,1024]{1,0:T(8,128)(2,1)S(1)} %get-tuple-element.48), channel_id=1, source_target_pairs={{0,16},{16,32},{32,48},{48,0},{1,17},{17,33},{33,49},{49,1},{2,18}... | collective-permute-start | bytes 491528 | tf_op jit(solution)/shard_map/ppermute | solution.py:337
  32.2 1.5 %collective-permute-start.9 = (bf16[80,1024]{1,0:T(8,128)(2,1)S(1)}, bf16[80,1024]{1,0:T(8,128)(2,1)}, u32[]{:S(2)}, u32[]{:S(2)}) collective-permute-start(bf16[80,1024]{1,0:T(8,128)(2,1)S(1)} %get-tuple-element.50), channel_id=1, source_target_pairs={{0,48},{16,0},{32,16},{48,32},{1,49},{17,1},{33,17},{49,33},{2,50}... | collective-permute-start | bytes 491528 | tf_op jit(solution)/shard_map/ppermute | solution.py:337
  33.7 0.8 %shard_map.175 = (bf16[96,1024]{1,0:T(8,128)(2,1)}, bf16[112,1024]{1,0:T(8,128)(2,1)}, bf16[160,1024]{1,0:T(8,128)(2,1)S(1)}) custom-call(bf16[64,1024]{1,0:T(8,128)(2,1)S(1)} %get-tuple-element.44.keep, bf16[80,1024]{1,0:T(8,128)(2,1)S(1)} %collective-permute-done.6.swapped, bf16[4,32,1024]{2,1,0:T(8,128)(2,1)S(1)} %get-tuple-element.46.blocks), custom_call_target="tpu_custom_call" | custom-call | tf_op jit(solution)/shard_map/pallas_call | solution.py:324
  34.9 1.1 %collective-permute-start.8 = (bf16[96,1024]{1,0:T(8,128)(2,1)}, bf16[96,1024]{1,0:T(8,128)(2,1)S(1)}, u32[]{:S(2)}, u32[]{:S(2)}) collective-permute-start(bf16[96,1024]{1,0:T(8,128)(2,1)} %get-tuple-element.49), channel_id=1, source_target_pairs={{0,16},{16,32},{32,48},{48,0},{1,17},{17,33},{33,49},{49,1},{2,18}... | collective-permute-start | bytes 589832 | tf_op jit(solution)/shard_map/ppermute | solution.py:337
  36.0 1.8 %collective-permute-done.7.low_far = bf16[80,1024]{1,0:T(8,128)(2,1)} collective-permute-done((bf16[80,1024]{1,0:T(8,128)(2,1)S(1)}, bf16[80,1024]{1,0:T(8,128)(2,1)}, u32[]{:S(2)}, u32[]{:S(2)}) %collective-permute-start.7) | collective-permute-done | bytes 163872 | tf_op jit(solution)/shard_map/ppermute | solution.py:337
  37.8 2.7 %collective-permute-start.12 = (bf16[80,1024]{1,0:T(8,128)(2,1)}, bf16[80,1024]{1,0:T(8,128)(2,1)S(1)}, u32[]{:S(2)}, u32[]{:S(2)}) collective-permute-start(bf16[80,1024]{1,0:T(8,128)(2,1)} %collective-permute-done.9.high_far), channel_id=1, source_target_pairs={{0,48},{16,0},{32,16},{48,32},{1,49},{17,1},{33,17},{49,33},{2,50}... | collective-permute-start | bytes 491528 | tf_op jit(solution)/shard_map/ppermute | solution.py:337
  41.0 1.1 %shard_map.177.strip = f32[2,128,512]{2,1,0:T(8,128)S(1)} custom-call(s32[8,640]{1,0:T(8,128)S(1)} %broadcast_in_dim.20.near, f32[32,4]{1,0:T(8,128)S(1)} %copy.19.table), custom_call_target="tpu_custom_call" | custom-call | tf_op jit(solution)/shard_map/pallas_call | solution.py:324
  42.4 3.0 %collective-permute-done.11.far_low = bf16[80,1024]{1,0:T(8,128)(2,1)S(1)} collective-permute-done((bf16[80,1024]{1,0:T(8,128)(2,1)}, bf16[80,1024]{1,0:T(8,128)(2,1)S(1)}, u32[]{:S(2)}, u32[]{:S(2)}) %collective-permute-start.11) | collective-permute-done | bytes 163872 | tf_op jit(solution)/shard_map/ppermute | solution.py:337
  45.9 1.4 %collective-permute-start.13 = (bf16[4,32,1024]{2,1,0:T(8,128)(2,1)S(1)}, bf16[4,32,1024]{2,1,0:T(8,128)(2,1)S(1)}, u32[]{:S(2)}, u32[]{:S(2)}) collective-permute-start(bf16[4,32,1024]{2,1,0:T(8,128)(2,1)S(1)} %get-tuple-element.54.mine), channel_id=1, source_target_pairs={{0,4},{4,0},{1,5},{5,1},{2,6},{6,2},{3,7},{7,3},{8,12},{12,8},{9,1... | collective-permute-start | bytes 786440 | tf_op jit(solution)/shard_map/ppermute | solution.py:337
  47.4 2.9 %shard_map.178 = (bf16[4,528,256]{2,1,0:T(8,128)(2,1)S(1)}, bf16[4,48,256]{2,1,0:T(8,128)(2,1)S(1)}, bf16[4,48,256]{2,1,0:T(8,128)(2,1)S(1)}) custom-call(s32[1]{0:T(128)S(6)} %copy.20.lens, bf16[160,1024]{1,0:T(8,128)(2,1)S(1)} %get-tuple-element.47.b0, bf16[80,1024]{1,0:T(8,128)(2,1)} %collective-permute-done.7.low_far, ...), custom_call_target="tpu_custom_call" | custom-call | flops 6000000000 | tf_op jit(solution)/shard_map/pallas_call | solution.py:324
  50.4 0.7 %shard_map.180 = (f32[4,64,256]{2,1,0:T(8,128)S(1)}, bf16[4,112,256]{2,1,0:T(8,128)(2,1)S(1)}, bf16[4,64,256]{2,1,0:T(8,128)(2,1)S(1)}, bf16[4,64,256]{2,1,0:T(8,128)(2,1)S(1)}) custom-call(bf16[4,528,256]{2,1,0:T(8,128)(2,1)S(1)} %get-tuple-element.53.res, bf16[4,32,1024]{2,1,0:T(8,128)(2,1)S(1)} %get-tuple-element.54.mine, ...), custom_call_target="tpu_custom_call" | custom-call | flops 1000000000 | tf_op jit(solution)/shard_map/pallas_call | solution.py:324
  51.2 1.3 %collective-permute-start.18 = (bf16[4,64,256]{2,1,0:T(8,128)(2,1)S(1)}, bf16[4,64,256]{2,1,0:T(8,128)(2,1)S(1)}, u32[]{:S(2)}, u32[]{:S(2)}) collective-permute-start(bf16[4,64,256]{2,1,0:T(8,128)(2,1)S(1)} %get-tuple-element.68), channel_id=1, source_target_pairs={{0,64},{64,0},{1,65},{65,1},{2,66},{66,2},{3,67},{67,3},{4,68},{68... | collective-permute-start | bytes 393224 | tf_op jit(solution)/shard_map/ppermute | solution.py:337
  52.5 0.8 %collective-permute-start.19 = (bf16[4,64,256]{2,1,0:T(8,128)(2,1)S(1)}, bf16[4,64,256]{2,1,0:T(8,128)(2,1)S(1)}, u32[]{:S(2)}, u32[]{:S(2)}) collective-permute-start(bf16[4,64,256]{2,1,0:T(8,128)(2,1)S(1)} %get-tuple-element.69), channel_id=1, source_target_pairs={{0,68},{4,64},{64,4},{68,0},{1,69},{5,65},{65,5},{69,1},{2,70},{6,... | collective-permute-start | bytes 393224 | tf_op jit(solution)/shard_map/ppermute | solution.py:429
  53.3 2.6 %shard_map.181 = (bf16[80,640]{1,0:T(8,128)(2,1)S(1)}, bf16[80,640]{1,0:T(8,128)(2,1)S(1)}, bf16[80,640]{1,0:T(8,128)(2,1)S(1)}, f32[80,640]{1,0:T(8,128)S(1)}, ...) custom-call(bf16[4,48,256]{2,1,0:T(8,128)(2,1)S(1)} %get-tuple-element.52.keep_r, ...), custom_call_target="tpu_custom_call" | custom-call | flops 1000000000 | tf_op jit(solution)/shard_map/pallas_call | solution.py:324
  55.9 0.8 %collective-permute-start.15 = (bf16[80,640]{1,0:T(8,128)(2,1)S(1)}, bf16[80,640]{1,0:T(8,128)(2,1)S(1)}, u32[]{:S(2)}, u32[]{:S(2)}) collective-permute-start(bf16[80,640]{1,0:T(8,128)(2,1)S(1)} %get-tuple-element.61), channel_id=1, source_target_pairs={{0,1},{1,2},{2,3},{3,0},{4,5},{5,6},{6,7},{7,4},{8,9},{9,10},{10,1... | collective-permute-start | bytes 307208 | tf_op jit(solution)/shard_map/ppermute | solution.py:337
  56.7 3.2 %collective-permute-start.16 = (bf16[80,640]{1,0:T(8,128)(2,1)S(1)}, bf16[80,640]{1,0:T(8,128)(2,1)S(1)}, u32[]{:S(2)}, u32[]{:S(2)}) collective-permute-start(bf16[80,640]{1,0:T(8,128)(2,1)S(1)} %get-tuple-element.62), channel_id=1, source_target_pairs={{0,2},{1,3},{2,0},{3,1},{4,6},{5,7},{6,4},{7,5},{8,10},{9,11},{10,... | collective-permute-start | bytes 307208 | tf_op jit(solution)/shard_map/ppermute | solution.py:337
  60.0 1.9 %collective-permute-done.15.r1.after = bf16[80,640]{1,0:T(8,128)(2,1)S(1)} collective-permute-done((bf16[80,640]{1,0:T(8,128)(2,1)S(1)}, bf16[80,640]{1,0:T(8,128)(2,1)S(1)}, u32[]{:S(2)}, u32[]{:S(2)}) %collective-permute-start.15) | collective-permute-done | bytes 102432 | tf_op jit(solution)/shard_map/ppermute | solution.py:337
  61.9 0.8 %shard_map.183 = (f32[64,512]{1,0:T(8,128)}, f32[64,512]{1,0:T(8,128)}, f32[64,512]{1,0:T(8,128)}, f32[64,512]{1,0:T(8,128)}) custom-call(f32[4,64,256]{2,1,0:T(8,128)S(1)} %get-tuple-element.59.after.keep, bf16[4,112,256]{2,1,0:T(8,128)(2,1)S(1)} %collective-permute-done.14.got_r.got, bf16[4,64,256]{2,1,0:T(8,128)(2,1)S(1)} %collective-permute-done.18.from_dp, ...), custom_call_target="tpu_custom_call" | custom-call | flops 6000000000 | tf_op jit(solution)/shard_map/pallas_call | solution.py:324
  62.8 2.5 %collective-permute-done.16.r2 = bf16[80,640]{1,0:T(8,128)(2,1)S(1)} collective-permute-done((bf16[80,640]{1,0:T(8,128)(2,1)S(1)}, bf16[80,640]{1,0:T(8,128)(2,1)S(1)}, u32[]{:S(2)}, u32[]{:S(2)}) %collective-permute-start.16) | collective-permute-done | bytes 102432 | tf_op jit(solution)/shard_map/ppermute | solution.py:337
  65.3 1.4 %shard_map.182 = (bf16[512,512]{1,0:T(8,128)(2,1)}, bf16[512,512]{1,0:T(8,128)(2,1)}) custom-call(s32[1]{0:T(128)S(6)} %copy.20.lens, f32[80,640]{1,0:T(8,128)S(1)} %get-tuple-element.60.keep, bf16[80,640]{1,0:T(8,128)(2,1)S(1)} %collective-permute-done.15.r1.after, bf16[80,640]{1,0:T(8,128)(2,1)S(1)} %collective-permute-done.16.r2, ...), custom_call_target="tpu_custom_call" | custom-call | flops 20000000000 | tf_op jit(solution)/shard_map/pallas_call | solution.py:324
  (52 shorter events, 2.2 us)
Async XLA Ops:
  3.2 13.1 %collective-permute-start = (bf16[80,512]{1,0:T(8,128)(2,1)S(1)}, bf16[80,512]{1,0:T(8,128)(2,1)S(1)}, u32[]{:S(2)}, u32[]{:S(2)}) collective-permute-start(bf16[80,512]{1,0:T(8,128)(2,1)S(1)} %get-tuple-element.40.piece), channel_id=1, source_target_pairs={{0,8},{8,0},{1,9},{9,1},{2,10},{10,2},{3,11},{11,3},{4,12},{12,4},... | collective-permute-start | bytes 245768 | tf_op jit(solution)/shard_map/ppermute | solution.py:337
  7.0 4.6 %collective-permute-start.1 = (f32[8,512]{1,0:T(8,128)S(1)}, f32[8,512]{1,0:T(8,128)S(1)}, u32[]{:S(2)}, u32[]{:S(2)}) collective-permute-start(f32[8,512]{1,0:T(8,128)S(1)} %get-tuple-element.42), channel_id=1, source_target_pairs={{0,4},{4,8},{8,12},{12,16},{16,20},{20,24},{24,28},{28,32},{32,36}... | collective-permute-start | bytes 49160 | tf_op jit(solution)/shard_map/ppermute | solution.py:357
  9.7 6.6 %collective-permute-start.2 = (f32[8,512]{1,0:T(8,128)S(1)}, f32[8,512]{1,0:T(8,128)S(1)}, u32[]{:S(2)}, u32[]{:S(2)}) collective-permute-start(f32[8,512]{1,0:T(8,128)S(1)} %get-tuple-element.42), channel_id=1, source_target_pairs={{0,12},{4,0},{8,4},{12,24},{16,28},{20,16},{24,20},{28,40},{32,44}... | collective-permute-start | bytes 49160 | tf_op jit(solution)/shard_map/ppermute | solution.py:360
  16.3 10.1 %copy-start = (bf16[2048,512]{1,0:T(8,128)(2,1)S(1)}, bf16[2048,512]{1,0:T(8,128)(2,1)}, u32[]{:S(2)}) copy-start(bf16[2048,512]{1,0:T(8,128)(2,1)} %wq.3) | copy-start | bytes 6291460
  16.3 10.1 %copy-start.1 = (bf16[2048,512]{1,0:T(8,128)(2,1)S(1)}, bf16[2048,512]{1,0:T(8,128)(2,1)}, u32[]{:S(2)}) copy-start(bf16[2048,512]{1,0:T(8,128)(2,1)} %wk.3) | copy-start | bytes 6291460
  16.3 10.1 %copy-start.3 = (bf16[2048,512]{1,0:T(8,128)(2,1)S(1)}, bf16[2048,512]{1,0:T(8,128)(2,1)}, u32[]{:S(2)}) copy-start(bf16[2048,512]{1,0:T(8,128)(2,1)} %wv.3) | copy-start | bytes 6291460
  16.3 10.1 %copy-start.5 = (bf16[2048,512]{1,0:T(8,128)(2,1)S(1)}, bf16[2048,512]{1,0:T(8,128)(2,1)}, u32[]{:S(2)}) copy-start(bf16[2048,512]{1,0:T(8,128)(2,1)} %wo.3) | copy-start | bytes 6291460
  16.4 6.6 %collective-permute-start.3 = (bf16[128,512]{1,0:T(8,128)(2,1)S(1)}, bf16[128,512]{1,0:T(8,128)(2,1)S(1)}, u32[]{:S(2)}, u32[]{:S(2)}) collective-permute-start(bf16[128,512]{1,0:T(8,128)(2,1)S(1)} %shard_map.173.p0), channel_id=1, source_target_pairs={{0,2},{1,3},{2,0},{3,1},{4,6},{5,7},{6,4},{7,5},{8,10},{9,11},{10,... | collective-permute-start | bytes 393224 | tf_op jit(solution)/shard_map/ppermute | solution.py:337
  20.1 6.3 %collective-permute-start.4 = (bf16[128,512]{1,0:T(8,128)(2,1)S(1)}, bf16[128,512]{1,0:T(8,128)(2,1)S(1)}, u32[]{:S(2)}, u32[]{:S(2)}) collective-permute-start(bf16[128,512]{1,0:T(8,128)(2,1)S(1)} %shard_map.173.p0), channel_id=1, source_target_pairs={{0,1},{1,2},{2,3},{3,0},{4,5},{5,6},{6,7},{7,4},{8,9},{9,10},{10,1... | collective-permute-start | bytes 393224 | tf_op jit(solution)/shard_map/ppermute | solution.py:337
  20.9 5.5 %collective-permute-start.5 = (bf16[128,512]{1,0:T(8,128)(2,1)S(1)}, bf16[128,512]{1,0:T(8,128)(2,1)S(1)}, u32[]{:S(2)}, u32[]{:S(2)}) collective-permute-start(bf16[128,512]{1,0:T(8,128)(2,1)S(1)} %shard_map.173.p0), channel_id=1, source_target_pairs={{0,3},{1,0},{2,1},{3,2},{4,7},{5,4},{6,5},{7,6},{8,11},{9,8},{10,9... | collective-permute-start | bytes 393224 | tf_op jit(solution)/shard_map/ppermute | solution.py:337
  26.4 14.0 %copy-start.11 = (s32[512]{0:T(512)S(1)}, s32[512]{0:T(512)}, u32[]{:S(2)}) copy-start(s32[512]{0:T(512)} %param.23) | copy-start | bytes 6148
  26.4 14.4 %copy-start.10 = (f32[32,4]{0,1:T(4,128)S(1)}, f32[32,4]{0,1:T(4,128)}, u32[]{:S(2)}) copy-start(f32[32,4]{0,1:T(4,128)} %param.22) | copy-start | bytes 1540
  28.0 2.9 %collective-permute-start.6 = (bf16[80,1024]{1,0:T(8,128)(2,1)S(1)}, bf16[80,1024]{1,0:T(8,128)(2,1)S(1)}, u32[]{:S(2)}, u32[]{:S(2)}) collective-permute-start(bf16[80,1024]{1,0:T(8,128)(2,1)S(1)} %get-tuple-element.45), channel_id=1, source_target_pairs={{0,4},{4,0},{1,5},{5,1},{2,6},{6,2},{3,7},{7,3},{8,12},{12,8},{9,1... | collective-permute-start | bytes 491528 | tf_op jit(solution)/shard_map/ppermute | solution.py:337
  31.0 6.8 %collective-permute-start.7 = (bf16[80,1024]{1,0:T(8,128)(2,1)S(1)}, bf16[80,1024]{1,0:T(8,128)(2,1)}, u32[]{:S(2)}, u32[]{:S(2)}) collective-permute-start(bf16[80,1024]{1,0:T(8,128)(2,1)S(1)} %get-tuple-element.48), channel_id=1, source_target_pairs={{0,16},{16,32},{32,48},{48,0},{1,17},{17,33},{33,49},{49,1},{2,18}... | collective-permute-start | bytes 491528 | tf_op jit(solution)/shard_map/ppermute | solution.py:337
  32.2 5.5 %collective-permute-start.9 = (bf16[80,1024]{1,0:T(8,128)(2,1)S(1)}, bf16[80,1024]{1,0:T(8,128)(2,1)}, u32[]{:S(2)}, u32[]{:S(2)}) collective-permute-start(bf16[80,1024]{1,0:T(8,128)(2,1)S(1)} %get-tuple-element.50), channel_id=1, source_target_pairs={{0,48},{16,0},{32,16},{48,32},{1,49},{17,1},{33,17},{49,33},{2,50}... | collective-permute-start | bytes 491528 | tf_op jit(solution)/shard_map/ppermute | solution.py:337
  34.5 7.9 %collective-permute-start.10 = (bf16[112,1024]{1,0:T(8,128)(2,1)}, bf16[112,1024]{1,0:T(8,128)(2,1)S(1)}, u32[]{:S(2)}, u32[]{:S(2)}) collective-permute-start(bf16[112,1024]{1,0:T(8,128)(2,1)} %get-tuple-element.51), channel_id=1, source_target_pairs={{0,48},{16,0},{32,16},{48,32},{1,49},{17,1},{33,17},{49,33},{2,50}... | collective-permute-start | bytes 688136 | tf_op jit(solution)/shard_map/ppermute | solution.py:337
  34.9 7.1 %collective-permute-start.8 = (bf16[96,1024]{1,0:T(8,128)(2,1)}, bf16[96,1024]{1,0:T(8,128)(2,1)S(1)}, u32[]{:S(2)}, u32[]{:S(2)}) collective-permute-start(bf16[96,1024]{1,0:T(8,128)(2,1)} %get-tuple-element.49), channel_id=1, source_target_pairs={{0,16},{16,32},{32,48},{48,0},{1,17},{17,33},{33,49},{49,1},{2,18}... | collective-permute-start | bytes 589832 | tf_op jit(solution)/shard_map/ppermute | solution.py:337
  37.8 7.7 %collective-permute-start.11 = (bf16[80,1024]{1,0:T(8,128)(2,1)}, bf16[80,1024]{1,0:T(8,128)(2,1)S(1)}, u32[]{:S(2)}, u32[]{:S(2)}) collective-permute-start(bf16[80,1024]{1,0:T(8,128)(2,1)} %collective-permute-done.7.low_far), channel_id=1, source_target_pairs={{0,16},{16,32},{32,48},{48,0},{1,17},{17,33},{33,49},{49,1},{2,18}... | collective-permute-start | bytes 491528 | tf_op jit(solution)/shard_map/ppermute | solution.py:337
  37.8 8.1 %collective-permute-start.12 = (bf16[80,1024]{1,0:T(8,128)(2,1)}, bf16[80,1024]{1,0:T(8,128)(2,1)S(1)}, u32[]{:S(2)}, u32[]{:S(2)}) collective-permute-start(bf16[80,1024]{1,0:T(8,128)(2,1)} %collective-permute-done.9.high_far), channel_id=1, source_target_pairs={{0,48},{16,0},{32,16},{48,32},{1,49},{17,1},{33,17},{49,33},{2,50}... | collective-permute-start | bytes 491528 | tf_op jit(solution)/shard_map/ppermute | solution.py:337
  45.9 4.4 %collective-permute-start.13 = (bf16[4,32,1024]{2,1,0:T(8,128)(2,1)S(1)}, bf16[4,32,1024]{2,1,0:T(8,128)(2,1)S(1)}, u32[]{:S(2)}, u32[]{:S(2)}) collective-permute-start(bf16[4,32,1024]{2,1,0:T(8,128)(2,1)S(1)} %get-tuple-element.54.mine), channel_id=1, source_target_pairs={{0,4},{4,0},{1,5},{5,1},{2,6},{6,2},{3,7},{7,3},{8,12},{12,8},{9,1... | collective-permute-start | bytes 786440 | tf_op jit(solution)/shard_map/ppermute | solution.py:337
  47.4 5.9 %copy-start.4 = (bf16[2048,512]{1,0:T(8,128)(2,1)S(1)}, bf16[2048,512]{1,0:T(8,128)(2,1)}, u32[]{:S(2)}) copy-start(bf16[2048,512]{1,0:T(8,128)(2,1)} %wv.3) | copy-start | bytes 6291460
  47.4 5.9 %copy-start.6 = (bf16[2048,512]{1,0:T(8,128)(2,1)S(1)}, bf16[2048,512]{1,0:T(8,128)(2,1)}, u32[]{:S(2)}) copy-start(bf16[2048,512]{1,0:T(8,128)(2,1)} %wo.3) | copy-start | bytes 6291460
  50.3 3.0 %copy-start.2 = (bf16[2048,512]{1,0:T(8,128)(2,1)S(1)}, bf16[2048,512]{1,0:T(8,128)(2,1)}, u32[]{:S(2)}) copy-start(bf16[2048,512]{1,0:T(8,128)(2,1)} %wk.3) | copy-start | bytes 6291460
  51.1 2.2 %collective-permute-start.14 = (bf16[4,112,256]{2,1,0:T(8,128)(2,1)S(1)}, bf16[4,112,256]{2,1,0:T(8,128)(2,1)S(1)}, u32[]{:S(2)}, u32[]{:S(2)}) collective-permute-start(bf16[4,112,256]{2,1,0:T(8,128)(2,1)S(1)} %get-tuple-element.56), channel_id=1, source_target_pairs={{0,4},{4,0},{1,5},{5,1},{2,6},{6,2},{3,7},{7,3},{8,12},{12,8},{9,1... | collective-permute-start | bytes 688136 | tf_op jit(solution)/shard_map/ppermute | solution.py:337
  51.2 8.8 %collective-permute-start.18 = (bf16[4,64,256]{2,1,0:T(8,128)(2,1)S(1)}, bf16[4,64,256]{2,1,0:T(8,128)(2,1)S(1)}, u32[]{:S(2)}, u32[]{:S(2)}) collective-permute-start(bf16[4,64,256]{2,1,0:T(8,128)(2,1)S(1)} %get-tuple-element.68), channel_id=1, source_target_pairs={{0,64},{64,0},{1,65},{65,1},{2,66},{66,2},{3,67},{67,3},{4,68},{68... | collective-permute-start | bytes 393224 | tf_op jit(solution)/shard_map/ppermute | solution.py:337
  52.5 7.5 %collective-permute-start.19 = (bf16[4,64,256]{2,1,0:T(8,128)(2,1)S(1)}, bf16[4,64,256]{2,1,0:T(8,128)(2,1)S(1)}, u32[]{:S(2)}, u32[]{:S(2)}) collective-permute-start(bf16[4,64,256]{2,1,0:T(8,128)(2,1)S(1)} %get-tuple-element.69), channel_id=1, source_target_pairs={{0,68},{4,64},{64,4},{68,0},{1,69},{5,65},{65,5},{69,1},{2,70},{6,... | collective-permute-start | bytes 393224 | tf_op jit(solution)/shard_map/ppermute | solution.py:429
  55.9 6.0 %collective-permute-start.15 = (bf16[80,640]{1,0:T(8,128)(2,1)S(1)}, bf16[80,640]{1,0:T(8,128)(2,1)S(1)}, u32[]{:S(2)}, u32[]{:S(2)}) collective-permute-start(bf16[80,640]{1,0:T(8,128)(2,1)S(1)} %get-tuple-element.61), channel_id=1, source_target_pairs={{0,1},{1,2},{2,3},{3,0},{4,5},{5,6},{6,7},{7,4},{8,9},{9,10},{10,1... | collective-permute-start | bytes 307208 | tf_op jit(solution)/shard_map/ppermute | solution.py:337
  56.7 8.6 %collective-permute-start.16 = (bf16[80,640]{1,0:T(8,128)(2,1)S(1)}, bf16[80,640]{1,0:T(8,128)(2,1)S(1)}, u32[]{:S(2)}, u32[]{:S(2)}) collective-permute-start(bf16[80,640]{1,0:T(8,128)(2,1)S(1)} %get-tuple-element.62), channel_id=1, source_target_pairs={{0,2},{1,3},{2,0},{3,1},{4,6},{5,7},{6,4},{7,5},{8,10},{9,11},{10,... | collective-permute-start | bytes 307208 | tf_op jit(solution)/shard_map/ppermute | solution.py:337
  59.9 5.4 %copy-start.7 = (f32[16,512]{1,0:T(8,128)S(1)}, f32[16,512]{1,0:T(8,128)}, u32[]{:S(2)}) copy-start(f32[16,512]{1,0:T(8,128)} %up_gain.1) | copy-start | bytes 98308
  59.9 5.4 %copy-start.8 = (f32[4,512]{1,0:T(4,128)S(1)}, f32[4,512]{1,0:T(4,128)}, u32[]{:S(2)}) copy-start(f32[4,512]{1,0:T(4,128)} %first.1) | copy-start | bytes 24580
  59.9 5.4 %copy-start.9 = (f32[4,512]{1,0:T(4,128)S(1)}, f32[4,512]{1,0:T(4,128)}, u32[]{:S(2)}) copy-start(f32[4,512]{1,0:T(4,128)} %second.1) | copy-start | bytes 24580
  59.9 5.3 %collective-permute-start.17 = (bf16[80,640]{1,0:T(8,128)(2,1)S(1)}, bf16[80,640]{1,0:T(8,128)(2,1)S(1)}, u32[]{:S(2)}, u32[]{:S(2)}) collective-permute-start(bf16[80,640]{1,0:T(8,128)(2,1)S(1)} %get-tuple-element.63), channel_id=1, source_target_pairs={{0,3},{1,0},{2,1},{3,2},{4,7},{5,4},{6,5},{7,6},{8,11},{9,8},{10,9... | collective-permute-start | bytes 307208 | tf_op jit(solution)/shard_map/ppermute | solution.py:337

commit v10 on v7

--- a/solution.py
+++ b/solution.py
@@ -52,21 +52,25 @@
 def byte_mask(ctx, doc_len):
     pos = ctx * SEG + 16 * lax.broadcasted_iota(jnp.int32, (CL, 16, WL), 0)
     pos = pos + lax.broadcasted_iota(jnp.int32, (CL, 16, WL), 1)
-    return (pos < doc_len).astype(F32)
+    return (pos < doc_len[None]).astype(F32)
 
 
 def before_kernel(
-    lens, tokens_h, grad_h, first_h, second_h, up_h, gain_h, piece, row, last, gain,
-    tokens, grad_out, first, second, up_gain, shift, sems,
-):
-    pairs = ((tokens_h, tokens), (first_h, first), (second_h, second), (grad_h, grad_out), (up_h, up_gain), (gain_h, gain))
+    lens_h, tokens_h, grad_h, first_h, second_h, up_h, gain_h, piece, row, last, gain, lens_out,
+    tokens, grad_out, first, second, up_gain, lens, shift, sems,
+):
+    pairs = (
+        (lens_h, lens), (tokens_h, tokens), (first_h, first), (second_h, second),
+        (grad_h, grad_out), (up_h, up_gain), (gain_h, gain),
+    )
     copies = [pltpu.make_async_copy(a, b, sems.at[i]) for i, (a, b) in enumerate(pairs)]
     for c in copies:
         c.start()
-    mask = byte_mask(Place().ctx, lens[0])
     u = lax.broadcasted_iota(jnp.int32, (CL, 16, WL), 1)
-    for c in copies[:3]:
+    for c in copies[:4]:
         c.wait()
+    lens_out[...] = jnp.broadcast_to(lens[...], (8, 128))
+    mask = byte_mask(Place().ctx, lens[...])
     taps = tap_weights(first[...], second[...])
     prod = tokens[...].astype(F32).reshape(CL, 16, WL) * mask * taps[None]
     own = jnp.sum(jnp.where(u == 0, prod, 0.0), axis=1)
@@ -78,7 +82,7 @@
     row[...] = jnp.broadcast_to(part[0:1], (8, WL))
     piece[64:80] = jnp.concatenate(list(in_three(part[0:1])) + [jnp.zeros((13, WL), F32)], axis=0).astype(BF16)
     last[...] = jnp.broadcast_to(shift[7 + CL : 8 + CL], (8, WL))
-    for c in copies[3:]:
+    for c in copies[4:]:
         c.wait()
     weighted = grad_out[...].astype(F32).reshape(CL, 16, WL) * mask * up_gain[...][None]
     piece[CL : 2 * CL] = jnp.sum(weighted, axis=1).astype(BF16)
@@ -108,7 +112,7 @@
 
 
 def project_kernel(
-    p0, r1, r2, r3, gain, wq, wk, wv, wo, keep, send, blocks, mine, craw, nrm, gco, both
+    p0, r2, r1, r3, gain, wq, wk, wv, wo, keep, send, blocks, mine, craw, nrm, gco, both
 ):
     at = Place()
     z, core, x, y = at.z, at.core, at.x, at.y
@@ -185,7 +189,7 @@
     res, keep, send, q, k, v, ga, score, dprob, sg, pb,
 ):
     at = Place()
-    ctx, core, x, doc_len = at.ctx, at.core, at.x, lens[0]
+    ctx, core, x, doc_len = at.ctx, at.core, at.x, lens[0:1, 0:1]
     for src, first, n, s, row in (
         (b0, 0, 128, 0, 0),
         (low_far, 0, 64, 1, 0),
@@ -299,7 +303,7 @@
     lens, keep, r1, r2, r3, cz, inv, gain, first, second, up_gain, update, grad, rows
 ):
     at = Place()
-    ctx, doc_len, z = at.ctx, lens[0], at.z
+    ctx, doc_len, z = at.ctx, lens[0:1, 0:1], at.z
     mask = byte_mask(ctx, doc_len)
     body = slice(0, WL)
     out = keep[0:CL, body]
@@ -346,15 +350,16 @@
     bias_table, buckets, up_gain, grad_out,
 ):
     weights = (w_query, w_key, w_value, w_out)
-    piece, row, last, gain = call(
+    piece, row, last, gain, lens = call(
         before_kernel,
-        [((80, WL), BF16), ((8, WL), F32), ((8, WL), F32), ((1, D), F32)],
-        (lengths, tokens[0], grad_out[0], conv_first, conv_second, up_gain, norm_gain[None]),
+        [((80, WL), BF16), ((8, WL), F32), ((8, WL), F32), ((1, D), F32), ((8, 128), jnp.int32)],
+        (lengths.reshape(1, 1), tokens[0], grad_out[0], conv_first, conv_second, up_gain, norm_gain[None]),
         [
             ((SEG, WL), BF16), ((SEG, WL), BF16), ((4, WL), F32), ((4, WL), F32), ((16, WL), F32),
-            ((CL + 8, WL), F32), pltpu.SemaphoreType.DMA((6,)),
+            ((1, 1), jnp.int32), ((CL + 8, WL), F32), pltpu.SemaphoreType.DMA((7,)),
         ],
-        hbm=(1, 2, 3, 4, 5, 6),
+        smem=(),
+        hbm=range(7),
         vmem=BIG,
     )
     line = ("x", "y", "core")
@@ -383,7 +388,7 @@
         (jnp.broadcast_to(near[None], (8, n)), bias_table),
         smem=(1,),
     )
-    pieces = [piece] + [shifted(piece, "tensor", s) for s in (1, 2, 3)]
+    pieces = [piece] + [shifted(piece, "tensor", s) for s in (2, 1, 3)]
     keep, send, blocks, crow = call(
         project_kernel,
         [((64, 4 * HW), BF16), ((80, 4 * HW), BF16), ((4, CL, 4 * HW), BF16), ((CL, D), BF16)],
@@ -415,8 +420,9 @@
     res, keep_r, send_r = call(
         attend_kernel,
         [((4, LC + 16, HW), BF16), ((4, ROWS, HW), BF16), ((4, ROWS, HW), BF16)],
-        (lengths, b0, low_far, low_near, high_far, high_near, far_low, far_high, strip),
+        (lens, b0, low_far, low_near, high_far, high_near, far_low, far_high, strip),
         [((LC, HW), BF16)] * 4 + [((NH, LC, LC), F32)] * 2 + [((NH, LC, LC), BF16)] * 2,
+        smem=(),
         flops=6 * 10**9,
         vmem=16 * 2**20,
     )
@@ -458,9 +464,10 @@
     update, grad_tokens = call(
         after_kernel,
         [((SEG, WL), BF16)] * 2,
-        (lengths, own, r1, r2, r3, cz, inv, gain, conv_first, conv_second, up_gain),
+        (lens, own, r1, r2, r3, cz, inv, gain, conv_first, conv_second, up_gain),
         [((ROWS, WL), F32)],
         flops=2 * 10**10,
+        smem=(),
         typed=False,
     )
     return (update[None], grad_tokens[None], *dw)

time: 66.3 us -> 66 us (level)
  transfers between devices with their start and end apart: 20 -> 20, of which waited for: 10 -> 11; matrix products, arithmetic and copies ran while one was open for 1% -> 1% of each run, Pallas kernels for 14% -> 14%
where the time goes in v10:
time: 66 us; the launch traced here: 65.7 us
  starting transfers between devices  32.9 us (50%)
  waiting for transfers between devices  16.8 us (25%)
  Pallas kernels  14 us (21%)
  between operations  1.48 us (2%)
    ppermute x18, starting transfers between devices, shifted(): return lax.ppermute(x, axis, [(i, (i + steps) % n) for i in range(n)])  28.3 us
    pallas_call x13, Pallas kernels, call(): pl.pallas_call(kernel, out_shape=[pltpu.VMEM(s, d) if typed else jax.Shap...  14 us
    ppermute x18, waiting for transfers between devices, shifted(): return lax.ppermute(x, axis, [(i, (i + steps) % n) for i in range(n)])  12.1 us
    ppermute x1, waiting for transfers between devices, local(): rim_across = lax.ppermute(last, line, over)  4.62 us
    ppermute x1, starting transfers between devices, local(): rim = lax.ppermute(last, line, [(i, i + 1) for i in range(15)])  2.71 us
    ppermute x1, starting transfers between devices, local(): rim_across = lax.ppermute(last, line, over)  1.92 us
  transfers between devices with their start and end apart: 20, of which 11 were waited for; matrix products, arithmetic and copies ran while one was open for 1% of the time, Pallas kernels for 14%

profile of v10, /device:TPU:1, one launch (start us, length us, event | category | flops | bytes accessed | tf_op | source)
XLA Modules:
  0.0 65.7 jit_solution(4934617004608986062)
XLA Ops:
  1.3 2.0 %shard_map.172 = (bf16[80,512]{1,0:T(8,128)(2,1)S(1)}, f32[8,512]{1,0:T(8,128)S(1)}, f32[8,512]{1,0:T(8,128)S(1)}, f32[1,2048]{1,0:T(1,128)S(1)}, s32[8,128]{1,0:T(8,128)S(1)}) custom-call(s32[1,1]{1,0:T(1,128)} %bitcast.8.lens_h, bf16[512,512]{1,0:T(8,128)(2,1)} %bitcast.9, bf16[512,512]{1,0:T(8,128)(2,1)} %bitcast.10, f32[4,512]{1,0:T(4,128)} %first.1, ...), custom_call_target="tpu_custom_call" | custom-call | tf_op jit(solution)/shard_map/pallas_call | solution.py:332
  3.3 3.8 %collective-permute-start = (bf16[80,512]{1,0:T(8,128)(2,1)S(1)}, bf16[80,512]{1,0:T(8,128)(2,1)S(1)}, u32[]{:S(2)}, u32[]{:S(2)}) collective-permute-start(bf16[80,512]{1,0:T(8,128)(2,1)S(1)} %get-tuple-element.42.piece), channel_id=1, source_target_pairs={{0,8},{8,0},{1,9},{9,1},{2,10},{10,2},{3,11},{11,3},{4,12},{12,4},... | collective-permute-start | bytes 245768 | tf_op jit(solution)/shard_map/ppermute | solution.py:345
  7.1 2.7 %collective-permute-start.1 = (f32[8,512]{1,0:T(8,128)S(1)}, f32[8,512]{1,0:T(8,128)S(1)}, u32[]{:S(2)}, u32[]{:S(2)}) collective-permute-start(f32[8,512]{1,0:T(8,128)S(1)} %get-tuple-element.44), channel_id=1, source_target_pairs={{0,4},{4,8},{8,12},{12,16},{16,20},{20,24},{24,28},{28,32},{32,36}... | collective-permute-start | bytes 49160 | tf_op jit(solution)/shard_map/ppermute | solution.py:366
  9.8 1.9 %collective-permute-start.2 = (f32[8,512]{1,0:T(8,128)S(1)}, f32[8,512]{1,0:T(8,128)S(1)}, u32[]{:S(2)}, u32[]{:S(2)}) collective-permute-start(f32[8,512]{1,0:T(8,128)S(1)} %get-tuple-element.44), channel_id=1, source_target_pairs={{0,12},{4,0},{8,4},{12,24},{16,28},{20,16},{24,20},{28,40},{32,44}... | collective-permute-start | bytes 49160 | tf_op jit(solution)/shard_map/ppermute | solution.py:369
  11.7 4.6 %collective-permute-done.2.rim_across = f32[8,512]{1,0:T(8,128)S(1)} collective-permute-done((f32[8,512]{1,0:T(8,128)S(1)}, f32[8,512]{1,0:T(8,128)S(1)}, u32[]{:S(2)}, u32[]{:S(2)}) %collective-permute-start.2) | collective-permute-done | bytes 16416 | tf_op jit(solution)/shard_map/ppermute | solution.py:369
  16.4 3.8 %collective-permute-start.3 = (bf16[128,512]{1,0:T(8,128)(2,1)S(1)}, bf16[128,512]{1,0:T(8,128)(2,1)S(1)}, u32[]{:S(2)}, u32[]{:S(2)}) collective-permute-start(bf16[128,512]{1,0:T(8,128)(2,1)S(1)} %shard_map.173.p0), channel_id=1, source_target_pairs={{0,2},{1,3},{2,0},{3,1},{4,6},{5,7},{6,4},{7,5},{8,10},{9,11},{10,... | collective-permute-start | bytes 393224 | tf_op jit(solution)/shard_map/ppermute | solution.py:345
  20.2 0.7 %collective-permute-start.4 = (bf16[128,512]{1,0:T(8,128)(2,1)S(1)}, bf16[128,512]{1,0:T(8,128)(2,1)S(1)}, u32[]{:S(2)}, u32[]{:S(2)}) collective-permute-start(bf16[128,512]{1,0:T(8,128)(2,1)S(1)} %shard_map.173.p0), channel_id=1, source_target_pairs={{0,1},{1,2},{2,3},{3,0},{4,5},{5,6},{6,7},{7,4},{8,9},{9,10},{10,1... | collective-permute-start | bytes 393224 | tf_op jit(solution)/shard_map/ppermute | solution.py:345
  20.9 1.9 %collective-permute-start.5 = (bf16[128,512]{1,0:T(8,128)(2,1)S(1)}, bf16[128,512]{1,0:T(8,128)(2,1)S(1)}, u32[]{:S(2)}, u32[]{:S(2)}) collective-permute-start(bf16[128,512]{1,0:T(8,128)(2,1)S(1)} %shard_map.173.p0), channel_id=1, source_target_pairs={{0,3},{1,0},{2,1},{3,2},{4,7},{5,4},{6,5},{7,6},{8,11},{9,8},{10,9... | collective-permute-start | bytes 393224 | tf_op jit(solution)/shard_map/ppermute | solution.py:345
  23.0 3.4 %collective-permute-done.4.r1 = bf16[128,512]{1,0:T(8,128)(2,1)S(1)} collective-permute-done((bf16[128,512]{1,0:T(8,128)(2,1)S(1)}, bf16[128,512]{1,0:T(8,128)(2,1)S(1)}, u32[]{:S(2)}, u32[]{:S(2)}) %collective-permute-start.4) | collective-permute-done | bytes 131104 | tf_op jit(solution)/shard_map/ppermute | solution.py:345
  26.5 1.6 %shard_map.174 = (bf16[64,1024]{1,0:T(8,128)(2,1)S(1)}, bf16[80,1024]{1,0:T(8,128)(2,1)S(1)}, bf16[4,32,1024]{2,1,0:T(8,128)(2,1)S(1)}, bf16[32,2048]{1,0:T(8,128)(2,1)S(1)}) custom-call(bf16[128,512]{1,0:T(8,128)(2,1)S(1)} %shard_map.173.p0, bf16[128,512]{1,0:T(8,128)(2,1)S(1)} %collective-permute-done.3.r2, ...), custom_call_target="tpu_custom_call" | custom-call | flops 1000000000 | tf_op jit(solution)/shard_map/pallas_call | solution.py:332
  28.1 1.9 %collective-permute-start.6 = (bf16[80,1024]{1,0:T(8,128)(2,1)S(1)}, bf16[80,1024]{1,0:T(8,128)(2,1)S(1)}, u32[]{:S(2)}, u32[]{:S(2)}) collective-permute-start(bf16[80,1024]{1,0:T(8,128)(2,1)S(1)} %get-tuple-element.47), channel_id=1, source_target_pairs={{0,4},{4,0},{1,5},{5,1},{2,6},{6,2},{3,7},{7,3},{8,12},{12,8},{9,1... | collective-permute-start | bytes 491528 | tf_op jit(solution)/shard_map/ppermute | solution.py:345
  30.0 1.0 %collective-permute-done.6.swapped = bf16[80,1024]{1,0:T(8,128)(2,1)S(1)} collective-permute-done((bf16[80,1024]{1,0:T(8,128)(2,1)S(1)}, bf16[80,1024]{1,0:T(8,128)(2,1)S(1)}, u32[]{:S(2)}, u32[]{:S(2)}) %collective-permute-start.6) | collective-permute-done | bytes 163872 | tf_op jit(solution)/shard_map/ppermute | solution.py:345
  31.0 1.3 %collective-permute-start.7 = (bf16[80,1024]{1,0:T(8,128)(2,1)S(1)}, bf16[80,1024]{1,0:T(8,128)(2,1)}, u32[]{:S(2)}, u32[]{:S(2)}) collective-permute-start(bf16[80,1024]{1,0:T(8,128)(2,1)S(1)} %get-tuple-element.50), channel_id=1, source_target_pairs={{0,16},{16,32},{32,48},{48,0},{1,17},{17,33},{33,49},{49,1},{2,18}... | collective-permute-start | bytes 491528 | tf_op jit(solution)/shard_map/ppermute | solution.py:345
  32.3 1.5 %collective-permute-start.9 = (bf16[80,1024]{1,0:T(8,128)(2,1)S(1)}, bf16[80,1024]{1,0:T(8,128)(2,1)}, u32[]{:S(2)}, u32[]{:S(2)}) collective-permute-start(bf16[80,1024]{1,0:T(8,128)(2,1)S(1)} %get-tuple-element.52), channel_id=1, source_target_pairs={{0,48},{16,0},{32,16},{48,32},{1,49},{17,1},{33,17},{49,33},{2,50}... | collective-permute-start | bytes 491528 | tf_op jit(solution)/shard_map/ppermute | solution.py:345
  33.8 0.8 %shard_map.175 = (bf16[96,1024]{1,0:T(8,128)(2,1)}, bf16[112,1024]{1,0:T(8,128)(2,1)}, bf16[160,1024]{1,0:T(8,128)(2,1)S(1)}) custom-call(bf16[64,1024]{1,0:T(8,128)(2,1)S(1)} %get-tuple-element.46.keep, bf16[80,1024]{1,0:T(8,128)(2,1)S(1)} %collective-permute-done.6.swapped, bf16[4,32,1024]{2,1,0:T(8,128)(2,1)S(1)} %get-tuple-element.48.blocks), custom_call_target="tpu_custom_call" | custom-call | tf_op jit(solution)/shard_map/pallas_call | solution.py:332
  35.0 1.1 %collective-permute-start.8 = (bf16[96,1024]{1,0:T(8,128)(2,1)}, bf16[96,1024]{1,0:T(8,128)(2,1)S(1)}, u32[]{:S(2)}, u32[]{:S(2)}) collective-permute-start(bf16[96,1024]{1,0:T(8,128)(2,1)} %get-tuple-element.51), channel_id=1, source_target_pairs={{0,16},{16,32},{32,48},{48,0},{1,17},{17,33},{33,49},{49,1},{2,18}... | collective-permute-start | bytes 589832 | tf_op jit(solution)/shard_map/ppermute | solution.py:345
  36.1 1.8 %collective-permute-done.7.low_far = bf16[80,1024]{1,0:T(8,128)(2,1)} collective-permute-done((bf16[80,1024]{1,0:T(8,128)(2,1)S(1)}, bf16[80,1024]{1,0:T(8,128)(2,1)}, u32[]{:S(2)}, u32[]{:S(2)}) %collective-permute-start.7) | collective-permute-done | bytes 163872 | tf_op jit(solution)/shard_map/ppermute | solution.py:345
  37.8 2.7 %collective-permute-start.12 = (bf16[80,1024]{1,0:T(8,128)(2,1)}, bf16[80,1024]{1,0:T(8,128)(2,1)S(1)}, u32[]{:S(2)}, u32[]{:S(2)}) collective-permute-start(bf16[80,1024]{1,0:T(8,128)(2,1)} %collective-permute-done.9.high_far), channel_id=1, source_target_pairs={{0,48},{16,0},{32,16},{48,32},{1,49},{17,1},{33,17},{49,33},{2,50}... | collective-permute-start | bytes 491528 | tf_op jit(solution)/shard_map/ppermute | solution.py:345
  41.0 1.1 %shard_map.177.strip = f32[2,128,512]{2,1,0:T(8,128)S(1)} custom-call(s32[8,640]{1,0:T(8,128)S(1)} %broadcast_in_dim.20.near, f32[32,4]{1,0:T(8,128)S(1)} %copy.19.table), custom_call_target="tpu_custom_call" | custom-call | tf_op jit(solution)/shard_map/pallas_call | solution.py:332
  42.5 3.0 %collective-permute-done.11.far_low = bf16[80,1024]{1,0:T(8,128)(2,1)S(1)} collective-permute-done((bf16[80,1024]{1,0:T(8,128)(2,1)}, bf16[80,1024]{1,0:T(8,128)(2,1)S(1)}, u32[]{:S(2)}, u32[]{:S(2)}) %collective-permute-start.11) | collective-permute-done | bytes 163872 | tf_op jit(solution)/shard_map/ppermute | solution.py:345
  46.0 1.4 %collective-permute-start.14 = (bf16[4,32,1024]{2,1,0:T(8,128)(2,1)S(1)}, bf16[4,32,1024]{2,1,0:T(8,128)(2,1)S(1)}, u32[]{:S(2)}, u32[]{:S(2)}) collective-permute-start(bf16[4,32,1024]{2,1,0:T(8,128)(2,1)S(1)} %get-tuple-element.59.mine), channel_id=1, source_target_pairs={{0,4},{4,0},{1,5},{5,1},{2,6},{6,2},{3,7},{7,3},{8,12},{12,8},{9,1... | collective-permute-start | bytes 786440 | tf_op jit(solution)/shard_map/ppermute | solution.py:345
  47.5 3.0 %shard_map.178 = (bf16[4,528,256]{2,1,0:T(8,128)(2,1)S(1)}, bf16[4,48,256]{2,1,0:T(8,128)(2,1)S(1)}, bf16[4,48,256]{2,1,0:T(8,128)(2,1)S(1)}) custom-call(s32[8,128]{1,0:T(8,128)S(1)} %get-tuple-element.41.lens, bf16[160,1024]{1,0:T(8,128)(2,1)S(1)} %get-tuple-element.49.b0, bf16[80,1024]{1,0:T(8,128)(2,1)} %collective-permute-done.7.low_far, ...), custom_call_target="tpu_custom_call" | custom-call | flops 6000000000 | tf_op jit(solution)/shard_map/pallas_call | solution.py:332
  50.6 0.5 shard_map.180
  51.1 1.3 %collective-permute-start.18 = (bf16[4,128,256]{2,1,0:T(8,128)(2,1)S(1)}, bf16[4,128,256]{2,1,0:T(8,128)(2,1)S(1)}, u32[]{:S(2)}, u32[]{:S(2)}) collective-permute-start(bf16[4,128,256]{2,1,0:T(8,128)(2,1)S(1)} %get-tuple-element.69), channel_id=1, source_target_pairs={{0,64},{64,0},{1,65},{65,1},{2,66},{66,2},{3,67},{67,3},{4,68},{68... | collective-permute-start | bytes 786440 | tf_op jit(solution)/shard_map/ppermute | solution.py:345
  52.5 2.6 %shard_map.181 = (bf16[80,640]{1,0:T(8,128)(2,1)S(1)}, bf16[80,640]{1,0:T(8,128)(2,1)S(1)}, bf16[80,640]{1,0:T(8,128)(2,1)S(1)}, f32[80,640]{1,0:T(8,128)S(1)}, ...) custom-call(bf16[4,48,256]{2,1,0:T(8,128)(2,1)S(1)} %get-tuple-element.54.keep_r, ...), custom_call_target="tpu_custom_call" | custom-call | flops 1000000000 | tf_op jit(solution)/shard_map/pallas_call | solution.py:332
  55.1 0.8 %collective-permute-start.15 = (bf16[80,640]{1,0:T(8,128)(2,1)S(1)}, bf16[80,640]{1,0:T(8,128)(2,1)S(1)}, u32[]{:S(2)}, u32[]{:S(2)}) collective-permute-start(bf16[80,640]{1,0:T(8,128)(2,1)S(1)} %get-tuple-element.62), channel_id=1, source_target_pairs={{0,1},{1,2},{2,3},{3,0},{4,5},{5,6},{6,7},{7,4},{8,9},{9,10},{10,1... | collective-permute-start | bytes 307208 | tf_op jit(solution)/shard_map/ppermute | solution.py:345
  55.9 2.8 %collective-permute-start.16 = (bf16[80,640]{1,0:T(8,128)(2,1)S(1)}, bf16[80,640]{1,0:T(8,128)(2,1)S(1)}, u32[]{:S(2)}, u32[]{:S(2)}) collective-permute-start(bf16[80,640]{1,0:T(8,128)(2,1)S(1)} %get-tuple-element.63), channel_id=1, source_target_pairs={{0,2},{1,3},{2,0},{3,1},{4,6},{5,7},{6,4},{7,5},{8,10},{9,11},{10,... | collective-permute-start | bytes 307208 | tf_op jit(solution)/shard_map/ppermute | solution.py:345
  59.0 0.8 %collective-permute-done.15.r1 = bf16[80,640]{1,0:T(8,128)(2,1)S(1)} collective-permute-done((bf16[80,640]{1,0:T(8,128)(2,1)S(1)}, bf16[80,640]{1,0:T(8,128)(2,1)S(1)}, u32[]{:S(2)}, u32[]{:S(2)}) %collective-permute-start.15) | collective-permute-done | bytes 102432 | tf_op jit(solution)/shard_map/ppermute | solution.py:345
  59.9 2.4 %collective-permute-start.19 = (bf16[4,64,256]{2,1,0:T(8,128)(2,1)S(1)}, bf16[4,64,256]{2,1,0:T(8,128)(2,1)S(1)}, u32[]{:S(2)}, u32[]{:S(2)}) collective-permute-start(bf16[4,64,256]{2,1,0:T(8,128)(2,1)S(1)} %get-tuple-element.71), channel_id=1, source_target_pairs={{0,4},{4,0},{1,5},{5,1},{2,6},{6,2},{3,7},{7,3},{8,12},{12,8},{9,1... | collective-permute-start | bytes 393224 | tf_op jit(solution)/shard_map/ppermute | solution.py:345
  62.8 0.6 collective-permute-done.17.r3
  63.4 1.5 %shard_map.182 = (bf16[512,512]{1,0:T(8,128)(2,1)}, bf16[512,512]{1,0:T(8,128)(2,1)}) custom-call(s32[8,128]{1,0:T(8,128)S(1)} %get-tuple-element.41.lens, f32[80,640]{1,0:T(8,128)S(1)} %get-tuple-element.61.keep, bf16[80,640]{1,0:T(8,128)(2,1)S(1)} %collective-permute-done.15.r1, bf16[80,640]{1,0:T(8,128)(2,1)S(1)} %collective-permute-done.16.r2, ...), custom_call_target="tpu_custom_call" | custom-call | flops 20000000000 | tf_op jit(solution)/shard_map/pallas_call | solution.py:332
  64.9 0.8 %shard_map.184 = (f32[64,512]{1,0:T(8,128)}, f32[64,512]{1,0:T(8,128)}, f32[64,512]{1,0:T(8,128)}, f32[64,512]{1,0:T(8,128)}) custom-call(f32[4,64,256]{2,1,0:T(8,128)S(1)} %get-tuple-element.70.own, bf16[4,64,256]{2,1,0:T(8,128)(2,1)S(1)} %collective-permute-done.19.other), custom_call_target="tpu_custom_call" | custom-call | flops 6000000000 | tf_op jit(solution)/shard_map/pallas_call | solution.py:332
  (53 shorter events, 3.0 us)
Async XLA Ops:
  3.3 13.1 %collective-permute-start = (bf16[80,512]{1,0:T(8,128)(2,1)S(1)}, bf16[80,512]{1,0:T(8,128)(2,1)S(1)}, u32[]{:S(2)}, u32[]{:S(2)}) collective-permute-start(bf16[80,512]{1,0:T(8,128)(2,1)S(1)} %get-tuple-element.42.piece), channel_id=1, source_target_pairs={{0,8},{8,0},{1,9},{9,1},{2,10},{10,2},{3,11},{11,3},{4,12},{12,4},... | collective-permute-start | bytes 245768 | tf_op jit(solution)/shard_map/ppermute | solution.py:345
  7.1 4.6 %collective-permute-start.1 = (f32[8,512]{1,0:T(8,128)S(1)}, f32[8,512]{1,0:T(8,128)S(1)}, u32[]{:S(2)}, u32[]{:S(2)}) collective-permute-start(f32[8,512]{1,0:T(8,128)S(1)} %get-tuple-element.44), channel_id=1, source_target_pairs={{0,4},{4,8},{8,12},{12,16},{16,20},{20,24},{24,28},{28,32},{32,36}... | collective-permute-start | bytes 49160 | tf_op jit(solution)/shard_map/ppermute | solution.py:366
  9.8 6.6 %collective-permute-start.2 = (f32[8,512]{1,0:T(8,128)S(1)}, f32[8,512]{1,0:T(8,128)S(1)}, u32[]{:S(2)}, u32[]{:S(2)}) collective-permute-start(f32[8,512]{1,0:T(8,128)S(1)} %get-tuple-element.44), channel_id=1, source_target_pairs={{0,12},{4,0},{8,4},{12,24},{16,28},{20,16},{24,20},{28,40},{32,44}... | collective-permute-start | bytes 49160 | tf_op jit(solution)/shard_map/ppermute | solution.py:369
  16.4 10.1 %copy-start = (bf16[2048,512]{1,0:T(8,128)(2,1)S(1)}, bf16[2048,512]{1,0:T(8,128)(2,1)}, u32[]{:S(2)}) copy-start(bf16[2048,512]{1,0:T(8,128)(2,1)} %wq.3) | copy-start | bytes 6291460
  16.4 10.1 %copy-start.1 = (bf16[2048,512]{1,0:T(8,128)(2,1)S(1)}, bf16[2048,512]{1,0:T(8,128)(2,1)}, u32[]{:S(2)}) copy-start(bf16[2048,512]{1,0:T(8,128)(2,1)} %wk.3) | copy-start | bytes 6291460
  16.4 10.1 %copy-start.3 = (bf16[2048,512]{1,0:T(8,128)(2,1)S(1)}, bf16[2048,512]{1,0:T(8,128)(2,1)}, u32[]{:S(2)}) copy-start(bf16[2048,512]{1,0:T(8,128)(2,1)} %wv.3) | copy-start | bytes 6291460
  16.4 10.1 %copy-start.5 = (bf16[2048,512]{1,0:T(8,128)(2,1)S(1)}, bf16[2048,512]{1,0:T(8,128)(2,1)}, u32[]{:S(2)}) copy-start(bf16[2048,512]{1,0:T(8,128)(2,1)} %wo.3) | copy-start | bytes 6291460
  16.4 6.6 %collective-permute-start.3 = (bf16[128,512]{1,0:T(8,128)(2,1)S(1)}, bf16[128,512]{1,0:T(8,128)(2,1)S(1)}, u32[]{:S(2)}, u32[]{:S(2)}) collective-permute-start(bf16[128,512]{1,0:T(8,128)(2,1)S(1)} %shard_map.173.p0), channel_id=1, source_target_pairs={{0,2},{1,3},{2,0},{3,1},{4,6},{5,7},{6,4},{7,5},{8,10},{9,11},{10,... | collective-permute-start | bytes 393224 | tf_op jit(solution)/shard_map/ppermute | solution.py:345
  20.2 6.3 %collective-permute-start.4 = (bf16[128,512]{1,0:T(8,128)(2,1)S(1)}, bf16[128,512]{1,0:T(8,128)(2,1)S(1)}, u32[]{:S(2)}, u32[]{:S(2)}) collective-permute-start(bf16[128,512]{1,0:T(8,128)(2,1)S(1)} %shard_map.173.p0), channel_id=1, source_target_pairs={{0,1},{1,2},{2,3},{3,0},{4,5},{5,6},{6,7},{7,4},{8,9},{9,10},{10,1... | collective-permute-start | bytes 393224 | tf_op jit(solution)/shard_map/ppermute | solution.py:345
  20.9 5.5 %collective-permute-start.5 = (bf16[128,512]{1,0:T(8,128)(2,1)S(1)}, bf16[128,512]{1,0:T(8,128)(2,1)S(1)}, u32[]{:S(2)}, u32[]{:S(2)}) collective-permute-start(bf16[128,512]{1,0:T(8,128)(2,1)S(1)} %shard_map.173.p0), channel_id=1, source_target_pairs={{0,3},{1,0},{2,1},{3,2},{4,7},{5,4},{6,5},{7,6},{8,11},{9,8},{10,9... | collective-permute-start | bytes 393224 | tf_op jit(solution)/shard_map/ppermute | solution.py:345
  26.5 14.0 %copy-start.11 = (s32[512]{0:T(512)S(1)}, s32[512]{0:T(512)}, u32[]{:S(2)}) copy-start(s32[512]{0:T(512)} %param.23) | copy-start | bytes 6148
  26.5 14.4 %copy-start.10 = (f32[32,4]{0,1:T(4,128)S(1)}, f32[32,4]{0,1:T(4,128)}, u32[]{:S(2)}) copy-start(f32[32,4]{0,1:T(4,128)} %param.22) | copy-start | bytes 1540
  28.1 2.9 %collective-permute-start.6 = (bf16[80,1024]{1,0:T(8,128)(2,1)S(1)}, bf16[80,1024]{1,0:T(8,128)(2,1)S(1)}, u32[]{:S(2)}, u32[]{:S(2)}) collective-permute-start(bf16[80,1024]{1,0:T(8,128)(2,1)S(1)} %get-tuple-element.47), channel_id=1, source_target_pairs={{0,4},{4,0},{1,5},{5,1},{2,6},{6,2},{3,7},{7,3},{8,12},{12,8},{9,1... | collective-permute-start | bytes 491528 | tf_op jit(solution)/shard_map/ppermute | solution.py:345
  31.0 6.8 %collective-permute-start.7 = (bf16[80,1024]{1,0:T(8,128)(2,1)S(1)}, bf16[80,1024]{1,0:T(8,128)(2,1)}, u32[]{:S(2)}, u32[]{:S(2)}) collective-permute-start(bf16[80,1024]{1,0:T(8,128)(2,1)S(1)} %get-tuple-element.50), channel_id=1, source_target_pairs={{0,16},{16,32},{32,48},{48,0},{1,17},{17,33},{33,49},{49,1},{2,18}... | collective-permute-start | bytes 491528 | tf_op jit(solution)/shard_map/ppermute | solution.py:345
  32.3 5.5 %collective-permute-start.9 = (bf16[80,1024]{1,0:T(8,128)(2,1)S(1)}, bf16[80,1024]{1,0:T(8,128)(2,1)}, u32[]{:S(2)}, u32[]{:S(2)}) collective-permute-start(bf16[80,1024]{1,0:T(8,128)(2,1)S(1)} %get-tuple-element.52), channel_id=1, source_target_pairs={{0,48},{16,0},{32,16},{48,32},{1,49},{17,1},{33,17},{49,33},{2,50}... | collective-permute-start | bytes 491528 | tf_op jit(solution)/shard_map/ppermute | solution.py:345
  34.6 7.9 %collective-permute-start.10 = (bf16[112,1024]{1,0:T(8,128)(2,1)}, bf16[112,1024]{1,0:T(8,128)(2,1)S(1)}, u32[]{:S(2)}, u32[]{:S(2)}) collective-permute-start(bf16[112,1024]{1,0:T(8,128)(2,1)} %get-tuple-element.53), channel_id=1, source_target_pairs={{0,48},{16,0},{32,16},{48,32},{1,49},{17,1},{33,17},{49,33},{2,50}... | collective-permute-start | bytes 688136 | tf_op jit(solution)/shard_map/ppermute | solution.py:345
  35.0 7.1 %collective-permute-start.8 = (bf16[96,1024]{1,0:T(8,128)(2,1)}, bf16[96,1024]{1,0:T(8,128)(2,1)S(1)}, u32[]{:S(2)}, u32[]{:S(2)}) collective-permute-start(bf16[96,1024]{1,0:T(8,128)(2,1)} %get-tuple-element.51), channel_id=1, source_target_pairs={{0,16},{16,32},{32,48},{48,0},{1,17},{17,33},{33,49},{49,1},{2,18}... | collective-permute-start | bytes 589832 | tf_op jit(solution)/shard_map/ppermute | solution.py:345
  37.8 7.7 %collective-permute-start.11 = (bf16[80,1024]{1,0:T(8,128)(2,1)}, bf16[80,1024]{1,0:T(8,128)(2,1)S(1)}, u32[]{:S(2)}, u32[]{:S(2)}) collective-permute-start(bf16[80,1024]{1,0:T(8,128)(2,1)} %collective-permute-done.7.low_far), channel_id=1, source_target_pairs={{0,16},{16,32},{32,48},{48,0},{1,17},{17,33},{33,49},{49,1},{2,18}... | collective-permute-start | bytes 491528 | tf_op jit(solution)/shard_map/ppermute | solution.py:345
  37.8 8.1 %collective-permute-start.12 = (bf16[80,1024]{1,0:T(8,128)(2,1)}, bf16[80,1024]{1,0:T(8,128)(2,1)S(1)}, u32[]{:S(2)}, u32[]{:S(2)}) collective-permute-start(bf16[80,1024]{1,0:T(8,128)(2,1)} %collective-permute-done.9.high_far), channel_id=1, source_target_pairs={{0,48},{16,0},{32,16},{48,32},{1,49},{17,1},{33,17},{49,33},{2,50}... | collective-permute-start | bytes 491528 | tf_op jit(solution)/shard_map/ppermute | solution.py:345
  46.0 4.6 %collective-permute-start.14 = (bf16[4,32,1024]{2,1,0:T(8,128)(2,1)S(1)}, bf16[4,32,1024]{2,1,0:T(8,128)(2,1)S(1)}, u32[]{:S(2)}, u32[]{:S(2)}) collective-permute-start(bf16[4,32,1024]{2,1,0:T(8,128)(2,1)S(1)} %get-tuple-element.59.mine), channel_id=1, source_target_pairs={{0,4},{4,0},{1,5},{5,1},{2,6},{6,2},{3,7},{7,3},{8,12},{12,8},{9,1... | collective-permute-start | bytes 786440 | tf_op jit(solution)/shard_map/ppermute | solution.py:345
  47.5 5.0 %copy-start.4 = (bf16[2048,512]{1,0:T(8,128)(2,1)S(1)}, bf16[2048,512]{1,0:T(8,128)(2,1)}, u32[]{:S(2)}) copy-start(bf16[2048,512]{1,0:T(8,128)(2,1)} %wv.3) | copy-start | bytes 6291460
  47.5 5.0 %copy-start.6 = (bf16[2048,512]{1,0:T(8,128)(2,1)S(1)}, bf16[2048,512]{1,0:T(8,128)(2,1)}, u32[]{:S(2)}) copy-start(bf16[2048,512]{1,0:T(8,128)(2,1)} %wo.3) | copy-start | bytes 6291460
  50.4 2.0 %copy-start.2 = (bf16[2048,512]{1,0:T(8,128)(2,1)S(1)}, bf16[2048,512]{1,0:T(8,128)(2,1)}, u32[]{:S(2)}) copy-start(bf16[2048,512]{1,0:T(8,128)(2,1)} %wk.3) | copy-start | bytes 6291460
  50.5 2.0 %collective-permute-start.13 = (bf16[4,48,256]{2,1,0:T(8,128)(2,1)S(1)}, bf16[4,48,256]{2,1,0:T(8,128)(2,1)S(1)}, u32[]{:S(2)}, u32[]{:S(2)}) collective-permute-start(bf16[4,48,256]{2,1,0:T(8,128)(2,1)S(1)} %get-tuple-element.55), channel_id=1, source_target_pairs={{0,4},{4,0},{1,5},{5,1},{2,6},{6,2},{3,7},{7,3},{8,12},{12,8},{9,1... | collective-permute-start | bytes 294920 | tf_op jit(solution)/shard_map/ppermute | solution.py:345
  51.1 8.8 %collective-permute-start.18 = (bf16[4,128,256]{2,1,0:T(8,128)(2,1)S(1)}, bf16[4,128,256]{2,1,0:T(8,128)(2,1)S(1)}, u32[]{:S(2)}, u32[]{:S(2)}) collective-permute-start(bf16[4,128,256]{2,1,0:T(8,128)(2,1)S(1)} %get-tuple-element.69), channel_id=1, source_target_pairs={{0,64},{64,0},{1,65},{65,1},{2,66},{66,2},{3,67},{67,3},{4,68},{68... | collective-permute-start | bytes 786440 | tf_op jit(solution)/shard_map/ppermute | solution.py:345
  52.5 10.9 %copy-start.7 = (f32[16,512]{1,0:T(8,128)S(1)}, f32[16,512]{1,0:T(8,128)}, u32[]{:S(2)}) copy-start(f32[16,512]{1,0:T(8,128)} %up_gain.1) | copy-start | bytes 98308
  52.5 10.9 %copy-start.8 = (f32[4,512]{1,0:T(4,128)S(1)}, f32[4,512]{1,0:T(4,128)}, u32[]{:S(2)}) copy-start(f32[4,512]{1,0:T(4,128)} %first.1) | copy-start | bytes 24580
  52.5 10.9 %copy-start.9 = (f32[4,512]{1,0:T(4,128)S(1)}, f32[4,512]{1,0:T(4,128)}, u32[]{:S(2)}) copy-start(f32[4,512]{1,0:T(4,128)} %second.1) | copy-start | bytes 24580
  55.1 4.8 %collective-permute-start.15 = (bf16[80,640]{1,0:T(8,128)(2,1)S(1)}, bf16[80,640]{1,0:T(8,128)(2,1)S(1)}, u32[]{:S(2)}, u32[]{:S(2)}) collective-permute-start(bf16[80,640]{1,0:T(8,128)(2,1)S(1)} %get-tuple-element.62), channel_id=1, source_target_pairs={{0,1},{1,2},{2,3},{3,0},{4,5},{5,6},{6,7},{7,4},{8,9},{9,10},{10,1... | collective-permute-start | bytes 307208 | tf_op jit(solution)/shard_map/ppermute | solution.py:345
  55.9 6.9 %collective-permute-start.16 = (bf16[80,640]{1,0:T(8,128)(2,1)S(1)}, bf16[80,640]{1,0:T(8,128)(2,1)S(1)}, u32[]{:S(2)}, u32[]{:S(2)}) collective-permute-start(bf16[80,640]{1,0:T(8,128)(2,1)S(1)} %get-tuple-element.63), channel_id=1, source_target_pairs={{0,2},{1,3},{2,0},{3,1},{4,6},{5,7},{6,4},{7,5},{8,10},{9,11},{10,... | collective-permute-start | bytes 307208 | tf_op jit(solution)/shard_map/ppermute | solution.py:345
  58.7 4.7 %collective-permute-start.17 = (bf16[80,640]{1,0:T(8,128)(2,1)S(1)}, bf16[80,640]{1,0:T(8,128)(2,1)S(1)}, u32[]{:S(2)}, u32[]{:S(2)}) collective-permute-start(bf16[80,640]{1,0:T(8,128)(2,1)S(1)} %get-tuple-element.64), channel_id=1, source_target_pairs={{0,3},{1,0},{2,1},{3,2},{4,7},{5,4},{6,5},{7,6},{8,11},{9,8},{10,9... | collective-permute-start | bytes 307208 | tf_op jit(solution)/shard_map/ppermute | solution.py:345
  59.9 4.9 %collective-permute-start.19 = (bf16[4,64,256]{2,1,0:T(8,128)(2,1)S(1)}, bf16[4,64,256]{2,1,0:T(8,128)(2,1)S(1)}, u32[]{:S(2)}, u32[]{:S(2)}) collective-permute-start(bf16[4,64,256]{2,1,0:T(8,128)(2,1)S(1)} %get-tuple-element.71), channel_id=1, source_target_pairs={{0,4},{4,0},{1,5},{5,1},{2,6},{6,2},{3,7},{7,3},{8,12},{12,8},{9,1... | collective-permute-start | bytes 393224 | tf_op jit(solution)/shard_map/ppermute | solution.py:345

commit v11 on v7

--- a/solution.py
+++ b/solution.py
@@ -108,7 +108,7 @@
 
 
 def project_kernel(
-    p0, r1, r2, r3, gain, wq, wk, wv, wo, keep, send, blocks, mine, craw, nrm, gco, both
+    p0, r1, r2, r3, gain, wq, wk, wv, wo, keep, send, blocks, mine, hown, craw, nrm, gco, both, hs
 ):
     at = Place()
     z, core, x, y = at.z, at.core, at.x, at.y
@@ -120,10 +120,16 @@
             gco[rows, cols] = src[2 * i * CL + CL : 2 * i * CL + 2 * CL]
     mine[...] = craw[pl.ds(pl.multiple_of(y * CL, CL), CL)]
     c = craw[...].astype(F32)
-    r = lax.rsqrt(jnp.sum(c * c, axis=1, keepdims=True) * (1.0 / D) + 1e-6)
+    square = jnp.sum(c * c, axis=1, keepdims=True) * (1.0 / D) + 1e-6
+    r = lax.rsqrt(square)
+    rms = jnp.sqrt(square)
     nrm[...] = (c * r * gain[...]).astype(BF16)
     for src, w, slot in ((gco, wo, 3), (nrm, wq, 0), (nrm, wk, 1), (nrm, wv, 2)):
-        v = jnp.dot(src[...], w[...], preferred_element_type=F32).astype(BF16)
+        full = jnp.dot(src[...], w[...], preferred_element_type=F32)
+        v = full.astype(BF16)
+        if slot < 3:
+            hs[...] = full * rms
+            hown[slot] = hs[pl.ds(pl.multiple_of(y * CL, CL), CL)]
         for half in range(2):
             both[half, :, slot * HW : slot * HW + HW] = v[:, half * HW : half * HW + HW]
     keep[...] = both[core]
@@ -165,12 +171,15 @@
     b0[128:160] = blocks[0]
 
 
-def gather_kernel(b0, low_near, high_near, far_low, far_high, swapped, mine, nxt):
+def gather_kernel(b0, low_near, high_near, far_low, far_high, after, mine):
     mine[0] = b0[128:160]
     mine[1] = low_near[0:32]
     mine[2, 0:16] = far_low[64:80]
     mine[2, 16:32] = far_high[64:80]
     mine[3] = high_near[0:32]
+
+
+def next_kernel(high_near, swapped, gain, wq, wk, wv, nxt, hnext):
     at = Place()
     wraps = jnp.logical_and(at.core == 1, at.y == 1)
     tops = jnp.where(wraps, high_near[96:112].astype(F32), swapped[64:80].astype(F32))
@@ -178,6 +187,9 @@
     for j in range(2):
         row = jnp.where(upper, tops[2 + j : 3 + j], tops[j : j + 1])
         nxt[:, j * 1024 : j * 1024 + 1024] = jnp.broadcast_to(row, (16, 1024)).astype(BF16)
+    gained = (nxt[...].astype(F32) * gain[...]).astype(BF16)
+    for i, w in enumerate((wq, wk, wv)):
+        hnext[i] = jnp.dot(gained, w[...], preferred_element_type=F32)
 
 
 def attend_kernel(
@@ -245,7 +257,7 @@
             out[w] = dg(src[:, cols], res[w, 0:LC], 0, 0).astype(out.dtype)
 
 
-def sum_kernel(keep, got, r1, own, send):
+def sum_kernel(keep, got, r2, own, send):
     core = Place().core
     for w in range(4):
         for c, out in ((core, own), (1 - core, send)):
@@ -253,39 +265,49 @@
             out[w] = (keep[w, rows] + got[w, rows].astype(F32)).astype(out.dtype)
 
 
-def partial_kernel(
-    keep_r, got_r, crow, nxt, after, gain, wq, wk, wv, wo, msg1, msg2, msg3, keep, cz, inv_out, g, c
-):
+def message(g, weights, t, msg):
+    part = pl.ds(pl.multiple_of(t * WL, WL), WL)
+    wq, wk, wv, wo = weights
+    gn = dg(g[0], wq[part], 1, 1) + dg(g[1], wk[part], 1, 1) + dg(g[2], wv[part], 1, 1)
+    msg[0:CL, 0:WL] = dg(g[3, 0:CL], wo[part], 1, 1).astype(msg.dtype)
+    msg[CL : CL + ROWS, 0:WL] = gn.astype(msg.dtype)
+    msg[0:CL, WL : WL + 128] = jnp.zeros((CL, 128), msg.dtype)
+
+
+def partial_far_kernel(keep_r, got_r, hown, hnext, after, wq, wk, wv, wo, msg2, g, sums):
     at = Place()
     z, core = at.z, at.core
     g[:, :, pl.ds(pl.multiple_of(core * HW, HW), HW)] = keep_r[...]
     g[:, :, pl.ds(pl.multiple_of((1 - core) * HW, HW), HW)] = got_r[...]
+    both = []
+    for rows, h in ((slice(0, CL), hown), (slice(CL, ROWS), hnext)):
+        total = sum(g[i, rows].astype(F32) * h[i] for i in range(3))
+        both.append(jnp.sum(total, axis=1, keepdims=True))
+    dots = jnp.concatenate(both, axis=0)
+    sums[...] = jnp.broadcast_to(dots, (ROWS, 128))
+    lane = lax.broadcasted_iota(jnp.int32, (ROWS, 128), 1)
+    hi = dots.astype(BF16).astype(F32)
+    lo = (dots - hi).astype(BF16).astype(F32)
+    lo2 = dots - hi - lo
+    packed = jnp.where(lane == 0, hi, jnp.where(lane == 1, lo, lo2))
+    message(g, (wq, wk, wv, wo), lax.rem(z + 2, 4), msg2)
+    msg2[CL : CL + ROWS, WL : WL + 128] = jnp.where(lane < 3, packed, 0.0).astype(BF16)
+
+
+def partial_near_kernel(g, sums, msg2, crow, nxt, wq, wk, wv, wo, msg1, msg3, keep, cz, inv_out, c):
+    z = Place().z
+    weights = (wq, wk, wv, wo)
+    for shift, msg in ((1, msg1), (3, msg3)):
+        message(g, weights, lax.rem(z + shift, 4), msg)
+        msg[CL : CL + ROWS, WL : WL + 128] = msg2[CL : CL + ROWS, WL : WL + 128]
+    message(g, weights, z, keep)
+    keep[CL : CL + ROWS, WL : WL + 128] = sums[...]
     c[0:CL] = crow[...]
     c[CL:ROWS] = nxt[...]
     cf = c[...].astype(F32)
     r = lax.rsqrt(jnp.sum(cf * cf, axis=1, keepdims=True) * (1.0 / D) + 1e-6)
     inv_out[...] = jnp.broadcast_to(r, (ROWS, 128))
-    lane = lax.broadcasted_iota(jnp.int32, (ROWS, 128), 1)
-    dots = jnp.zeros((ROWS, 1), F32)
-    for shift, msg in ((1, msg1), (2, msg2), (3, msg3), (0, keep)):
-        t = lax.rem(z + shift, 4)
-        part = pl.ds(pl.multiple_of(t * WL, WL), WL)
-        gn = dg(g[0], wq[part], 1, 1) + dg(g[1], wk[part], 1, 1) + dg(g[2], wv[part], 1, 1)
-        cb = c[:, part]
-        dots = dots + jnp.sum(gn * gain[0:1, part] * cb.astype(F32), axis=1, keepdims=True)
-        msg[0:CL, 0:WL] = dg(g[3, 0:CL], wo[part], 1, 1).astype(msg.dtype)
-        msg[CL : CL + ROWS, 0:WL] = gn.astype(msg.dtype)
-        msg[0:CL, WL : WL + 128] = jnp.zeros((CL, 128), msg.dtype)
-        if shift == 0:
-            cz[...] = cb
-    keep[CL : CL + ROWS, WL : WL + 128] = jnp.broadcast_to(dots, (ROWS, 128))
-    hi = dots.astype(BF16)
-    lo = (dots - hi.astype(F32)).astype(BF16)
-    lo2 = (dots - hi.astype(F32) - lo.astype(F32)).astype(BF16)
-    packed = jnp.where(lane == 0, hi.astype(F32), jnp.where(lane == 1, lo.astype(F32), lo2.astype(F32)))
-    packed = jnp.where(lane < 3, packed, 0.0).astype(BF16)
-    for msg in (msg1, msg2, msg3):
-        msg[CL : CL + ROWS, WL : WL + 128] = packed
+    cz[...] = c[:, pl.ds(pl.multiple_of(z * WL, WL), WL)]
 
 
 def total_kernel(own, other, o0, o1, o2, o3):
@@ -384,11 +406,11 @@
         smem=(1,),
     )
     pieces = [piece] + [shifted(piece, "tensor", s) for s in (1, 2, 3)]
-    keep, send, blocks, crow = call(
+    keep, send, blocks, crow, hown = call(
         project_kernel,
-        [((64, 4 * HW), BF16), ((80, 4 * HW), BF16), ((4, CL, 4 * HW), BF16), ((CL, D), BF16)],
+        [((64, 4 * HW), BF16), ((80, 4 * HW), BF16), ((4, CL, 4 * HW), BF16), ((CL, D), BF16), ((3, CL, WL), F32)],
         (*pieces, gain, *weights),
-        [((2 * CL, D), BF16), ((2 * CL, D), BF16), ((2 * CL, D), BF16), ((2, 2 * CL, 4 * HW), BF16)],
+        [((2 * CL, D), BF16), ((2 * CL, D), BF16), ((2 * CL, D), BF16), ((2, 2 * CL, 4 * HW), BF16), ((2 * CL, WL), F32)],
         smem=(),
         flops=10**9,
     )
@@ -405,10 +427,17 @@
     low_far, high_far = shifted(up_far, "x", 1), shifted(down_far, "x", -1)
     low_near, high_near = shifted(up_near, "x", 1), shifted(down_near, "x", -1)
     far_low, far_high = shifted(low_far, "x", 1), shifted(high_far, "x", -1)
-    mine, nxt = call(
+    nxt, hnext = call(
+        next_kernel,
+        [((16, D), BF16), ((3, 16, WL), F32)],
+        (high_near, swapped, gain, *weights[:3]),
+        smem=(),
+        flops=10**9,
+    )
+    (mine,) = call(
         gather_kernel,
-        [((4, CL, 4 * HW), BF16), ((16, D), BF16)],
-        (b0, low_near, high_near, far_low, far_high, swapped),
+        [((4, CL, 4 * HW), BF16)],
+        (b0, low_near, high_near, far_low, far_high, nxt),
         smem=(),
     )
     other_rows = shifted(mine, "core", 1)
@@ -431,11 +460,18 @@
     )
     dw_got = shifted(dw_send, "dp", 1)
     msg = (CL + ROWS, WL + 128)
-    m1, m2, m3, own, cz, inv = call(
-        partial_kernel,
-        [(msg, BF16), (msg, BF16), (msg, BF16), (msg, F32), ((ROWS, WL), BF16), ((ROWS, 128), F32)],
-        (keep_r, got_r, crow, nxt, dw_keep, gain, *weights),
-        [((4, ROWS, WL), BF16), ((ROWS, D), BF16)],
+    m2, g, sums = call(
+        partial_far_kernel,
+        [(msg, BF16), ((4, ROWS, WL), BF16), ((ROWS, 128), F32)],
+        (keep_r, got_r, hown, hnext, dw_keep, *weights),
+        smem=(),
+        flops=3 * 10**8,
+    )
+    m1, m3, own, cz, inv = call(
+        partial_near_kernel,
+        [(msg, BF16), (msg, BF16), (msg, F32), ((ROWS, WL), BF16), ((ROWS, 128), F32)],
+        (g, sums, m2, crow, nxt, *weights),
+        [((ROWS, D), BF16)],
         smem=(),
         flops=10**9,
     )
@@ -443,7 +479,7 @@
     dw_own, dw_other = call(
         sum_kernel,
         [((4, 64, HW), F32), ((4, 64, HW), BF16)],
-        (dw_keep, dw_got, r1),
+        (dw_keep, dw_got, r2),
         smem=(),
     )
     dw_other = shifted(dw_other, "core", 1)

time: 66.3 us -> 68.5 us (1.033)
  local copies, waits for them, and re-layouts: 0.5 us -> 4.34 us
  waiting for transfers between devices: 16.5 us -> 12.8 us
  Pallas kernels: 13.8 us -> 14.9 us
    unnamed x27 -> x33, local copies, waits for them, and re-layouts: 0.32 us -> 4.17 us
    ppermute x18, waiting for transfers between devices: 11.9 us -> 8.13 us  [shifted(): return lax.ppermute(x, axis, [(i, (i + steps) % n) for i in range(n)])]
    pallas_call x13 -> x15, Pallas kernels: 13.8 us -> 14.9 us  [call(): pl.pallas_call(kernel, out_shape=[pltpu.VMEM(s, d) if typed else jax.Shap...]
  transfers between devices with their start and end apart: 20 -> 20, of which waited for: 10 -> 8; matrix products, arithmetic and copies ran while one was open for 1% -> 1% of each run, Pallas kernels for 14% -> 14%
where the time goes in v11:
time: 68.5 us; the launch traced here: 67.3 us
  starting transfers between devices  33.8 us (49%)
  Pallas kernels  14.9 us (22%)
  waiting for transfers between devices  12.8 us (19%)
  local copies, waits for them, and re-layouts  4.34 us (6%)
  between operations  1.48 us (2%)
    ppermute x18, starting transfers between devices, shifted(): return lax.ppermute(x, axis, [(i, (i + steps) % n) for i in range(n)])  29.2 us
    pallas_call x15, Pallas kernels, call(): pl.pallas_call(kernel, out_shape=[pltpu.VMEM(s, d) if typed else jax.Shap...  14.9 us
    ppermute x18, waiting for transfers between devices, shifted(): return lax.ppermute(x, axis, [(i, (i + steps) % n) for i in range(n)])  8.13 us
    ppermute x1, waiting for transfers between devices, local(): rim_across = lax.ppermute(last, line, over)  4.62 us
    unnamed x33, local copies, waits for them, and re-layouts  4.17 us
    ppermute x1, starting transfers between devices, local(): rim = lax.ppermute(last, line, [(i, i + 1) for i in range(15)])  2.71 us
    ppermute x1, starting transfers between devices, local(): rim_across = lax.ppermute(last, line, over)  1.92 us
  transfers between devices with their start and end apart: 20, of which 8 were waited for; matrix products, arithmetic and copies ran while one was open for 1% of the time, Pallas kernels for 14%

profile of v11, /device:TPU:1, one launch (start us, length us, event | category | flops | bytes accessed | tf_op | source)
XLA Modules:
  0.0 67.3 jit_solution(6999248778896223873)
XLA Ops:
  1.3 1.9 %shard_map.172 = (bf16[80,512]{1,0:T(8,128)(2,1)S(1)}, f32[8,512]{1,0:T(8,128)S(1)}, f32[8,512]{1,0:T(8,128)S(1)}, f32[1,2048]{1,0:T(1,128)S(1)}) custom-call(s32[1]{0:T(128)S(6)} %copy.20.lens, bf16[512,512]{1,0:T(8,128)(2,1)} %bitcast.7, bf16[512,512]{1,0:T(8,128)(2,1)} %bitcast.8, f32[4,512]{1,0:T(4,128)} %first.1, f32[4,512]{1,0:T(4,128)} %second.1, ...), custom_call_target="tpu_custom_call" | custom-call | tf_op jit(solution)/shard_map/pallas_call | solution.py:350
  3.2 3.8 %collective-permute-start = (bf16[80,512]{1,0:T(8,128)(2,1)S(1)}, bf16[80,512]{1,0:T(8,128)(2,1)S(1)}, u32[]{:S(2)}, u32[]{:S(2)}) collective-permute-start(bf16[80,512]{1,0:T(8,128)(2,1)S(1)} %get-tuple-element.43.piece), channel_id=1, source_target_pairs={{0,8},{8,0},{1,9},{9,1},{2,10},{10,2},{3,11},{11,3},{4,12},{12,4},... | collective-permute-start | bytes 245768 | tf_op jit(solution)/shard_map/ppermute | solution.py:363
  7.0 2.7 %collective-permute-start.1 = (f32[8,512]{1,0:T(8,128)S(1)}, f32[8,512]{1,0:T(8,128)S(1)}, u32[]{:S(2)}, u32[]{:S(2)}) collective-permute-start(f32[8,512]{1,0:T(8,128)S(1)} %get-tuple-element.45), channel_id=1, source_target_pairs={{0,4},{4,8},{8,12},{12,16},{16,20},{20,24},{24,28},{28,32},{32,36}... | collective-permute-start | bytes 49160 | tf_op jit(solution)/shard_map/ppermute | solution.py:383
  9.7 1.9 %collective-permute-start.2 = (f32[8,512]{1,0:T(8,128)S(1)}, f32[8,512]{1,0:T(8,128)S(1)}, u32[]{:S(2)}, u32[]{:S(2)}) collective-permute-start(f32[8,512]{1,0:T(8,128)S(1)} %get-tuple-element.45), channel_id=1, source_target_pairs={{0,12},{4,0},{8,4},{12,24},{16,28},{20,16},{24,20},{28,40},{32,44}... | collective-permute-start | bytes 49160 | tf_op jit(solution)/shard_map/ppermute | solution.py:386
  11.7 4.6 %collective-permute-done.2.rim_across = f32[8,512]{1,0:T(8,128)S(1)} collective-permute-done((f32[8,512]{1,0:T(8,128)S(1)}, f32[8,512]{1,0:T(8,128)S(1)}, u32[]{:S(2)}, u32[]{:S(2)}) %collective-permute-start.2) | collective-permute-done | bytes 16416 | tf_op jit(solution)/shard_map/ppermute | solution.py:386
  16.4 1.8 %collective-permute-start.3 = (bf16[128,512]{1,0:T(8,128)(2,1)S(1)}, bf16[128,512]{1,0:T(8,128)(2,1)S(1)}, u32[]{:S(2)}, u32[]{:S(2)}) collective-permute-start(bf16[128,512]{1,0:T(8,128)(2,1)S(1)} %shard_map.173.p0), channel_id=1, source_target_pairs={{0,1},{1,2},{2,3},{3,0},{4,5},{5,6},{6,7},{7,4},{8,9},{9,10},{10,1... | collective-permute-start | bytes 393224 | tf_op jit(solution)/shard_map/ppermute | solution.py:363
  18.2 3.3 %collective-permute-start.4 = (bf16[128,512]{1,0:T(8,128)(2,1)S(1)}, bf16[128,512]{1,0:T(8,128)(2,1)S(1)}, u32[]{:S(2)}, u32[]{:S(2)}) collective-permute-start(bf16[128,512]{1,0:T(8,128)(2,1)S(1)} %shard_map.173.p0), channel_id=1, source_target_pairs={{0,2},{1,3},{2,0},{3,1},{4,6},{5,7},{6,4},{7,5},{8,10},{9,11},{10,... | collective-permute-start | bytes 393224 | tf_op jit(solution)/shard_map/ppermute | solution.py:363
  22.2 0.9 %collective-permute-done.3.r1 = bf16[128,512]{1,0:T(8,128)(2,1)S(1)} collective-permute-done((bf16[128,512]{1,0:T(8,128)(2,1)S(1)}, bf16[128,512]{1,0:T(8,128)(2,1)S(1)}, u32[]{:S(2)}, u32[]{:S(2)}) %collective-permute-start.3) | collective-permute-done | bytes 131104 | tf_op jit(solution)/shard_map/ppermute | solution.py:363
  23.1 3.4 %collective-permute-done.4.r2 = bf16[128,512]{1,0:T(8,128)(2,1)S(1)} collective-permute-done((bf16[128,512]{1,0:T(8,128)(2,1)S(1)}, bf16[128,512]{1,0:T(8,128)(2,1)S(1)}, u32[]{:S(2)}, u32[]{:S(2)}) %collective-permute-start.4) | collective-permute-done | bytes 131104 | tf_op jit(solution)/shard_map/ppermute | solution.py:363
  26.7 1.6 %shard_map.174 = (bf16[64,1024]{1,0:T(8,128)(2,1)S(1)}, bf16[80,1024]{1,0:T(8,128)(2,1)S(1)}, bf16[4,32,1024]{2,1,0:T(8,128)(2,1)S(1)}, bf16[32,2048]{1,0:T(8,128)(2,1)S(1)}, f32[3,32,512]{2,1,0:T(8,128)S(1)}) custom-call(bf16[128,512]{1,0:T(8,128)(2,1)S(1)} %shard_map.173.p0, bf16[128,512]{1,0:T(8,128)(2,1)S(1)} %collective-permute-done.3.r1, ...), custom_call_target="tpu_custom_call" | custom-call | flops 1000000000 | tf_op jit(solution)/shard_map/pallas_call | solution.py:350
  28.4 2.1 %collective-permute-start.6 = (bf16[80,1024]{1,0:T(8,128)(2,1)S(1)}, bf16[80,1024]{1,0:T(8,128)(2,1)S(1)}, u32[]{:S(2)}, u32[]{:S(2)}) collective-permute-start(bf16[80,1024]{1,0:T(8,128)(2,1)S(1)} %get-tuple-element.48), channel_id=1, source_target_pairs={{0,4},{4,0},{1,5},{5,1},{2,6},{6,2},{3,7},{7,3},{8,12},{12,8},{9,1... | collective-permute-start | bytes 491528 | tf_op jit(solution)/shard_map/ppermute | solution.py:363
  30.5 1.0 %collective-permute-done.6.swapped = bf16[80,1024]{1,0:T(8,128)(2,1)S(1)} collective-permute-done((bf16[80,1024]{1,0:T(8,128)(2,1)S(1)}, bf16[80,1024]{1,0:T(8,128)(2,1)S(1)}, u32[]{:S(2)}, u32[]{:S(2)}) %collective-permute-start.6) | collective-permute-done | bytes 163872 | tf_op jit(solution)/shard_map/ppermute | solution.py:363
  31.5 0.8 %shard_map.176 = (bf16[80,1024]{1,0:T(8,128)(2,1)}, bf16[80,1024]{1,0:T(8,128)(2,1)}) custom-call(bf16[64,1024]{1,0:T(8,128)(2,1)S(1)} %get-tuple-element.47.keep, bf16[80,1024]{1,0:T(8,128)(2,1)S(1)} %collective-permute-done.6.swapped, bf16[4,32,1024]{2,1,0:T(8,128)(2,1)S(1)} %get-tuple-element.49.blocks), custom_call_target="tpu_custom_call" | custom-call | tf_op jit(solution)/shard_map/pallas_call | solution.py:350
  32.3 1.2 %collective-permute-start.7 = (bf16[80,1024]{1,0:T(8,128)(2,1)}, bf16[80,1024]{1,0:T(8,128)(2,1)}, u32[]{:S(2)}, u32[]{:S(2)}) collective-permute-start(bf16[80,1024]{1,0:T(8,128)(2,1)} %get-tuple-element.51), channel_id=1, source_target_pairs={{0,16},{16,32},{32,48},{48,0},{1,17},{17,33},{33,49},{49,1},{2,18}... | collective-permute-start | bytes 491528 | tf_op jit(solution)/shard_map/ppermute | solution.py:363
  33.5 1.5 %collective-permute-start.9 = (bf16[80,1024]{1,0:T(8,128)(2,1)}, bf16[80,1024]{1,0:T(8,128)(2,1)}, u32[]{:S(2)}, u32[]{:S(2)}) collective-permute-start(bf16[80,1024]{1,0:T(8,128)(2,1)} %get-tuple-element.53), channel_id=1, source_target_pairs={{0,48},{16,0},{32,16},{48,32},{1,49},{17,1},{33,17},{49,33},{2,50}... | collective-permute-start | bytes 491528 | tf_op jit(solution)/shard_map/ppermute | solution.py:363
  36.6 1.0 %collective-permute-start.8 = (bf16[96,1024]{1,0:T(8,128)(2,1)}, bf16[96,1024]{1,0:T(8,128)(2,1)S(1)}, u32[]{:S(2)}, u32[]{:S(2)}) collective-permute-start(bf16[96,1024]{1,0:T(8,128)(2,1)} %copy-done.12), channel_id=1, source_target_pairs={{0,16},{16,32},{32,48},{48,0},{1,17},{17,33},{33,49},{49,1},{2,18}... | collective-permute-start | bytes 589832 | tf_op jit(solution)/shard_map/ppermute | solution.py:363
  37.6 1.6 %collective-permute-done.7.low_far = bf16[80,1024]{1,0:T(8,128)(2,1)} collective-permute-done((bf16[80,1024]{1,0:T(8,128)(2,1)}, bf16[80,1024]{1,0:T(8,128)(2,1)}, u32[]{:S(2)}, u32[]{:S(2)}) %collective-permute-start.7) | collective-permute-done | bytes 163872 | tf_op jit(solution)/shard_map/ppermute | solution.py:363
  39.2 2.7 %collective-permute-start.12 = (bf16[80,1024]{1,0:T(8,128)(2,1)}, bf16[80,1024]{1,0:T(8,128)(2,1)S(1)}, u32[]{:S(2)}, u32[]{:S(2)}) collective-permute-start(bf16[80,1024]{1,0:T(8,128)(2,1)} %collective-permute-done.9.high_far), channel_id=1, source_target_pairs={{0,48},{16,0},{32,16},{48,32},{1,49},{17,1},{33,17},{49,33},{2,50}... | collective-permute-start | bytes 491528 | tf_op jit(solution)/shard_map/ppermute | solution.py:363
  42.0 1.1 %shard_map.177.strip = f32[2,128,512]{2,1,0:T(8,128)S(1)} custom-call(s32[8,640]{1,0:T(8,128)S(1)} %broadcast_in_dim.20.near, f32[32,4]{1,0:T(8,128)S(1)} %copy.19.table), custom_call_target="tpu_custom_call" | custom-call | tf_op jit(solution)/shard_map/pallas_call | solution.py:350
  43.7 1.6 %copy-done.2 = bf16[2048,512]{1,0:T(8,128)(2,1)S(1)} copy-done((bf16[2048,512]{1,0:T(8,128)(2,1)S(1)}, bf16[2048,512]{1,0:T(8,128)(2,1)}, u32[]{:S(2)}) %copy-start.2) | copy-done | bytes 2097176
  45.3 1.6 %copy-done.5 = bf16[2048,512]{1,0:T(8,128)(2,1)S(1)} copy-done((bf16[2048,512]{1,0:T(8,128)(2,1)S(1)}, bf16[2048,512]{1,0:T(8,128)(2,1)}, u32[]{:S(2)}) %copy-start.5) | copy-done | bytes 2097176
  46.9 0.9 %shard_map.179 = (bf16[16,2048]{1,0:T(8,128)(2,1)S(1)}, f32[3,16,512]{2,1,0:T(8,128)S(1)}) custom-call(bf16[112,1024]{1,0:T(8,128)(2,1)S(1)} %collective-permute-done.10.high_near, bf16[80,1024]{1,0:T(8,128)(2,1)S(1)} %collective-permute-done.6.swapped, f32[1,2048]{1,0:T(1,128)S(1)} %get-tuple-element.46.gain, bf16[2048,512]{1,0:T(8,128)(2,1)S(1)} %copy-done, ...), custom_call_target="tpu_custom_call" | custom-call | flops 1000000000 | tf_op jit(solution)/shard_map/pallas_call | solution.py:350
  47.9 2.7 %collective-permute-start.14 = (bf16[4,32,1024]{2,1,0:T(8,128)(2,1)S(1)}, bf16[4,32,1024]{2,1,0:T(8,128)(2,1)S(1)}, u32[]{:S(2)}, u32[]{:S(2)}) collective-permute-start(bf16[4,32,1024]{2,1,0:T(8,128)(2,1)S(1)} %shard_map.180.mine), channel_id=1, source_target_pairs={{0,4},{4,0},{1,5},{5,1},{2,6},{6,2},{3,7},{7,3},{8,12},{12,8},{9,1... | collective-permute-start | bytes 786440 | tf_op jit(solution)/shard_map/ppermute | solution.py:363
  50.6 2.9 %shard_map.178 = (bf16[4,528,256]{2,1,0:T(8,128)(2,1)S(1)}, bf16[4,48,256]{2,1,0:T(8,128)(2,1)S(1)}, bf16[4,48,256]{2,1,0:T(8,128)(2,1)S(1)}) custom-call(s32[1]{0:T(128)S(6)} %copy.20.lens, bf16[160,1024]{1,0:T(8,128)(2,1)S(1)} %get-tuple-element.50.b0, bf16[80,1024]{1,0:T(8,128)(2,1)} %collective-permute-done.7.low_far, ...), custom_call_target="tpu_custom_call" | custom-call | flops 6000000000 | tf_op jit(solution)/shard_map/pallas_call | solution.py:350
  54.2 1.4 %collective-permute-start.18 = (bf16[4,128,256]{2,1,0:T(8,128)(2,1)S(1)}, bf16[4,128,256]{2,1,0:T(8,128)(2,1)S(1)}, u32[]{:S(2)}, u32[]{:S(2)}) collective-permute-start(bf16[4,128,256]{2,1,0:T(8,128)(2,1)S(1)} %get-tuple-element.73), channel_id=1, source_target_pairs={{0,64},{64,0},{1,65},{65,1},{2,66},{66,2},{3,67},{67,3},{4,68},{68... | collective-permute-start | bytes 786440 | tf_op jit(solution)/shard_map/ppermute | solution.py:363
  55.6 0.8 %shard_map.182 = (bf16[80,640]{1,0:T(8,128)(2,1)S(1)}, bf16[4,48,512]{2,1,0:T(8,128)(2,1)S(1)}, f32[48,128]{1,0:T(8,128)S(1)}) custom-call(bf16[4,48,256]{2,1,0:T(8,128)(2,1)S(1)} %get-tuple-element.55.keep_r, bf16[4,48,256]{2,1,0:T(8,128)(2,1)S(1)} %collective-permute-done.13.got_r, f32[3,32,512]{2,1,0:T(8,128)S(1)} %get-tuple-element.57.hown, ...), custom_call_target="tpu_custom_call" | custom-call | flops 300000000 | tf_op jit(solution)/shard_map/pallas_call | solution.py:350
  56.3 2.0 %collective-permute-start.16 = (bf16[80,640]{1,0:T(8,128)(2,1)S(1)}, bf16[80,640]{1,0:T(8,128)(2,1)S(1)}, u32[]{:S(2)}, u32[]{:S(2)}) collective-permute-start(bf16[80,640]{1,0:T(8,128)(2,1)S(1)} %get-tuple-element.64.msg2), channel_id=1, source_target_pairs={{0,2},{1,3},{2,0},{3,1},{4,6},{5,7},{6,4},{7,5},{8,10},{9,11},{10,... | collective-permute-start | bytes 307208 | tf_op jit(solution)/shard_map/ppermute | solution.py:363
  58.4 1.9 %shard_map.183 = (bf16[80,640]{1,0:T(8,128)(2,1)S(1)}, bf16[80,640]{1,0:T(8,128)(2,1)S(1)}, f32[80,640]{1,0:T(8,128)S(1)}, bf16[48,512]{1,0:T(8,128)(2,1)S(1)}, f32[48,128]{1,0:T(8,128)S(1)}) custom-call(bf16[4,48,512]{2,1,0:T(8,128)(2,1)S(1)} %get-tuple-element.62.g, f32[48,128]{1,0:T(8,128)S(1)} %get-tuple-element.63.sums, ...), custom_call_target="tpu_custom_call" | custom-call | flops 1000000000 | tf_op jit(solution)/shard_map/pallas_call | solution.py:350
  60.8 2.2 %collective-permute-start.17 = (bf16[80,640]{1,0:T(8,128)(2,1)S(1)}, bf16[80,640]{1,0:T(8,128)(2,1)S(1)}, u32[]{:S(2)}, u32[]{:S(2)}) collective-permute-start(bf16[80,640]{1,0:T(8,128)(2,1)S(1)} %get-tuple-element.68), channel_id=1, source_target_pairs={{0,3},{1,0},{2,1},{3,2},{4,7},{5,4},{6,5},{7,6},{8,11},{9,8},{10,9... | collective-permute-start | bytes 307208 | tf_op jit(solution)/shard_map/ppermute | solution.py:363
  63.1 1.7 %collective-permute-start.19 = (bf16[4,64,256]{2,1,0:T(8,128)(2,1)S(1)}, bf16[4,64,256]{2,1,0:T(8,128)(2,1)S(1)}, u32[]{:S(2)}, u32[]{:S(2)}) collective-permute-start(bf16[4,64,256]{2,1,0:T(8,128)(2,1)S(1)} %get-tuple-element.75), channel_id=1, source_target_pairs={{0,4},{4,0},{1,5},{5,1},{2,6},{6,2},{3,7},{7,3},{8,12},{12,8},{9,1... | collective-permute-start | bytes 393224 | tf_op jit(solution)/shard_map/ppermute | solution.py:363
  65.1 1.4 %shard_map.184 = (bf16[512,512]{1,0:T(8,128)(2,1)}, bf16[512,512]{1,0:T(8,128)(2,1)}) custom-call(s32[1]{0:T(128)S(6)} %copy.20.lens, f32[80,640]{1,0:T(8,128)S(1)} %get-tuple-element.66.keep, bf16[80,640]{1,0:T(8,128)(2,1)S(1)} %collective-permute-done.15.r1, bf16[80,640]{1,0:T(8,128)(2,1)S(1)} %collective-permute-done.16.r2, ...), custom_call_target="tpu_custom_call" | custom-call | flops 20000000000 | tf_op jit(solution)/shard_map/pallas_call | solution.py:350
  66.5 0.8 %shard_map.186 = (f32[64,512]{1,0:T(8,128)}, f32[64,512]{1,0:T(8,128)}, f32[64,512]{1,0:T(8,128)}, f32[64,512]{1,0:T(8,128)}) custom-call(f32[4,64,256]{2,1,0:T(8,128)S(1)} %get-tuple-element.74.own, bf16[4,64,256]{2,1,0:T(8,128)(2,1)S(1)} %collective-permute-done.19.other), custom_call_target="tpu_custom_call" | custom-call | flops 6000000000 | tf_op jit(solution)/shard_map/pallas_call | solution.py:350
  (61 shorter events, 5.0 us)
Async XLA Ops:
  3.2 13.1 %collective-permute-start = (bf16[80,512]{1,0:T(8,128)(2,1)S(1)}, bf16[80,512]{1,0:T(8,128)(2,1)S(1)}, u32[]{:S(2)}, u32[]{:S(2)}) collective-permute-start(bf16[80,512]{1,0:T(8,128)(2,1)S(1)} %get-tuple-element.43.piece), channel_id=1, source_target_pairs={{0,8},{8,0},{1,9},{9,1},{2,10},{10,2},{3,11},{11,3},{4,12},{12,4},... | collective-permute-start | bytes 245768 | tf_op jit(solution)/shard_map/ppermute | solution.py:363
  7.0 4.6 %collective-permute-start.1 = (f32[8,512]{1,0:T(8,128)S(1)}, f32[8,512]{1,0:T(8,128)S(1)}, u32[]{:S(2)}, u32[]{:S(2)}) collective-permute-start(f32[8,512]{1,0:T(8,128)S(1)} %get-tuple-element.45), channel_id=1, source_target_pairs={{0,4},{4,8},{8,12},{12,16},{16,20},{20,24},{24,28},{28,32},{32,36}... | collective-permute-start | bytes 49160 | tf_op jit(solution)/shard_map/ppermute | solution.py:383
  9.7 6.6 %collective-permute-start.2 = (f32[8,512]{1,0:T(8,128)S(1)}, f32[8,512]{1,0:T(8,128)S(1)}, u32[]{:S(2)}, u32[]{:S(2)}) collective-permute-start(f32[8,512]{1,0:T(8,128)S(1)} %get-tuple-element.45), channel_id=1, source_target_pairs={{0,12},{4,0},{8,4},{12,24},{16,28},{20,16},{24,20},{28,40},{32,44}... | collective-permute-start | bytes 49160 | tf_op jit(solution)/shard_map/ppermute | solution.py:386
  16.3 10.4 %copy-start = (bf16[2048,512]{1,0:T(8,128)(2,1)S(1)}, bf16[2048,512]{1,0:T(8,128)(2,1)}, u32[]{:S(2)}) copy-start(bf16[2048,512]{1,0:T(8,128)(2,1)} %wq.7) | copy-start | bytes 6291460
  16.3 10.4 %copy-start.1 = (bf16[2048,512]{1,0:T(8,128)(2,1)S(1)}, bf16[2048,512]{1,0:T(8,128)(2,1)}, u32[]{:S(2)}) copy-start(bf16[2048,512]{1,0:T(8,128)(2,1)} %wk.7) | copy-start | bytes 6291460
  16.3 10.4 %copy-start.4 = (bf16[2048,512]{1,0:T(8,128)(2,1)S(1)}, bf16[2048,512]{1,0:T(8,128)(2,1)}, u32[]{:S(2)}) copy-start(bf16[2048,512]{1,0:T(8,128)(2,1)} %wv.7) | copy-start | bytes 6291460
  16.3 10.4 %copy-start.7 = (bf16[2048,512]{1,0:T(8,128)(2,1)S(1)}, bf16[2048,512]{1,0:T(8,128)(2,1)}, u32[]{:S(2)}) copy-start(bf16[2048,512]{1,0:T(8,128)(2,1)} %wo.5) | copy-start | bytes 6291460
  16.4 6.8 %collective-permute-start.3 = (bf16[128,512]{1,0:T(8,128)(2,1)S(1)}, bf16[128,512]{1,0:T(8,128)(2,1)S(1)}, u32[]{:S(2)}, u32[]{:S(2)}) collective-permute-start(bf16[128,512]{1,0:T(8,128)(2,1)S(1)} %shard_map.173.p0), channel_id=1, source_target_pairs={{0,1},{1,2},{2,3},{3,0},{4,5},{5,6},{6,7},{7,4},{8,9},{9,10},{10,1... | collective-permute-start | bytes 393224 | tf_op jit(solution)/shard_map/ppermute | solution.py:363
  18.2 8.3 %collective-permute-start.4 = (bf16[128,512]{1,0:T(8,128)(2,1)S(1)}, bf16[128,512]{1,0:T(8,128)(2,1)S(1)}, u32[]{:S(2)}, u32[]{:S(2)}) collective-permute-start(bf16[128,512]{1,0:T(8,128)(2,1)S(1)} %shard_map.173.p0), channel_id=1, source_target_pairs={{0,2},{1,3},{2,0},{3,1},{4,6},{5,7},{6,4},{7,5},{8,10},{9,11},{10,... | collective-permute-start | bytes 393224 | tf_op jit(solution)/shard_map/ppermute | solution.py:363
  21.5 5.2 %collective-permute-start.5 = (bf16[128,512]{1,0:T(8,128)(2,1)S(1)}, bf16[128,512]{1,0:T(8,128)(2,1)S(1)}, u32[]{:S(2)}, u32[]{:S(2)}) collective-permute-start(bf16[128,512]{1,0:T(8,128)(2,1)S(1)} %shard_map.173.p0), channel_id=1, source_target_pairs={{0,3},{1,0},{2,1},{3,2},{4,7},{5,4},{6,5},{7,6},{8,11},{9,8},{10,9... | collective-permute-start | bytes 393224 | tf_op jit(solution)/shard_map/ppermute | solution.py:363
  26.7 9.5 %copy-start.14 = (s32[512]{0:T(512)S(1)}, s32[512]{0:T(512)}, u32[]{:S(2)}) copy-start(s32[512]{0:T(512)} %param.23) | copy-start | bytes 6148
  26.7 9.8 %copy-start.13 = (f32[32,4]{0,1:T(4,128)S(1)}, f32[32,4]{0,1:T(4,128)}, u32[]{:S(2)}) copy-start(f32[32,4]{0,1:T(4,128)} %param.22) | copy-start | bytes 1540
  28.4 3.2 %collective-permute-start.6 = (bf16[80,1024]{1,0:T(8,128)(2,1)S(1)}, bf16[80,1024]{1,0:T(8,128)(2,1)S(1)}, u32[]{:S(2)}, u32[]{:S(2)}) collective-permute-start(bf16[80,1024]{1,0:T(8,128)(2,1)S(1)} %get-tuple-element.48), channel_id=1, source_target_pairs={{0,4},{4,0},{1,5},{5,1},{2,6},{6,2},{3,7},{7,3},{8,12},{12,8},{9,1... | collective-permute-start | bytes 491528 | tf_op jit(solution)/shard_map/ppermute | solution.py:363
  32.3 6.9 %collective-permute-start.7 = (bf16[80,1024]{1,0:T(8,128)(2,1)}, bf16[80,1024]{1,0:T(8,128)(2,1)}, u32[]{:S(2)}, u32[]{:S(2)}) collective-permute-start(bf16[80,1024]{1,0:T(8,128)(2,1)} %get-tuple-element.51), channel_id=1, source_target_pairs={{0,16},{16,32},{32,48},{48,0},{1,17},{17,33},{33,49},{49,1},{2,18}... | collective-permute-start | bytes 491528 | tf_op jit(solution)/shard_map/ppermute | solution.py:363
  33.5 5.7 %collective-permute-start.9 = (bf16[80,1024]{1,0:T(8,128)(2,1)}, bf16[80,1024]{1,0:T(8,128)(2,1)}, u32[]{:S(2)}, u32[]{:S(2)}) collective-permute-start(bf16[80,1024]{1,0:T(8,128)(2,1)} %get-tuple-element.53), channel_id=1, source_target_pairs={{0,48},{16,0},{32,16},{48,32},{1,49},{17,1},{33,17},{49,33},{2,50}... | collective-permute-start | bytes 491528 | tf_op jit(solution)/shard_map/ppermute | solution.py:363
  35.7 8.0 %collective-permute-start.10 = (bf16[112,1024]{1,0:T(8,128)(2,1)S(1)}, bf16[112,1024]{1,0:T(8,128)(2,1)S(1)}, u32[]{:S(2)}, u32[]{:S(2)}) collective-permute-start(bf16[112,1024]{1,0:T(8,128)(2,1)S(1)} %get-tuple-element.54), channel_id=1, source_target_pairs={{0,48},{16,0},{32,16},{48,32},{1,49},{17,1},{33,17},{49,33},{2,50}... | collective-permute-start | bytes 688136 | tf_op jit(solution)/shard_map/ppermute | solution.py:363
  36.6 11.2 %collective-permute-start.8 = (bf16[96,1024]{1,0:T(8,128)(2,1)}, bf16[96,1024]{1,0:T(8,128)(2,1)S(1)}, u32[]{:S(2)}, u32[]{:S(2)}) collective-permute-start(bf16[96,1024]{1,0:T(8,128)(2,1)} %copy-done.12), channel_id=1, source_target_pairs={{0,16},{16,32},{32,48},{48,0},{1,17},{17,33},{33,49},{49,1},{2,18}... | collective-permute-start | bytes 589832 | tf_op jit(solution)/shard_map/ppermute | solution.py:363
  39.2 8.6 %collective-permute-start.11 = (bf16[80,1024]{1,0:T(8,128)(2,1)}, bf16[80,1024]{1,0:T(8,128)(2,1)S(1)}, u32[]{:S(2)}, u32[]{:S(2)}) collective-permute-start(bf16[80,1024]{1,0:T(8,128)(2,1)} %collective-permute-done.7.low_far), channel_id=1, source_target_pairs={{0,16},{16,32},{32,48},{48,0},{1,17},{17,33},{33,49},{49,1},{2,18}... | collective-permute-start | bytes 491528 | tf_op jit(solution)/shard_map/ppermute | solution.py:363
  39.2 8.6 %collective-permute-start.12 = (bf16[80,1024]{1,0:T(8,128)(2,1)}, bf16[80,1024]{1,0:T(8,128)(2,1)S(1)}, u32[]{:S(2)}, u32[]{:S(2)}) collective-permute-start(bf16[80,1024]{1,0:T(8,128)(2,1)} %collective-permute-done.9.high_far), channel_id=1, source_target_pairs={{0,48},{16,0},{32,16},{48,32},{1,49},{17,1},{33,17},{49,33},{2,50}... | collective-permute-start | bytes 491528 | tf_op jit(solution)/shard_map/ppermute | solution.py:363
  47.9 5.8 %collective-permute-start.14 = (bf16[4,32,1024]{2,1,0:T(8,128)(2,1)S(1)}, bf16[4,32,1024]{2,1,0:T(8,128)(2,1)S(1)}, u32[]{:S(2)}, u32[]{:S(2)}) collective-permute-start(bf16[4,32,1024]{2,1,0:T(8,128)(2,1)S(1)} %shard_map.180.mine), channel_id=1, source_target_pairs={{0,4},{4,0},{1,5},{5,1},{2,6},{6,2},{3,7},{7,3},{8,12},{12,8},{9,1... | collective-permute-start | bytes 786440 | tf_op jit(solution)/shard_map/ppermute | solution.py:363
  50.6 5.0 %copy-start.6 = (bf16[2048,512]{1,0:T(8,128)(2,1)S(1)}, bf16[2048,512]{1,0:T(8,128)(2,1)}, u32[]{:S(2)}) copy-start(bf16[2048,512]{1,0:T(8,128)(2,1)} %wv.7) | copy-start | bytes 6291460
  50.6 5.0 %copy-start.8 = (bf16[2048,512]{1,0:T(8,128)(2,1)S(1)}, bf16[2048,512]{1,0:T(8,128)(2,1)}, u32[]{:S(2)}) copy-start(bf16[2048,512]{1,0:T(8,128)(2,1)} %wo.5) | copy-start | bytes 6291460
  53.5 2.1 %copy-start.3 = (bf16[2048,512]{1,0:T(8,128)(2,1)S(1)}, bf16[2048,512]{1,0:T(8,128)(2,1)}, u32[]{:S(2)}) copy-start(bf16[2048,512]{1,0:T(8,128)(2,1)} %wk.7) | copy-start | bytes 6291460
  53.5 2.1 %collective-permute-start.13 = (bf16[4,48,256]{2,1,0:T(8,128)(2,1)S(1)}, bf16[4,48,256]{2,1,0:T(8,128)(2,1)S(1)}, u32[]{:S(2)}, u32[]{:S(2)}) collective-permute-start(bf16[4,48,256]{2,1,0:T(8,128)(2,1)S(1)} %get-tuple-element.56), channel_id=1, source_target_pairs={{0,4},{4,0},{1,5},{5,1},{2,6},{6,2},{3,7},{7,3},{8,12},{12,8},{9,1... | collective-permute-start | bytes 294920 | tf_op jit(solution)/shard_map/ppermute | solution.py:363
  54.2 8.8 %collective-permute-start.18 = (bf16[4,128,256]{2,1,0:T(8,128)(2,1)S(1)}, bf16[4,128,256]{2,1,0:T(8,128)(2,1)S(1)}, u32[]{:S(2)}, u32[]{:S(2)}) collective-permute-start(bf16[4,128,256]{2,1,0:T(8,128)(2,1)S(1)} %get-tuple-element.73), channel_id=1, source_target_pairs={{0,64},{64,0},{1,65},{65,1},{2,66},{66,2},{3,67},{67,3},{4,68},{68... | collective-permute-start | bytes 786440 | tf_op jit(solution)/shard_map/ppermute | solution.py:363
  56.3 6.6 %collective-permute-start.16 = (bf16[80,640]{1,0:T(8,128)(2,1)S(1)}, bf16[80,640]{1,0:T(8,128)(2,1)S(1)}, u32[]{:S(2)}, u32[]{:S(2)}) collective-permute-start(bf16[80,640]{1,0:T(8,128)(2,1)S(1)} %get-tuple-element.64.msg2), channel_id=1, source_target_pairs={{0,2},{1,3},{2,0},{3,1},{4,6},{5,7},{6,4},{7,5},{8,10},{9,11},{10,... | collective-permute-start | bytes 307208 | tf_op jit(solution)/shard_map/ppermute | solution.py:363
  58.3 6.7 %copy-start.9 = (f32[16,512]{1,0:T(8,128)S(1)}, f32[16,512]{1,0:T(8,128)}, u32[]{:S(2)}) copy-start(f32[16,512]{1,0:T(8,128)} %up_gain.1) | copy-start | bytes 98308
  58.3 6.7 %copy-start.10 = (f32[4,512]{1,0:T(4,128)S(1)}, f32[4,512]{1,0:T(4,128)}, u32[]{:S(2)}) copy-start(f32[4,512]{1,0:T(4,128)} %first.1) | copy-start | bytes 24580
  58.4 6.7 %copy-start.11 = (f32[4,512]{1,0:T(4,128)S(1)}, f32[4,512]{1,0:T(4,128)}, u32[]{:S(2)}) copy-start(f32[4,512]{1,0:T(4,128)} %second.1) | copy-start | bytes 24580
  60.3 4.8 %collective-permute-start.15 = (bf16[80,640]{1,0:T(8,128)(2,1)S(1)}, bf16[80,640]{1,0:T(8,128)(2,1)S(1)}, u32[]{:S(2)}, u32[]{:S(2)}) collective-permute-start(bf16[80,640]{1,0:T(8,128)(2,1)S(1)} %get-tuple-element.67), channel_id=1, source_target_pairs={{0,1},{1,2},{2,3},{3,0},{4,5},{5,6},{6,7},{7,4},{8,9},{9,10},{10,1... | collective-permute-start | bytes 307208 | tf_op jit(solution)/shard_map/ppermute | solution.py:363
  60.8 4.2 %collective-permute-start.17 = (bf16[80,640]{1,0:T(8,128)(2,1)S(1)}, bf16[80,640]{1,0:T(8,128)(2,1)S(1)}, u32[]{:S(2)}, u32[]{:S(2)}) collective-permute-start(bf16[80,640]{1,0:T(8,128)(2,1)S(1)} %get-tuple-element.68), channel_id=1, source_target_pairs={{0,3},{1,0},{2,1},{3,2},{4,7},{5,4},{6,5},{7,6},{8,11},{9,8},{10,9... | collective-permute-start | bytes 307208 | tf_op jit(solution)/shard_map/ppermute | solution.py:363
  63.1 3.5 %collective-permute-start.19 = (bf16[4,64,256]{2,1,0:T(8,128)(2,1)S(1)}, bf16[4,64,256]{2,1,0:T(8,128)(2,1)S(1)}, u32[]{:S(2)}, u32[]{:S(2)}) collective-permute-start(bf16[4,64,256]{2,1,0:T(8,128)(2,1)S(1)} %get-tuple-element.75), channel_id=1, source_target_pairs={{0,4},{4,0},{1,5},{5,1},{2,6},{6,2},{3,7},{7,3},{8,12},{12,8},{9,1... | collective-permute-start | bytes 393224 | tf_op jit(solution)/shard_map/ppermute | solution.py:363
  (3 other events, 3.9 us)

commit v12 on v11

--- a/solution.py
+++ b/solution.py
@@ -124,18 +124,24 @@
     r = lax.rsqrt(square)
     rms = jnp.sqrt(square)
     nrm[...] = (c * r * gain[...]).astype(BF16)
+    heads_of = [[], []]
     for src, w, slot in ((gco, wo, 3), (nrm, wq, 0), (nrm, wk, 1), (nrm, wv, 2)):
         full = jnp.dot(src[...], w[...], preferred_element_type=F32)
         v = full.astype(BF16)
         if slot < 3:
-            hs[...] = full * rms
+            h = full * rms
+            hs[...] = h
+            for i in range(2):
+                heads_of[i].append(in_three(h[i * CL : i * CL + 1])[:2])
             hown[slot] = hs[pl.ds(pl.multiple_of(y * CL, CL), CL)]
         for half in range(2):
             both[half, :, slot * HW : slot * HW + HW] = v[:, half * HW : half * HW + HW]
     keep[...] = both[core]
     send[0:64] = both[1 - core]
     tops = [c[i * CL : i * CL + 1, j * 1024 : j * 1024 + 1024] for i in range(2) for j in range(2)]
-    send[64:80] = jnp.concatenate(tops + [jnp.zeros((12, 1024), F32)], axis=0).astype(BF16)
+    for (q_hi, q_lo), (k_hi, k_lo), (v_hi, v_lo) in heads_of:
+        tops += [jnp.concatenate(p, axis=1) for p in ((q_hi, k_hi), (v_hi, q_lo), (k_lo, v_lo))]
+    send[64:80] = jnp.concatenate(tops + [jnp.zeros((6, 1024), F32)], axis=0).astype(BF16)
     for s in range(4):
         for d in range(2):
             chip = lax.rem(x + s, 4) * 2 + y
@@ -171,15 +177,12 @@
     b0[128:160] = blocks[0]
 
 
-def gather_kernel(b0, low_near, high_near, far_low, far_high, after, mine):
+def gather_kernel(b0, low_near, high_near, far_low, far_high, swapped, mine, nxt, hnext):
     mine[0] = b0[128:160]
     mine[1] = low_near[0:32]
     mine[2, 0:16] = far_low[64:80]
     mine[2, 16:32] = far_high[64:80]
     mine[3] = high_near[0:32]
-
-
-def next_kernel(high_near, swapped, gain, wq, wk, wv, nxt, hnext):
     at = Place()
     wraps = jnp.logical_and(at.core == 1, at.y == 1)
     tops = jnp.where(wraps, high_near[96:112].astype(F32), swapped[64:80].astype(F32))
@@ -187,9 +190,11 @@
     for j in range(2):
         row = jnp.where(upper, tops[2 + j : 3 + j], tops[j : j + 1])
         nxt[:, j * 1024 : j * 1024 + 1024] = jnp.broadcast_to(row, (16, 1024)).astype(BF16)
-    gained = (nxt[...].astype(F32) * gain[...]).astype(BF16)
-    for i, w in enumerate((wq, wk, wv)):
-        hnext[i] = jnp.dot(gained, w[...], preferred_element_type=F32)
+    a, b, c = [jnp.where(upper, tops[7 + j : 8 + j], tops[4 + j : 5 + j]) for j in range(3)]
+    left, right = slice(0, WL), slice(WL, 2 * WL)
+    products = (a[:, left] + b[:, right], a[:, right] + c[:, left], b[:, left] + c[:, right])
+    for i, h in enumerate(products):
+        hnext[i] = jnp.broadcast_to(h, (16, WL))
 
 
 def attend_kernel(
@@ -427,17 +432,10 @@
     low_far, high_far = shifted(up_far, "x", 1), shifted(down_far, "x", -1)
     low_near, high_near = shifted(up_near, "x", 1), shifted(down_near, "x", -1)
     far_low, far_high = shifted(low_far, "x", 1), shifted(high_far, "x", -1)
-    nxt, hnext = call(
-        next_kernel,
-        [((16, D), BF16), ((3, 16, WL), F32)],
-        (high_near, swapped, gain, *weights[:3]),
-        smem=(),
-        flops=10**9,
-    )
-    (mine,) = call(
+    mine, nxt, hnext = call(
         gather_kernel,
-        [((4, CL, 4 * HW), BF16)],
-        (b0, low_near, high_near, far_low, far_high, nxt),
+        [((4, CL, 4 * HW), BF16), ((16, D), BF16), ((3, 16, WL), F32)],
+        (b0, low_near, high_near, far_low, far_high, swapped),
         smem=(),
     )
     other_rows = shifted(mine, "core", 1)

time: 68.5 us -> 66.5 us (0.971)
  local copies, waits for them, and re-layouts: 4.34 us -> 2.91 us
  starting transfers between devices: 33.8 us -> 32.6 us
  Pallas kernels: 14.9 us -> 14 us
  waiting for transfers between devices: 12.8 us -> 13.6 us
  other arithmetic: 0.08 us -> 0.77 us
    unnamed x33, local copies, waits for them, and re-layouts: 4.17 us -> 2.23 us
    ppermute x18, starting transfers between devices: 29.2 us -> 27.9 us  [shifted(): return lax.ppermute(x, axis, [(i, (i + steps) % n) for i in range(n)])]
    ppermute x18, waiting for transfers between devices: 8.13 us -> 9.02 us  [shifted(): return lax.ppermute(x, axis, [(i, (i + steps) % n) for i in range(n)])]
    pallas_call x15 -> x14, Pallas kernels: 14.9 us -> 14 us  [call(): pl.pallas_call(kernel, out_shape=[pltpu.VMEM(s, d) if typed else jax.Shap...]
    concatenate x1, other arithmetic: 0.08 us -> 0.77 us  [local(): jnp.concatenate([jnp.flip(buckets[:385]), jnp.full((n - LC,), bias_table....]
  transfers between devices with their start and end apart: 20 -> 20, of which waited for: 8 -> 9; matrix products, arithmetic and copies ran while one was open for 1% -> 5% of each run, Pallas kernels for 14% -> 15%
where the time goes in v12:
time: 66.5 us; the launch traced here: 65.4 us
  starting transfers between devices  32.6 us (49%)
  Pallas kernels  14 us (21%)
  waiting for transfers between devices  13.6 us (20%)
  local copies, waits for them, and re-layouts  2.91 us (4%)
  between operations  1.51 us (2%)
  other arithmetic  0.77 us (1%)
    ppermute x18, starting transfers between devices, shifted(): return lax.ppermute(x, axis, [(i, (i + steps) % n) for i in range(n)])  27.9 us
    pallas_call x14, Pallas kernels, call(): pl.pallas_call(kernel, out_shape=[pltpu.VMEM(s, d) if typed else jax.Shap...  14 us
    ppermute x18, waiting for transfers between devices, shifted(): return lax.ppermute(x, axis, [(i, (i + steps) % n) for i in range(n)])  9.02 us
    ppermute x1, waiting for transfers between devices, local(): rim_across = lax.ppermute(last, line, over)  4.62 us
    ppermute x1, starting transfers between devices, local(): rim = lax.ppermute(last, line, [(i, i + 1) for i in range(15)])  2.71 us
    unnamed x33, local copies, waits for them, and re-layouts  2.23 us
    ppermute x1, starting transfers between devices, local(): rim_across = lax.ppermute(last, line, over)  1.92 us
  transfers between devices with their start and end apart: 20, of which 9 were waited for; matrix products, arithmetic and copies ran while one was open for 5% of the time, Pallas kernels for 15%

profile of v12, /device:TPU:1, one launch (start us, length us, event | category | flops | bytes accessed | tf_op | source)
XLA Modules:
  0.0 65.4 jit_solution(6812476976266374060)
XLA Ops:
  1.3 1.9 %shard_map.172 = (bf16[80,512]{1,0:T(8,128)(2,1)S(1)}, f32[8,512]{1,0:T(8,128)S(1)}, f32[8,512]{1,0:T(8,128)S(1)}, f32[1,2048]{1,0:T(1,128)S(1)}) custom-call(s32[1]{0:T(128)S(6)} %copy.20.lens, bf16[512,512]{1,0:T(8,128)(2,1)} %bitcast.7, bf16[512,512]{1,0:T(8,128)(2,1)} %bitcast.8, f32[4,512]{1,0:T(4,128)} %first.1, f32[4,512]{1,0:T(4,128)} %second.1, ...), custom_call_target="tpu_custom_call" | custom-call | tf_op jit(solution)/shard_map/pallas_call | solution.py:355
  3.2 3.8 %collective-permute-start = (bf16[80,512]{1,0:T(8,128)(2,1)S(1)}, bf16[80,512]{1,0:T(8,128)(2,1)S(1)}, u32[]{:S(2)}, u32[]{:S(2)}) collective-permute-start(bf16[80,512]{1,0:T(8,128)(2,1)S(1)} %get-tuple-element.44.piece), channel_id=1, source_target_pairs={{0,8},{8,0},{1,9},{9,1},{2,10},{10,2},{3,11},{11,3},{4,12},{12,4},... | collective-permute-start | bytes 245768 | tf_op jit(solution)/shard_map/ppermute | solution.py:368
  7.0 2.7 %collective-permute-start.1 = (f32[8,512]{1,0:T(8,128)S(1)}, f32[8,512]{1,0:T(8,128)S(1)}, u32[]{:S(2)}, u32[]{:S(2)}) collective-permute-start(f32[8,512]{1,0:T(8,128)S(1)} %get-tuple-element.46), channel_id=1, source_target_pairs={{0,4},{4,8},{8,12},{12,16},{16,20},{20,24},{24,28},{28,32},{32,36}... | collective-permute-start | bytes 49160 | tf_op jit(solution)/shard_map/ppermute | solution.py:388
  9.8 1.9 %collective-permute-start.2 = (f32[8,512]{1,0:T(8,128)S(1)}, f32[8,512]{1,0:T(8,128)S(1)}, u32[]{:S(2)}, u32[]{:S(2)}) collective-permute-start(f32[8,512]{1,0:T(8,128)S(1)} %get-tuple-element.46), channel_id=1, source_target_pairs={{0,12},{4,0},{8,4},{12,24},{16,28},{20,16},{24,20},{28,40},{32,44}... | collective-permute-start | bytes 49160 | tf_op jit(solution)/shard_map/ppermute | solution.py:391
  11.7 4.6 %collective-permute-done.2.rim_across = f32[8,512]{1,0:T(8,128)S(1)} collective-permute-done((f32[8,512]{1,0:T(8,128)S(1)}, f32[8,512]{1,0:T(8,128)S(1)}, u32[]{:S(2)}, u32[]{:S(2)}) %collective-permute-start.2) | collective-permute-done | bytes 16416 | tf_op jit(solution)/shard_map/ppermute | solution.py:391
  16.4 1.8 %collective-permute-start.3 = (bf16[128,512]{1,0:T(8,128)(2,1)S(1)}, bf16[128,512]{1,0:T(8,128)(2,1)S(1)}, u32[]{:S(2)}, u32[]{:S(2)}) collective-permute-start(bf16[128,512]{1,0:T(8,128)(2,1)S(1)} %shard_map.173.p0), channel_id=1, source_target_pairs={{0,1},{1,2},{2,3},{3,0},{4,5},{5,6},{6,7},{7,4},{8,9},{9,10},{10,1... | collective-permute-start | bytes 393224 | tf_op jit(solution)/shard_map/ppermute | solution.py:368
  18.2 3.3 %collective-permute-start.4 = (bf16[128,512]{1,0:T(8,128)(2,1)S(1)}, bf16[128,512]{1,0:T(8,128)(2,1)S(1)}, u32[]{:S(2)}, u32[]{:S(2)}) collective-permute-start(bf16[128,512]{1,0:T(8,128)(2,1)S(1)} %shard_map.173.p0), channel_id=1, source_target_pairs={{0,2},{1,3},{2,0},{3,1},{4,6},{5,7},{6,4},{7,5},{8,10},{9,11},{10,... | collective-permute-start | bytes 393224 | tf_op jit(solution)/shard_map/ppermute | solution.py:368
  22.2 0.9 %collective-permute-done.3.r1 = bf16[128,512]{1,0:T(8,128)(2,1)S(1)} collective-permute-done((bf16[128,512]{1,0:T(8,128)(2,1)S(1)}, bf16[128,512]{1,0:T(8,128)(2,1)S(1)}, u32[]{:S(2)}, u32[]{:S(2)}) %collective-permute-start.3) | collective-permute-done | bytes 131104 | tf_op jit(solution)/shard_map/ppermute | solution.py:368
  23.1 3.4 %collective-permute-done.4.r2 = bf16[128,512]{1,0:T(8,128)(2,1)S(1)} collective-permute-done((bf16[128,512]{1,0:T(8,128)(2,1)S(1)}, bf16[128,512]{1,0:T(8,128)(2,1)S(1)}, u32[]{:S(2)}, u32[]{:S(2)}) %collective-permute-start.4) | collective-permute-done | bytes 131104 | tf_op jit(solution)/shard_map/ppermute | solution.py:368
  26.7 1.6 %shard_map.174 = (bf16[64,1024]{1,0:T(8,128)(2,1)S(1)}, bf16[80,1024]{1,0:T(8,128)(2,1)S(1)}, bf16[4,32,1024]{2,1,0:T(8,128)(2,1)S(1)}, bf16[32,2048]{1,0:T(8,128)(2,1)S(1)}, f32[3,32,512]{2,1,0:T(8,128)S(1)}) custom-call(bf16[128,512]{1,0:T(8,128)(2,1)S(1)} %shard_map.173.p0, bf16[128,512]{1,0:T(8,128)(2,1)S(1)} %collective-permute-done.3.r1, ...), custom_call_target="tpu_custom_call" | custom-call | flops 1000000000 | tf_op jit(solution)/shard_map/pallas_call | solution.py:355
  29.0 2.0 %collective-permute-start.6 = (bf16[80,1024]{1,0:T(8,128)(2,1)S(1)}, bf16[80,1024]{1,0:T(8,128)(2,1)S(1)}, u32[]{:S(2)}, u32[]{:S(2)}) collective-permute-start(bf16[80,1024]{1,0:T(8,128)(2,1)S(1)} %get-tuple-element.49), channel_id=1, source_target_pairs={{0,4},{4,0},{1,5},{5,1},{2,6},{6,2},{3,7},{7,3},{8,12},{12,8},{9,1... | collective-permute-start | bytes 491528 | tf_op jit(solution)/shard_map/ppermute | solution.py:368
  31.1 1.0 %collective-permute-done.6.swapped = bf16[80,1024]{1,0:T(8,128)(2,1)S(1)} collective-permute-done((bf16[80,1024]{1,0:T(8,128)(2,1)S(1)}, bf16[80,1024]{1,0:T(8,128)(2,1)S(1)}, u32[]{:S(2)}, u32[]{:S(2)}) %collective-permute-start.6) | collective-permute-done | bytes 163872 | tf_op jit(solution)/shard_map/ppermute | solution.py:368
  32.1 1.3 %collective-permute-start.7 = (bf16[80,1024]{1,0:T(8,128)(2,1)S(1)}, bf16[80,1024]{1,0:T(8,128)(2,1)}, u32[]{:S(2)}, u32[]{:S(2)}) collective-permute-start(bf16[80,1024]{1,0:T(8,128)(2,1)S(1)} %get-tuple-element.52), channel_id=1, source_target_pairs={{0,16},{16,32},{32,48},{48,0},{1,17},{17,33},{33,49},{49,1},{2,18}... | collective-permute-start | bytes 491528 | tf_op jit(solution)/shard_map/ppermute | solution.py:368
  33.4 1.5 %collective-permute-start.9 = (bf16[80,1024]{1,0:T(8,128)(2,1)S(1)}, bf16[80,1024]{1,0:T(8,128)(2,1)}, u32[]{:S(2)}, u32[]{:S(2)}) collective-permute-start(bf16[80,1024]{1,0:T(8,128)(2,1)S(1)} %get-tuple-element.54), channel_id=1, source_target_pairs={{0,48},{16,0},{32,16},{48,32},{1,49},{17,1},{33,17},{49,33},{2,50}... | collective-permute-start | bytes 491528 | tf_op jit(solution)/shard_map/ppermute | solution.py:368
  34.9 0.8 %shard_map.175 = (bf16[96,1024]{1,0:T(8,128)(2,1)}, bf16[112,1024]{1,0:T(8,128)(2,1)}, bf16[160,1024]{1,0:T(8,128)(2,1)S(1)}) custom-call(bf16[64,1024]{1,0:T(8,128)(2,1)S(1)} %get-tuple-element.48.keep, bf16[80,1024]{1,0:T(8,128)(2,1)S(1)} %collective-permute-done.6.swapped, bf16[4,32,1024]{2,1,0:T(8,128)(2,1)S(1)} %get-tuple-element.50.blocks), custom_call_target="tpu_custom_call" | custom-call | tf_op jit(solution)/shard_map/pallas_call | solution.py:355
  36.2 1.0 %collective-permute-start.8 = (bf16[96,1024]{1,0:T(8,128)(2,1)}, bf16[96,1024]{1,0:T(8,128)(2,1)S(1)}, u32[]{:S(2)}, u32[]{:S(2)}) collective-permute-start(bf16[96,1024]{1,0:T(8,128)(2,1)} %get-tuple-element.53), channel_id=1, source_target_pairs={{0,16},{16,32},{32,48},{48,0},{1,17},{17,33},{33,49},{49,1},{2,18}... | collective-permute-start | bytes 589832 | tf_op jit(solution)/shard_map/ppermute | solution.py:368
  37.2 1.8 %collective-permute-done.7.low_far = bf16[80,1024]{1,0:T(8,128)(2,1)} collective-permute-done((bf16[80,1024]{1,0:T(8,128)(2,1)S(1)}, bf16[80,1024]{1,0:T(8,128)(2,1)}, u32[]{:S(2)}, u32[]{:S(2)}) %collective-permute-start.7) | collective-permute-done | bytes 163872 | tf_op jit(solution)/shard_map/ppermute | solution.py:368
  38.9 2.7 %collective-permute-start.12 = (bf16[80,1024]{1,0:T(8,128)(2,1)}, bf16[80,1024]{1,0:T(8,128)(2,1)S(1)}, u32[]{:S(2)}, u32[]{:S(2)}) collective-permute-start(bf16[80,1024]{1,0:T(8,128)(2,1)} %collective-permute-done.9.high_far), channel_id=1, source_target_pairs={{0,48},{16,0},{32,16},{48,32},{1,49},{17,1},{33,17},{49,33},{2,50}... | collective-permute-start | bytes 491528 | tf_op jit(solution)/shard_map/ppermute | solution.py:368
  43.0 0.8 %copy.19.table = f32[32,4]{1,0:T(8,128)S(1)} copy(f32[32,4]{0,1:T(4,128)} %param.22) | data formatting | bytes 1024 | tf_op args[9]
  43.8 0.8 %pad_add_fusion = s32[640]{0:T(1024)S(1)} fusion(s32[127]{0:T(128)} %rev.9, s32[128]{0:T(128)S(1)} %broadcast_in_dim.19, s32[385]{0:T(512)} %slice.8), kind=kLoop, calls=%fused_computation | loop fusion | flops 1280 | bytes 5120 | tf_op jit(solution)/shard_map/concatenate | solution.py:400
  44.6 1.1 %shard_map.177.strip = f32[2,128,512]{2,1,0:T(8,128)S(1)} custom-call(s32[8,640]{1,0:T(8,128)S(1)} %broadcast_in_dim.20.near, f32[32,4]{1,0:T(8,128)S(1)} %copy.19.table), custom_call_target="tpu_custom_call" | custom-call | tf_op jit(solution)/shard_map/pallas_call | solution.py:355
  45.7 0.9 %collective-permute-done.11.far_low = bf16[80,1024]{1,0:T(8,128)(2,1)S(1)} collective-permute-done((bf16[80,1024]{1,0:T(8,128)(2,1)}, bf16[80,1024]{1,0:T(8,128)(2,1)S(1)}, u32[]{:S(2)}, u32[]{:S(2)}) %collective-permute-start.11) | collective-permute-done | bytes 163872 | tf_op jit(solution)/shard_map/ppermute | solution.py:368
  47.1 1.4 %collective-permute-start.14 = (bf16[4,32,1024]{2,1,0:T(8,128)(2,1)S(1)}, bf16[4,32,1024]{2,1,0:T(8,128)(2,1)S(1)}, u32[]{:S(2)}, u32[]{:S(2)}) collective-permute-start(bf16[4,32,1024]{2,1,0:T(8,128)(2,1)S(1)} %get-tuple-element.61.mine), channel_id=1, source_target_pairs={{0,4},{4,0},{1,5},{5,1},{2,6},{6,2},{3,7},{7,3},{8,12},{12,8},{9,1... | collective-permute-start | bytes 786440 | tf_op jit(solution)/shard_map/ppermute | solution.py:368
  48.6 2.9 %shard_map.178 = (bf16[4,528,256]{2,1,0:T(8,128)(2,1)S(1)}, bf16[4,48,256]{2,1,0:T(8,128)(2,1)S(1)}, bf16[4,48,256]{2,1,0:T(8,128)(2,1)S(1)}) custom-call(s32[1]{0:T(128)S(6)} %copy.20.lens, bf16[160,1024]{1,0:T(8,128)(2,1)S(1)} %get-tuple-element.51.b0, bf16[80,1024]{1,0:T(8,128)(2,1)} %collective-permute-done.7.low_far, ...), custom_call_target="tpu_custom_call" | custom-call | flops 6000000000 | tf_op jit(solution)/shard_map/pallas_call | solution.py:355
  52.2 1.4 %collective-permute-start.18 = (bf16[4,128,256]{2,1,0:T(8,128)(2,1)S(1)}, bf16[4,128,256]{2,1,0:T(8,128)(2,1)S(1)}, u32[]{:S(2)}, u32[]{:S(2)}) collective-permute-start(bf16[4,128,256]{2,1,0:T(8,128)(2,1)S(1)} %get-tuple-element.75), channel_id=1, source_target_pairs={{0,64},{64,0},{1,65},{65,1},{2,66},{66,2},{3,67},{67,3},{4,68},{68... | collective-permute-start | bytes 786440 | tf_op jit(solution)/shard_map/ppermute | solution.py:368
  53.6 0.8 %shard_map.181 = (bf16[80,640]{1,0:T(8,128)(2,1)S(1)}, bf16[4,48,512]{2,1,0:T(8,128)(2,1)S(1)}, f32[48,128]{1,0:T(8,128)S(1)}) custom-call(bf16[4,48,256]{2,1,0:T(8,128)(2,1)S(1)} %get-tuple-element.56.keep_r, bf16[4,48,256]{2,1,0:T(8,128)(2,1)S(1)} %collective-permute-done.13.got_r, f32[3,32,512]{2,1,0:T(8,128)S(1)} %get-tuple-element.58.hown, ...), custom_call_target="tpu_custom_call" | custom-call | flops 300000000 | tf_op jit(solution)/shard_map/pallas_call | solution.py:355
  54.4 2.0 %collective-permute-start.16 = (bf16[80,640]{1,0:T(8,128)(2,1)S(1)}, bf16[80,640]{1,0:T(8,128)(2,1)S(1)}, u32[]{:S(2)}, u32[]{:S(2)}) collective-permute-start(bf16[80,640]{1,0:T(8,128)(2,1)S(1)} %get-tuple-element.65.msg2), channel_id=1, source_target_pairs={{0,2},{1,3},{2,0},{3,1},{4,6},{5,7},{6,4},{7,5},{8,10},{9,11},{10,... | collective-permute-start | bytes 307208 | tf_op jit(solution)/shard_map/ppermute | solution.py:368
  56.4 1.9 %shard_map.182 = (bf16[80,640]{1,0:T(8,128)(2,1)S(1)}, bf16[80,640]{1,0:T(8,128)(2,1)S(1)}, f32[80,640]{1,0:T(8,128)S(1)}, bf16[48,512]{1,0:T(8,128)(2,1)S(1)}, f32[48,128]{1,0:T(8,128)S(1)}) custom-call(bf16[4,48,512]{2,1,0:T(8,128)(2,1)S(1)} %get-tuple-element.63.g, f32[48,128]{1,0:T(8,128)S(1)} %get-tuple-element.64.sums, ...), custom_call_target="tpu_custom_call" | custom-call | flops 1000000000 | tf_op jit(solution)/shard_map/pallas_call | solution.py:355
  58.9 2.2 %collective-permute-start.17 = (bf16[80,640]{1,0:T(8,128)(2,1)S(1)}, bf16[80,640]{1,0:T(8,128)(2,1)S(1)}, u32[]{:S(2)}, u32[]{:S(2)}) collective-permute-start(bf16[80,640]{1,0:T(8,128)(2,1)S(1)} %get-tuple-element.70), channel_id=1, source_target_pairs={{0,3},{1,0},{2,1},{3,2},{4,7},{5,4},{6,5},{7,6},{8,11},{9,8},{10,9... | collective-permute-start | bytes 307208 | tf_op jit(solution)/shard_map/ppermute | solution.py:368
  61.1 1.7 %collective-permute-start.19 = (bf16[4,64,256]{2,1,0:T(8,128)(2,1)S(1)}, bf16[4,64,256]{2,1,0:T(8,128)(2,1)S(1)}, u32[]{:S(2)}, u32[]{:S(2)}) collective-permute-start(bf16[4,64,256]{2,1,0:T(8,128)(2,1)S(1)} %get-tuple-element.77), channel_id=1, source_target_pairs={{0,4},{4,0},{1,5},{5,1},{2,6},{6,2},{3,7},{7,3},{8,12},{12,8},{9,1... | collective-permute-start | bytes 393224 | tf_op jit(solution)/shard_map/ppermute | solution.py:368
  63.1 1.4 %shard_map.183 = (bf16[512,512]{1,0:T(8,128)(2,1)}, bf16[512,512]{1,0:T(8,128)(2,1)}) custom-call(s32[1]{0:T(128)S(6)} %copy.20.lens, f32[80,640]{1,0:T(8,128)S(1)} %get-tuple-element.68.keep, bf16[80,640]{1,0:T(8,128)(2,1)S(1)} %collective-permute-done.15.r1, bf16[80,640]{1,0:T(8,128)(2,1)S(1)} %collective-permute-done.16.r2, ...), custom_call_target="tpu_custom_call" | custom-call | flops 20000000000 | tf_op jit(solution)/shard_map/pallas_call | solution.py:355
  64.6 0.8 %shard_map.185 = (f32[64,512]{1,0:T(8,128)}, f32[64,512]{1,0:T(8,128)}, f32[64,512]{1,0:T(8,128)}, f32[64,512]{1,0:T(8,128)}) custom-call(f32[4,64,256]{2,1,0:T(8,128)S(1)} %get-tuple-element.76.own, bf16[4,64,256]{2,1,0:T(8,128)(2,1)S(1)} %collective-permute-done.19.other), custom_call_target="tpu_custom_call" | custom-call | flops 6000000000 | tf_op jit(solution)/shard_map/pallas_call | solution.py:355
  (60 shorter events, 5.7 us)
Async XLA Ops:
  3.2 23.5 %copy-start.12 = (f32[1,2048]{1,0:T(1,128)}, f32[1,2048]{1,0:T(1,128)S(1)}, u32[]{:S(2)}) copy-start(f32[1,2048]{1,0:T(1,128)S(1)} %get-tuple-element.47.gain) | copy-start | bytes 24580
  3.2 13.1 %collective-permute-start = (bf16[80,512]{1,0:T(8,128)(2,1)S(1)}, bf16[80,512]{1,0:T(8,128)(2,1)S(1)}, u32[]{:S(2)}, u32[]{:S(2)}) collective-permute-start(bf16[80,512]{1,0:T(8,128)(2,1)S(1)} %get-tuple-element.44.piece), channel_id=1, source_target_pairs={{0,8},{8,0},{1,9},{9,1},{2,10},{10,2},{3,11},{11,3},{4,12},{12,4},... | collective-permute-start | bytes 245768 | tf_op jit(solution)/shard_map/ppermute | solution.py:368
  7.0 4.6 %collective-permute-start.1 = (f32[8,512]{1,0:T(8,128)S(1)}, f32[8,512]{1,0:T(8,128)S(1)}, u32[]{:S(2)}, u32[]{:S(2)}) collective-permute-start(f32[8,512]{1,0:T(8,128)S(1)} %get-tuple-element.46), channel_id=1, source_target_pairs={{0,4},{4,8},{8,12},{12,16},{16,20},{20,24},{24,28},{28,32},{32,36}... | collective-permute-start | bytes 49160 | tf_op jit(solution)/shard_map/ppermute | solution.py:388
  9.8 6.6 %collective-permute-start.2 = (f32[8,512]{1,0:T(8,128)S(1)}, f32[8,512]{1,0:T(8,128)S(1)}, u32[]{:S(2)}, u32[]{:S(2)}) collective-permute-start(f32[8,512]{1,0:T(8,128)S(1)} %get-tuple-element.46), channel_id=1, source_target_pairs={{0,12},{4,0},{8,4},{12,24},{16,28},{20,16},{24,20},{28,40},{32,44}... | collective-permute-start | bytes 49160 | tf_op jit(solution)/shard_map/ppermute | solution.py:391
  16.3 10.4 %copy-start = (bf16[2048,512]{1,0:T(8,128)(2,1)S(1)}, bf16[2048,512]{1,0:T(8,128)(2,1)}, u32[]{:S(2)}) copy-start(bf16[2048,512]{1,0:T(8,128)(2,1)} %wq.5) | copy-start | bytes 6291460
  16.3 10.4 %copy-start.1 = (bf16[2048,512]{1,0:T(8,128)(2,1)S(1)}, bf16[2048,512]{1,0:T(8,128)(2,1)}, u32[]{:S(2)}) copy-start(bf16[2048,512]{1,0:T(8,128)(2,1)} %wk.5) | copy-start | bytes 6291460
  16.3 10.4 %copy-start.3 = (bf16[2048,512]{1,0:T(8,128)(2,1)S(1)}, bf16[2048,512]{1,0:T(8,128)(2,1)}, u32[]{:S(2)}) copy-start(bf16[2048,512]{1,0:T(8,128)(2,1)} %wv.5) | copy-start | bytes 6291460
  16.3 10.4 %copy-start.5 = (bf16[2048,512]{1,0:T(8,128)(2,1)S(1)}, bf16[2048,512]{1,0:T(8,128)(2,1)}, u32[]{:S(2)}) copy-start(bf16[2048,512]{1,0:T(8,128)(2,1)} %wo.5) | copy-start | bytes 6291460
  16.4 6.8 %collective-permute-start.3 = (bf16[128,512]{1,0:T(8,128)(2,1)S(1)}, bf16[128,512]{1,0:T(8,128)(2,1)S(1)}, u32[]{:S(2)}, u32[]{:S(2)}) collective-permute-start(bf16[128,512]{1,0:T(8,128)(2,1)S(1)} %shard_map.173.p0), channel_id=1, source_target_pairs={{0,1},{1,2},{2,3},{3,0},{4,5},{5,6},{6,7},{7,4},{8,9},{9,10},{10,1... | collective-permute-start | bytes 393224 | tf_op jit(solution)/shard_map/ppermute | solution.py:368
  18.2 8.3 %collective-permute-start.4 = (bf16[128,512]{1,0:T(8,128)(2,1)S(1)}, bf16[128,512]{1,0:T(8,128)(2,1)S(1)}, u32[]{:S(2)}, u32[]{:S(2)}) collective-permute-start(bf16[128,512]{1,0:T(8,128)(2,1)S(1)} %shard_map.173.p0), channel_id=1, source_target_pairs={{0,2},{1,3},{2,0},{3,1},{4,6},{5,7},{6,4},{7,5},{8,10},{9,11},{10,... | collective-permute-start | bytes 393224 | tf_op jit(solution)/shard_map/ppermute | solution.py:368
  21.5 5.2 %collective-permute-start.5 = (bf16[128,512]{1,0:T(8,128)(2,1)S(1)}, bf16[128,512]{1,0:T(8,128)(2,1)S(1)}, u32[]{:S(2)}, u32[]{:S(2)}) collective-permute-start(bf16[128,512]{1,0:T(8,128)(2,1)S(1)} %shard_map.173.p0), channel_id=1, source_target_pairs={{0,3},{1,0},{2,1},{3,2},{4,7},{5,4},{6,5},{7,6},{8,11},{9,8},{10,9... | collective-permute-start | bytes 393224 | tf_op jit(solution)/shard_map/ppermute | solution.py:368
  26.7 14.9 %copy-start.14 = (s32[512]{0:T(512)S(1)}, s32[512]{0:T(512)}, u32[]{:S(2)}) copy-start(s32[512]{0:T(512)} %param.23) | copy-start | bytes 6148
  29.0 3.1 %collective-permute-start.6 = (bf16[80,1024]{1,0:T(8,128)(2,1)S(1)}, bf16[80,1024]{1,0:T(8,128)(2,1)S(1)}, u32[]{:S(2)}, u32[]{:S(2)}) collective-permute-start(bf16[80,1024]{1,0:T(8,128)(2,1)S(1)} %get-tuple-element.49), channel_id=1, source_target_pairs={{0,4},{4,0},{1,5},{5,1},{2,6},{6,2},{3,7},{7,3},{8,12},{12,8},{9,1... | collective-permute-start | bytes 491528 | tf_op jit(solution)/shard_map/ppermute | solution.py:368
  32.1 6.8 %collective-permute-start.7 = (bf16[80,1024]{1,0:T(8,128)(2,1)S(1)}, bf16[80,1024]{1,0:T(8,128)(2,1)}, u32[]{:S(2)}, u32[]{:S(2)}) collective-permute-start(bf16[80,1024]{1,0:T(8,128)(2,1)S(1)} %get-tuple-element.52), channel_id=1, source_target_pairs={{0,16},{16,32},{32,48},{48,0},{1,17},{17,33},{33,49},{49,1},{2,18}... | collective-permute-start | bytes 491528 | tf_op jit(solution)/shard_map/ppermute | solution.py:368
  33.4 5.5 %collective-permute-start.9 = (bf16[80,1024]{1,0:T(8,128)(2,1)S(1)}, bf16[80,1024]{1,0:T(8,128)(2,1)}, u32[]{:S(2)}, u32[]{:S(2)}) collective-permute-start(bf16[80,1024]{1,0:T(8,128)(2,1)S(1)} %get-tuple-element.54), channel_id=1, source_target_pairs={{0,48},{16,0},{32,16},{48,32},{1,49},{17,1},{33,17},{49,33},{2,50}... | collective-permute-start | bytes 491528 | tf_op jit(solution)/shard_map/ppermute | solution.py:368
  35.7 10.0 %collective-permute-start.10 = (bf16[112,1024]{1,0:T(8,128)(2,1)}, bf16[112,1024]{1,0:T(8,128)(2,1)S(1)}, u32[]{:S(2)}, u32[]{:S(2)}) collective-permute-start(bf16[112,1024]{1,0:T(8,128)(2,1)} %get-tuple-element.55), channel_id=1, source_target_pairs={{0,48},{16,0},{32,16},{48,32},{1,49},{17,1},{33,17},{49,33},{2,50}... | collective-permute-start | bytes 688136 | tf_op jit(solution)/shard_map/ppermute | solution.py:368
  36.2 9.5 %collective-permute-start.8 = (bf16[96,1024]{1,0:T(8,128)(2,1)}, bf16[96,1024]{1,0:T(8,128)(2,1)S(1)}, u32[]{:S(2)}, u32[]{:S(2)}) collective-permute-start(bf16[96,1024]{1,0:T(8,128)(2,1)} %get-tuple-element.53), channel_id=1, source_target_pairs={{0,16},{16,32},{32,48},{48,0},{1,17},{17,33},{33,49},{49,1},{2,18}... | collective-permute-start | bytes 589832 | tf_op jit(solution)/shard_map/ppermute | solution.py:368
  38.9 7.7 %collective-permute-start.11 = (bf16[80,1024]{1,0:T(8,128)(2,1)}, bf16[80,1024]{1,0:T(8,128)(2,1)S(1)}, u32[]{:S(2)}, u32[]{:S(2)}) collective-permute-start(bf16[80,1024]{1,0:T(8,128)(2,1)} %collective-permute-done.7.low_far), channel_id=1, source_target_pairs={{0,16},{16,32},{32,48},{48,0},{1,17},{17,33},{33,49},{49,1},{2,18}... | collective-permute-start | bytes 491528 | tf_op jit(solution)/shard_map/ppermute | solution.py:368
  38.9 8.1 %collective-permute-start.12 = (bf16[80,1024]{1,0:T(8,128)(2,1)}, bf16[80,1024]{1,0:T(8,128)(2,1)S(1)}, u32[]{:S(2)}, u32[]{:S(2)}) collective-permute-start(bf16[80,1024]{1,0:T(8,128)(2,1)} %collective-permute-done.9.high_far), channel_id=1, source_target_pairs={{0,48},{16,0},{32,16},{48,32},{1,49},{17,1},{33,17},{49,33},{2,50}... | collective-permute-start | bytes 491528 | tf_op jit(solution)/shard_map/ppermute | solution.py:368
  47.1 4.5 %collective-permute-start.14 = (bf16[4,32,1024]{2,1,0:T(8,128)(2,1)S(1)}, bf16[4,32,1024]{2,1,0:T(8,128)(2,1)S(1)}, u32[]{:S(2)}, u32[]{:S(2)}) collective-permute-start(bf16[4,32,1024]{2,1,0:T(8,128)(2,1)S(1)} %get-tuple-element.61.mine), channel_id=1, source_target_pairs={{0,4},{4,0},{1,5},{5,1},{2,6},{6,2},{3,7},{7,3},{8,12},{12,8},{9,1... | collective-permute-start | bytes 786440 | tf_op jit(solution)/shard_map/ppermute | solution.py:368
  48.6 5.0 %copy-start.4 = (bf16[2048,512]{1,0:T(8,128)(2,1)S(1)}, bf16[2048,512]{1,0:T(8,128)(2,1)}, u32[]{:S(2)}) copy-start(bf16[2048,512]{1,0:T(8,128)(2,1)} %wv.5) | copy-start | bytes 6291460
  48.6 5.0 %copy-start.6 = (bf16[2048,512]{1,0:T(8,128)(2,1)S(1)}, bf16[2048,512]{1,0:T(8,128)(2,1)}, u32[]{:S(2)}) copy-start(bf16[2048,512]{1,0:T(8,128)(2,1)} %wo.5) | copy-start | bytes 6291460
  51.5 2.1 %collective-permute-start.13 = (bf16[4,48,256]{2,1,0:T(8,128)(2,1)S(1)}, bf16[4,48,256]{2,1,0:T(8,128)(2,1)S(1)}, u32[]{:S(2)}, u32[]{:S(2)}) collective-permute-start(bf16[4,48,256]{2,1,0:T(8,128)(2,1)S(1)} %get-tuple-element.57), channel_id=1, source_target_pairs={{0,4},{4,0},{1,5},{5,1},{2,6},{6,2},{3,7},{7,3},{8,12},{12,8},{9,1... | collective-permute-start | bytes 294920 | tf_op jit(solution)/shard_map/ppermute | solution.py:368
  52.2 8.9 %collective-permute-start.18 = (bf16[4,128,256]{2,1,0:T(8,128)(2,1)S(1)}, bf16[4,128,256]{2,1,0:T(8,128)(2,1)S(1)}, u32[]{:S(2)}, u32[]{:S(2)}) collective-permute-start(bf16[4,128,256]{2,1,0:T(8,128)(2,1)S(1)} %get-tuple-element.75), channel_id=1, source_target_pairs={{0,64},{64,0},{1,65},{65,1},{2,66},{66,2},{3,67},{67,3},{4,68},{68... | collective-permute-start | bytes 786440 | tf_op jit(solution)/shard_map/ppermute | solution.py:368
  54.4 6.7 %collective-permute-start.16 = (bf16[80,640]{1,0:T(8,128)(2,1)S(1)}, bf16[80,640]{1,0:T(8,128)(2,1)S(1)}, u32[]{:S(2)}, u32[]{:S(2)}) collective-permute-start(bf16[80,640]{1,0:T(8,128)(2,1)S(1)} %get-tuple-element.65.msg2), channel_id=1, source_target_pairs={{0,2},{1,3},{2,0},{3,1},{4,6},{5,7},{6,4},{7,5},{8,10},{9,11},{10,... | collective-permute-start | bytes 307208 | tf_op jit(solution)/shard_map/ppermute | solution.py:368
  56.4 6.7 %copy-start.9 = (f32[16,512]{1,0:T(8,128)S(1)}, f32[16,512]{1,0:T(8,128)}, u32[]{:S(2)}) copy-start(f32[16,512]{1,0:T(8,128)} %up_gain.1) | copy-start | bytes 98308
  56.4 6.7 %copy-start.10 = (f32[4,512]{1,0:T(4,128)S(1)}, f32[4,512]{1,0:T(4,128)}, u32[]{:S(2)}) copy-start(f32[4,512]{1,0:T(4,128)} %first.1) | copy-start | bytes 24580
  56.4 6.7 %copy-start.11 = (f32[4,512]{1,0:T(4,128)S(1)}, f32[4,512]{1,0:T(4,128)}, u32[]{:S(2)}) copy-start(f32[4,512]{1,0:T(4,128)} %second.1) | copy-start | bytes 24580
  56.4 6.7 %copy-start.13 = (f32[1,2048]{1,0:T(1,128)S(1)}, f32[1,2048]{1,0:T(1,128)}, u32[]{:S(2)}) copy-start(f32[1,2048]{1,0:T(1,128)} %copy-done.12) | copy-start | bytes 24580
  58.3 4.8 %collective-permute-start.15 = (bf16[80,640]{1,0:T(8,128)(2,1)S(1)}, bf16[80,640]{1,0:T(8,128)(2,1)S(1)}, u32[]{:S(2)}, u32[]{:S(2)}) collective-permute-start(bf16[80,640]{1,0:T(8,128)(2,1)S(1)} %get-tuple-element.69), channel_id=1, source_target_pairs={{0,1},{1,2},{2,3},{3,0},{4,5},{5,6},{6,7},{7,4},{8,9},{9,10},{10,1... | collective-permute-start | bytes 307208 | tf_op jit(solution)/shard_map/ppermute | solution.py:368
  58.9 4.2 %collective-permute-start.17 = (bf16[80,640]{1,0:T(8,128)(2,1)S(1)}, bf16[80,640]{1,0:T(8,128)(2,1)S(1)}, u32[]{:S(2)}, u32[]{:S(2)}) collective-permute-start(bf16[80,640]{1,0:T(8,128)(2,1)S(1)} %get-tuple-element.70), channel_id=1, source_target_pairs={{0,3},{1,0},{2,1},{3,2},{4,7},{5,4},{6,5},{7,6},{8,11},{9,8},{10,9... | collective-permute-start | bytes 307208 | tf_op jit(solution)/shard_map/ppermute | solution.py:368
  61.1 3.5 %collective-permute-start.19 = (bf16[4,64,256]{2,1,0:T(8,128)(2,1)S(1)}, bf16[4,64,256]{2,1,0:T(8,128)(2,1)S(1)}, u32[]{:S(2)}, u32[]{:S(2)}) collective-permute-start(bf16[4,64,256]{2,1,0:T(8,128)(2,1)S(1)} %get-tuple-element.77), channel_id=1, source_target_pairs={{0,4},{4,0},{1,5},{5,1},{2,6},{6,2},{3,7},{7,3},{8,12},{12,8},{9,1... | collective-permute-start | bytes 393224 | tf_op jit(solution)/shard_map/ppermute | solution.py:368
  (3 other events, 5.5 us)

commit v13 on v12

--- a/solution.py
+++ b/solution.py
@@ -108,7 +108,7 @@
 
 
 def project_kernel(
-    p0, r1, r2, r3, gain, wq, wk, wv, wo, keep, send, blocks, mine, hown, craw, nrm, gco, both, hs
+    p0, r1, r2, r3, gain, wq, wk, wv, wo, keep, send, blocks, cown, iown, hown, craw, nrm, gco, both, hs
 ):
     at = Place()
     z, core, x, y = at.z, at.core, at.x, at.y
@@ -118,11 +118,14 @@
             rows = slice(i * CL, i * CL + CL)
             craw[rows, cols] = src[2 * i * CL : 2 * i * CL + CL]
             gco[rows, cols] = src[2 * i * CL + CL : 2 * i * CL + 2 * CL]
-    mine[...] = craw[pl.ds(pl.multiple_of(y * CL, CL), CL)]
+    own_rows = pl.ds(pl.multiple_of(y * CL, CL), CL)
+    cown[...] = craw[own_rows, pl.ds(pl.multiple_of(z * WL, WL), WL)]
     c = craw[...].astype(F32)
     square = jnp.sum(c * c, axis=1, keepdims=True) * (1.0 / D) + 1e-6
     r = lax.rsqrt(square)
     rms = jnp.sqrt(square)
+    hs[:, 0:128] = jnp.broadcast_to(r, (2 * CL, 128))
+    iown[...] = hs[own_rows, 0:128]
     nrm[...] = (c * r * gain[...]).astype(BF16)
     heads_of = [[], []]
     for src, w, slot in ((gco, wo, 3), (nrm, wq, 0), (nrm, wk, 1), (nrm, wv, 2)):
@@ -177,7 +180,7 @@
     b0[128:160] = blocks[0]
 
 
-def gather_kernel(b0, low_near, high_near, far_low, far_high, swapped, mine, nxt, hnext):
+def gather_kernel(b0, low_near, high_near, far_low, far_high, swapped, mine, cnext, inext, hnext, row):
     mine[0] = b0[128:160]
     mine[1] = low_near[0:32]
     mine[2, 0:16] = far_low[64:80]
@@ -187,9 +190,13 @@
     wraps = jnp.logical_and(at.core == 1, at.y == 1)
     tops = jnp.where(wraps, high_near[96:112].astype(F32), swapped[64:80].astype(F32))
     upper = jnp.where(at.core == 0, at.y, 1 - at.y) == 1
+    square = jnp.zeros((1, 1), F32)
     for j in range(2):
-        row = jnp.where(upper, tops[2 + j : 3 + j], tops[j : j + 1])
-        nxt[:, j * 1024 : j * 1024 + 1024] = jnp.broadcast_to(row, (16, 1024)).astype(BF16)
+        half = jnp.where(upper, tops[2 + j : 3 + j], tops[j : j + 1])
+        square = square + jnp.sum(half * half, axis=1, keepdims=True)
+        row[:, j * 1024 : j * 1024 + 1024] = jnp.broadcast_to(half, (16, 1024)).astype(BF16)
+    inext[...] = jnp.broadcast_to(lax.rsqrt(square * (1.0 / D) + 1e-6), (16, 128))
+    cnext[...] = row[:, pl.ds(pl.multiple_of(at.z * WL, WL), WL)]
     a, b, c = [jnp.where(upper, tops[7 + j : 8 + j], tops[4 + j : 5 + j]) for j in range(3)]
     left, right = slice(0, WL), slice(WL, 2 * WL)
     products = (a[:, left] + b[:, right], a[:, right] + c[:, left], b[:, left] + c[:, right])
@@ -279,11 +286,17 @@
     msg[0:CL, WL : WL + 128] = jnp.zeros((CL, 128), msg.dtype)
 
 
-def partial_far_kernel(keep_r, got_r, hown, hnext, after, wq, wk, wv, wo, msg2, g, sums):
+def partial_far_kernel(
+    keep_r, got_r, hown, hnext, cown, cnext, iown, inext, after, wq, wk, wv, wo, msg2, g, sums, cz, inv_out
+):
     at = Place()
     z, core = at.z, at.core
     g[:, :, pl.ds(pl.multiple_of(core * HW, HW), HW)] = keep_r[...]
     g[:, :, pl.ds(pl.multiple_of((1 - core) * HW, HW), HW)] = got_r[...]
+    cz[0:CL] = cown[...]
+    cz[CL:ROWS] = cnext[...]
+    inv_out[0:CL] = iown[...]
+    inv_out[CL:ROWS] = inext[...]
     both = []
     for rows, h in ((slice(0, CL), hown), (slice(CL, ROWS), hnext)):
         total = sum(g[i, rows].astype(F32) * h[i] for i in range(3))
@@ -299,7 +312,9 @@
     msg2[CL : CL + ROWS, WL : WL + 128] = jnp.where(lane < 3, packed, 0.0).astype(BF16)
 
 
-def partial_near_kernel(g, sums, msg2, crow, nxt, wq, wk, wv, wo, msg1, msg3, keep, cz, inv_out, c):
+def partial_near_kernel(
+    g, sums, msg2, wq, wk, wv, wo, msg1, msg3, keep
+):
     z = Place().z
     weights = (wq, wk, wv, wo)
     for shift, msg in ((1, msg1), (3, msg3)):
@@ -307,12 +322,6 @@
         msg[CL : CL + ROWS, WL : WL + 128] = msg2[CL : CL + ROWS, WL : WL + 128]
     message(g, weights, z, keep)
     keep[CL : CL + ROWS, WL : WL + 128] = sums[...]
-    c[0:CL] = crow[...]
-    c[CL:ROWS] = nxt[...]
-    cf = c[...].astype(F32)
-    r = lax.rsqrt(jnp.sum(cf * cf, axis=1, keepdims=True) * (1.0 / D) + 1e-6)
-    inv_out[...] = jnp.broadcast_to(r, (ROWS, 128))
-    cz[...] = c[:, pl.ds(pl.multiple_of(z * WL, WL), WL)]
 
 
 def total_kernel(own, other, o0, o1, o2, o3):
@@ -411,9 +420,9 @@
         smem=(1,),
     )
     pieces = [piece] + [shifted(piece, "tensor", s) for s in (1, 2, 3)]
-    keep, send, blocks, crow, hown = call(
+    keep, send, blocks, cown, iown, hown = call(
         project_kernel,
-        [((64, 4 * HW), BF16), ((80, 4 * HW), BF16), ((4, CL, 4 * HW), BF16), ((CL, D), BF16), ((3, CL, WL), F32)],
+        [((64, 4 * HW), BF16), ((80, 4 * HW), BF16), ((4, CL, 4 * HW), BF16), ((CL, WL), BF16), ((CL, 128), F32), ((3, CL, WL), F32)],
         (*pieces, gain, *weights),
         [((2 * CL, D), BF16), ((2 * CL, D), BF16), ((2 * CL, D), BF16), ((2, 2 * CL, 4 * HW), BF16), ((2 * CL, WL), F32)],
         smem=(),
@@ -432,10 +441,11 @@
     low_far, high_far = shifted(up_far, "x", 1), shifted(down_far, "x", -1)
     low_near, high_near = shifted(up_near, "x", 1), shifted(down_near, "x", -1)
     far_low, far_high = shifted(low_far, "x", 1), shifted(high_far, "x", -1)
-    mine, nxt, hnext = call(
+    mine, cnext, inext, hnext = call(
         gather_kernel,
-        [((4, CL, 4 * HW), BF16), ((16, D), BF16), ((3, 16, WL), F32)],
+        [((4, CL, 4 * HW), BF16), ((16, WL), BF16), ((16, 128), F32), ((3, 16, WL), F32)],
         (b0, low_near, high_near, far_low, far_high, swapped),
+        [((16, D), BF16)],
         smem=(),
     )
     other_rows = shifted(mine, "core", 1)
@@ -445,7 +455,7 @@
         (lengths, b0, low_far, low_near, high_far, high_near, far_low, far_high, strip),
         [((LC, HW), BF16)] * 4 + [((NH, LC, LC), F32)] * 2 + [((NH, LC, LC), BF16)] * 2,
         flops=6 * 10**9,
-        vmem=16 * 2**20,
+        vmem=10 * 2**20,
     )
     got_r = shifted(send_r, "core", 1)
     dw_keep, dw_send = call(
@@ -458,18 +468,17 @@
     )
     dw_got = shifted(dw_send, "dp", 1)
     msg = (CL + ROWS, WL + 128)
-    m2, g, sums = call(
+    m2, g, sums, cz, inv = call(
         partial_far_kernel,
-        [(msg, BF16), ((4, ROWS, WL), BF16), ((ROWS, 128), F32)],
-        (keep_r, got_r, hown, hnext, dw_keep, *weights),
+        [(msg, BF16), ((4, ROWS, WL), BF16), ((ROWS, 128), F32), ((ROWS, WL), BF16), ((ROWS, 128), F32)],
+        (keep_r, got_r, hown, hnext, cown, cnext, iown, inext, dw_keep, *weights),
         smem=(),
         flops=3 * 10**8,
     )
-    m1, m3, own, cz, inv = call(
+    m1, m3, own = call(
         partial_near_kernel,
-        [(msg, BF16), (msg, BF16), (msg, F32), ((ROWS, WL), BF16), ((ROWS, 128), F32)],
-        (g, sums, m2, crow, nxt, *weights),
-        [((ROWS, D), BF16)],
+        [(msg, BF16), (msg, BF16), (msg, F32)],
+        (g, sums, m2, *weights),
         smem=(),
         flops=10**9,
     )

time: 66.5 us -> 66 us (level)
    unnamed x33 -> x37, local copies, waits for them, and re-layouts: 2.23 us -> 1.59 us
where the time goes in v13:
time: 66 us; the launch traced here: 64.9 us
  starting transfers between devices  32.7 us (50%)
  Pallas kernels  14.1 us (21%)
  waiting for transfers between devices  13.5 us (20%)
  local copies, waits for them, and re-layouts  2.34 us (4%)
  between operations  1.55 us (2%)
  other arithmetic  0.76 us (1%)
    ppermute x18, starting transfers between devices, shifted(): return lax.ppermute(x, axis, [(i, (i + steps) % n) for i in range(n)])  28 us
    pallas_call x14, Pallas kernels, call(): pl.pallas_call(kernel, out_shape=[pltpu.VMEM(s, d) if typed else jax.Shap...  14.1 us
    ppermute x18, waiting for transfers between devices, shifted(): return lax.ppermute(x, axis, [(i, (i + steps) % n) for i in range(n)])  8.89 us
    ppermute x1, waiting for transfers between devices, local(): rim_across = lax.ppermute(last, line, over)  4.62 us
    ppermute x1, starting transfers between devices, local(): rim = lax.ppermute(last, line, [(i, i + 1) for i in range(15)])  2.71 us
    ppermute x1, starting transfers between devices, local(): rim_across = lax.ppermute(last, line, over)  1.92 us
    unnamed x37, local copies, waits for them, and re-layouts  1.59 us
  transfers between devices with their start and end apart: 20, of which 9 were waited for; matrix products, arithmetic and copies ran while one was open for 5% of the time, Pallas kernels for 15%

profile of v13, /device:TPU:1, one launch (start us, length us, event | category | flops | bytes accessed | tf_op | source)
XLA Modules:
  0.0 64.9 jit_solution(10265011156951652914)
XLA Ops:
  1.3 1.9 %shard_map.172 = (bf16[80,512]{1,0:T(8,128)(2,1)S(1)}, f32[8,512]{1,0:T(8,128)S(1)}, f32[8,512]{1,0:T(8,128)S(1)}, f32[1,2048]{1,0:T(1,128)S(1)}) custom-call(s32[1]{0:T(128)S(6)} %copy.20.lens, bf16[512,512]{1,0:T(8,128)(2,1)} %bitcast.7, bf16[512,512]{1,0:T(8,128)(2,1)} %bitcast.8, f32[4,512]{1,0:T(4,128)} %first.1, f32[4,512]{1,0:T(4,128)} %second.1, ...), custom_call_target="tpu_custom_call" | custom-call | tf_op jit(solution)/shard_map/pallas_call | solution.py:364
  3.2 3.8 %collective-permute-start = (bf16[80,512]{1,0:T(8,128)(2,1)S(1)}, bf16[80,512]{1,0:T(8,128)(2,1)S(1)}, u32[]{:S(2)}, u32[]{:S(2)}) collective-permute-start(bf16[80,512]{1,0:T(8,128)(2,1)S(1)} %get-tuple-element.46.piece), channel_id=1, source_target_pairs={{0,8},{8,0},{1,9},{9,1},{2,10},{10,2},{3,11},{11,3},{4,12},{12,4},... | collective-permute-start | bytes 245768 | tf_op jit(solution)/shard_map/ppermute | solution.py:377
  7.0 2.7 %collective-permute-start.1 = (f32[8,512]{1,0:T(8,128)S(1)}, f32[8,512]{1,0:T(8,128)S(1)}, u32[]{:S(2)}, u32[]{:S(2)}) collective-permute-start(f32[8,512]{1,0:T(8,128)S(1)} %get-tuple-element.48), channel_id=1, source_target_pairs={{0,4},{4,8},{8,12},{12,16},{16,20},{20,24},{24,28},{28,32},{32,36}... | collective-permute-start | bytes 49160 | tf_op jit(solution)/shard_map/ppermute | solution.py:397
  9.8 1.9 %collective-permute-start.2 = (f32[8,512]{1,0:T(8,128)S(1)}, f32[8,512]{1,0:T(8,128)S(1)}, u32[]{:S(2)}, u32[]{:S(2)}) collective-permute-start(f32[8,512]{1,0:T(8,128)S(1)} %get-tuple-element.48), channel_id=1, source_target_pairs={{0,12},{4,0},{8,4},{12,24},{16,28},{20,16},{24,20},{28,40},{32,44}... | collective-permute-start | bytes 49160 | tf_op jit(solution)/shard_map/ppermute | solution.py:400
  11.7 4.6 %collective-permute-done.2.rim_across = f32[8,512]{1,0:T(8,128)S(1)} collective-permute-done((f32[8,512]{1,0:T(8,128)S(1)}, f32[8,512]{1,0:T(8,128)S(1)}, u32[]{:S(2)}, u32[]{:S(2)}) %collective-permute-start.2) | collective-permute-done | bytes 16416 | tf_op jit(solution)/shard_map/ppermute | solution.py:400
  16.4 1.8 %collective-permute-start.3 = (bf16[128,512]{1,0:T(8,128)(2,1)S(1)}, bf16[128,512]{1,0:T(8,128)(2,1)S(1)}, u32[]{:S(2)}, u32[]{:S(2)}) collective-permute-start(bf16[128,512]{1,0:T(8,128)(2,1)S(1)} %shard_map.173.p0), channel_id=1, source_target_pairs={{0,1},{1,2},{2,3},{3,0},{4,5},{5,6},{6,7},{7,4},{8,9},{9,10},{10,1... | collective-permute-start | bytes 393224 | tf_op jit(solution)/shard_map/ppermute | solution.py:377
  18.2 3.3 %collective-permute-start.4 = (bf16[128,512]{1,0:T(8,128)(2,1)S(1)}, bf16[128,512]{1,0:T(8,128)(2,1)S(1)}, u32[]{:S(2)}, u32[]{:S(2)}) collective-permute-start(bf16[128,512]{1,0:T(8,128)(2,1)S(1)} %shard_map.173.p0), channel_id=1, source_target_pairs={{0,2},{1,3},{2,0},{3,1},{4,6},{5,7},{6,4},{7,5},{8,10},{9,11},{10,... | collective-permute-start | bytes 393224 | tf_op jit(solution)/shard_map/ppermute | solution.py:377
  22.2 0.9 %collective-permute-done.3.r1 = bf16[128,512]{1,0:T(8,128)(2,1)S(1)} collective-permute-done((bf16[128,512]{1,0:T(8,128)(2,1)S(1)}, bf16[128,512]{1,0:T(8,128)(2,1)S(1)}, u32[]{:S(2)}, u32[]{:S(2)}) %collective-permute-start.3) | collective-permute-done | bytes 131104 | tf_op jit(solution)/shard_map/ppermute | solution.py:377
  23.1 3.4 %collective-permute-done.4.r2 = bf16[128,512]{1,0:T(8,128)(2,1)S(1)} collective-permute-done((bf16[128,512]{1,0:T(8,128)(2,1)S(1)}, bf16[128,512]{1,0:T(8,128)(2,1)S(1)}, u32[]{:S(2)}, u32[]{:S(2)}) %collective-permute-start.4) | collective-permute-done | bytes 131104 | tf_op jit(solution)/shard_map/ppermute | solution.py:377
  26.7 1.6 %shard_map.174 = (bf16[64,1024]{1,0:T(8,128)(2,1)S(1)}, bf16[80,1024]{1,0:T(8,128)(2,1)S(1)}, bf16[4,32,1024]{2,1,0:T(8,128)(2,1)S(1)}, bf16[32,512]{1,0:T(8,128...) custom-call(bf16[128,512]{1,0:T(8,128)(2,1)S(1)} %shard_map.173.p0, ...), custom_call_target="tpu_custom_call" | custom-call | flops 1000000000 | tf_op jit(solution)/shard_map/pallas_call | solution.py:364
  28.4 2.1 %collective-permute-start.6 = (bf16[80,1024]{1,0:T(8,128)(2,1)S(1)}, bf16[80,1024]{1,0:T(8,128)(2,1)S(1)}, u32[]{:S(2)}, u32[]{:S(2)}) collective-permute-start(bf16[80,1024]{1,0:T(8,128)(2,1)S(1)} %get-tuple-element.51), channel_id=1, source_target_pairs={{0,4},{4,0},{1,5},{5,1},{2,6},{6,2},{3,7},{7,3},{8,12},{12,8},{9,1... | collective-permute-start | bytes 491528 | tf_op jit(solution)/shard_map/ppermute | solution.py:377
  30.5 1.0 %collective-permute-done.6.swapped = bf16[80,1024]{1,0:T(8,128)(2,1)S(1)} collective-permute-done((bf16[80,1024]{1,0:T(8,128)(2,1)S(1)}, bf16[80,1024]{1,0:T(8,128)(2,1)S(1)}, u32[]{:S(2)}, u32[]{:S(2)}) %collective-permute-start.6) | collective-permute-done | bytes 163872 | tf_op jit(solution)/shard_map/ppermute | solution.py:377
  31.6 1.3 %collective-permute-start.7 = (bf16[80,1024]{1,0:T(8,128)(2,1)S(1)}, bf16[80,1024]{1,0:T(8,128)(2,1)}, u32[]{:S(2)}, u32[]{:S(2)}) collective-permute-start(bf16[80,1024]{1,0:T(8,128)(2,1)S(1)} %get-tuple-element.54), channel_id=1, source_target_pairs={{0,16},{16,32},{32,48},{48,0},{1,17},{17,33},{33,49},{49,1},{2,18}... | collective-permute-start | bytes 491528 | tf_op jit(solution)/shard_map/ppermute | solution.py:377
  32.8 1.5 %collective-permute-start.9 = (bf16[80,1024]{1,0:T(8,128)(2,1)S(1)}, bf16[80,1024]{1,0:T(8,128)(2,1)}, u32[]{:S(2)}, u32[]{:S(2)}) collective-permute-start(bf16[80,1024]{1,0:T(8,128)(2,1)S(1)} %get-tuple-element.56), channel_id=1, source_target_pairs={{0,48},{16,0},{32,16},{48,32},{1,49},{17,1},{33,17},{49,33},{2,50}... | collective-permute-start | bytes 491528 | tf_op jit(solution)/shard_map/ppermute | solution.py:377
  34.3 0.8 %shard_map.175 = (bf16[96,1024]{1,0:T(8,128)(2,1)}, bf16[112,1024]{1,0:T(8,128)(2,1)}, bf16[160,1024]{1,0:T(8,128)(2,1)S(1)}) custom-call(bf16[64,1024]{1,0:T(8,128)(2,1)S(1)} %get-tuple-element.50.keep, bf16[80,1024]{1,0:T(8,128)(2,1)S(1)} %collective-permute-done.6.swapped, bf16[4,32,1024]{2,1,0:T(8,128)(2,1)S(1)} %get-tuple-element.52.blocks), custom_call_target="tpu_custom_call" | custom-call | tf_op jit(solution)/shard_map/pallas_call | solution.py:364
  35.6 1.0 %collective-permute-start.8 = (bf16[96,1024]{1,0:T(8,128)(2,1)}, bf16[96,1024]{1,0:T(8,128)(2,1)S(1)}, u32[]{:S(2)}, u32[]{:S(2)}) collective-permute-start(bf16[96,1024]{1,0:T(8,128)(2,1)} %get-tuple-element.55), channel_id=1, source_target_pairs={{0,16},{16,32},{32,48},{48,0},{1,17},{17,33},{33,49},{49,1},{2,18}... | collective-permute-start | bytes 589832 | tf_op jit(solution)/shard_map/ppermute | solution.py:377
  36.6 1.8 %collective-permute-done.7.low_far = bf16[80,1024]{1,0:T(8,128)(2,1)} collective-permute-done((bf16[80,1024]{1,0:T(8,128)(2,1)S(1)}, bf16[80,1024]{1,0:T(8,128)(2,1)}, u32[]{:S(2)}, u32[]{:S(2)}) %collective-permute-start.7) | collective-permute-done | bytes 163872 | tf_op jit(solution)/shard_map/ppermute | solution.py:377
  38.4 2.7 %collective-permute-start.12 = (bf16[80,1024]{1,0:T(8,128)(2,1)}, bf16[80,1024]{1,0:T(8,128)(2,1)S(1)}, u32[]{:S(2)}, u32[]{:S(2)}) collective-permute-start(bf16[80,1024]{1,0:T(8,128)(2,1)} %collective-permute-done.9.high_far), channel_id=1, source_target_pairs={{0,48},{16,0},{32,16},{48,32},{1,49},{17,1},{33,17},{49,33},{2,50}... | collective-permute-start | bytes 491528 | tf_op jit(solution)/shard_map/ppermute | solution.py:377
  42.6 0.8 %copy.19.table = f32[32,4]{1,0:T(8,128)S(1)} copy(f32[32,4]{0,1:T(4,128)} %param.22) | data formatting | bytes 1024 | tf_op args[9]
  43.4 0.8 %pad_add_fusion = s32[640]{0:T(1024)S(1)} fusion(s32[127]{0:T(128)} %rev.9, s32[128]{0:T(128)S(1)} %broadcast_in_dim.19, s32[385]{0:T(512)} %slice.8), kind=kLoop, calls=%fused_computation | loop fusion | flops 1280 | bytes 5120 | tf_op jit(solution)/shard_map/concatenate | solution.py:409
  44.2 1.1 %shard_map.177.strip = f32[2,128,512]{2,1,0:T(8,128)S(1)} custom-call(s32[8,640]{1,0:T(8,128)S(1)} %broadcast_in_dim.20.near, f32[32,4]{1,0:T(8,128)S(1)} %copy.19.table), custom_call_target="tpu_custom_call" | custom-call | tf_op jit(solution)/shard_map/pallas_call | solution.py:364
  45.3 0.8 %collective-permute-done.11.far_low = bf16[80,1024]{1,0:T(8,128)(2,1)S(1)} collective-permute-done((bf16[80,1024]{1,0:T(8,128)(2,1)}, bf16[80,1024]{1,0:T(8,128)(2,1)S(1)}, u32[]{:S(2)}, u32[]{:S(2)}) %collective-permute-start.11) | collective-permute-done | bytes 163872 | tf_op jit(solution)/shard_map/ppermute | solution.py:377
  46.7 1.4 %collective-permute-start.14 = (bf16[4,32,1024]{2,1,0:T(8,128)(2,1)S(1)}, bf16[4,32,1024]{2,1,0:T(8,128)(2,1)S(1)}, u32[]{:S(2)}, u32[]{:S(2)}) collective-permute-start(bf16[4,32,1024]{2,1,0:T(8,128)(2,1)S(1)} %get-tuple-element.67.mine), channel_id=1, source_target_pairs={{0,4},{4,0},{1,5},{5,1},{2,6},{6,2},{3,7},{7,3},{8,12},{12,8},{9,1... | collective-permute-start | bytes 786440 | tf_op jit(solution)/shard_map/ppermute | solution.py:377
  48.1 2.9 %shard_map.178 = (bf16[4,528,256]{2,1,0:T(8,128)(2,1)S(1)}, bf16[4,48,256]{2,1,0:T(8,128)(2,1)S(1)}, bf16[4,48,256]{2,1,0:T(8,128)(2,1)S(1)}) custom-call(s32[1]{0:T(128)S(6)} %copy.20.lens, bf16[160,1024]{1,0:T(8,128)(2,1)S(1)} %get-tuple-element.53.b0, bf16[80,1024]{1,0:T(8,128)(2,1)} %collective-permute-done.7.low_far, ...), custom_call_target="tpu_custom_call" | custom-call | flops 6000000000 | tf_op jit(solution)/shard_map/pallas_call | solution.py:364
  51.7 1.4 %collective-permute-start.18 = (bf16[4,128,256]{2,1,0:T(8,128)(2,1)S(1)}, bf16[4,128,256]{2,1,0:T(8,128)(2,1)S(1)}, u32[]{:S(2)}, u32[]{:S(2)}) collective-permute-start(bf16[4,128,256]{2,1,0:T(8,128)(2,1)S(1)} %get-tuple-element.79), channel_id=1, source_target_pairs={{0,64},{64,0},{1,65},{65,1},{2,66},{66,2},{3,67},{67,3},{4,68},{68... | collective-permute-start | bytes 786440 | tf_op jit(solution)/shard_map/ppermute | solution.py:377
  53.2 0.8 %shard_map.181 = (bf16[80,640]{1,0:T(8,128)(2,1)S(1)}, bf16[4,48,512]{2,1,0:T(8,128)(2,1)S(1)}, f32[48,128]{1,0:T(8,128)S(1)}, bf16[48,512]{1,0:T(8,128)(2,1)S(1)}, f32[48,128]{1,0:T(8,128)S(1)}) custom-call(bf16[4,48,256]{2,1,0:T(8,128)(2,1)S(1)} %get-tuple-element.58.keep_r, bf16[4,48,256]{2,1,0:T(8,128)(2,1)S(1)} %collective-permute-done.13.got_r, ...), custom_call_target="tpu_custom_call" | custom-call | flops 300000000 | tf_op jit(solution)/shard_map/pallas_call | solution.py:364
  53.9 2.0 %collective-permute-start.16 = (bf16[80,640]{1,0:T(8,128)(2,1)S(1)}, bf16[80,640]{1,0:T(8,128)(2,1)S(1)}, u32[]{:S(2)}, u32[]{:S(2)}) collective-permute-start(bf16[80,640]{1,0:T(8,128)(2,1)S(1)} %get-tuple-element.71.msg2), channel_id=1, source_target_pairs={{0,2},{1,3},{2,0},{3,1},{4,6},{5,7},{6,4},{7,5},{8,10},{9,11},{10,... | collective-permute-start | bytes 307208 | tf_op jit(solution)/shard_map/ppermute | solution.py:377
  55.9 1.9 %shard_map.182 = (bf16[80,640]{1,0:T(8,128)(2,1)S(1)}, bf16[80,640]{1,0:T(8,128)(2,1)S(1)}, f32[80,640]{1,0:T(8,128)S(1)}) custom-call(bf16[4,48,512]{2,1,0:T(8,128)(2,1)S(1)} %get-tuple-element.69.g, f32[48,128]{1,0:T(8,128)S(1)} %get-tuple-element.70.sums, bf16[80,640]{1,0:T(8,128)(2,1)S(1)} %get-tuple-element.71.msg2, bf16[2048,512]{1,0:T(8,128)(2,1)S(1)} %copy-done, ...), custom_call_target="tpu_custom_call" | custom-call | flops 1000000000 | tf_op jit(solution)/shard_map/pallas_call | solution.py:364
  58.4 2.2 %collective-permute-start.17 = (bf16[80,640]{1,0:T(8,128)(2,1)S(1)}, bf16[80,640]{1,0:T(8,128)(2,1)S(1)}, u32[]{:S(2)}, u32[]{:S(2)}) collective-permute-start(bf16[80,640]{1,0:T(8,128)(2,1)S(1)} %get-tuple-element.74), channel_id=1, source_target_pairs={{0,3},{1,0},{2,1},{3,2},{4,7},{5,4},{6,5},{7,6},{8,11},{9,8},{10,9... | collective-permute-start | bytes 307208 | tf_op jit(solution)/shard_map/ppermute | solution.py:377
  60.6 1.7 %collective-permute-start.19 = (bf16[4,64,256]{2,1,0:T(8,128)(2,1)S(1)}, bf16[4,64,256]{2,1,0:T(8,128)(2,1)S(1)}, u32[]{:S(2)}, u32[]{:S(2)}) collective-permute-start(bf16[4,64,256]{2,1,0:T(8,128)(2,1)S(1)} %get-tuple-element.81), channel_id=1, source_target_pairs={{0,4},{4,0},{1,5},{5,1},{2,6},{6,2},{3,7},{7,3},{8,12},{12,8},{9,1... | collective-permute-start | bytes 393224 | tf_op jit(solution)/shard_map/ppermute | solution.py:377
  62.6 1.4 %shard_map.183 = (bf16[512,512]{1,0:T(8,128)(2,1)}, bf16[512,512]{1,0:T(8,128)(2,1)}) custom-call(s32[1]{0:T(128)S(6)} %copy.20.lens, f32[80,640]{1,0:T(8,128)S(1)} %get-tuple-element.72.keep, bf16[80,640]{1,0:T(8,128)(2,1)S(1)} %collective-permute-done.15.r1, bf16[80,640]{1,0:T(8,128)(2,1)S(1)} %collective-permute-done.16.r2, ...), custom_call_target="tpu_custom_call" | custom-call | flops 20000000000 | tf_op jit(solution)/shard_map/pallas_call | solution.py:364
  64.1 0.8 %shard_map.185 = (f32[64,512]{1,0:T(8,128)}, f32[64,512]{1,0:T(8,128)}, f32[64,512]{1,0:T(8,128)}, f32[64,512]{1,0:T(8,128)}) custom-call(f32[4,64,256]{2,1,0:T(8,128)S(1)} %get-tuple-element.80.own, bf16[4,64,256]{2,1,0:T(8,128)(2,1)S(1)} %collective-permute-done.19.other), custom_call_target="tpu_custom_call" | custom-call | flops 6000000000 | tf_op jit(solution)/shard_map/pallas_call | solution.py:364
  (64 shorter events, 5.2 us)
Async XLA Ops:
  3.2 23.5 %copy-start.14 = (f32[1,2048]{1,0:T(1,128)}, f32[1,2048]{1,0:T(1,128)S(1)}, u32[]{:S(2)}) copy-start(f32[1,2048]{1,0:T(1,128)S(1)} %get-tuple-element.49.gain) | copy-start | bytes 24580
  3.2 13.1 %collective-permute-start = (bf16[80,512]{1,0:T(8,128)(2,1)S(1)}, bf16[80,512]{1,0:T(8,128)(2,1)S(1)}, u32[]{:S(2)}, u32[]{:S(2)}) collective-permute-start(bf16[80,512]{1,0:T(8,128)(2,1)S(1)} %get-tuple-element.46.piece), channel_id=1, source_target_pairs={{0,8},{8,0},{1,9},{9,1},{2,10},{10,2},{3,11},{11,3},{4,12},{12,4},... | collective-permute-start | bytes 245768 | tf_op jit(solution)/shard_map/ppermute | solution.py:377
  7.0 4.6 %collective-permute-start.1 = (f32[8,512]{1,0:T(8,128)S(1)}, f32[8,512]{1,0:T(8,128)S(1)}, u32[]{:S(2)}, u32[]{:S(2)}) collective-permute-start(f32[8,512]{1,0:T(8,128)S(1)} %get-tuple-element.48), channel_id=1, source_target_pairs={{0,4},{4,8},{8,12},{12,16},{16,20},{20,24},{24,28},{28,32},{32,36}... | collective-permute-start | bytes 49160 | tf_op jit(solution)/shard_map/ppermute | solution.py:397
  9.8 6.6 %collective-permute-start.2 = (f32[8,512]{1,0:T(8,128)S(1)}, f32[8,512]{1,0:T(8,128)S(1)}, u32[]{:S(2)}, u32[]{:S(2)}) collective-permute-start(f32[8,512]{1,0:T(8,128)S(1)} %get-tuple-element.48), channel_id=1, source_target_pairs={{0,12},{4,0},{8,4},{12,24},{16,28},{20,16},{24,20},{28,40},{32,44}... | collective-permute-start | bytes 49160 | tf_op jit(solution)/shard_map/ppermute | solution.py:400
  16.3 10.4 %copy-start = (bf16[2048,512]{1,0:T(8,128)(2,1)S(1)}, bf16[2048,512]{1,0:T(8,128)(2,1)}, u32[]{:S(2)}) copy-start(bf16[2048,512]{1,0:T(8,128)(2,1)} %wq.5) | copy-start | bytes 6291460
  16.3 10.4 %copy-start.1 = (bf16[2048,512]{1,0:T(8,128)(2,1)S(1)}, bf16[2048,512]{1,0:T(8,128)(2,1)}, u32[]{:S(2)}) copy-start(bf16[2048,512]{1,0:T(8,128)(2,1)} %wk.5) | copy-start | bytes 6291460
  16.3 10.4 %copy-start.3 = (bf16[2048,512]{1,0:T(8,128)(2,1)S(1)}, bf16[2048,512]{1,0:T(8,128)(2,1)}, u32[]{:S(2)}) copy-start(bf16[2048,512]{1,0:T(8,128)(2,1)} %wv.5) | copy-start | bytes 6291460
  16.3 10.4 %copy-start.5 = (bf16[2048,512]{1,0:T(8,128)(2,1)S(1)}, bf16[2048,512]{1,0:T(8,128)(2,1)}, u32[]{:S(2)}) copy-start(bf16[2048,512]{1,0:T(8,128)(2,1)} %wo.5) | copy-start | bytes 6291460
  16.4 6.8 %collective-permute-start.3 = (bf16[128,512]{1,0:T(8,128)(2,1)S(1)}, bf16[128,512]{1,0:T(8,128)(2,1)S(1)}, u32[]{:S(2)}, u32[]{:S(2)}) collective-permute-start(bf16[128,512]{1,0:T(8,128)(2,1)S(1)} %shard_map.173.p0), channel_id=1, source_target_pairs={{0,1},{1,2},{2,3},{3,0},{4,5},{5,6},{6,7},{7,4},{8,9},{9,10},{10,1... | collective-permute-start | bytes 393224 | tf_op jit(solution)/shard_map/ppermute | solution.py:377
  18.2 8.3 %collective-permute-start.4 = (bf16[128,512]{1,0:T(8,128)(2,1)S(1)}, bf16[128,512]{1,0:T(8,128)(2,1)S(1)}, u32[]{:S(2)}, u32[]{:S(2)}) collective-permute-start(bf16[128,512]{1,0:T(8,128)(2,1)S(1)} %shard_map.173.p0), channel_id=1, source_target_pairs={{0,2},{1,3},{2,0},{3,1},{4,6},{5,7},{6,4},{7,5},{8,10},{9,11},{10,... | collective-permute-start | bytes 393224 | tf_op jit(solution)/shard_map/ppermute | solution.py:377
  21.5 5.2 %collective-permute-start.5 = (bf16[128,512]{1,0:T(8,128)(2,1)S(1)}, bf16[128,512]{1,0:T(8,128)(2,1)S(1)}, u32[]{:S(2)}, u32[]{:S(2)}) collective-permute-start(bf16[128,512]{1,0:T(8,128)(2,1)S(1)} %shard_map.173.p0), channel_id=1, source_target_pairs={{0,3},{1,0},{2,1},{3,2},{4,7},{5,4},{6,5},{7,6},{8,11},{9,8},{10,9... | collective-permute-start | bytes 393224 | tf_op jit(solution)/shard_map/ppermute | solution.py:377
  26.7 14.4 %copy-start.16 = (s32[512]{0:T(512)S(1)}, s32[512]{0:T(512)}, u32[]{:S(2)}) copy-start(s32[512]{0:T(512)} %param.23) | copy-start | bytes 6148
  28.3 10.0 %copy-start.7 = (bf16[32,512]{1,0:T(8,128)(2,1)}, bf16[32,512]{1,0:T(8,128)(2,1)S(1)}, u32[]{:S(2)}) copy-start(bf16[32,512]{1,0:T(8,128)(2,1)S(1)} %get-tuple-element.62.cown) | copy-start | bytes 98308
  28.4 10.0 %copy-start.10 = (f32[32,128]{1,0:T(8,128)}, f32[32,128]{1,0:T(8,128)S(1)}, u32[]{:S(2)}) copy-start(f32[32,128]{1,0:T(8,128)S(1)} %get-tuple-element.64.iown) | copy-start | bytes 49156
  28.4 3.2 %collective-permute-start.6 = (bf16[80,1024]{1,0:T(8,128)(2,1)S(1)}, bf16[80,1024]{1,0:T(8,128)(2,1)S(1)}, u32[]{:S(2)}, u32[]{:S(2)}) collective-permute-start(bf16[80,1024]{1,0:T(8,128)(2,1)S(1)} %get-tuple-element.51), channel_id=1, source_target_pairs={{0,4},{4,0},{1,5},{5,1},{2,6},{6,2},{3,7},{7,3},{8,12},{12,8},{9,1... | collective-permute-start | bytes 491528 | tf_op jit(solution)/shard_map/ppermute | solution.py:377
  31.6 6.8 %collective-permute-start.7 = (bf16[80,1024]{1,0:T(8,128)(2,1)S(1)}, bf16[80,1024]{1,0:T(8,128)(2,1)}, u32[]{:S(2)}, u32[]{:S(2)}) collective-permute-start(bf16[80,1024]{1,0:T(8,128)(2,1)S(1)} %get-tuple-element.54), channel_id=1, source_target_pairs={{0,16},{16,32},{32,48},{48,0},{1,17},{17,33},{33,49},{49,1},{2,18}... | collective-permute-start | bytes 491528 | tf_op jit(solution)/shard_map/ppermute | solution.py:377
  32.8 5.5 %collective-permute-start.9 = (bf16[80,1024]{1,0:T(8,128)(2,1)S(1)}, bf16[80,1024]{1,0:T(8,128)(2,1)}, u32[]{:S(2)}, u32[]{:S(2)}) collective-permute-start(bf16[80,1024]{1,0:T(8,128)(2,1)S(1)} %get-tuple-element.56), channel_id=1, source_target_pairs={{0,48},{16,0},{32,16},{48,32},{1,49},{17,1},{33,17},{49,33},{2,50}... | collective-permute-start | bytes 491528 | tf_op jit(solution)/shard_map/ppermute | solution.py:377
  35.1 10.1 %collective-permute-start.10 = (bf16[112,1024]{1,0:T(8,128)(2,1)}, bf16[112,1024]{1,0:T(8,128)(2,1)S(1)}, u32[]{:S(2)}, u32[]{:S(2)}) collective-permute-start(bf16[112,1024]{1,0:T(8,128)(2,1)} %get-tuple-element.57), channel_id=1, source_target_pairs={{0,48},{16,0},{32,16},{48,32},{1,49},{17,1},{33,17},{49,33},{2,50}... | collective-permute-start | bytes 688136 | tf_op jit(solution)/shard_map/ppermute | solution.py:377
  35.6 9.7 %collective-permute-start.8 = (bf16[96,1024]{1,0:T(8,128)(2,1)}, bf16[96,1024]{1,0:T(8,128)(2,1)S(1)}, u32[]{:S(2)}, u32[]{:S(2)}) collective-permute-start(bf16[96,1024]{1,0:T(8,128)(2,1)} %get-tuple-element.55), channel_id=1, source_target_pairs={{0,16},{16,32},{32,48},{48,0},{1,17},{17,33},{33,49},{49,1},{2,18}... | collective-permute-start | bytes 589832 | tf_op jit(solution)/shard_map/ppermute | solution.py:377
  38.4 7.7 %collective-permute-start.11 = (bf16[80,1024]{1,0:T(8,128)(2,1)}, bf16[80,1024]{1,0:T(8,128)(2,1)S(1)}, u32[]{:S(2)}, u32[]{:S(2)}) collective-permute-start(bf16[80,1024]{1,0:T(8,128)(2,1)} %collective-permute-done.7.low_far), channel_id=1, source_target_pairs={{0,16},{16,32},{32,48},{48,0},{1,17},{17,33},{33,49},{49,1},{2,18}... | collective-permute-start | bytes 491528 | tf_op jit(solution)/shard_map/ppermute | solution.py:377
  38.4 8.1 %collective-permute-start.12 = (bf16[80,1024]{1,0:T(8,128)(2,1)}, bf16[80,1024]{1,0:T(8,128)(2,1)S(1)}, u32[]{:S(2)}, u32[]{:S(2)}) collective-permute-start(bf16[80,1024]{1,0:T(8,128)(2,1)} %collective-permute-done.9.high_far), channel_id=1, source_target_pairs={{0,48},{16,0},{32,16},{48,32},{1,49},{17,1},{33,17},{49,33},{2,50}... | collective-permute-start | bytes 491528 | tf_op jit(solution)/shard_map/ppermute | solution.py:377
  46.7 4.5 %collective-permute-start.14 = (bf16[4,32,1024]{2,1,0:T(8,128)(2,1)S(1)}, bf16[4,32,1024]{2,1,0:T(8,128)(2,1)S(1)}, u32[]{:S(2)}, u32[]{:S(2)}) collective-permute-start(bf16[4,32,1024]{2,1,0:T(8,128)(2,1)S(1)} %get-tuple-element.67.mine), channel_id=1, source_target_pairs={{0,4},{4,0},{1,5},{5,1},{2,6},{6,2},{3,7},{7,3},{8,12},{12,8},{9,1... | collective-permute-start | bytes 786440 | tf_op jit(solution)/shard_map/ppermute | solution.py:377
  51.1 2.0 %collective-permute-start.13 = (bf16[4,48,256]{2,1,0:T(8,128)(2,1)S(1)}, bf16[4,48,256]{2,1,0:T(8,128)(2,1)S(1)}, u32[]{:S(2)}, u32[]{:S(2)}) collective-permute-start(bf16[4,48,256]{2,1,0:T(8,128)(2,1)S(1)} %get-tuple-element.59), channel_id=1, source_target_pairs={{0,4},{4,0},{1,5},{5,1},{2,6},{6,2},{3,7},{7,3},{8,12},{12,8},{9,1... | collective-permute-start | bytes 294920 | tf_op jit(solution)/shard_map/ppermute | solution.py:377
  51.7 8.8 %collective-permute-start.18 = (bf16[4,128,256]{2,1,0:T(8,128)(2,1)S(1)}, bf16[4,128,256]{2,1,0:T(8,128)(2,1)S(1)}, u32[]{:S(2)}, u32[]{:S(2)}) collective-permute-start(bf16[4,128,256]{2,1,0:T(8,128)(2,1)S(1)} %get-tuple-element.79), channel_id=1, source_target_pairs={{0,64},{64,0},{1,65},{65,1},{2,66},{66,2},{3,67},{67,3},{4,68},{68... | collective-permute-start | bytes 786440 | tf_op jit(solution)/shard_map/ppermute | solution.py:377
  53.9 6.6 %collective-permute-start.16 = (bf16[80,640]{1,0:T(8,128)(2,1)S(1)}, bf16[80,640]{1,0:T(8,128)(2,1)S(1)}, u32[]{:S(2)}, u32[]{:S(2)}) collective-permute-start(bf16[80,640]{1,0:T(8,128)(2,1)S(1)} %get-tuple-element.71.msg2), channel_id=1, source_target_pairs={{0,2},{1,3},{2,0},{3,1},{4,6},{5,7},{6,4},{7,5},{8,10},{9,11},{10,... | collective-permute-start | bytes 307208 | tf_op jit(solution)/shard_map/ppermute | solution.py:377
  55.9 6.7 %copy-start.9 = (f32[16,512]{1,0:T(8,128)S(1)}, f32[16,512]{1,0:T(8,128)}, u32[]{:S(2)}) copy-start(f32[16,512]{1,0:T(8,128)} %up_gain.1) | copy-start | bytes 98308
  55.9 6.7 %copy-start.12 = (f32[4,512]{1,0:T(4,128)S(1)}, f32[4,512]{1,0:T(4,128)}, u32[]{:S(2)}) copy-start(f32[4,512]{1,0:T(4,128)} %first.1) | copy-start | bytes 24580
  55.9 6.7 %copy-start.13 = (f32[4,512]{1,0:T(4,128)S(1)}, f32[4,512]{1,0:T(4,128)}, u32[]{:S(2)}) copy-start(f32[4,512]{1,0:T(4,128)} %second.1) | copy-start | bytes 24580
  55.9 6.7 %copy-start.15 = (f32[1,2048]{1,0:T(1,128)S(1)}, f32[1,2048]{1,0:T(1,128)}, u32[]{:S(2)}) copy-start(f32[1,2048]{1,0:T(1,128)} %copy-done.14) | copy-start | bytes 24580
  57.9 4.7 %collective-permute-start.15 = (bf16[80,640]{1,0:T(8,128)(2,1)S(1)}, bf16[80,640]{1,0:T(8,128)(2,1)S(1)}, u32[]{:S(2)}, u32[]{:S(2)}) collective-permute-start(bf16[80,640]{1,0:T(8,128)(2,1)S(1)} %get-tuple-element.73), channel_id=1, source_target_pairs={{0,1},{1,2},{2,3},{3,0},{4,5},{5,6},{6,7},{7,4},{8,9},{9,10},{10,1... | collective-permute-start | bytes 307208 | tf_op jit(solution)/shard_map/ppermute | solution.py:377
  58.4 4.2 %collective-permute-start.17 = (bf16[80,640]{1,0:T(8,128)(2,1)S(1)}, bf16[80,640]{1,0:T(8,128)(2,1)S(1)}, u32[]{:S(2)}, u32[]{:S(2)}) collective-permute-start(bf16[80,640]{1,0:T(8,128)(2,1)S(1)} %get-tuple-element.74), channel_id=1, source_target_pairs={{0,3},{1,0},{2,1},{3,2},{4,7},{5,4},{6,5},{7,6},{8,11},{9,8},{10,9... | collective-permute-start | bytes 307208 | tf_op jit(solution)/shard_map/ppermute | solution.py:377
  60.6 3.5 %collective-permute-start.19 = (bf16[4,64,256]{2,1,0:T(8,128)(2,1)S(1)}, bf16[4,64,256]{2,1,0:T(8,128)(2,1)S(1)}, u32[]{:S(2)}, u32[]{:S(2)}) collective-permute-start(bf16[4,64,256]{2,1,0:T(8,128)(2,1)S(1)} %get-tuple-element.81), channel_id=1, source_target_pairs={{0,4},{4,0},{1,5},{5,1},{2,6},{6,2},{3,7},{7,3},{8,12},{12,8},{9,1... | collective-permute-start | bytes 393224 | tf_op jit(solution)/shard_map/ppermute | solution.py:377
  (5 other events, 16.3 us)
